TPU v7x, 32 devices: a whole 2x2x4 slice. The times are simulated.
32 devices in a mesh: genome: 16 (over z, y, x), sample: 2 (over core).
Axes of the slice: x: 2, y: 2, z: 4, core: 2. Of those that a mesh axis runs over, the one named last changes fastest.
Arguments:
- genotypes: bfloat16 [8192, 8192], P('genome', 'sample'), may hold values from 0.049804688 to 2
- phenotypes: bfloat16 [1024, 8192], P('genome', 'sample'), may hold values from -60 to 60
- environment: float32 [8192], P('sample'), may hold values from 0.3 to 3
- shuffles: int32 [4, 8192], P(None, 'sample'), may hold values from 0 to 8191, each once within a row
- window_start: int32 [1024], replicated, may hold values from 0 to 31, as said below
- window_end: int32 [1024], replicated, may hold values from 1 to 32, as said below
- chrom_bounds: int32 [15], replicated, may hold values from 1 to 31, as said below
Outputs:
- maxima: float32 [5, 1024], P(None, 'genome')
Inputs may be any that keep to these rules, and one draw needn't show every extreme that they name: `window_start`: for gene g on genome index d = g // 64 the window is [c - l, c + r + 1) cut to [0, 32), where d * 2 <= c < (d + 1) * 2 and 1 <= l, r <= 7; the first gene of every index has c = d * 2 and l = 7, the last has c = (d + 1) * 2 - 1 and r = 7. `window_end`: the end of the window described for window_start. `chrom_bounds`: strictly increasing.
All inputs are finite; a program needn't handle non-finite values.
Results may differ from a plain program's by a relative error of at most 0.0024.
Values may be sent and summed in bfloat16 or wider, within the bound.
No kernel may reach another device: no remote copies, remote signals or barrier semaphores. Data moves between devices by JAX's collectives and lax.ppermute only.
A program may use at most 128 MiB of HBM per device.

v0:
```python
import jax
import jax.numpy as jnp
from jax import lax
from jax.sharding import PartitionSpec as P

SNP_BLOCK = 256
HALF_BLK = 7


def passed_along(x, axis, by):
    count = lax.axis_size(axis)
    pairs = [(i, i + by) for i in range(count) if 0 <= i + by < count]
    return lax.ppermute(x, axis, pairs)


def window_bounds(window_start, window_end, chrom_bounds, total_blocks):
    middle = (window_start + window_end - 1) // 2
    before = chrom_bounds[None, :] <= middle[:, None]
    lower_edge = jnp.max(jnp.where(before, chrom_bounds[None, :], 0), axis=1)
    upper_edge = jnp.min(jnp.where(before, total_blocks, chrom_bounds[None, :]), axis=1)
    return (jnp.maximum(window_start, lower_edge), jnp.minimum(window_end, upper_edge))


def window_scores(reduced, square_sum, cross_sum, inter_sum):
    half_cols = reduced.shape[1] // 2
    marginal = reduced[:, :half_cols]
    interact = reduced[:, half_cols:]
    regression = cross_sum / square_sum
    resid_norm = inter_sum - cross_sum * regression
    divisor = resid_norm + 0.1 * inter_sum
    numerator = interact - regression[:, None] * marginal
    return numerator * numerator / divisor[:, None]


def label_rows(local_rows, whole_rows, shuffles):
    labels = shuffles.shape[0] + 1
    shuffled = jnp.take(whole_rows, shuffles, axis=1)
    block = jnp.concatenate([local_rows[None], jnp.transpose(shuffled, (1, 0, 2))], axis=0)
    return block.reshape(labels * local_rows.shape[0], local_rows.shape[1])


def shards(genotypes, phenotypes, environment, shuffles, window_start, window_end, chrom_bounds):
    snp_rows, local_samples = genotypes.shape
    gene_rows = phenotypes.shape[0]
    labels = shuffles.shape[0] + 1
    genome_size = lax.axis_size("genome")
    sample_size = lax.axis_size("sample")
    genome_pos = lax.axis_index("genome")
    sample_pos = lax.axis_index("sample")
    blocks_dev = snp_rows // SNP_BLOCK
    reach_dev = (HALF_BLK + blocks_dev - 1) // blocks_dev
    total_blocks = snp_rows * genome_size // SNP_BLOCK
    full_rows = lax.all_gather(phenotypes, "sample", axis=1, tiled=True)
    all_samples = full_rows.shape[1]
    row_power = jnp.sum(jnp.square(full_rows.astype(jnp.float32)), axis=1)
    own_block = label_rows(phenotypes, full_rows, shuffles)
    geno_float = genotypes.astype(jnp.float32)
    squares = geno_float * geno_float
    local_moments = jnp.stack(
        [
            jnp.sum(squares, axis=1),
            jnp.sum(squares * environment[None, :], axis=1),
            jnp.sum(squares * (environment * environment)[None, :], axis=1),
        ]
    )
    moments = lax.psum(local_moments, "sample")
    share_rows = snp_rows // sample_size
    first_row = sample_pos * share_rows
    row_moments = lax.dynamic_slice_in_dim(moments, first_row, share_rows, 1)
    row_blocks = (
        genome_pos * snp_rows + first_row + jnp.arange(share_rows, dtype=jnp.int32)
    ) // SNP_BLOCK
    lower_edge, upper_edge = window_bounds(window_start, window_end, chrom_bounds, total_blocks)
    padding = jnp.zeros((reach_dev * gene_rows,), jnp.int32)
    band_slots = 2 * reach_dev + 1
    lower_band = lax.dynamic_slice_in_dim(
        jnp.concatenate([padding, lower_edge, padding]),
        genome_pos * gene_rows,
        band_slots * gene_rows,
        0,
    ).reshape(band_slots, gene_rows)
    upper_band = lax.dynamic_slice_in_dim(
        jnp.concatenate([padding, upper_edge, padding]),
        genome_pos * gene_rows,
        band_slots * gene_rows,
        0,
    ).reshape(band_slots, gene_rows)
    pieces = {0: own_block}
    for offset in range(-reach_dev, reach_dev + 1):
        if offset != 0:
            pieces[offset] = passed_along(own_block, "genome", -offset)
    partials = []
    for offset in range(-reach_dev, reach_dev + 1):
        incoming = pieces[offset]
        weighted = (incoming.astype(jnp.float32) * environment[None, :]).astype(jnp.bfloat16)
        operand = jnp.concatenate([incoming, weighted], axis=0)

        def product(start_row, row_count, operand=operand):
            return lax.dot_general(
                genotypes, operand, (((1,), (1,)), ((), ())), preferred_element_type=jnp.float32
            )

        reduced = lax.psum_scatter(
            product(jnp.int32(0), lax.axis_size("sample") * share_rows),
            "sample",
            scatter_dimension=0,
            tiled=True,
        )
        scores = window_scores(reduced, row_moments[0], row_moments[1], row_moments[2])
        scores = scores.reshape(share_rows, labels, gene_rows)
        slot_index = offset + reach_dev
        inside = (row_blocks[:, None] >= lower_band[slot_index][None, :]) & (
            row_blocks[:, None] < upper_band[slot_index][None, :]
        )
        partials.append(jnp.max(jnp.where(inside[:, None, :], scores, 0.0), axis=0))
    best_peak = partials[reach_dev]
    for offset in range(-reach_dev, reach_dev + 1):
        if offset != 0:
            arrived = passed_along(partials[offset + reach_dev], "genome", offset)
            best_peak = jnp.maximum(best_peak, arrived)
    best_peak = lax.pmax(best_peak, "sample")
    return jnp.sqrt(best_peak / (row_power[None, :] / all_samples + 1e-05))


def solution(mesh):
    placed = (
        P("genome", "sample"),
        P("genome", "sample"),
        P("sample"),
        P(None, "sample"),
        P(),
        P(),
        P(),
    )
    return jax.shard_map(
        shards, mesh=mesh, in_specs=placed, out_specs=P(None, "genome"), check_vma=False
    )
```

profile of v0, /device:TPU:0, one launch (start us, length us, event | category | flops | bytes accessed | tf_op | source)
XLA Modules:
  0.0 590.5 jit_solution(1958664540041762025)
XLA Ops:
  10.8 11.6 %all-gather.2.cloned.1.call-done = bf16[64,8192]{0,1:T(8,128)(2,1)} async-done(((bf16[64,4096]{0,1:T(8,128)(2,1)}), bf16[64,8192]{0,1:T(8,128)(2,1)}) %all-gather.2.cloned.1.call-update) | async-done | bytes 1048592 | tf_op jit(solution)/shard_map/all_gather | solution.py:53
  22.4 56.8 %gather_fusion = bf16[16384,64]{1,0:T(8,128)(2,1)} fusion(bf16[64,8192]{0,1:T(8,128)(2,1)} %all-gather.2.cloned.1.call-done, s32[16384]{0:T(1024)S(1)} %broadcast_clamp_fusion), kind=kCustom, calls=%fused_computation | custom fusion | bytes 4259840 | tf_op jit(solution)/shard_map/jit(_take)/gather | solution.py:37
  79.2 3.6 copy.13
  87.2 4.7 collective-permute-start.6
  91.9 4.6 collective-permute-start.4
  96.5 49.3 %collective-permute-done.12 = bf16[320,4096]{1,0:T(8,128)(2,1)S(1)} collective-permute-done((bf16[320,4096]{1,0:T(8,128)(2,1)S(1)}, bf16[320,4096]{1,0:T(8,128)(2,1)S(1)}, u32[]{:S(2)}, u32[]{:S(2)}) %collective-permute-start.12) | collective-permute-done | bytes 2621472 | tf_op jit(solution)/shard_map/ppermute | solution.py:13
  145.8 4.1 collective-permute-start.2
  149.9 51.4 %collective-permute-done.10 = bf16[320,4096]{1,0:T(8,128)(2,1)S(1)} collective-permute-done((bf16[320,4096]{1,0:T(8,128)(2,1)S(1)}, bf16[320,4096]{1,0:T(8,128)(2,1)S(1)}, u32[]{:S(2)}, u32[]{:S(2)}) %collective-permute-start.10) | collective-permute-done | bytes 2621472 | tf_op jit(solution)/shard_map/ppermute | solution.py:13
  201.3 116.2 %collective-permute-start = (bf16[320,4096]{1,0:T(8,128)(2,1)S(1)}, bf16[320,4096]{1,0:T(8,128)(2,1)S(1)}, u32[]{:S(2)}, u32[]{:S(2)}) collective-permute-start(bf16[320,4096]{1,0:T(8,128)(2,1)S(1)} %bitcast.57), channel_id=1, source_target_pairs={{0,8},{2,10},{4,12},{6,14},{8,16},{10,18},{12,20},{14,22},{16,24},... | collective-permute-start | bytes 7864328 | tf_op jit(solution)/shard_map/ppermute | solution.py:13
  318.9 54.7 %collective-permute-done = bf16[320,4096]{1,0:T(8,128)(2,1)S(1)} collective-permute-done((bf16[320,4096]{1,0:T(8,128)(2,1)S(1)}, bf16[320,4096]{1,0:T(8,128)(2,1)S(1)}, u32[]{:S(2)}, u32[]{:S(2)}) %collective-permute-start) | collective-permute-done | bytes 2621472 | tf_op jit(solution)/shard_map/ppermute | solution.py:13
  378.0 14.7 %multiply_convert_fusion.3 = (bf16[320,4096]{1,0:T(8,128)(2,1)}, bf16[320,4096]{1,0:T(8,128)(2,1)}, bf16[320,4096]{1,0:T(8,128)(2,1)}, bf16[320,4096]{1,0:T(8,12...) fusion(bf16[320,4096]{1,0:T(8,128)(2,1)} %copy-done.5, ...), kind=kLoop, calls=%fused_computation.44 | loop fusion | flops 35389440 | bytes 47202304 | tf_op jit(solution)/shard_map/convert_element_type | solution.py:95
  392.8 7.8 %fusion.58 = f32[512,640]{0,1:T(8,128)} fusion(bf16[512,4096]{1,0:T(8,128)(2,1)} %param.7, bf16[320,4096]{1,0:T(8,128)(2,1)} %get-tuple-element.22, bf16[320,4096]{1,0:T(8,128)(2,1)} %copy-done.7), kind=kOutput, calls=%fused_computation.60 | convolution fusion | flops 2694840320 | bytes 10747904 | tf_op jit(solution)/shard_map/dot_general | solution.py:99
  400.8 7.7 %fusion.46 = f32[512,640]{0,1:T(8,128)} fusion(bf16[512,4096]{1,0:T(8,128)(2,1)} %param.7, bf16[320,4096]{1,0:T(8,128)(2,1)} %get-tuple-element.21, bf16[320,4096]{1,0:T(8,128)(2,1)} %copy-done.5), kind=kOutput, calls=%fused_computation.56 | convolution fusion | flops 2694840320 | bytes 10747904 | tf_op jit(solution)/shard_map/dot_general | solution.py:99
  408.6 7.7 %fusion.55 = f32[512,640]{0,1:T(8,128)} fusion(bf16[512,4096]{1,0:T(8,128)(2,1)} %param.7, bf16[320,4096]{1,0:T(8,128)(2,1)} %get-tuple-element.23, bf16[320,4096]{1,0:T(8,128)(2,1)} %copy-done.6), kind=kOutput, calls=%fused_computation.59 | convolution fusion | flops 2694840320 | bytes 10747904 | tf_op jit(solution)/shard_map/dot_general | solution.py:99
  416.4 7.7 %fusion.52 = f32[512,640]{0,1:T(8,128)} fusion(bf16[512,4096]{1,0:T(8,128)(2,1)} %param.7, bf16[320,4096]{1,0:T(8,128)(2,1)} %get-tuple-element.24, bf16[320,4096]{1,0:T(8,128)(2,1)} %copy-done.4), kind=kOutput, calls=%fused_computation.58 | convolution fusion | flops 2694840320 | bytes 10747904 | tf_op jit(solution)/shard_map/dot_general | solution.py:99
  424.2 7.7 %fusion.49 = f32[512,640]{0,1:T(8,128)} fusion(bf16[512,4096]{1,0:T(8,128)(2,1)} %param.7, bf16[320,4096]{1,0:T(8,128)(2,1)} %get-tuple-element.25, bf16[320,4096]{1,0:T(8,128)(2,1)} %copy-done.3), kind=kOutput, calls=%fused_computation.57 | convolution fusion | flops 2694840320 | bytes 10747904 | tf_op jit(solution)/shard_map/dot_general | solution.py:99
  432.2 7.7 %fusion.43 = f32[512,640]{0,1:T(8,128)} fusion(bf16[512,4096]{1,0:T(8,128)(2,1)} %param.7, bf16[320,4096]{1,0:T(8,128)(2,1)} %get-tuple-element.26, bf16[320,4096]{1,0:T(8,128)(2,1)} %copy-done.2), kind=kOutput, calls=%fused_computation.55 | convolution fusion | flops 2694840320 | bytes 10747904 | tf_op jit(solution)/shard_map/dot_general | solution.py:99
  440.0 7.7 %fusion.40 = f32[512,640]{0,1:T(8,128)} fusion(bf16[512,4096]{1,0:T(8,128)(2,1)} %param.7, bf16[320,4096]{1,0:T(8,128)(2,1)} %get-tuple-element.27, bf16[320,4096]{1,0:T(8,128)(2,1)} %copy-done.1), kind=kOutput, calls=%fused_computation.54 | convolution fusion | flops 2694840320 | bytes 10747904 | tf_op jit(solution)/shard_map/dot_general | solution.py:99
  447.8 7.8 %fusion.37 = f32[512,640]{0,1:T(8,128)} fusion(bf16[512,4096]{1,0:T(8,128)(2,1)} %param.7, bf16[320,4096]{1,0:T(8,128)(2,1)} %get-tuple-element.28, bf16[320,4096]{1,0:T(8,128)(2,1)} %collective-permute-done.14), kind=kOutput, calls=%fused_computation.53 | convolution fusion | flops 2694840320 | bytes 10747904 | tf_op jit(solution)/shard_map/dot_general | solution.py:99
  455.7 7.4 %fusion.61 = f32[512,640]{0,1:T(8,128)} fusion(bf16[512,4096]{1,0:T(8,128)(2,1)} %param.7, bf16[320,4096]{1,0:T(8,128)(2,1)} %get-tuple-element.29, bf16[320,4096]{1,0:T(8,128)(2,1)S(1)} %bitcast.59), kind=kOutput, calls=%fused_computation.61 | convolution fusion | flops 2694840320 | bytes 10747904 | tf_op jit(solution)/shard_map/dot_general | solution.py:99
  463.4 3.9 fusion
  472.4 12.0 %reduce-scatter.14.cloned.1.call-done = f32[256,640]{0,1:T(8,128)} async-done(((f32[512,640]{0,1:T(8,128)}), f32[256,640]{0,1:T(8,128)}) %reduce-scatter.14.cloned.1.call-update) | async-done | bytes 655376 | tf_op jit(solution)/shard_map/reduce_scatter | solution.py:103
  484.4 12.2 %reduce-scatter.16.cloned.1.call-done = f32[256,640]{0,1:T(8,128)} async-done(((f32[512,640]{0,1:T(8,128)}), f32[256,640]{0,1:T(8,128)}) %reduce-scatter.16.cloned.1.call-update) | async-done | bytes 655376 | tf_op jit(solution)/shard_map/reduce_scatter | solution.py:103
  496.6 12.1 %reduce-scatter.18.cloned.1.call-done = f32[256,640]{0,1:T(8,128)} async-done(((f32[512,640]{0,1:T(8,128)}), f32[256,640]{0,1:T(8,128)}) %reduce-scatter.18.cloned.1.call-update) | async-done | bytes 655376 | tf_op jit(solution)/shard_map/reduce_scatter | solution.py:103
  511.5 3.7 collective-permute-start.9
  521.1 12.2 %reduce-scatter.24.cloned.1.call-done = f32[256,640]{0,1:T(8,128)} async-done(((f32[512,640]{0,1:T(8,128)}), f32[256,640]{0,1:T(8,128)}) %reduce-scatter.24.cloned.1.call-update) | async-done | bytes 655376 | tf_op jit(solution)/shard_map/reduce_scatter | solution.py:103
  533.3 12.4 %reduce-scatter.26.cloned.1.call-done = f32[256,640]{0,1:T(8,128)} async-done(((f32[512,640]{0,1:T(8,128)}), f32[256,640]{0,1:T(8,128)}) %reduce-scatter.26.cloned.1.call-update) | async-done | bytes 655376 | tf_op jit(solution)/shard_map/reduce_scatter | solution.py:103
  545.7 12.1 %reduce-scatter.10.cloned.1.call-done = f32[256,640]{0,1:T(8,128)} async-done(((f32[512,640]{0,1:T(8,128)}), f32[256,640]{0,1:T(8,128)}) %reduce-scatter.10.cloned.1.call-update) | async-done | bytes 655376 | tf_op jit(solution)/shard_map/reduce_scatter | solution.py:103
  561.6 5.7 collective-permute-start.15
  567.4 3.4 collective-permute-start.13
  570.8 4.3 collective-permute-start.11
  576.5 4.1 collective-permute-done.1
  (115 shorter events, 37.4 us)
Async XLA Ops:
  6.5 15.8 %all-gather.2.cloned.1.call-start = ((), (), s32[]{:S(2)}) async-start(), calls=%async_computation.9 | async-start | bytes 3145728 | tf_op jit(solution)/shard_map/all_gather | solution.py:53
  8.9 462.4 %reduce-scatter.12.cloned.1.call-start = ((), (), s32[]{:S(2)}) async-start(), calls=%async_computation.11 | async-start | bytes 1966080 | tf_op jit(solution)/shard_map/reduce_scatter | solution.py:103
  82.8 295.2 %copy-start.9 = (f32[4096]{0:T(1024)S(1)}, f32[4096]{0:T(1024)}, u32[]{:S(2)}) copy-start(f32[4096]{0:T(1024)} %param.9) | copy-start | bytes 49156
  83.3 62.5 %collective-permute-start.12 = (bf16[320,4096]{1,0:T(8,128)(2,1)S(1)}, bf16[320,4096]{1,0:T(8,128)(2,1)S(1)}, u32[]{:S(2)}, u32[]{:S(2)}) collective-permute-start(bf16[320,4096]{1,0:T(8,128)(2,1)S(1)} %bitcast.51), channel_id=1, source_target_pairs={{6,0},{8,2},{10,4},{12,6},{14,8},{16,10},{18,12},{20,14},{22,16},{... | collective-permute-start | bytes 7864328 | tf_op jit(solution)/shard_map/ppermute | solution.py:13
  84.6 116.7 %collective-permute-start.10 = (bf16[320,4096]{1,0:T(8,128)(2,1)S(1)}, bf16[320,4096]{1,0:T(8,128)(2,1)S(1)}, u32[]{:S(2)}, u32[]{:S(2)}) collective-permute-start(bf16[320,4096]{1,0:T(8,128)(2,1)S(1)} %bitcast.52), channel_id=1, source_target_pairs={{4,0},{6,2},{8,4},{10,6},{12,8},{14,10},{16,12},{18,14},{20,16},{2... | collective-permute-start | bytes 7864328 | tf_op jit(solution)/shard_map/ppermute | solution.py:13
  85.9 231.6 %collective-permute-start.8 = (bf16[320,4096]{1,0:T(8,128)(2,1)S(1)}, bf16[320,4096]{1,0:T(8,128)(2,1)S(1)}, u32[]{:S(2)}, u32[]{:S(2)}) collective-permute-start(bf16[320,4096]{1,0:T(8,128)(2,1)S(1)} %bitcast.53), channel_id=1, source_target_pairs={{2,0},{4,2},{6,4},{8,6},{10,8},{12,10},{14,12},{16,14},{18,16},{20... | collective-permute-start | bytes 7864328 | tf_op jit(solution)/shard_map/ppermute | solution.py:13
  87.2 231.6 %collective-permute-start.6 = (bf16[320,4096]{1,0:T(8,128)(2,1)S(1)}, bf16[320,4096]{1,0:T(8,128)(2,1)S(1)}, u32[]{:S(2)}, u32[]{:S(2)}) collective-permute-start(bf16[320,4096]{1,0:T(8,128)(2,1)S(1)} %bitcast.54), channel_id=1, source_target_pairs={{0,2},{2,4},{4,6},{6,8},{8,10},{10,12},{12,14},{14,16},{16,18},{18... | collective-permute-start | bytes 7864328 | tf_op jit(solution)/shard_map/ppermute | solution.py:13
  91.9 226.9 %collective-permute-start.4 = (bf16[320,4096]{1,0:T(8,128)(2,1)S(1)}, bf16[320,4096]{1,0:T(8,128)(2,1)S(1)}, u32[]{:S(2)}, u32[]{:S(2)}) collective-permute-start(bf16[320,4096]{1,0:T(8,128)(2,1)S(1)} %bitcast.55), channel_id=1, source_target_pairs={{0,4},{2,6},{4,8},{6,10},{8,12},{10,14},{12,16},{14,18},{16,20},{1... | collective-permute-start | bytes 7864328 | tf_op jit(solution)/shard_map/ppermute | solution.py:13
  145.8 247.0 %copy-start.1 = (bf16[320,4096]{1,0:T(8,128)(2,1)}, bf16[320,4096]{1,0:T(8,128)(2,1)S(1)}, u32[]{:S(2)}) copy-start(bf16[320,4096]{1,0:T(8,128)(2,1)S(1)} %collective-permute-done.12) | copy-start | bytes 7864324
  145.8 173.0 %collective-permute-start.2 = (bf16[320,4096]{1,0:T(8,128)(2,1)S(1)}, bf16[320,4096]{1,0:T(8,128)(2,1)S(1)}, u32[]{:S(2)}, u32[]{:S(2)}) collective-permute-start(bf16[320,4096]{1,0:T(8,128)(2,1)S(1)} %bitcast.56), channel_id=1, source_target_pairs={{0,6},{2,8},{4,10},{6,12},{8,14},{10,16},{12,18},{14,20},{16,22},{... | collective-permute-start | bytes 7864328 | tf_op jit(solution)/shard_map/ppermute | solution.py:13
  201.3 172.3 %copy-start.2 = (bf16[320,4096]{1,0:T(8,128)(2,1)}, bf16[320,4096]{1,0:T(8,128)(2,1)S(1)}, u32[]{:S(2)}) copy-start(bf16[320,4096]{1,0:T(8,128)(2,1)S(1)} %collective-permute-done.10) | copy-start | bytes 7864324
  201.3 172.3 %collective-permute-start = (bf16[320,4096]{1,0:T(8,128)(2,1)S(1)}, bf16[320,4096]{1,0:T(8,128)(2,1)S(1)}, u32[]{:S(2)}, u32[]{:S(2)}) collective-permute-start(bf16[320,4096]{1,0:T(8,128)(2,1)S(1)} %bitcast.57), channel_id=1, source_target_pairs={{0,8},{2,10},{4,12},{6,14},{8,16},{10,18},{12,20},{14,22},{16,24},... | collective-permute-start | bytes 7864328 | tf_op jit(solution)/shard_map/ppermute | solution.py:13
  317.5 56.1 %copy-start.5 = (bf16[320,4096]{1,0:T(8,128)(2,1)}, bf16[320,4096]{1,0:T(8,128)(2,1)S(1)}, u32[]{:S(2)}) copy-start(bf16[320,4096]{1,0:T(8,128)(2,1)S(1)} %collective-permute-done.8) | copy-start | bytes 7864324
  317.5 60.5 %collective-permute-start.14 = (bf16[320,4096]{1,0:T(8,128)(2,1)S(1)}, bf16[320,4096]{1,0:T(8,128)(2,1)}, u32[]{:S(2)}, u32[]{:S(2)}) collective-permute-start(bf16[320,4096]{1,0:T(8,128)(2,1)S(1)} %bitcast.58), channel_id=1, source_target_pairs={{8,0},{10,2},{12,4},{14,6},{16,8},{18,10},{20,12},{22,14},{24,16},... | collective-permute-start | bytes 7864328 | tf_op jit(solution)/shard_map/ppermute | solution.py:13
  318.8 54.8 %copy-start.3 = (bf16[320,4096]{1,0:T(8,128)(2,1)}, bf16[320,4096]{1,0:T(8,128)(2,1)S(1)}, u32[]{:S(2)}) copy-start(bf16[320,4096]{1,0:T(8,128)(2,1)S(1)} %collective-permute-done.6) | copy-start | bytes 7864324
  318.8 54.8 %copy-start.4 = (bf16[320,4096]{1,0:T(8,128)(2,1)}, bf16[320,4096]{1,0:T(8,128)(2,1)S(1)}, u32[]{:S(2)}) copy-start(bf16[320,4096]{1,0:T(8,128)(2,1)S(1)} %collective-permute-done.4) | copy-start | bytes 7864324
  400.5 71.9 %reduce-scatter.20.cloned.1.call-start = ((), (), s32[]{:S(2)}) async-start(), calls=%async_computation.15 | async-start | bytes 1966080 | tf_op jit(solution)/shard_map/reduce_scatter | solution.py:103
  408.5 75.9 %reduce-scatter.14.cloned.1.call-start = ((), (), s32[]{:S(2)}) async-start(), calls=%async_computation.12 | async-start | bytes 1966080 | tf_op jit(solution)/shard_map/reduce_scatter | solution.py:103
  416.3 80.3 %reduce-scatter.16.cloned.1.call-start = ((), (), s32[]{:S(2)}) async-start(), calls=%async_computation.13 | async-start | bytes 1966080 | tf_op jit(solution)/shard_map/reduce_scatter | solution.py:103
  424.1 84.6 %reduce-scatter.18.cloned.1.call-start = ((), (), s32[]{:S(2)}) async-start(), calls=%async_computation.14 | async-start | bytes 1966080 | tf_op jit(solution)/shard_map/reduce_scatter | solution.py:103
  431.9 89.2 %reduce-scatter.22.cloned.1.call-start = ((), (), s32[]{:S(2)}) async-start(), calls=%async_computation.16 | async-start | bytes 1966080 | tf_op jit(solution)/shard_map/reduce_scatter | solution.py:103
  440.0 93.3 %reduce-scatter.24.cloned.1.call-start = ((), (), s32[]{:S(2)}) async-start(), calls=%async_computation.17 | async-start | bytes 1966080 | tf_op jit(solution)/shard_map/reduce_scatter | solution.py:103
  447.8 97.9 %reduce-scatter.26.cloned.1.call-start = ((), (), s32[]{:S(2)}) async-start(), calls=%async_computation.18 | async-start | bytes 1966080 | tf_op jit(solution)/shard_map/reduce_scatter | solution.py:103
  455.6 102.1 %reduce-scatter.10.cloned.1.call-start = ((), (), s32[]{:S(2)}) async-start(), calls=%async_computation.10 | async-start | bytes 1966080 | tf_op jit(solution)/shard_map/reduce_scatter | solution.py:103
  511.5 55.9 %collective-permute-start.9 = (f32[5,64]{1,0:T(8,128)S(1)}, f32[5,64]{1,0:T(8,128)S(1)}, u32[]{:S(2)}, u32[]{:S(2)}) collective-permute-start(f32[5,64]{1,0:T(8,128)S(1)} %reduce_max.120), channel_id=1, source_target_pairs={{0,2},{2,4},{4,6},{6,8},{8,10},{10,12},{12,14},{14,16},{16,18},{18... | collective-permute-start | bytes 3848 | tf_op jit(solution)/shard_map/ppermute | solution.py:13
  515.2 55.6 %collective-permute-start.7 = (f32[5,64]{1,0:T(8,128)S(1)}, f32[5,64]{1,0:T(8,128)S(1)}, u32[]{:S(2)}, u32[]{:S(2)}) collective-permute-start(f32[5,64]{1,0:T(8,128)S(1)} %reduce_max.118), channel_id=1, source_target_pairs={{2,0},{4,2},{6,4},{8,6},{10,8},{12,10},{14,12},{16,14},{18,16},{20... | collective-permute-start | bytes 3848 | tf_op jit(solution)/shard_map/ppermute | solution.py:13
  516.5 58.6 %collective-permute-start.5 = (f32[5,64]{1,0:T(8,128)S(1)}, f32[5,64]{1,0:T(8,128)S(1)}, u32[]{:S(2)}, u32[]{:S(2)}) collective-permute-start(f32[5,64]{1,0:T(8,128)S(1)} %reduce_max.116), channel_id=1, source_target_pairs={{4,0},{6,2},{8,4},{10,6},{12,8},{14,10},{16,12},{18,14},{20,16},{2... | collective-permute-start | bytes 3848 | tf_op jit(solution)/shard_map/ppermute | solution.py:13
  560.3 16.1 %collective-permute-start.3 = (f32[5,64]{1,0:T(8,128)S(1)}, f32[5,64]{1,0:T(8,128)S(1)}, u32[]{:S(2)}, u32[]{:S(2)}) collective-permute-start(f32[5,64]{1,0:T(8,128)S(1)} %reduce_max.114), channel_id=1, source_target_pairs={{6,0},{8,2},{10,4},{12,6},{14,8},{16,10},{18,12},{20,14},{22,16},{... | collective-permute-start | bytes 3848 | tf_op jit(solution)/shard_map/ppermute | solution.py:13
  561.6 14.9 %collective-permute-start.15 = (f32[5,64]{1,0:T(8,128)S(1)}, f32[5,64]{1,0:T(8,128)S(1)}, u32[]{:S(2)}, u32[]{:S(2)}) collective-permute-start(f32[5,64]{1,0:T(8,128)S(1)} %reduce_max.126), channel_id=1, source_target_pairs={{0,8},{2,10},{4,12},{6,14},{8,16},{10,18},{12,20},{14,22},{16,24},... | collective-permute-start | bytes 3848 | tf_op jit(solution)/shard_map/ppermute | solution.py:13
  567.4 9.1 %collective-permute-start.13 = (f32[5,64]{1,0:T(8,128)S(1)}, f32[5,64]{1,0:T(8,128)S(1)}, u32[]{:S(2)}, u32[]{:S(2)}) collective-permute-start(f32[5,64]{1,0:T(8,128)S(1)} %reduce_max.124), channel_id=1, source_target_pairs={{0,6},{2,8},{4,10},{6,12},{8,14},{10,16},{12,18},{14,20},{16,22},{... | collective-permute-start | bytes 3848 | tf_op jit(solution)/shard_map/ppermute | solution.py:13
  570.8 5.7 collective-permute-start.11
  575.1 5.5 collective-permute-start.1
  (7 other events, 89.7 us)
Sparse Core Ops, SparseCore 0:
  9.1 13.2 all-gather.1
  400.7 59.3 reduce-scatter.11
  462.4 9.9 reduce-scatter.19
  474.5 9.9 reduce-scatter.13
  486.6 9.9 reduce-scatter.15
  498.7 9.9 reduce-scatter.17
  511.1 9.9 reduce-scatter.21
  523.3 9.9 reduce-scatter.23
  535.6 9.9 reduce-scatter.25
  547.8 9.9 reduce-scatter.9
where the time goes:
time: 591 us
  waiting for transfers between devices  251 us (42%)
  starting transfers between devices  158 us (27%)
  matrix products  69.3 us (12%)
  local copies, waits for them, and re-layouts  65.3 us (11%)
  other arithmetic  27.5 us (5%)
  between operations  14.1 us (2%)
    ppermute x16, waiting for transfers between devices, passed_along(): return lax.ppermute(x, axis, pairs)  162 us
    ppermute x16, starting transfers between devices, passed_along(): return lax.ppermute(x, axis, pairs)  157 us
    reduce_scatter x9, waiting for transfers between devices, shards(): lax.psum_scatter(product(jnp.int32(0), lax.axis_size('sample') * share_ro...  77.3 us
    dot_general x9, matrix products, product(): lax.dot_general(genotypes, operand, (((1,), (1,)), ((), ())), preferred_e...  69.3 us
    gather x2, local copies, waits for them, and re-layouts, label_rows(): shuffled = jnp.take(whole_rows, shuffles, axis=1)  60.4 us
    convert_element_type x1, other arithmetic, shards(): (incoming.astype(jnp.float32) * environment[None, :]).astype(jnp.bfloat16)  14.7 us
  transfers between devices with their start and end apart: 26, of which 14 were waited for; matrix products, arithmetic and copies ran while one was open for 13% of the time, Pallas kernels for 0%

commit v1 on v0

v1 whole, which is shorter than its diff:
```python
import functools

import jax
import jax.numpy as jnp
from jax import lax
from jax.experimental import pallas as pl
from jax.experimental.pallas import tpu as pltpu
from jax.sharding import PartitionSpec as P

SNP_BLOCK = 256
HALF_BLK = 7
LANES = 128
ROWS_STEP = 16
UNROLL = 16
MIB = 2**20


def passed_along(x, axis, by):
    count = lax.axis_size(axis)
    pairs = [(i, i + by) for i in range(count) if 0 <= i + by < count]
    return lax.ppermute(x, axis, pairs)


def swapped(x):
    count = lax.axis_size("sample")
    return lax.ppermute(x, "sample", [(i, (i + 1) % count) for i in range(count)])


def window_bounds(window_start, window_end, chrom_bounds, total_blocks):
    middle = (window_start + window_end - 1) // 2
    before = chrom_bounds[None, :] <= middle[:, None]
    lower_edge = jnp.max(jnp.where(before, chrom_bounds[None, :], 0), axis=1)
    upper_edge = jnp.min(jnp.where(before, total_blocks, chrom_bounds[None, :]), axis=1)
    return (jnp.maximum(window_start, lower_edge), jnp.minimum(window_end, upper_edge))


def snp_side_kernel(
    idx_ref, core_ref, env_ref, own_ref, other_ref, out_ref, inv_ref,
    geno, table, dest, stage, moments, slope, in_sems, out_sems,
):
    snp_rows, all_samples = geno.shape
    half = all_samples // 2
    chunk = 1024
    chunks = all_samples // chunk
    words = snp_rows // LANES
    labels = out_ref.shape[1] // snp_rows

    def load(k):
        source = own_ref if k * chunk < half else other_ref
        return pltpu.make_async_copy(
            source.at[:, pl.ds((k * chunk) % half, chunk)],
            geno.at[:, pl.ds(k * chunk, chunk)],
            in_sems.at[k],
        )

    for k in range(chunks):
        load(k).start()
    moments[...] = jnp.zeros_like(moments)
    for k in range(chunks):
        load(k).wait()

        def add_rows(i, carry, k=k):
            first = pl.multiple_of(i * ROWS_STEP, ROWS_STEP)
            sums = [moments[m, pl.ds(first, ROWS_STEP), :] for m in range(3)]
            for t in range(chunk // LANES):
                at = k * chunk + t * LANES
                x = geno[pl.ds(first, ROWS_STEP), pl.ds(at, LANES)].astype(jnp.float32)
                e = env_ref[:, pl.ds(at, LANES)]
                x = x * x
                sums[0] = sums[0] + x
                x = x * e
                sums[1] = sums[1] + x
                sums[2] = sums[2] + x * e
            for m in range(3):
                moments[m, pl.ds(first, ROWS_STEP), :] = sums[m]
            return carry

        lax.fori_loop(0, snp_rows // ROWS_STEP, add_rows, 0)
    square_sum = jnp.sum(moments[0], axis=1, keepdims=True)
    cross_sum = jnp.sum(moments[1], axis=1, keepdims=True)
    inter_sum = jnp.sum(moments[2], axis=1, keepdims=True)
    regression = cross_sum / square_sum
    divisor = inter_sum - cross_sum * regression + 0.1 * inter_sum
    slope[...] = jnp.broadcast_to(regression, slope.shape)
    inv_ref[...] = jnp.broadcast_to(1.0 / divisor, slope.shape).T[: inv_ref.shape[0]]

    side = 2 * LANES
    unit = (
        lax.broadcasted_iota(jnp.int32, (side, side), 0)
        == lax.broadcasted_iota(jnp.int32, (side, side), 1)
    ).astype(jnp.bfloat16)
    share = snp_rows // 2

    def turn(k, carry):
        at = pl.multiple_of(k * side, side)
        e = env_ref[:, pl.ds(at, side)]
        turned = []
        for j in range(snp_rows // side):
            rows = pl.ds(j * side, side)
            x = geno[rows, pl.ds(at, side)].astype(jnp.float32)
            r = slope[rows, :]
            a = x * (e - jnp.concatenate([r, r], axis=1))
            t = lax.dot_general(
                unit, a.astype(jnp.bfloat16), (((1,), (1,)), ((), ())),
                preferred_element_type=jnp.float32,
            )
            for c in range(side // LANES):
                table[pl.ds(k * (side * words) + j * (side // LANES) + c, side, stride=words), :] = (
                    t[:, c * LANES : (c + 1) * LANES]
                )
            turned.append(t)
        turned = jnp.concatenate(turned, axis=1)
        kept = jnp.where(core_ref[0] == 0, turned[:, :share], turned[:, share:])
        stage[pl.ds(at, side), pl.ds(0, share)] = kept.astype(jnp.bfloat16)
        return carry

    lax.fori_loop(0, all_samples // side, turn, 0)
    first_out = pltpu.make_async_copy(
        stage.at[:, pl.ds(0, share)],
        out_ref.at[:, pl.ds(labels * snp_rows, share)],
        out_sems.at[0],
    )
    first_out.start()

    parts = out_sems.shape[0]
    part_rows = all_samples // parts

    def save(q, part):
        rows = pl.ds(part * part_rows, part_rows)
        return pltpu.make_async_copy(
            stage.at[rows], out_ref.at[rows, pl.ds(q * snp_rows, snp_rows)], out_sems.at[part]
        )

    for q in range(labels):

        def scatter(i, carry, q=q):
            first = pl.multiple_of(i * UNROLL, UNROLL)
            base = pl.multiple_of(first * words, UNROLL * words)
            held = [table[pl.ds(base + u * words, words), :] for u in range(UNROLL)]
            for u in range(UNROLL):
                to = pl.multiple_of(idx_ref[q * all_samples + first + u], words)
                dest[pl.ds(to, words), :] = held[u]
            return carry

        lax.fori_loop(0, all_samples // UNROLL, scatter, 0)
        if q == 0:
            first_out.wait()
        for part in range(parts):
            if q > 0:
                save(q - 1, part).wait()

            def narrow(k, carry, part=part):
                at = pl.multiple_of(part * part_rows + k * side, side)
                for c in range(words):
                    v = dest[pl.ds(at * words + c, side, stride=words), :]
                    stage[pl.ds(at, side), pl.ds(c * LANES, LANES)] = v.astype(jnp.bfloat16)
                return carry

            lax.fori_loop(0, part_rows // side, narrow, 0)
            save(q, part).start()
    for part in range(parts):
        save(labels - 1, part).wait()


def snp_side(idx, core, env, own, other, labels):
    snp_rows, half = own.shape
    all_samples = 2 * half
    words = snp_rows // LANES
    width = labels * snp_rows + snp_rows // 2
    any_spec = pl.BlockSpec(memory_space=pl.ANY)
    smem = pl.BlockSpec(memory_space=pltpu.SMEM)
    vmem = pl.BlockSpec(memory_space=pltpu.VMEM)
    return pl.pallas_call(
        snp_side_kernel,
        out_shape=(
            jax.ShapeDtypeStruct((all_samples, width), jnp.bfloat16),
            jax.ShapeDtypeStruct((8, snp_rows), jnp.float32),
        ),
        in_specs=[smem, smem, vmem, any_spec, any_spec],
        out_specs=(any_spec, vmem),
        scratch_shapes=[
            pltpu.VMEM((snp_rows, all_samples), jnp.bfloat16),
            pltpu.VMEM((all_samples * words, LANES), jnp.float32),
            pltpu.VMEM((all_samples * words, LANES), jnp.float32),
            pltpu.VMEM((all_samples, snp_rows), jnp.bfloat16),
            pltpu.VMEM((3, snp_rows, LANES), jnp.float32),
            pltpu.VMEM((snp_rows, LANES), jnp.float32),
            pltpu.SemaphoreType.DMA((all_samples // 1024,)),
            pltpu.SemaphoreType.DMA((4,)),
        ],
        compiler_params=pltpu.CompilerParams(vmem_limit_bytes=60 * MIB),
        cost_estimate=pl.CostEstimate(
            flops=40 * 10**9, bytes_accessed=60 * 10**6, transcendentals=0
        ),
        name="snp_side",
    )(idx, core, env, own, other)


def product_kernel(
    pos_ref, inv_ref, low_ref, high_ref, own_ref, other_ref, weights_ref, out_ref, total, power,
    *, labels, snp_rows, power_row,
):
    step = pl.program_id(0)
    steps = pl.num_programs(0)
    genes = own_ref.shape[0]
    width = weights_ref.shape[1]
    block = SNP_BLOCK

    @pl.when(step == 0)
    def _():
        total[...] = jnp.zeros_like(total)
        power[...] = jnp.zeros_like(power)

    def add(rows_ref):
        rows = rows_ref[...]
        for n in range(width // block):
            cols = pl.ds(n * block, block)
            total[pl.ds(0, genes), cols] += jnp.dot(
                rows, weights_ref[:, cols], preferred_element_type=jnp.float32
            )
        x = rows_ref[pl.ds(power_row, LANES), :].astype(jnp.float32)
        x = x * x
        kept = power[...]
        for t in range(x.shape[1] // LANES):
            kept = kept + x[:, t * LANES : (t + 1) * LANES]
        power[...] = kept

    @pl.when(step < steps // 2)
    def _():
        add(own_ref)

    @pl.when(step >= steps // 2)
    def _():
        add(other_ref)

    @pl.when(step == steps - 1)
    def _():
        first_block = pos_ref[0] * (snp_rows // block)
        share_blocks = snp_rows // 2 // block
        low = low_ref[...]
        high = high_ref[...]

        def peak(col, inv_col, snp_block):
            v = total[:, pl.ds(col, block)]
            v = v * v * inv_ref[0:1, pl.ds(inv_col, block)]
            best = v[:, :LANES]
            for t in range(1, block // LANES):
                best = jnp.maximum(best, v[:, t * LANES : (t + 1) * LANES])
            best = jnp.max(best.T, axis=0, keepdims=True)
            inside = (snp_block >= low) & (snp_block < high)
            return jnp.where(inside, best, 0.0)

        rows = []
        for q in range(labels):
            best = jnp.zeros_like(low, jnp.float32)
            for b in range(snp_rows // block):
                best = jnp.maximum(
                    best, peak(q * snp_rows + b * block, b * block, first_block + b)
                )
            rows.append(best)
        best = jnp.zeros_like(low, jnp.float32)
        for b in range(share_blocks):
            start = pos_ref[1] * share_blocks + b
            best = jnp.maximum(
                best,
                peak(
                    labels * snp_rows + b * block,
                    pl.multiple_of(start * block, block),
                    first_block + start,
                ),
            )
        rows.append(best)
        powers = jnp.sum(power[...].T, axis=0, keepdims=True)
        rows.append(jnp.concatenate([powers] * (low.shape[1] // LANES), axis=1))
        while len(rows) < out_ref.shape[0]:
            rows.append(jnp.zeros_like(low, jnp.float32))
        out_ref[...] = jnp.concatenate(rows, axis=0)


def products(pos, inv, low, high, own, other, weights, labels, snp_rows, power_row):
    genes, half = own.shape
    all_samples, width = weights.shape
    padded = low.shape[1]
    depth = 1024
    own_steps = half // depth
    smem = pl.BlockSpec(memory_space=pltpu.SMEM)
    return pl.pallas_call(
        functools.partial(product_kernel, labels=labels, snp_rows=snp_rows, power_row=power_row),
        grid=(all_samples // depth,),
        out_shape=jax.ShapeDtypeStruct((8, padded), jnp.float32),
        in_specs=[
            smem,
            pl.BlockSpec((8, snp_rows), lambda k: (0, 0)),
            pl.BlockSpec((1, padded), lambda k: (0, 0)),
            pl.BlockSpec((1, padded), lambda k: (0, 0)),
            pl.BlockSpec((genes, depth), lambda k: (0, jnp.minimum(k, own_steps - 1))),
            pl.BlockSpec((genes, depth), lambda k: (0, jnp.maximum(k - own_steps, 0))),
            pl.BlockSpec((depth, width), lambda k: (k, 0)),
        ],
        out_specs=pl.BlockSpec((8, padded), lambda k: (0, 0)),
        scratch_shapes=[
            pltpu.VMEM((padded, width), jnp.float32),
            pltpu.VMEM((LANES, LANES), jnp.float32),
        ],
        compiler_params=pltpu.CompilerParams(vmem_limit_bytes=48 * MIB),
        cost_estimate=pl.CostEstimate(
            flops=2 * genes * all_samples * width,
            bytes_accessed=2 * all_samples * (width + genes),
            transcendentals=0,
        ),
        name="products",
    )(pos, inv, low, high, own, other, weights)


def shards(genotypes, phenotypes, environment, shuffles, window_start, window_end, chrom_bounds):
    snp_rows, half = genotypes.shape
    gene_rows = phenotypes.shape[0]
    perms = shuffles.shape[0]
    genome_size = lax.axis_size("genome")
    sample_size = lax.axis_size("sample")
    genome_pos = lax.axis_index("genome")
    sample_pos = lax.axis_index("sample")
    blocks_dev = snp_rows // SNP_BLOCK
    reach_dev = (HALF_BLK + blocks_dev - 1) // blocks_dev
    total_blocks = snp_rows * genome_size // SNP_BLOCK
    all_samples = half * sample_size
    labels = perms // sample_size
    band_slots = 2 * reach_dev + 1

    other_geno = swapped(genotypes)
    small = jnp.concatenate([shuffles.astype(jnp.float32), environment[None]], axis=0)
    other_small = swapped(small)
    pieces = []
    for offset in range(-reach_dev, reach_dev + 1):
        pieces.append(
            phenotypes if offset == 0 else passed_along(phenotypes, "genome", -offset)
        )

    env = jnp.concatenate([environment, other_small[perms]])[None]
    first_label = sample_pos * labels
    idx = jnp.concatenate(
        [
            lax.dynamic_slice_in_dim(shuffles, first_label, labels, 0),
            lax.dynamic_slice_in_dim(other_small, first_label, labels, 0).astype(jnp.int32),
        ],
        axis=1,
    )
    idx = idx - sample_pos * half
    idx = jnp.where(idx < 0, idx + all_samples, idx) * (snp_rows // LANES)
    core = jnp.full((1,), sample_pos, jnp.int32)
    weights, inv = snp_side(idx.reshape(-1), core, env, genotypes, other_geno, labels)

    lower_edge, upper_edge = window_bounds(window_start, window_end, chrom_bounds, total_blocks)
    band_genes = band_slots * gene_rows
    padded = -(-band_genes // LANES) * LANES
    margin = reach_dev * gene_rows
    edges = jnp.pad(
        jnp.stack([lower_edge, upper_edge]), ((0, 0), (margin, margin + padded - band_genes))
    )
    band = lax.dynamic_slice_in_dim(edges, genome_pos * gene_rows, padded, 1)
    low, high = band[0:1], band[1:2]
    high = jnp.where(lax.broadcasted_iota(jnp.int32, high.shape, 1) < band_genes, high, 0)

    own_stack = jnp.concatenate(pieces, axis=0)
    other_stack = swapped(own_stack)
    pos = jnp.stack([genome_pos, sample_pos]).astype(jnp.int32)
    found = products(
        pos, inv, low, high, own_stack, other_stack, weights, labels, snp_rows,
        reach_dev * gene_rows,
    )

    peaks = jnp.zeros((perms + 1, genome_size * gene_rows + 2 * margin), jnp.float32)
    at = genome_pos * gene_rows
    peaks = lax.dynamic_update_slice(peaks, found[:labels, :band_genes], (1 + first_label, at))
    peaks = lax.dynamic_update_slice(peaks, found[labels : labels + 1, :band_genes], (0, at))
    peaks = lax.pmax(peaks[:, margin : margin + genome_size * gene_rows], ("genome", "sample"))
    peak = lax.dynamic_slice_in_dim(peaks, at, gene_rows, 1)
    row_power = found[labels + 1, :gene_rows]
    return jnp.sqrt(peak / (row_power[None, :] / all_samples + 1e-05))


def solution(mesh):
    placed = (
        P("genome", "sample"),
        P("genome", "sample"),
        P("sample"),
        P(None, "sample"),
        P(),
        P(),
        P(),
    )
    return jax.shard_map(
        shards, mesh=mesh, in_specs=placed, out_specs=P(None, "genome"), check_vma=False
    )
```

time: 591 us -> 182 us (0.31)
  waiting for transfers between devices: 251 us -> 41.2 us
  starting transfers between devices: 158 us -> 21.2 us
  matrix products: 69.3 us -> 0 us
  Pallas kernels: 0 us -> 60.2 us
  local copies, waits for them, and re-layouts: 65.3 us -> 10.1 us
  blocking collectives: 4.98 us -> 41.7 us
  other arithmetic: 27.5 us -> 6.64 us
  between operations: 14.1 us -> 0.24 us
    ppermute x16 -> x8, starting transfers between devices: 157 us -> 20.7 us  [passed_along(): return lax.ppermute(x, axis, pairs)]
    ppermute x16 -> x8, waiting for transfers between devices: 162 us -> 41.2 us  [passed_along(): return lax.ppermute(x, axis, pairs)]
    reduce_scatter x9 -> x0, waiting for transfers between devices: 77.3 us -> none  [shards(): lax.psum_scatter(product(jnp.int32(0), lax.axis_size('sample') * share_ro...]
    dot_general x9 -> x0, matrix products: 69.3 us -> none  [product(): lax.dot_general(genotypes, operand, (((1,), (1,)), ((), ())), preferred_e...]
    gather x2 -> x0, local copies, waits for them, and re-layouts: 60.4 us -> none  [label_rows(): shuffled = jnp.take(whole_rows, shuffles, axis=1)]
    pallas_call x0 -> x2, Pallas kernels: none -> 60.2 us  [the longest x1 41.8 us: snp_side(): pl.pallas_call(snp_side_kernel, out_shape=(jax.ShapeDtypeStruct((all_samp...]
    pmax x1, blocking collectives: 2.47 us -> 41.7 us  [shards(): lax.pmax(peaks[:, margin:margin + genome_size * gene_rows], ('genome', 's...]
    convert_element_type x1 -> x2, other arithmetic: 14.7 us -> 0.88 us  [the longest x1 0.85 us: shards(): shuffles.astype(jnp.float32)]
  transfers between devices with their start and end apart: 26 -> 11, of which waited for: 14 -> 3; matrix products, arithmetic and copies ran while one was open for 13% -> 8% of each run, Pallas kernels for 0% -> 23%
where the time goes in v1:
time: 182 us; the launch traced here: 181 us
  Pallas kernels  60.2 us (33%)
  blocking collectives  41.7 us (23%)
  waiting for transfers between devices  41.2 us (23%)
  starting transfers between devices  21.2 us (12%)
  local copies, waits for them, and re-layouts  10.1 us (6%)
  other arithmetic  6.64 us (4%)
    pallas_call x1, Pallas kernels, snp_side(): pl.pallas_call(snp_side_kernel, out_shape=(jax.ShapeDtypeStruct((all_samp...  41.8 us
    pmax x1, blocking collectives, shards(): lax.pmax(peaks[:, margin:margin + genome_size * gene_rows], ('genome', 's...  41.7 us
    ppermute x8, waiting for transfers between devices, passed_along(): return lax.ppermute(x, axis, pairs)  41.2 us
    ppermute x8, starting transfers between devices, passed_along(): return lax.ppermute(x, axis, pairs)  20.7 us
    pallas_call x1, Pallas kernels, products(): pl.pallas_call(functools.partial(product_kernel, labels=labels, snp_rows=...  18.5 us
    unnamed x15, local copies, waits for them, and re-layouts  7.48 us
  transfers between devices with their start and end apart: 11, of which 3 were waited for; matrix products, arithmetic and copies ran while one was open for 8% of the time, Pallas kernels for 23%

profile of v1, /device:TPU:0, one launch (start us, length us, event | category | flops | bytes accessed | tf_op | source)
XLA Modules:
  0.0 181.3 jit_solution(13079136510619354715)
XLA Ops:
  0.0 5.1 %collective-permute-start.2 = (bf16[64,4096]{1,0:T(8,128)(2,1)}, bf16[64,4096]{1,0:T(8,128)(2,1)S(1)}, u32[]{:S(2)}, u32[]{:S(2)}) collective-permute-start(bf16[64,4096]{1,0:T(8,128)(2,1)} %param.8), channel_id=1, source_target_pairs={{0,8},{2,10},{4,12},{6,14},{8,16},{10,18},{12,20},{14,22},{16,24},... | collective-permute-start | bytes 1572872 | tf_op jit(solution)/shard_map/ppermute | solution.py:21
  5.1 4.4 %collective-permute-start.3 = (bf16[64,4096]{1,0:T(8,128)(2,1)}, bf16[64,4096]{1,0:T(8,128)(2,1)S(1)}, u32[]{:S(2)}, u32[]{:S(2)}) collective-permute-start(bf16[64,4096]{1,0:T(8,128)(2,1)} %param.8), channel_id=1, source_target_pairs={{0,6},{2,8},{4,10},{6,12},{8,14},{10,16},{12,18},{14,20},{16,22},{... | collective-permute-start | bytes 1572872 | tf_op jit(solution)/shard_map/ppermute | solution.py:21
  9.5 3.4 %collective-permute-start.4 = (bf16[64,4096]{1,0:T(8,128)(2,1)}, bf16[64,4096]{1,0:T(8,128)(2,1)S(1)}, u32[]{:S(2)}, u32[]{:S(2)}) collective-permute-start(bf16[64,4096]{1,0:T(8,128)(2,1)} %param.8), channel_id=1, source_target_pairs={{0,4},{2,6},{4,8},{6,10},{8,12},{10,14},{12,16},{14,18},{16,20},{1... | collective-permute-start | bytes 1572872 | tf_op jit(solution)/shard_map/ppermute | solution.py:21
  12.9 2.5 %collective-permute-start.5 = (bf16[64,4096]{1,0:T(8,128)(2,1)}, bf16[64,4096]{1,0:T(8,128)(2,1)S(1)}, u32[]{:S(2)}, u32[]{:S(2)}) collective-permute-start(bf16[64,4096]{1,0:T(8,128)(2,1)} %param.8), channel_id=1, source_target_pairs={{0,2},{2,4},{4,6},{6,8},{8,10},{10,12},{12,14},{14,16},{16,18},{18... | collective-permute-start | bytes 1572872 | tf_op jit(solution)/shard_map/ppermute | solution.py:21
  15.4 1.3 collective-permute-start.6
  16.7 0.9 convert_element_type.6
  17.6 0.7 add_select_fusion
  18.3 0.8 fusion
  19.1 0.7 max.5
  19.8 0.7 min.3
  20.5 0.7 pad_maximum_fusion
  21.3 0.9 constant_dynamic-slice_fusion
  22.3 1.4 collective-permute-start.7
  23.7 0.9 constant_dynamic-update-slice_fusion.8
  24.6 11.9 %collective-permute-done.3 = bf16[64,4096]{1,0:T(8,128)(2,1)S(1)} collective-permute-done((bf16[64,4096]{1,0:T(8,128)(2,1)}, bf16[64,4096]{1,0:T(8,128)(2,1)S(1)}, u32[]{:S(2)}, u32[]{:S(2)}) %collective-permute-start.3) | collective-permute-done | bytes 524320 | tf_op jit(solution)/shard_map/ppermute | solution.py:21
  36.5 1.3 collective-permute-start.8
  37.8 0.8 constant_dynamic-update-slice_fusion.7
  38.6 18.9 %collective-permute-done.4 = bf16[64,4096]{1,0:T(8,128)(2,1)S(1)} collective-permute-done((bf16[64,4096]{1,0:T(8,128)(2,1)}, bf16[64,4096]{1,0:T(8,128)(2,1)S(1)}, u32[]{:S(2)}, u32[]{:S(2)}) %collective-permute-start.4) | collective-permute-done | bytes 524320 | tf_op jit(solution)/shard_map/ppermute | solution.py:21
  57.5 0.8 constant_dynamic-update-slice_fusion.6
  58.4 1.3 collective-permute-start.9
  59.6 0.9 constant_dynamic-update-slice_fusion.5
  60.5 0.8 constant_dynamic-update-slice_fusion.4
  61.8 0.8 constant_dynamic-update-slice_fusion.3
  62.7 0.8 constant_dynamic-update-slice_fusion.2
  63.5 0.9 constant_dynamic-update-slice_fusion.1
  64.4 10.4 %collective-permute-done.9 = bf16[64,4096]{1,0:T(8,128)(2,1)S(1)} collective-permute-done((bf16[64,4096]{1,0:T(8,128)(2,1)}, bf16[64,4096]{1,0:T(8,128)(2,1)S(1)}, u32[]{:S(2)}, u32[]{:S(2)}) %collective-permute-start.9) | collective-permute-done | bytes 524320 | tf_op jit(solution)/shard_map/ppermute | solution.py:21
  74.8 0.8 constant_dynamic-update-slice_fusion.own_ref
  77.0 41.8 %snp_side.1 = (bf16[8192,1280]{1,0:T(8,128)(2,1)}, f32[8,512]{1,0:T(8,128)}) custom-call(s32[16384]{0:T(1024)} %fusion.2.idx_ref, s32[1]{0:T(128)} %bitcast.1.core_ref, f32[1,8192]{1,0:T(1,128)} %bitcast.15, bf16[512,4096]{1,0:T(8,128)(2,1)} %own_ref.1, bf16[512,4096]{1,0:T(8,128)(2,1)} %collective-permute-done.1.other_ref), custom_call_target="tpu_custom_call" | custom-call | flops 40000000000 | bytes 60000000 | tf_op jit(solution)/shard_map/snp_side/pallas_call | solution.py:173
  118.8 0.7 copy-done
  119.5 18.5 %products.1 = f32[8,640]{1,0:T(8,128)S(1)} custom-call(s32[2]{0:T(128)S(1)} %pad_add_fusion.1.pos_ref, f32[8,512]{1,0:T(8,128)S(1)} %copy-done, s32[1,640]{1,0:T(1,128)S(1)} %get-tuple-element.12.low_ref, s32[1,640]{1,0:T(1,128)S(1)} %get-tuple-element.11.high_ref, bf16[576,4096]{1,0:T(8,128)(2,1)} %constant_dynamic-update-slice_fusion.own_ref, ...), custom_call_target="tpu_custom_call" | custom-call | flops 12079595520 | bytes 30408704 | tf_op jit(solution)/shard_map/products/pallas_call | solution.py:287
  138.9 41.7 %pmax.7 = f32[5,1024]{1,0:T(8,128)S(1)} all-reduce(f32[5,1024]{1,0:T(8,128)S(1)} %slice.31), channel_id=1, replica_groups=mesh['genome'=16,'sample'=2] {'genome','sample'}, use_global_device_ids=true, to_apply=%region_2.3 | all-reduce | flops 5120 | bytes 40960 | tf_op jit(solution)/shard_map/pmax | solution.py:376
  180.7 0.7 divide_sqrt_fusion
  (32 shorter events, 3.0 us)
Async XLA Ops:
  0.0 60.5 %copy-start.1 = (bf16[64,4096]{1,0:T(8,128)(2,1)S(1)}, bf16[64,4096]{1,0:T(8,128)(2,1)}, u32[]{:S(2)}) copy-start(bf16[64,4096]{1,0:T(8,128)(2,1)} %param.8) | copy-start | bytes 1572868
  0.0 22.3 %collective-permute-start.2 = (bf16[64,4096]{1,0:T(8,128)(2,1)}, bf16[64,4096]{1,0:T(8,128)(2,1)S(1)}, u32[]{:S(2)}, u32[]{:S(2)}) collective-permute-start(bf16[64,4096]{1,0:T(8,128)(2,1)} %param.8), channel_id=1, source_target_pairs={{0,8},{2,10},{4,12},{6,14},{8,16},{10,18},{12,20},{14,22},{16,24},... | collective-permute-start | bytes 1572872 | tf_op jit(solution)/shard_map/ppermute | solution.py:21
  5.1 31.4 %collective-permute-start.3 = (bf16[64,4096]{1,0:T(8,128)(2,1)}, bf16[64,4096]{1,0:T(8,128)(2,1)S(1)}, u32[]{:S(2)}, u32[]{:S(2)}) collective-permute-start(bf16[64,4096]{1,0:T(8,128)(2,1)} %param.8), channel_id=1, source_target_pairs={{0,6},{2,8},{4,10},{6,12},{8,14},{10,16},{12,18},{14,20},{16,22},{... | collective-permute-start | bytes 1572872 | tf_op jit(solution)/shard_map/ppermute | solution.py:21
  9.5 48.0 %collective-permute-start.4 = (bf16[64,4096]{1,0:T(8,128)(2,1)}, bf16[64,4096]{1,0:T(8,128)(2,1)S(1)}, u32[]{:S(2)}, u32[]{:S(2)}) collective-permute-start(bf16[64,4096]{1,0:T(8,128)(2,1)} %param.8), channel_id=1, source_target_pairs={{0,4},{2,6},{4,8},{6,10},{8,12},{10,14},{12,16},{14,18},{16,20},{1... | collective-permute-start | bytes 1572872 | tf_op jit(solution)/shard_map/ppermute | solution.py:21
  12.9 45.4 %collective-permute-start.5 = (bf16[64,4096]{1,0:T(8,128)(2,1)}, bf16[64,4096]{1,0:T(8,128)(2,1)S(1)}, u32[]{:S(2)}, u32[]{:S(2)}) collective-permute-start(bf16[64,4096]{1,0:T(8,128)(2,1)} %param.8), channel_id=1, source_target_pairs={{0,2},{2,4},{4,6},{6,8},{8,10},{10,12},{12,14},{14,16},{16,18},{18... | collective-permute-start | bytes 1572872 | tf_op jit(solution)/shard_map/ppermute | solution.py:21
  15.4 45.9 %collective-permute-start.6 = (bf16[64,4096]{1,0:T(8,128)(2,1)}, bf16[64,4096]{1,0:T(8,128)(2,1)S(1)}, u32[]{:S(2)}, u32[]{:S(2)}) collective-permute-start(bf16[64,4096]{1,0:T(8,128)(2,1)} %param.8), channel_id=1, source_target_pairs={{2,0},{4,2},{6,4},{8,6},{10,8},{12,10},{14,12},{16,14},{18,16},{20... | collective-permute-start | bytes 1572872 | tf_op jit(solution)/shard_map/ppermute | solution.py:21
  22.3 53.5 %copy-start.2 = (f32[4096]{0:T(1024)S(1)}, f32[4096]{0:T(1024)}, u32[]{:S(2)}) copy-start(f32[4096]{0:T(1024)} %param.9) | copy-start | bytes 49156
  22.3 40.4 %collective-permute-start.7 = (bf16[64,4096]{1,0:T(8,128)(2,1)}, bf16[64,4096]{1,0:T(8,128)(2,1)S(1)}, u32[]{:S(2)}, u32[]{:S(2)}) collective-permute-start(bf16[64,4096]{1,0:T(8,128)(2,1)} %param.8), channel_id=1, source_target_pairs={{4,0},{6,2},{8,4},{10,6},{12,8},{14,10},{16,12},{18,14},{20,16},{2... | collective-permute-start | bytes 1572872 | tf_op jit(solution)/shard_map/ppermute | solution.py:21
  36.5 27.0 %collective-permute-start.8 = (bf16[64,4096]{1,0:T(8,128)(2,1)}, bf16[64,4096]{1,0:T(8,128)(2,1)S(1)}, u32[]{:S(2)}, u32[]{:S(2)}) collective-permute-start(bf16[64,4096]{1,0:T(8,128)(2,1)} %param.8), channel_id=1, source_target_pairs={{6,0},{8,2},{10,4},{12,6},{14,8},{16,10},{18,12},{20,14},{22,16},{... | collective-permute-start | bytes 1572872 | tf_op jit(solution)/shard_map/ppermute | solution.py:21
  57.5 19.5 %collective-permute-start.1 = (bf16[512,4096]{1,0:T(8,128)(2,1)}, bf16[512,4096]{1,0:T(8,128)(2,1)}, u32[]{:S(2)}, u32[]{:S(2)}) collective-permute-start(bf16[512,4096]{1,0:T(8,128)(2,1)} %own_ref.1), channel_id=1, source_target_pairs={{0,1},{1,0},{2,3},{3,2},{4,5},{5,4},{6,7},{7,6},{8,9},{9,8},{10,11... | collective-permute-start | bytes 12582920 | tf_op jit(solution)/shard_map/ppermute | solution.py:26
  58.4 16.4 %collective-permute-start.9 = (bf16[64,4096]{1,0:T(8,128)(2,1)}, bf16[64,4096]{1,0:T(8,128)(2,1)S(1)}, u32[]{:S(2)}, u32[]{:S(2)}) collective-permute-start(bf16[64,4096]{1,0:T(8,128)(2,1)} %param.8), channel_id=1, source_target_pairs={{8,0},{10,2},{12,4},{14,6},{16,8},{18,10},{20,12},{22,14},{24,16},... | collective-permute-start | bytes 1572872 | tf_op jit(solution)/shard_map/ppermute | solution.py:21
  61.3 14.3 %collective-permute-start = (f32[5,4096]{1,0:T(8,128)S(1)}, f32[5,4096]{1,0:T(8,128)S(1)}, u32[]{:S(2)}, u32[]{:S(2)}) collective-permute-start(f32[5,4096]{1,0:T(8,128)S(1)} %pad_maximum_fusion), channel_id=1, source_target_pairs={{0,1},{1,0},{2,3},{3,2},{4,5},{5,4},{6,7},{7,6},{8,9},{9,8},{10,11... | collective-permute-start | bytes 245768 | tf_op jit(solution)/shard_map/ppermute | solution.py:26
  75.6 43.1 %collective-permute-start.10 = (bf16[576,4096]{1,0:T(8,128)(2,1)}, bf16[576,4096]{1,0:T(8,128)(2,1)}, u32[]{:S(2)}, u32[]{:S(2)}) collective-permute-start(bf16[576,4096]{1,0:T(8,128)(2,1)} %constant_dynamic-update-slice_fusion.own_ref), channel_id=1, source_target_pairs={{0,1},{1,0},{2,3},{3,2},{4,5},{5,4},{6,7},{7,6},{8,9},{9,8},{10,11... | collective-permute-start | bytes 14155784 | tf_op jit(solution)/shard_map/ppermute | solution.py:26
  118.8 0.7 copy-start

commit v2 on v1

v2 whole, which is shorter than its diff:
```python
import functools

import jax
import jax.numpy as jnp
from jax import lax
from jax.experimental import pallas as pl
from jax.experimental.pallas import tpu as pltpu
from jax.sharding import PartitionSpec as P

SNP_BLOCK = 256
HALF_BLK = 7
LANES = 128
ROWS_STEP = 16
UNROLL = 16
MIB = 2**20


def passed_along(x, axis, by):
    count = lax.axis_size(axis)
    pairs = [(i, i + by) for i in range(count) if 0 <= i + by < count]
    return lax.ppermute(x, axis, pairs)


def swapped(x):
    count = lax.axis_size("sample")
    return lax.ppermute(x, "sample", [(i, (i + 1) % count) for i in range(count)])


def moments_kernel(geno_ref, env_ref, out_ref, sums):
    step = pl.program_id(0)
    snp_rows, chunk = geno_ref.shape

    @pl.when(step == 0)
    def _():
        sums[...] = jnp.zeros_like(sums)

    def add_rows(i, carry):
        first = pl.multiple_of(i * ROWS_STEP, ROWS_STEP)
        held = [sums[m, pl.ds(first, ROWS_STEP), :] for m in range(3)]
        for t in range(chunk // LANES):
            x = geno_ref[pl.ds(first, ROWS_STEP), pl.ds(t * LANES, LANES)].astype(jnp.float32)
            e = env_ref[:, pl.ds(t * LANES, LANES)]
            x = x * x
            held[0] = held[0] + x
            x = x * e
            held[1] = held[1] + x
            held[2] = held[2] + x * e
        for m in range(3):
            sums[m, pl.ds(first, ROWS_STEP), :] = held[m]
        return carry

    lax.fori_loop(0, snp_rows // ROWS_STEP, add_rows, 0, unroll=2)

    @pl.when(step == pl.num_programs(0) - 1)
    def _():
        rows = [jnp.sum(sums[m].T, axis=0, keepdims=True) for m in range(3)]
        rows.append(jnp.zeros((out_ref.shape[0] - 3, snp_rows), jnp.float32))
        out_ref[...] = jnp.concatenate(rows, axis=0)


def local_moments(geno, env):
    snp_rows, half = geno.shape
    chunk = 1024
    return pl.pallas_call(
        moments_kernel,
        grid=(half // chunk,),
        out_shape=jax.ShapeDtypeStruct((8, snp_rows), jnp.float32),
        in_specs=[
            pl.BlockSpec((snp_rows, chunk), lambda k: (0, k)),
            pl.BlockSpec((1, chunk), lambda k: (0, k)),
        ],
        out_specs=pl.BlockSpec((8, snp_rows), lambda k: (0, 0)),
        scratch_shapes=[pltpu.VMEM((3, snp_rows, LANES), jnp.float32)],
        compiler_params=pltpu.CompilerParams(vmem_limit_bytes=60 * MIB),
        cost_estimate=pl.CostEstimate(
            flops=5 * 10**9, bytes_accessed=2 * snp_rows * half, transcendentals=0
        ),
        name="local_moments",
    )(geno, env)


def snp_side_kernel(
    idx_ref, core_ref, env_ref, sums_ref, own_ref, other_ref, out_ref,
    geno, table, dest, stage, slope, in_sems, out_sems,
):
    snp_rows, all_samples = geno.shape
    half = all_samples // 2
    chunk = 1024
    chunks = all_samples // chunk
    words = snp_rows // LANES
    labels = out_ref.shape[1] // snp_rows

    def load(k):
        source = own_ref if k * chunk < half else other_ref
        return pltpu.make_async_copy(
            source.at[:, pl.ds((k * chunk) % half, chunk)],
            geno.at[:, pl.ds(k * chunk, chunk)],
            in_sems.at[k],
        )

    for k in range(chunks):
        load(k).start()
    regression = sums_ref[1:2, :] / sums_ref[0:1, :]
    slope[...] = jnp.broadcast_to(regression, (LANES, snp_rows)).T
    for k in range(chunks):
        load(k).wait()

    side = 2 * LANES
    unit = (
        lax.broadcasted_iota(jnp.int32, (side, side), 0)
        == lax.broadcasted_iota(jnp.int32, (side, side), 1)
    ).astype(jnp.bfloat16)
    share = snp_rows // 2

    def turn(k, carry):
        at = pl.multiple_of(k * side, side)
        e = env_ref[:, pl.ds(at, side)]
        turned = []
        for j in range(snp_rows // side):
            rows = pl.ds(j * side, side)
            x = geno[rows, pl.ds(at, side)].astype(jnp.float32)
            r = slope[rows, :]
            a = x * (e - jnp.concatenate([r, r], axis=1))
            t = lax.dot_general(
                unit, a.astype(jnp.bfloat16), (((1,), (1,)), ((), ())),
                preferred_element_type=jnp.float32,
            )
            for c in range(side // LANES):
                table[pl.ds(k * (side * words) + j * (side // LANES) + c, side, stride=words), :] = (
                    t[:, c * LANES : (c + 1) * LANES]
                )
            turned.append(t)
        turned = jnp.concatenate(turned, axis=1)
        kept = jnp.where(core_ref[0] == 0, turned[:, :share], turned[:, share:])
        stage[pl.ds(at, side), pl.ds(0, share)] = kept.astype(jnp.bfloat16)
        return carry

    lax.fori_loop(0, all_samples // side, turn, 0)
    def save_first(h):
        to = pl.multiple_of(jnp.where(core_ref[0] == h, 0, half), half)
        return pltpu.make_async_copy(
            stage.at[pl.ds(h * half, half), pl.ds(0, share)],
            out_ref.at[pl.ds(to, half), pl.ds(labels * snp_rows, share)],
            out_sems.at[h],
        )

    save_first(0).start()
    save_first(1).start()

    parts = out_sems.shape[0]
    part_rows = all_samples // parts

    def save(q, part):
        rows = pl.ds(part * part_rows, part_rows)
        return pltpu.make_async_copy(
            stage.at[rows], out_ref.at[rows, pl.ds(q * snp_rows, snp_rows)], out_sems.at[part]
        )

    for q in range(labels):

        def scatter(i, carry, q=q):
            first = pl.multiple_of(i * UNROLL, UNROLL)
            base = pl.multiple_of(first * words, UNROLL * words)
            held = [table[pl.ds(base + u * words, words), :] for u in range(UNROLL)]
            for u in range(UNROLL):
                to = pl.multiple_of(idx_ref[q * all_samples + first + u], words)
                dest[pl.ds(to, words), :] = held[u]
            return carry

        lax.fori_loop(0, all_samples // UNROLL, scatter, 0)
        if q == 0:
            save_first(0).wait()
            save_first(1).wait()
        for part in range(parts):
            if q > 0:
                save(q - 1, part).wait()

            def narrow(k, carry, part=part):
                at = pl.multiple_of(part * part_rows + k * side, side)
                for c in range(words):
                    v = dest[pl.ds(at * words + c, side, stride=words), :]
                    stage[pl.ds(at, side), pl.ds(c * LANES, LANES)] = v.astype(jnp.bfloat16)
                return carry

            lax.fori_loop(0, part_rows // side, narrow, 0)
            save(q, part).start()
    for part in range(parts):
        save(labels - 1, part).wait()


def snp_side(idx, core, env, sums, own, other, labels):
    snp_rows, half = own.shape
    all_samples = 2 * half
    words = snp_rows // LANES
    width = labels * snp_rows + snp_rows // 2
    any_spec = pl.BlockSpec(memory_space=pl.ANY)
    smem = pl.BlockSpec(memory_space=pltpu.SMEM)
    vmem = pl.BlockSpec(memory_space=pltpu.VMEM)
    return pl.pallas_call(
        snp_side_kernel,
        out_shape=jax.ShapeDtypeStruct((all_samples, width), jnp.bfloat16),
        in_specs=[smem, smem, vmem, vmem, any_spec, any_spec],
        out_specs=any_spec,
        scratch_shapes=[
            pltpu.VMEM((snp_rows, all_samples), jnp.bfloat16),
            pltpu.VMEM((all_samples * words, LANES), jnp.float32),
            pltpu.VMEM((all_samples * words, LANES), jnp.float32),
            pltpu.VMEM((all_samples, snp_rows), jnp.bfloat16),
            pltpu.VMEM((snp_rows, LANES), jnp.float32),
            pltpu.SemaphoreType.DMA((all_samples // 1024,)),
            pltpu.SemaphoreType.DMA((4,)),
        ],
        compiler_params=pltpu.CompilerParams(vmem_limit_bytes=60 * MIB),
        cost_estimate=pl.CostEstimate(
            flops=40 * 10**9, bytes_accessed=60 * 10**6, transcendentals=0
        ),
        name="snp_side",
    )(idx, core, env, sums, own, other)


def window_plan(start, end, bounds_ref, n_bounds, total_blocks):
    middle = (start + end - 1) // 2
    lower_edge = jnp.zeros_like(start)
    upper_edge = jnp.full_like(end, total_blocks)
    for i in range(n_bounds):
        edge = bounds_ref[i]
        before = edge <= middle
        lower_edge = jnp.where(before, jnp.maximum(lower_edge, edge), lower_edge)
        upper_edge = jnp.where(before, upper_edge, jnp.minimum(upper_edge, edge))
    return jnp.maximum(start, lower_edge), jnp.minimum(end, upper_edge)


def select_kernel(
    round_ref, pos_ref, bounds_ref, start_ref, end_ref, own_ref, other_ref, order_ref,
    rounds_ref, plan_ref, full_ref, *rest, caps, blocks_dev,
):
    del order_ref
    pay_refs, (slots, edges) = rest[: len(caps)], rest[len(caps) :]
    reach = len(caps)
    chips, genes = start_ref.shape
    half = own_ref.shape[1]
    chip, core = pos_ref[0], pos_ref[1]
    turn = round_ref[0]
    low, high = window_plan(
        start_ref[...], end_ref[...], bounds_ref, bounds_ref.shape[0], chips * blocks_dev
    )
    edges[0] = low
    edges[1] = high
    at = lax.broadcasted_iota(jnp.int32, (chips, genes), 0)
    upto = (
        lax.broadcasted_iota(jnp.int32, (genes, genes), 0)
        <= lax.broadcasted_iota(jnp.int32, (genes, genes), 1)
    ).astype(jnp.bfloat16)
    rounds = jnp.int32(0)
    for way in range(2):
        for k in range(1, reach + 1):
            to = at + (k if way == 0 else -k)
            need = (
                (low < (to + 1) * blocks_dev) & (high > to * blocks_dev)
                & (low < high) & (to >= 0) & (to < chips)
            )
            rank = jnp.dot(
                need.astype(jnp.float32).astype(jnp.bfloat16), upto,
                preferred_element_type=jnp.float32,
            ).astype(jnp.int32)
            cap = caps[k - 1]
            slot = rank - 1 - turn * cap
            slots[way * reach + k - 1] = jnp.where(
                need & (slot >= 0) & (slot < cap), slot, -1
            )
            rounds = jnp.maximum(rounds, (jnp.max(rank) + cap - 1) // cap)
    rounds_ref[0] = rounds

    plan_ref[...] = jnp.zeros_like(plan_ref)
    plan_ref[0, pl.ds(0, 1), :] = lax.broadcasted_iota(jnp.int32, (1, genes), 1)
    plan_ref[1, pl.ds(0, 1), :] = edges[0, pl.ds(chip, 1), :]
    plan_ref[2, pl.ds(0, 1), :] = edges[1, pl.ds(chip, 1), :]
    for side in range(2):
        way = core if side == 0 else 1 - core
        for k in range(1, reach + 1):
            source = chip + (2 * way - 1) * k
            valid = (source >= 0) & (source < chips)
            row = jnp.clip(source, 0, chips - 1)
            to = pl.ds(1 + side * reach + k - 1, 1)
            slot = slots[way * reach + k - 1, pl.ds(row, 1), :]
            plan_ref[0, to, :] = jnp.where(valid, slot, -1)
            plan_ref[1, to, :] = edges[0, pl.ds(row, 1), :]
            plan_ref[2, to, :] = jnp.where(valid, edges[1, pl.ds(row, 1), :], 0)

    picks = []
    for k in range(1, reach + 1):
        slot = slots[core * reach + k - 1, pl.ds(chip, 1), :]
        rows = lax.broadcasted_iota(jnp.int32, (caps[k - 1], genes), 0)
        picks.append((rows == slot).astype(jnp.float32).astype(jnp.bfloat16))
    step = 1024

    def copy(i, carry):
        cols = pl.ds(pl.multiple_of(i * step, step), step)
        late = pl.ds(pl.multiple_of(half + i * step, step), step)
        a, b = own_ref[:, cols], other_ref[:, cols]
        first = jnp.where(core == 0, a, b)
        second = jnp.where(core == 0, b, a)
        full_ref[:, cols] = first
        full_ref[:, late] = second
        for pick, pay in zip(picks, pay_refs):
            for part, to in ((first, cols), (second, late)):
                pay[:, to] = jnp.dot(
                    pick, part, preferred_element_type=jnp.float32
                ).astype(jnp.bfloat16)
        return carry

    lax.fori_loop(0, half // step, copy, 0)


def select(turn, pos, bounds, start, end, own, other, order, caps, blocks_dev):
    genes, half = own.shape
    chips = start.shape[0]
    reach = len(caps)
    smem = pl.BlockSpec(memory_space=pltpu.SMEM)
    vmem = pl.BlockSpec(memory_space=pltpu.VMEM)
    plan_rows = -(-(2 * reach + 1) // 8) * 8
    return pl.pallas_call(
        functools.partial(select_kernel, caps=caps, blocks_dev=blocks_dev),
        out_shape=(
            jax.ShapeDtypeStruct((1,), jnp.int32),
            jax.ShapeDtypeStruct((3, plan_rows, genes), jnp.int32),
            jax.ShapeDtypeStruct((genes, 2 * half), jnp.bfloat16),
            *[jax.ShapeDtypeStruct((cap, 2 * half), jnp.bfloat16) for cap in caps],
        ),
        in_specs=[smem, smem, smem, vmem, vmem, vmem, vmem, pl.BlockSpec(memory_space=pl.ANY)],
        out_specs=(smem, vmem, vmem, *[vmem for _ in caps]),
        scratch_shapes=[
            pltpu.VMEM((2 * reach, chips, genes), jnp.int32),
            pltpu.VMEM((2, chips, genes), jnp.int32),
        ],
        compiler_params=pltpu.CompilerParams(vmem_limit_bytes=24 * MIB),
        name="select",
    )(turn, pos, bounds, start, end, own, other, order)


def product_kernel(
    pos_ref, sums_ref, plan_ref, *rest, caps, labels, genes, blocks_dev
):
    reach = len(caps)
    n_in = 1 + 2 * reach
    gene_refs = rest[:n_in]
    weights_ref, out_ref, power_ref, rows, total, power = rest[n_in:]
    step = pl.program_id(0)
    steps = pl.num_programs(0)
    snp_rows = sums_ref.shape[1]
    depth, width = weights_ref.shape
    block = SNP_BLOCK
    sizes = (genes,) + tuple(caps) + tuple(caps)
    starts = [sum(sizes[:i]) for i in range(n_in)]
    used = sum(sizes)

    @pl.when(step == 0)
    def _():
        total[...] = jnp.zeros_like(total)
        power[...] = jnp.zeros_like(power)

    for ref, start, size in zip(gene_refs, starts, sizes):
        rows[pl.ds(start, size), :] = ref[...]
    for n in range(width // block):
        cols = pl.ds(n * block, block)
        total[pl.ds(0, used), cols] += jnp.dot(
            rows[...], weights_ref[:, cols], preferred_element_type=jnp.float32
        )
    kept = power[...]
    for t in range(depth // LANES):
        x = gene_refs[0][:, pl.ds(t * LANES, LANES)].astype(jnp.float32)
        kept = kept + x * x
    power[...] = kept

    @pl.when(step == steps - 1)
    def _():
        chip, core = pos_ref[0], pos_ref[1]
        share_blocks = blocks_dev // 2
        cross = sums_ref[1:2, :]
        inter = sums_ref[2:3, :]
        inv = 1.0 / (inter - cross * (cross / sums_ref[0:1, :]) + 0.1 * inter)

        def peak(col, inv_block):
            v = total[:, pl.ds(col, block)]
            v = v * v * inv_block
            best = v[:, :LANES]
            for t in range(1, block // LANES):
                best = jnp.maximum(best, v[:, t * LANES : (t + 1) * LANES])
            return jnp.max(best.T, axis=0, keepdims=True)

        peaks = []
        for q in range(labels):
            for b in range(blocks_dev):
                peaks.append(
                    peak(q * snp_rows + b * block, inv[:, b * block : (b + 1) * block])
                )
        for b in range(share_blocks):
            mine = inv[:, b * block : (b + 1) * block]
            late = inv[:, (share_blocks + b) * block : (share_blocks + b + 1) * block]
            peaks.append(
                peak(labels * snp_rows + b * block, jnp.where(core == 0, mine, late))
            )
        while len(peaks) % 8:
            peaks.append(jnp.zeros_like(peaks[0]))
        peaks = jnp.concatenate(peaks, axis=0)
        out_ref[...] = jnp.zeros_like(out_ref)
        slot_of = lax.broadcasted_iota(jnp.int32, (total.shape[0], genes), 0)
        for i in range(n_in):
            slot = plan_ref[0, pl.ds(i, 1), :]
            slot = jnp.where(slot >= 0, slot + starts[i], -1)
            low = plan_ref[1, pl.ds(i, 1), :]
            high = plan_ref[2, pl.ds(i, 1), :]
            spread = jnp.dot(
                peaks, (slot_of == slot).astype(jnp.float32),
                precision=lax.Precision.HIGHEST, preferred_element_type=jnp.float32,
            )

            def masked(row, snp_block):
                inside = (snp_block >= low) & (snp_block < high)
                return jnp.where(inside, spread[row : row + 1], 0.0)

            found = []
            for q in range(labels):
                best = jnp.zeros((1, genes), jnp.float32)
                for b in range(blocks_dev):
                    best = jnp.maximum(best, masked(q * blocks_dev + b, chip * blocks_dev + b))
                found.append(best)
            best = jnp.zeros((1, genes), jnp.float32)
            for b in range(share_blocks):
                best = jnp.maximum(
                    best,
                    masked(
                        labels * blocks_dev + b, chip * blocks_dev + core * share_blocks + b
                    ),
                )
            out_rows = [best]
            for c in range(2):
                out_rows += [jnp.where(core == c, v, 0.0) for v in found]
            while len(out_rows) % 8:
                out_rows.append(jnp.zeros_like(best))
            if i == 0:
                target = chip
            else:
                way = core if i <= reach else 1 - core
                target = chip + (2 * way - 1) * ((i - 1) % reach + 1)
            out_ref[target + reach] = jnp.concatenate(out_rows, axis=0)
        powers = jnp.sum(power[...].T, axis=0, keepdims=True)
        power_ref[...] = jnp.broadcast_to(powers, power_ref.shape)


def products(pos, sums, plan, full, mine, other, weights, caps, labels, chips, blocks_dev):
    genes, all_samples = full.shape
    width = weights.shape[1]
    snp_rows = sums.shape[1]
    reach = len(caps)
    depth = 1024
    used = genes + 2 * sum(caps)
    padded = -(-used // LANES) * LANES
    out_rows = -(-(1 + 2 * labels) // 8) * 8

    def blocked(x):
        return pl.BlockSpec((x.shape[0], depth), lambda k: (0, k))

    arrays = (full, *mine, *other)
    return pl.pallas_call(
        functools.partial(
            product_kernel, caps=caps, labels=labels, genes=genes, blocks_dev=blocks_dev
        ),
        grid=(all_samples // depth,),
        out_shape=(
            jax.ShapeDtypeStruct((chips + 2 * reach, out_rows, genes), jnp.float32),
            jax.ShapeDtypeStruct((8, genes), jnp.float32),
        ),
        in_specs=[
            pl.BlockSpec(memory_space=pltpu.SMEM),
            pl.BlockSpec(sums.shape, lambda k: (0, 0)),
            pl.BlockSpec(plan.shape, lambda k: (0, 0, 0)),
            *[blocked(x) for x in arrays],
            pl.BlockSpec((depth, width), lambda k: (k, 0)),
        ],
        out_specs=(
            pl.BlockSpec((chips + 2 * reach, out_rows, genes), lambda k: (0, 0, 0)),
            pl.BlockSpec((8, genes), lambda k: (0, 0)),
        ),
        scratch_shapes=[
            pltpu.VMEM((used, depth), jnp.bfloat16),
            pltpu.VMEM((padded, width), jnp.float32),
            pltpu.VMEM((genes, LANES), jnp.float32),
        ],
        compiler_params=pltpu.CompilerParams(vmem_limit_bytes=48 * MIB),
        cost_estimate=pl.CostEstimate(
            flops=2 * used * all_samples * width,
            bytes_accessed=2 * all_samples * (width + used),
            transcendentals=0,
        ),
        name="products",
    )(pos, sums, plan, *arrays, weights)


def shards(genotypes, phenotypes, environment, shuffles, window_start, window_end, chrom_bounds):
    snp_rows, half = genotypes.shape
    genes = phenotypes.shape[0]
    perms = shuffles.shape[0]
    chips = lax.axis_size("genome")
    cores = lax.axis_size("sample")
    genome_pos = lax.axis_index("genome")
    sample_pos = lax.axis_index("sample")
    blocks_dev = snp_rows // SNP_BLOCK
    reach = (HALF_BLK + blocks_dev - 1) // blocks_dev
    all_samples = half * cores
    labels = perms // cores
    caps = tuple(min(genes, genes * 4 >> k) for k in range(1, reach + 1))

    small = jnp.concatenate([shuffles.astype(jnp.float32), environment[None]], axis=0)
    other_small = swapped(small)
    other_pheno = swapped(phenotypes)
    other_geno = swapped(genotypes)
    pos = jnp.stack([genome_pos, sample_pos]).astype(jnp.int32)
    start = window_start.reshape(chips, genes)
    end = window_end.reshape(chips, genes)

    def chosen(turn):
        return select(
            turn, pos, chrom_bounds, start, end, phenotypes, other_pheno, other_small, caps,
            blocks_dev,
        )

    def travel(payloads):
        mine = []
        for k, payload in enumerate(payloads, 1):
            pairs = [(i * cores, (i + k) * cores) for i in range(chips - k)]
            pairs += [((i + k) * cores + 1, i * cores + 1) for i in range(chips - k)]
            mine.append(lax.ppermute(payload, ("genome", "sample"), pairs))
        return mine

    rounds, plan, full, *payloads = chosen(jnp.zeros((1,), jnp.int32))
    mine = travel(payloads)

    sums = lax.psum(local_moments(genotypes, environment[None]), "sample")
    env = jnp.concatenate([environment, other_small[perms]])[None]
    first_label = sample_pos * labels
    idx = jnp.concatenate(
        [
            lax.dynamic_slice_in_dim(shuffles, first_label, labels, 0),
            lax.dynamic_slice_in_dim(other_small, first_label, labels, 0).astype(jnp.int32),
        ],
        axis=1,
    ) * (snp_rows // LANES)
    weights = snp_side(
        idx.reshape(-1), pos[1:], env, sums, genotypes, other_geno, labels
    )

    def met(plan, full, mine):
        other = [swapped(x) for x in mine]
        return products(
            pos, sums, plan, full, mine, other, weights, caps, labels, chips, blocks_dev
        )

    *mine, weights = lax.optimization_barrier((*mine, weights))
    found, power = met(plan, full, mine)

    def more(carry):
        return carry[0] < rounds[0]

    def again(carry):
        turn, best = carry
        _, plan, full, *payloads = chosen(jnp.full((1,), turn, jnp.int32))
        return turn + 1, jnp.maximum(best, met(plan, full, travel(payloads))[0])

    _, found = lax.while_loop(more, again, (jnp.int32(1), found))
    found = found[reach : reach + chips]
    sent = jnp.broadcast_to(found[:, None], (chips, cores) + found.shape[1:])
    sent = sent.reshape((chips * cores,) + found.shape[1:])
    peak = jnp.max(lax.all_to_all(sent, ("genome", "sample"), 0, 0, tiled=True), axis=0)
    return jnp.sqrt(peak[: perms + 1] / (power[0:1] / all_samples + 1e-05))


def solution(mesh):
    placed = (
        P("genome", "sample"),
        P("genome", "sample"),
        P("sample"),
        P(None, "sample"),
        P(),
        P(),
        P(),
    )
    return jax.shard_map(
        shards, mesh=mesh, in_specs=placed, out_specs=P(None, "genome"), check_vma=False
    )
```

time: 182 us -> 111 us (0.61)
  blocking collectives: 41.7 us -> 3.99 us
  waiting for transfers between devices: 41.2 us -> 11.8 us
  local copies, waits for them, and re-layouts: 10.1 us -> 3.56 us
  other arithmetic: 6.64 us -> 3.79 us
  Pallas kernels: 60.2 us -> 62.8 us
  starting transfers between devices: 21.2 us -> 23.6 us
    pmax x1 -> x0, blocking collectives: 41.7 us -> none  [shards(): lax.pmax(peaks[:, margin:margin + genome_size * gene_rows], ('genome', 's...]
    ppermute x8 -> x4, waiting for transfers between devices: 41.2 us -> 0.01 us  [travel(): mine.append(lax.ppermute(payload, ('genome', 'sample'), pairs))]
    all_to_all x0 -> x1, waiting for transfers between devices: none -> 7.4 us  [shards(): lax.all_to_all(sent, ('genome', 'sample'), 0, 0, tiled=True)]
    unnamed x15 -> x19, local copies, waits for them, and re-layouts: 7.48 us -> 1.48 us
    all_to_all x0 -> x1, starting transfers between devices: none -> 5.49 us  [shards(): lax.all_to_all(sent, ('genome', 'sample'), 0, 0, tiled=True)]
    ppermute x8 -> x4, starting transfers between devices: 20.7 us -> 16 us  [travel(): mine.append(lax.ppermute(payload, ('genome', 'sample'), pairs))]
    ppermute x3 -> x7, waiting for transfers between devices: 0.01 us -> 4.41 us  [swapped(): lax.ppermute(x, 'sample', [(i, (i + 1) % count) for i in range(count)])]
    psum x0 -> x1, blocking collectives: none -> 3.99 us  [shards(): sums = lax.psum(local_moments(genotypes, environment[None]), 'sample')]
  transfers between devices with their start and end apart: 11 -> 12, of which waited for: 3 -> 2; matrix products, arithmetic and copies ran while one was open for 8% -> 4% of each run, Pallas kernels for 23% -> 42%
where the time goes in v2:
time: 111 us; the launch traced here: 110 us
  Pallas kernels  62.8 us (57%)
  starting transfers between devices  23.6 us (21%)
  waiting for transfers between devices  11.8 us (11%)
  blocking collectives  3.99 us (4%)
  other arithmetic  3.79 us (3%)
  local copies, waits for them, and re-layouts  3.56 us (3%)
    pallas_call x1, Pallas kernels, snp_side(): pl.pallas_call(snp_side_kernel, out_shape=jax.ShapeDtypeStruct((all_sampl...  37.2 us
    pallas_call x1, Pallas kernels, products(): pl.pallas_call(functools.partial(product_kernel, caps=caps, labels=labels...  16.6 us
    ppermute x4, starting transfers between devices, travel(): mine.append(lax.ppermute(payload, ('genome', 'sample'), pairs))  16 us
    all_to_all x1, waiting for transfers between devices, shards(): lax.all_to_all(sent, ('genome', 'sample'), 0, 0, tiled=True)  7.4 us
    all_to_all x1, starting transfers between devices, shards(): lax.all_to_all(sent, ('genome', 'sample'), 0, 0, tiled=True)  5.49 us
    pallas_call x1, Pallas kernels, local_moments(): pl.pallas_call(moments_kernel, grid=(half // chunk,), out_shape=jax.Shape...  5.35 us
    ppermute x7, waiting for transfers between devices, swapped(): lax.ppermute(x, 'sample', [(i, (i + 1) % count) for i in range(count)])  4.41 us
    psum x1, blocking collectives, shards(): sums = lax.psum(local_moments(genotypes, environment[None]), 'sample')  3.99 us
  transfers between devices with their start and end apart: 12, of which 2 were waited for; matrix products, arithmetic and copies ran while one was open for 4% of the time, Pallas kernels for 42%

profile of v2, /device:TPU:0, one launch (start us, length us, event | category | flops | bytes accessed | tf_op | source)
XLA Modules:
  0.0 110.4 jit_solution(15809543013048755067)
XLA Ops:
  0.0 0.5 collective-permute-start.14
  0.5 0.9 convert_element_type.6
  1.3 0.8 pad_maximum_fusion
  2.1 0.1 collective-permute-start.9
  2.2 0.5 collective-permute-start.8
  2.6 0.8 reshape.14.start_ref
  3.4 0.8 reshape.15.end_ref
  4.2 5.3 %local_moments.1 = f32[8,512]{1,0:T(8,128)} custom-call(bf16[512,4096]{1,0:T(8,128)(2,1)} %own_ref.3, f32[1,4096]{1,0:T(1,128)} %bitcast.20), custom_call_target="tpu_custom_call" | custom-call | flops 5000000000 | bytes 4194304 | tf_op jit(solution)/shard_map/local_moments/pallas_call | solution.py:64
  9.5 4.0 %psum.7.sums_ref = f32[8,512]{1,0:T(8,128)S(1)} all-reduce(f32[8,512]{1,0:T(8,128)} %local_moments.1), channel_id=1, replica_groups=mesh['genome'=16,'sample'=2] {'sample'}, use_global_device_ids=true, to_apply=%region_0.0 | all-reduce | flops 4096 | bytes 32768 | tf_op jit(solution)/shard_map/psum | solution.py:539
  13.5 0.1 pad_add_fusion.pos_ref
  13.7 0.6 copy.8
  14.3 0.6 pad_maximum_fusion.1
  15.0 3.7 %select.2 = (s32[1]{0:T(128)}, s32[3,16,64]{2,1,0:T(8,128)S(1)}, bf16[64,8192]{1,0:T(8,128)(2,1)S(1)}, bf16[64,8192]{1,0:T(8,128)(2,1)}, bf16[64,8192]{1,0:T(8,1...) custom-call(s32[1]{0:T(128)} %constant.6.clone.1.round_ref, s32[2]{0:T(128)S(1)} %pad_add_fusion.pos_ref, ...), custom_call_target="tpu_custom_call" | custom-call | tf_op jit(solution)/shard_map/select/pallas_call | solution.py:322
  18.7 4.8 %collective-permute-start.10 = (bf16[64,8192]{1,0:T(8,128)(2,1)}, bf16[64,8192]{1,0:T(8,128)(2,1)S(1)}, u32[]{:S(2)}, u32[]{:S(2)}) collective-permute-start(bf16[64,8192]{1,0:T(8,128)(2,1)} %get-tuple-element.91), channel_id=1, source_target_pairs={{0,2},{2,4},{4,6},{6,8},{8,10},{10,12},{12,14},{14,16},{16,18},{18... | collective-permute-start | bytes 3145736 | tf_op jit(solution)/shard_map/ppermute | solution.py:533
  23.5 3.4 %collective-permute-start.11 = (bf16[64,8192]{1,0:T(8,128)(2,1)}, bf16[64,8192]{1,0:T(8,128)(2,1)S(1)}, u32[]{:S(2)}, u32[]{:S(2)}) collective-permute-start(bf16[64,8192]{1,0:T(8,128)(2,1)} %get-tuple-element.92), channel_id=1, source_target_pairs={{0,4},{2,6},{4,8},{6,10},{8,12},{10,14},{12,16},{14,18},{16,20},{1... | collective-permute-start | bytes 3145736 | tf_op jit(solution)/shard_map/ppermute | solution.py:533
  26.9 5.1 %collective-permute-start.12 = (bf16[32,8192]{1,0:T(8,128)(2,1)S(1)}, bf16[32,8192]{1,0:T(8,128)(2,1)}, u32[]{:S(2)}, u32[]{:S(2)}) collective-permute-start(bf16[32,8192]{1,0:T(8,128)(2,1)S(1)} %get-tuple-element.93), channel_id=1, source_target_pairs={{0,6},{2,8},{4,10},{6,12},{8,14},{10,16},{12,18},{14,20},{16,22},{... | collective-permute-start | bytes 1572872 | tf_op jit(solution)/shard_map/ppermute | solution.py:533
  32.0 2.7 %collective-permute-start.13 = (bf16[16,8192]{1,0:T(8,128)(2,1)}, bf16[16,8192]{1,0:T(8,128)(2,1)S(1)}, u32[]{:S(2)}, u32[]{:S(2)}) collective-permute-start(bf16[16,8192]{1,0:T(8,128)(2,1)} %get-tuple-element.94), channel_id=1, source_target_pairs={{0,8},{2,10},{4,12},{6,14},{8,16},{10,18},{12,20},{14,22},{16,24},... | collective-permute-start | bytes 786440 | tf_op jit(solution)/shard_map/ppermute | solution.py:533
  34.7 37.2 %snp_side.1.rest_9_ = bf16[8192,1280]{1,0:T(8,128)(2,1)} custom-call(s32[16384]{0:T(1024)} %bitcast.17, s32[1]{0:T(128)} %bitcast.3.core_ref, f32[1,8192]{1,0:T(1,128)} %bitcast.21, f32[8,512]{1,0:T(8,128)S(1)} %psum.7.sums_ref, bf16[512,4096]{1,0:T(8,128)(2,1)} %own_ref.3, bf16[512,4096]{1,0:T(8,128)(2,1)} %collective-permute-done.14.other_ref), custom_call_target="tpu_custom_call" | custom-call | flops 40000000000 | bytes 60000000 | tf_op jit(solution)/shard_map/snp_side/pallas_call | solution.py:199
  72.0 0.2 collective-permute-start.15
  72.2 0.4 collective-permute-start.16
  72.6 0.1 collective-permute-start.17
  72.7 0.4 collective-permute-start.18
  73.1 4.4 %collective-permute-done.18.rest_8_ = bf16[16,8192]{1,0:T(8,128)(2,1)} collective-permute-done((bf16[16,8192]{1,0:T(8,128)(2,1)S(1)}, bf16[16,8192]{1,0:T(8,128)(2,1)}, u32[]{:S(2)}, u32[]{:S(2)}) %collective-permute-start.18) | collective-permute-done | bytes 262176 | tf_op jit(solution)/shard_map/ppermute | solution.py:26
  77.5 16.6 %products.2 = (f32[24,8,64]{2,1,0:T(8,128)S(1)}, f32[8,64]{1,0:T(8,128)S(1)}) custom-call(s32[2]{0:T(128)} %copy-done.6, f32[8,512]{1,0:T(8,128)} %copy-done.7, s32[3,16,64]{2,1,0:T(8,128)S(1)} %get-tuple-element.89.plan_ref, bf16[64,8192]{1,0:T(8,128)(2,1)S(1)} %get-tuple-element.90.rest_0_, bf16[64,8192]{1,0:T(8,128)(2,1)S(1)} %collective-permute-done.10.rest_1_, ...), custom_call_target="tpu_custom_call" | custom-call | flops 8724152320 | bytes 27787264 | tf_op jit(solution)/shard_map/products/pallas_call | solution.py:465
  94.1 0.6 while.10
  94.7 0.7 reshape.17
  95.4 5.5 %all-to-all-start = ((f32[32,1,512]{2,1,0:T(1,128)}), f32[32,1,512]{2,1,0:T(1,128)S(1)}, u32[]{:S(2)}, u32[]{:S(2)}) async-start(f32[32,1,512]{2,1,0:T(1,128)} %reshape.17), calls=%async_computation | async-start | bytes 131072 | tf_op jit(solution)/shard_map/all_to_all | solution.py:574
  100.9 7.4 %all-to-all-done = f32[32,1,512]{2,1,0:T(1,128)S(1)} async-done(((f32[32,1,512]{2,1,0:T(1,128)}), f32[32,1,512]{2,1,0:T(1,128)S(1)}, u32[]{:S(2)}, u32[]{:S(2)}) %all-to-all-start) | async-done | bytes 65568 | tf_op jit(solution)/shard_map/all_to_all | solution.py:574
  108.3 0.5 broadcast.5
  108.9 0.8 reduce
  109.7 0.1 reshape.18
  109.8 0.6 divide_sqrt_fusion
  (34 shorter events, 0.2 us)
Async XLA Ops:
  0.0 34.7 %collective-permute-start.14 = (bf16[512,4096]{1,0:T(8,128)(2,1)}, bf16[512,4096]{1,0:T(8,128)(2,1)}, u32[]{:S(2)}, u32[]{:S(2)}) collective-permute-start(bf16[512,4096]{1,0:T(8,128)(2,1)} %own_ref.3), channel_id=1, source_target_pairs={{0,1},{1,0},{2,3},{3,2},{4,5},{5,4},{6,7},{7,6},{8,9},{9,8},{10,11... | collective-permute-start | bytes 12582920 | tf_op jit(solution)/shard_map/ppermute | solution.py:26
  2.1 11.6 %collective-permute-start.9 = (f32[5,4096]{1,0:T(8,128)S(1)}, f32[5,4096]{1,0:T(8,128)S(1)}, u32[]{:S(2)}, u32[]{:S(2)}) collective-permute-start(f32[5,4096]{1,0:T(8,128)S(1)} %pad_maximum_fusion), channel_id=1, source_target_pairs={{0,1},{1,0},{2,3},{3,2},{4,5},{5,4},{6,7},{7,6},{8,9},{9,8},{10,11... | collective-permute-start | bytes 245768 | tf_op jit(solution)/shard_map/ppermute | solution.py:26
  2.2 12.8 %collective-permute-start.8 = (bf16[64,4096]{1,0:T(8,128)(2,1)}, bf16[64,4096]{1,0:T(8,128)(2,1)S(1)}, u32[]{:S(2)}, u32[]{:S(2)}) collective-permute-start(bf16[64,4096]{1,0:T(8,128)(2,1)} %own_ref.2), channel_id=1, source_target_pairs={{0,1},{1,0},{2,3},{3,2},{4,5},{5,4},{6,7},{7,6},{8,9},{9,8},{10,11... | collective-permute-start | bytes 1572872 | tf_op jit(solution)/shard_map/ppermute | solution.py:26
  4.1 9.3 %copy-start.3 = (s32[4,4096]{1,0:T(4,128)S(1)}, s32[4,4096]{1,0:T(4,128)}, u32[]{:S(2)}) copy-start(s32[4,4096]{1,0:T(4,128)} %param.12) | copy-start | bytes 196612
  4.2 10.2 %copy-start.4 = (f32[4096]{0:T(1024)S(1)}, f32[4096]{0:T(1024)}, u32[]{:S(2)}) copy-start(f32[4096]{0:T(1024)} %param.11) | copy-start | bytes 49156
  4.2 10.8 %copy-start = (bf16[64,4096]{1,0:T(8,128)(2,1)S(1)}, bf16[64,4096]{1,0:T(8,128)(2,1)}, u32[]{:S(2)}) copy-start(bf16[64,4096]{1,0:T(8,128)(2,1)} %own_ref.2) | copy-start | bytes 1572868
  4.2 10.8 %copy-start.5 = (s32[15]{0:T(128)S(1)}, s32[15]{0:T(128)}, u32[]{:S(2)}) copy-start(s32[15]{0:T(128)} %bounds_ref.1) | copy-start | bytes 184
  13.5 58.5 %copy-start.7 = (f32[8,512]{1,0:T(8,128)}, f32[8,512]{1,0:T(8,128)S(1)}, u32[]{:S(2)}) copy-start(f32[8,512]{1,0:T(8,128)S(1)} %psum.7.sums_ref) | copy-start | bytes 49156
  13.6 58.4 %copy-start.6 = (s32[2]{0:T(128)}, s32[2]{0:T(128)S(1)}, u32[]{:S(2)}) copy-start(s32[2]{0:T(128)S(1)} %pad_add_fusion.pos_ref) | copy-start | bytes 28
  13.6 9.8 %copy-start.2 = (f32[5,4096]{1,0:T(8,128)}, f32[5,4096]{1,0:T(8,128)S(1)}, u32[]{:S(2)}) copy-start(f32[5,4096]{1,0:T(8,128)S(1)} %collective-permute-done.9.order_ref) | copy-start | bytes 245764
  15.0 3.7 %copy-start.1 = (bf16[64,4096]{1,0:T(8,128)(2,1)}, bf16[64,4096]{1,0:T(8,128)(2,1)S(1)}, u32[]{:S(2)}) copy-start(bf16[64,4096]{1,0:T(8,128)(2,1)S(1)} %collective-permute-done.8.other_ref) | copy-start | bytes 1572868
  18.7 53.3 %collective-permute-start.10 = (bf16[64,8192]{1,0:T(8,128)(2,1)}, bf16[64,8192]{1,0:T(8,128)(2,1)S(1)}, u32[]{:S(2)}, u32[]{:S(2)}) collective-permute-start(bf16[64,8192]{1,0:T(8,128)(2,1)} %get-tuple-element.91), channel_id=1, source_target_pairs={{0,2},{2,4},{4,6},{6,8},{8,10},{10,12},{12,14},{14,16},{16,18},{18... | collective-permute-start | bytes 3145736 | tf_op jit(solution)/shard_map/ppermute | solution.py:533
  23.5 48.5 %collective-permute-start.11 = (bf16[64,8192]{1,0:T(8,128)(2,1)}, bf16[64,8192]{1,0:T(8,128)(2,1)S(1)}, u32[]{:S(2)}, u32[]{:S(2)}) collective-permute-start(bf16[64,8192]{1,0:T(8,128)(2,1)} %get-tuple-element.92), channel_id=1, source_target_pairs={{0,4},{2,6},{4,8},{6,10},{8,12},{10,14},{12,16},{14,18},{16,20},{1... | collective-permute-start | bytes 3145736 | tf_op jit(solution)/shard_map/ppermute | solution.py:533
  26.9 45.1 %collective-permute-start.12 = (bf16[32,8192]{1,0:T(8,128)(2,1)S(1)}, bf16[32,8192]{1,0:T(8,128)(2,1)}, u32[]{:S(2)}, u32[]{:S(2)}) collective-permute-start(bf16[32,8192]{1,0:T(8,128)(2,1)S(1)} %get-tuple-element.93), channel_id=1, source_target_pairs={{0,6},{2,8},{4,10},{6,12},{8,14},{10,16},{12,18},{14,20},{16,22},{... | collective-permute-start | bytes 1572872 | tf_op jit(solution)/shard_map/ppermute | solution.py:533
  32.0 40.0 %collective-permute-start.13 = (bf16[16,8192]{1,0:T(8,128)(2,1)}, bf16[16,8192]{1,0:T(8,128)(2,1)S(1)}, u32[]{:S(2)}, u32[]{:S(2)}) collective-permute-start(bf16[16,8192]{1,0:T(8,128)(2,1)} %get-tuple-element.94), channel_id=1, source_target_pairs={{0,8},{2,10},{4,12},{6,14},{8,16},{10,18},{12,20},{14,22},{16,24},... | collective-permute-start | bytes 786440 | tf_op jit(solution)/shard_map/ppermute | solution.py:533
  72.0 5.5 %collective-permute-start.15 = (bf16[64,8192]{1,0:T(8,128)(2,1)S(1)}, bf16[64,8192]{1,0:T(8,128)(2,1)}, u32[]{:S(2)}, u32[]{:S(2)}) collective-permute-start(bf16[64,8192]{1,0:T(8,128)(2,1)S(1)} %collective-permute-done.10.rest_1_), channel_id=1, source_target_pairs={{0,1},{1,0},{2,3},{3,2},{4,5},{5,4},{6,7},{7,6},{8,9},{9,8},{10,11... | collective-permute-start | bytes 3145736 | tf_op jit(solution)/shard_map/ppermute | solution.py:26
  72.2 5.3 %collective-permute-start.16 = (bf16[64,8192]{1,0:T(8,128)(2,1)S(1)}, bf16[64,8192]{1,0:T(8,128)(2,1)}, u32[]{:S(2)}, u32[]{:S(2)}) collective-permute-start(bf16[64,8192]{1,0:T(8,128)(2,1)S(1)} %collective-permute-done.11.rest_2_), channel_id=1, source_target_pairs={{0,1},{1,0},{2,3},{3,2},{4,5},{5,4},{6,7},{7,6},{8,9},{9,8},{10,11... | collective-permute-start | bytes 3145736 | tf_op jit(solution)/shard_map/ppermute | solution.py:26
  72.6 4.9 %collective-permute-start.17 = (bf16[32,8192]{1,0:T(8,128)(2,1)}, bf16[32,8192]{1,0:T(8,128)(2,1)}, u32[]{:S(2)}, u32[]{:S(2)}) collective-permute-start(bf16[32,8192]{1,0:T(8,128)(2,1)} %collective-permute-done.12.rest_3_), channel_id=1, source_target_pairs={{0,1},{1,0},{2,3},{3,2},{4,5},{5,4},{6,7},{7,6},{8,9},{9,8},{10,11... | collective-permute-start | bytes 1572872 | tf_op jit(solution)/shard_map/ppermute | solution.py:26
  72.7 4.8 %collective-permute-start.18 = (bf16[16,8192]{1,0:T(8,128)(2,1)S(1)}, bf16[16,8192]{1,0:T(8,128)(2,1)}, u32[]{:S(2)}, u32[]{:S(2)}) collective-permute-start(bf16[16,8192]{1,0:T(8,128)(2,1)S(1)} %collective-permute-done.13.rest_4_), channel_id=1, source_target_pairs={{0,1},{1,0},{2,3},{3,2},{4,5},{5,4},{6,7},{7,6},{8,9},{9,8},{10,11... | collective-permute-start | bytes 786440 | tf_op jit(solution)/shard_map/ppermute | solution.py:26
  95.4 12.9 %all-to-all-start = ((f32[32,1,512]{2,1,0:T(1,128)}), f32[32,1,512]{2,1,0:T(1,128)S(1)}, u32[]{:S(2)}, u32[]{:S(2)}) async-start(f32[32,1,512]{2,1,0:T(1,128)} %reshape.17), calls=%async_computation | async-start | bytes 131072 | tf_op jit(solution)/shard_map/all_to_all | solution.py:574

commit v3 on v2

v3 whole, which is shorter than its diff:
```python
import functools

import jax
import jax.numpy as jnp
from jax import lax
from jax.experimental import pallas as pl
from jax.experimental.pallas import tpu as pltpu
from jax.sharding import PartitionSpec as P

SNP_BLOCK = 256
HALF_BLK = 7
LANES = 128
ROWS_STEP = 16
UNROLL = 16
SLOT = 8
CHUNK = 1024
MIB = 2**20


def passed_along(x, axis, by):
    count = lax.axis_size(axis)
    pairs = [(i, i + by) for i in range(count) if 0 <= i + by < count]
    return lax.ppermute(x, axis, pairs)


def swapped(x):
    count = lax.axis_size("sample")
    return lax.ppermute(x, "sample", [(i, (i + 1) % count) for i in range(count)])


def moments_kernel(geno_ref, env_ref, out_ref, sums):
    step = pl.program_id(0)
    snp_rows, chunk = geno_ref.shape

    @pl.when(step == 0)
    def _():
        sums[...] = jnp.zeros_like(sums)

    def add_rows(i, carry):
        first = pl.multiple_of(i * ROWS_STEP, ROWS_STEP)
        held = [sums[m, pl.ds(first, ROWS_STEP), :] for m in range(3)]
        for t in range(chunk // LANES):
            x = geno_ref[pl.ds(first, ROWS_STEP), pl.ds(t * LANES, LANES)].astype(jnp.float32)
            e = env_ref[:, pl.ds(t * LANES, LANES)]
            x = x * x
            held[0] = held[0] + x
            x = x * e
            held[1] = held[1] + x
            held[2] = held[2] + x * e
        for m in range(3):
            sums[m, pl.ds(first, ROWS_STEP), :] = held[m]
        return carry

    lax.fori_loop(0, snp_rows // ROWS_STEP, add_rows, 0, unroll=4)

    @pl.when(step == pl.num_programs(0) - 1)
    def _():
        rows = [jnp.sum(sums[m].T, axis=0, keepdims=True) for m in range(3)]
        rows.append(jnp.zeros((out_ref.shape[0] - 3, snp_rows), jnp.float32))
        out_ref[...] = jnp.concatenate(rows, axis=0)


def local_moments(geno, env):
    snp_rows, half = geno.shape
    chunk = CHUNK
    return pl.pallas_call(
        moments_kernel,
        grid=(half // chunk,),
        out_shape=jax.ShapeDtypeStruct((8, snp_rows), jnp.float32),
        in_specs=[
            pl.BlockSpec((snp_rows, chunk), lambda k: (0, k)),
            pl.BlockSpec((1, chunk), lambda k: (0, k)),
        ],
        out_specs=pl.BlockSpec((8, snp_rows), lambda k: (0, 0)),
        scratch_shapes=[pltpu.VMEM((3, snp_rows, LANES), jnp.float32)],
        compiler_params=pltpu.CompilerParams(vmem_limit_bytes=60 * MIB),
        cost_estimate=pl.CostEstimate(
            flops=5 * 10**9, bytes_accessed=2 * snp_rows * half, transcendentals=0
        ),
        name="local_moments",
    )(geno, env)


def snp_side_kernel(
    core_ref, env_own, env_other, sums_own, sums_other, shuf_own, shuf_other, own_ref, other_ref,
    out_ref,
    idx, geno, table, dest, stage, first_stage, slope, idx_sems, in_sems, out_sems, first_sems,
    *, labels,
):
    snp_rows, half = own_ref.shape
    all_samples = 2 * half
    chunks = all_samples // CHUNK
    words = snp_rows // LANES
    share = snp_rows // 2
    side = 2 * LANES
    core = core_ref[0]
    depth = geno.shape[0]

    def load(k):
        source = own_ref if k * CHUNK < half else other_ref
        return pltpu.make_async_copy(
            source.at[:, pl.ds((k * CHUNK) % half, CHUNK)], geno.at[k % depth],
            in_sems.at[k % depth],
        )

    def load_idx(q, h):
        source = shuf_own if h == 0 else shuf_other
        return pltpu.make_async_copy(
            source.at[core * labels + q],
            idx.at[pl.ds(q * all_samples + h * half, half)],
            idx_sems.at[2 * q + h],
        )

    def save_first(k):
        there = jnp.where(core == 0, k * CHUNK, (k * CHUNK + half) % all_samples)
        rows = pl.ds(pl.multiple_of(there, CHUNK), CHUNK)
        return pltpu.make_async_copy(
            first_stage.at[k % 2], out_ref.at[rows, pl.ds(labels * snp_rows, share)],
            first_sems.at[k % 2],
        )

    def save(q, k):
        return pltpu.make_async_copy(
            stage.at[k % 2],
            out_ref.at[pl.ds(k * CHUNK, CHUNK), pl.ds(q * snp_rows, snp_rows)],
            out_sems.at[k % 2],
        )

    for k in range(depth):
        load(k).start()
    for q in range(labels):
        for h in range(2):
            load_idx(q, h).start()
    sums = sums_own[...] + sums_other[...]
    slope[...] = jnp.broadcast_to(sums[1:2, :] / sums[0:1, :], (LANES, snp_rows)).T
    unit = (
        lax.broadcasted_iota(jnp.int32, (side, side), 0)
        == lax.broadcasted_iota(jnp.int32, (side, side), 1)
    ).astype(jnp.bfloat16)

    for k in range(chunks):
        load(k).wait()
        if k >= 2:
            save_first(k - 2).wait()
        env_ref = env_own if k * CHUNK < half else env_other

        def turn(i, carry, k=k, env_ref=env_ref):
            at = pl.multiple_of(i * side, side)
            e = env_ref[:, pl.ds((k * CHUNK) % half + at, side)]
            turned = []
            for j in range(snp_rows // side):
                rows = pl.ds(j * side, side)
                x = geno[k % depth, rows, pl.ds(at, side)].astype(jnp.float32)
                r = slope[rows, :]
                a = x * (e - jnp.concatenate([r] * (side // LANES), axis=1))
                t = lax.dot_general(
                    unit, a.astype(jnp.bfloat16), (((1,), (1,)), ((), ())),
                    preferred_element_type=jnp.float32,
                )
                for c in range(side // LANES):
                    word = j * (side // LANES) + c
                    table[pl.ds((k * CHUNK + at) * words + word, side, stride=words), :] = (
                        t[:, c * LANES : (c + 1) * LANES]
                    )
                turned.append(t)
            turned = jnp.concatenate(turned, axis=1)
            kept = jnp.where(core == 0, turned[:, :share], turned[:, share:])
            first_stage[k % 2, pl.ds(at, side), :] = kept.astype(jnp.bfloat16)
            return carry

        lax.fori_loop(0, CHUNK // side, turn, 0, unroll=2)
        save_first(k).start()
        if k + depth < chunks:
            load(k + depth).start()

    for q in range(labels):
        for h in range(2):
            load_idx(q, h).wait()

        def scatter(i, carry, q=q):
            first = pl.multiple_of(i * UNROLL, UNROLL)
            base = pl.multiple_of(first * words, UNROLL * words)
            held = [table[pl.ds(base + u * words, SLOT), :] for u in range(UNROLL)]
            for u in range(UNROLL):
                to = pl.multiple_of(idx[q * all_samples + first + u] * SLOT, SLOT)
                dest[pl.ds(to, SLOT), :] = held[u]
            return carry

        lax.fori_loop(0, all_samples // UNROLL, scatter, 0)
        for k in range(chunks):
            if q * chunks + k >= 2:
                save((q * chunks + k - 2) // chunks, (k - 2) % chunks).wait()

            def narrow(i, carry, k=k):
                at = pl.multiple_of(i * side, side)
                for c in range(words):
                    v = dest[pl.ds((k * CHUNK + at) * SLOT + c, side, stride=SLOT), :]
                    stage[k % 2, pl.ds(at, side), pl.ds(c * LANES, LANES)] = v.astype(jnp.bfloat16)
                return carry

            lax.fori_loop(0, CHUNK // side, narrow, 0)
            save(q, k).start()
    for k in range(chunks - 2, chunks):
        save_first(k).wait()
        save(labels - 1, k).wait()


def snp_side(core, env_own, env_other, sums_own, sums_other, shuf_own, shuf_other, own, other,
             labels):
    snp_rows, half = own.shape
    all_samples = 2 * half
    words = snp_rows // LANES
    width = labels * snp_rows + snp_rows // 2
    any_spec = pl.BlockSpec(memory_space=pl.ANY)
    smem = pl.BlockSpec(memory_space=pltpu.SMEM)
    vmem = pl.BlockSpec(memory_space=pltpu.VMEM)
    return pl.pallas_call(
        functools.partial(snp_side_kernel, labels=labels),
        out_shape=jax.ShapeDtypeStruct((all_samples, width), jnp.bfloat16),
        in_specs=[smem, vmem, vmem, vmem, vmem, any_spec, any_spec, any_spec, any_spec],
        out_specs=any_spec,
        scratch_shapes=[
            pltpu.SMEM((labels * all_samples,), jnp.int32),
            pltpu.VMEM((3, snp_rows, CHUNK), jnp.bfloat16),
            pltpu.VMEM((all_samples * words + SLOT, LANES), jnp.float32),
            pltpu.VMEM((all_samples * SLOT, LANES), jnp.float32),
            pltpu.VMEM((2, CHUNK, snp_rows), jnp.bfloat16),
            pltpu.VMEM((2, CHUNK, snp_rows // 2), jnp.bfloat16),
            pltpu.VMEM((snp_rows, LANES), jnp.float32),
            pltpu.SemaphoreType.DMA((2 * labels,)),
            pltpu.SemaphoreType.DMA((3,)),
            pltpu.SemaphoreType.DMA((2,)),
            pltpu.SemaphoreType.DMA((2,)),
        ],
        compiler_params=pltpu.CompilerParams(vmem_limit_bytes=61 * MIB),
        cost_estimate=pl.CostEstimate(
            flops=40 * 10**9, bytes_accessed=60 * 10**6, transcendentals=0
        ),
        name="snp_side",
    )(core, env_own, env_other, sums_own, sums_other, shuf_own, shuf_other, own, other)


def window_plan(start, end, bounds_ref, n_bounds, total_blocks):
    middle = (start + end - 1) // 2
    lower_edge = jnp.zeros_like(start)
    upper_edge = jnp.full_like(end, total_blocks)
    for i in range(n_bounds):
        edge = bounds_ref[i]
        before = edge <= middle
        lower_edge = jnp.where(before, jnp.maximum(lower_edge, edge), lower_edge)
        upper_edge = jnp.where(before, upper_edge, jnp.minimum(upper_edge, edge))
    return jnp.maximum(start, lower_edge), jnp.minimum(end, upper_edge)


def select_kernel(
    round_ref, pos_ref, bounds_ref, start_ref, end_ref, own_ref, other_ref,
    rounds_ref, plan_ref, full_ref, *rest, caps, blocks_dev,
):
    pay_refs, (slots, edges) = rest[: len(caps)], rest[len(caps) :]
    reach = len(caps)
    genes, half = own_ref.shape
    shape = start_ref.shape
    per_row = LANES // genes
    chips = shape[0] * per_row
    chip, core = pos_ref[0], pos_ref[1]
    turn = round_ref[0]
    low, high = window_plan(
        start_ref[...], end_ref[...], bounds_ref, bounds_ref.shape[0], chips * blocks_dev
    )
    edges[0] = low
    edges[1] = high
    at = lax.broadcasted_iota(jnp.int32, shape, 0) * per_row
    at = at + lax.broadcasted_iota(jnp.int32, shape, 1) // genes
    a = lax.broadcasted_iota(jnp.int32, (LANES, LANES), 0)
    b = lax.broadcasted_iota(jnp.int32, (LANES, LANES), 1)
    upto = ((a <= b) & (a // genes == b // genes)).astype(jnp.float32).astype(jnp.bfloat16)
    rounds = jnp.int32(0)
    for way in range(2):
        for k in range(1, reach + 1):
            to = at + (k if way == 0 else -k)
            need = (
                (low < (to + 1) * blocks_dev) & (high > to * blocks_dev)
                & (low < high) & (to >= 0) & (to < chips)
            )
            rank = jnp.dot(
                need.astype(jnp.float32).astype(jnp.bfloat16), upto,
                preferred_element_type=jnp.float32,
            ).astype(jnp.int32)
            cap = caps[k - 1]
            slot = rank - 1 - turn * cap
            slots[way * reach + k - 1] = jnp.where(
                need & (slot >= 0) & (slot < cap), slot, -1
            )
            rounds = jnp.maximum(rounds, (jnp.max(rank) + cap - 1) // cap)
    rounds_ref[0] = rounds

    def of_chip(ref, index, which):
        row = ref[index, pl.ds(which // per_row, 1), :]
        out = row[:, :genes]
        for part in range(1, per_row):
            out = jnp.where(
                which % per_row == part, row[:, part * genes : (part + 1) * genes], out
            )
        return out

    plan_ref[...] = jnp.zeros_like(plan_ref)
    plan_ref[0, pl.ds(0, 1), :] = lax.broadcasted_iota(jnp.int32, (1, genes), 1)
    plan_ref[1, pl.ds(0, 1), :] = of_chip(edges, 0, chip)
    plan_ref[2, pl.ds(0, 1), :] = of_chip(edges, 1, chip)
    for side in range(2):
        way = core if side == 0 else 1 - core
        for k in range(1, reach + 1):
            source = chip + (2 * way - 1) * k
            valid = (source >= 0) & (source < chips)
            source = jnp.clip(source, 0, chips - 1)
            to = pl.ds(1 + side * reach + k - 1, 1)
            slot = of_chip(slots, way * reach + k - 1, source)
            plan_ref[0, to, :] = jnp.where(valid, slot, -1)
            plan_ref[1, to, :] = of_chip(edges, 0, source)
            plan_ref[2, to, :] = jnp.where(valid, of_chip(edges, 1, source), 0)

    picks = []
    for k in range(1, reach + 1):
        slot = of_chip(slots, core * reach + k - 1, chip)
        rows = lax.broadcasted_iota(jnp.int32, (caps[k - 1], genes), 0)
        picks.append((rows == slot).astype(jnp.float32))
    picks = jnp.concatenate(picks, axis=0).astype(jnp.bfloat16)
    step = 1024

    def copy(i, carry):
        cols = pl.ds(pl.multiple_of(i * step, step), step)
        late = pl.ds(pl.multiple_of(half + i * step, step), step)
        a, b = own_ref[:, cols], other_ref[:, cols]
        first = jnp.where(core == 0, a, b)
        second = jnp.where(core == 0, b, a)
        full_ref[:, cols] = first
        full_ref[:, late] = second
        for part, to in ((first, cols), (second, late)):
            chosen = jnp.dot(picks, part, preferred_element_type=jnp.float32)
            chosen = chosen.astype(jnp.bfloat16)
            row = 0
            for pay in pay_refs:
                pay[:, to] = chosen[row : row + pay.shape[0]]
                row += pay.shape[0]
        return carry

    lax.fori_loop(0, half // step, copy, 0)


def select(turn, pos, bounds, start, end, own, other, caps, blocks_dev):
    genes, half = own.shape
    reach = len(caps)
    smem = pl.BlockSpec(memory_space=pltpu.SMEM)
    vmem = pl.BlockSpec(memory_space=pltpu.VMEM)
    plan_rows = -(-(2 * reach + 1) // 8) * 8
    return pl.pallas_call(
        functools.partial(select_kernel, caps=caps, blocks_dev=blocks_dev),
        out_shape=(
            jax.ShapeDtypeStruct((1,), jnp.int32),
            jax.ShapeDtypeStruct((3, plan_rows, genes), jnp.int32),
            jax.ShapeDtypeStruct((genes, 2 * half), jnp.bfloat16),
            *[jax.ShapeDtypeStruct((cap, 2 * half), jnp.bfloat16) for cap in caps],
        ),
        in_specs=[smem, smem, smem, vmem, vmem, vmem, vmem],
        out_specs=(smem, vmem, vmem, *[vmem for _ in caps]),
        scratch_shapes=[
            pltpu.VMEM((2 * reach,) + start.shape, jnp.int32),
            pltpu.VMEM((2,) + start.shape, jnp.int32),
        ],
        compiler_params=pltpu.CompilerParams(vmem_limit_bytes=24 * MIB),
        name="select",
    )(turn, pos, bounds, start, end, own, other)


def product_kernel(
    pos_ref, sums_own, sums_other, *rest, n_in, sizes, labels, blocks_dev, last
):
    if last:
        plan_ref, before_ref = rest[:2]
        rest = rest[2:]
    gene_refs = rest[:n_in]
    weights_ref, out_ref, *rest = rest[n_in:]
    if not last:
        power_ref, *rest = rest
    rows, total, *rest = rest
    step = pl.program_id(0)
    steps = pl.num_programs(0)
    snp_rows = sums_own.shape[1]
    depth, width = weights_ref.shape
    block = SNP_BLOCK
    used = rows.shape[0]

    @pl.when(step == 0)
    def _():
        total[...] = jnp.zeros_like(total)

    at = 0
    for ref in gene_refs:
        rows[pl.ds(at, ref.shape[0]), :] = ref[...]
        at += ref.shape[0]
    for n in range(width // block):
        cols = pl.ds(n * block, block)
        total[pl.ds(0, used), cols] += jnp.dot(
            rows[...], weights_ref[:, cols], preferred_element_type=jnp.float32
        )
    if not last:
        power = rest[0]
        kept = jnp.where(step == 0, 0.0, power[...])
        for t in range(depth // LANES):
            x = gene_refs[0][:, pl.ds(t * LANES, LANES)].astype(jnp.float32)
            kept = kept + x * x
        power[...] = kept

    @pl.when(step == steps - 1)
    def _():
        chip, core = pos_ref[0], pos_ref[1]
        share_blocks = blocks_dev // 2
        sums = sums_own[...] + sums_other[...]
        cross = sums[1:2, :]
        inter = sums[2:3, :]
        inv = 1.0 / (inter - cross * (cross / sums[0:1, :]) + 0.1 * inter)

        def peak(col, inv_block):
            v = total[:, pl.ds(col, block)]
            v = v * v * inv_block
            best = v[:, :LANES]
            for t in range(1, block // LANES):
                best = jnp.maximum(best, v[:, t * LANES : (t + 1) * LANES])
            return jnp.max(best.T, axis=0, keepdims=True)

        peaks = []
        for q in range(labels):
            for b in range(blocks_dev):
                peaks.append(
                    peak(q * snp_rows + b * block, inv[:, b * block : (b + 1) * block])
                )
        for b in range(share_blocks):
            mine = inv[:, b * block : (b + 1) * block]
            late = inv[:, (share_blocks + b) * block : (share_blocks + b + 1) * block]
            peaks.append(
                peak(labels * snp_rows + b * block, jnp.where(core == 0, mine, late))
            )
        while len(peaks) % 8:
            peaks.append(jnp.zeros_like(peaks[0]))
        peaks = jnp.concatenate(peaks, axis=0)
        if not last:
            out_ref[...] = peaks
            powers = jnp.sum(rest[0][...].T, axis=0, keepdims=True)
            power_ref[...] = jnp.broadcast_to(powers, power_ref.shape)
            return

        genes = plan_ref.shape[2]
        chips = out_ref.shape[0] // 2
        reach = (len(sizes) - 1) // 2
        before = before_ref[...]
        out_ref[...] = jnp.zeros_like(out_ref)
        start = 0
        for i, size in enumerate(sizes):
            if i == n_in + 1:
                start = 0
            values = before if i <= reach else peaks
            slot = plan_ref[0, pl.ds(i, 1), :]
            slot = jnp.where(slot >= 0, slot + start, -1)
            start += size
            low = plan_ref[1, pl.ds(i, 1), :]
            high = plan_ref[2, pl.ds(i, 1), :]
            slot_of = lax.broadcasted_iota(jnp.int32, (values.shape[1], genes), 0)
            spread = jnp.dot(
                values, (slot_of == slot).astype(jnp.float32),
                precision=lax.Precision.HIGHEST, preferred_element_type=jnp.float32,
            )

            def masked(row, snp_block):
                inside = (snp_block >= low) & (snp_block < high)
                return jnp.where(inside, spread[row : row + 1], 0.0)

            found = []
            for q in range(labels):
                best = jnp.zeros((1, genes), jnp.float32)
                for b in range(blocks_dev):
                    best = jnp.maximum(best, masked(q * blocks_dev + b, chip * blocks_dev + b))
                found.append(best)
            best = jnp.zeros((1, genes), jnp.float32)
            for b in range(share_blocks):
                best = jnp.maximum(
                    best,
                    masked(
                        labels * blocks_dev + b, chip * blocks_dev + core * share_blocks + b
                    ),
                )
            out_rows = [best]
            for c in range(2):
                out_rows += [jnp.where(core == c, v, 0.0) for v in found]
            while len(out_rows) % 8:
                out_rows.append(jnp.zeros_like(best))
            if i == 0:
                target = chip
            else:
                way = core if i <= reach else 1 - core
                target = chip + (2 * way - 1) * ((i - 1) % reach + 1)

            @pl.when((target >= 0) & (target < chips))
            def _(out_rows=out_rows, target=target):
                for c in range(2):
                    out_ref[2 * target + c, :, pl.ds(0, genes)] = jnp.concatenate(
                        out_rows, axis=0
                    )


def products(pos, sums, arrays, weights, caps, labels, blocks_dev, before=None, plan=None,
             chips=None):
    all_samples, width = weights.shape
    genes = arrays[0].shape[0] if plan is None else plan.shape[2]
    sizes = (genes,) + tuple(caps) + tuple(caps)
    used = sum(x.shape[0] for x in arrays)
    padded = -(-used // LANES) * LANES
    out_rows = -(-(1 + 2 * labels) // 8) * 8
    peak_rows = -(-(labels * blocks_dev + blocks_dev // 2) // 8) * 8
    last = plan is not None
    extra = (plan, before) if last else ()

    def whole(x):
        return pl.BlockSpec(x.shape, lambda k: (0,) * x.ndim)

    if last:
        outs = (jax.ShapeDtypeStruct((2 * chips, out_rows, LANES), jnp.float32),)
    else:
        outs = (
            jax.ShapeDtypeStruct((peak_rows, padded), jnp.float32),
            jax.ShapeDtypeStruct((8, genes), jnp.float32),
        )
    scratch = [
        pltpu.VMEM((used, CHUNK), jnp.bfloat16),
        pltpu.VMEM((padded, width), jnp.float32),
    ]
    if not last:
        scratch.append(pltpu.VMEM((genes, LANES), jnp.float32))
    return pl.pallas_call(
        functools.partial(
            product_kernel, n_in=len(arrays), sizes=sizes, labels=labels,
            blocks_dev=blocks_dev, last=last,
        ),
        grid=(all_samples // CHUNK,),
        out_shape=outs,
        in_specs=[
            pl.BlockSpec(memory_space=pltpu.SMEM),
            *[whole(x) for x in (*sums, *extra)],
            *[pl.BlockSpec((x.shape[0], CHUNK), lambda k: (0, k)) for x in arrays],
            pl.BlockSpec((CHUNK, width), lambda k: (k, 0)),
        ],
        out_specs=tuple(whole(x) for x in outs),
        scratch_shapes=scratch,
        compiler_params=pltpu.CompilerParams(vmem_limit_bytes=48 * MIB),
        cost_estimate=pl.CostEstimate(
            flops=2 * used * all_samples * width,
            bytes_accessed=2 * all_samples * (width + used),
            transcendentals=0,
        ),
        name="products_last" if last else "products",
    )(pos, *sums, *extra, *arrays, weights)


def finish_kernel(gathered_ref, power_ref, out_ref, *, samples):
    best = gathered_ref[0]
    for i in range(1, gathered_ref.shape[0]):
        best = jnp.maximum(best, gathered_ref[i])
    labels, genes = out_ref.shape
    peak = best[:labels, :genes]
    out_ref[...] = jnp.sqrt(peak / (power_ref[0:1, :] / samples + 1e-05))


def shards(genotypes, phenotypes, environment, shuffles, window_start, window_end, chrom_bounds):
    snp_rows, half = genotypes.shape
    genes = phenotypes.shape[0]
    perms = shuffles.shape[0]
    chips = lax.axis_size("genome")
    cores = lax.axis_size("sample")
    genome_pos = lax.axis_index("genome")
    sample_pos = lax.axis_index("sample")
    blocks_dev = snp_rows // SNP_BLOCK
    reach = (HALF_BLK + blocks_dev - 1) // blocks_dev
    all_samples = half * cores
    labels = perms // cores
    caps = tuple(min(genes, genes * 4 >> k) for k in range(1, reach + 1))

    other_pheno = swapped(phenotypes)
    other_geno = swapped(genotypes)
    env = environment[None]
    other_env = swapped(env)
    other_shuffles = swapped(shuffles)
    pos = jnp.stack([genome_pos, sample_pos]).astype(jnp.int32)
    start = window_start.reshape(-1, LANES)
    end = window_end.reshape(-1, LANES)

    def chosen(turn):
        return select(
            turn, pos, chrom_bounds, start, end, phenotypes, other_pheno, caps, blocks_dev
        )

    def travel(payloads):
        mine = []
        for k, payload in enumerate(payloads, 1):
            pairs = [(i * cores, (i + k) * cores) for i in range(chips - k)]
            pairs += [((i + k) * cores + 1, i * cores + 1) for i in range(chips - k)]
            mine.append(lax.ppermute(payload, ("genome", "sample"), pairs))
        return mine

    rounds, plan, full, *payloads = chosen(jnp.zeros((1,), jnp.int32))
    mine = travel(payloads)
    own_sums = local_moments(genotypes, env)
    sums = (own_sums, swapped(own_sums))
    weights = snp_side(
        pos[1:], env, other_env, *sums, shuffles, other_shuffles, genotypes, other_geno, labels
    )

    def met(plan, full, mine):
        other = [swapped(x) for x in mine]
        before, power = products(
            pos, sums, (full, *mine), weights, caps, labels, blocks_dev
        )
        (found,) = products(
            pos, sums, other, weights, caps, labels, blocks_dev, before, plan, chips
        )
        return found, power

    *mine, weights = lax.optimization_barrier((*mine, weights))
    found, power = met(plan, full, mine)

    def more(carry):
        return carry[0] < rounds[0]

    def again(carry):
        turn, best = carry
        _, plan, full, *payloads = chosen(jnp.full((1,), turn, jnp.int32))
        return turn + 1, jnp.maximum(best, met(plan, full, travel(payloads))[0])

    _, found = lax.while_loop(more, again, (jnp.int32(1), found))
    gathered = lax.all_to_all(found, ("genome", "sample"), 0, 0, tiled=True)
    return pl.pallas_call(
        functools.partial(finish_kernel, samples=all_samples),
        out_shape=jax.ShapeDtypeStruct((perms + 1, genes), jnp.float32),
        name="finish",
    )(gathered, power)


def solution(mesh):
    placed = (
        P("genome", "sample"),
        P("genome", "sample"),
        P("sample"),
        P(None, "sample"),
        P(),
        P(),
        P(),
    )
    return jax.shard_map(
        shards, mesh=mesh, in_specs=placed, out_specs=P(None, "genome"), check_vma=False
    )
```

time: 111 us -> 113 us (1.018)
  Pallas kernels: 62.8 us -> 79.1 us
  waiting for transfers between devices: 11.8 us -> 2.07 us
  blocking collectives: 3.99 us -> 11.5 us
  starting transfers between devices: 23.6 us -> 18.4 us
  other arithmetic: 3.79 us -> 0.07 us
  local copies, waits for them, and re-layouts: 3.56 us -> 0.66 us
    pallas_call x2 -> x4, Pallas kernels: 53.8 us -> 70.4 us  [the longest x1 42.3 us: snp_side(): pl.pallas_call(functools.partial(snp_side_kernel, labels=labels), out_sha...]
    all_to_all x0 -> x1, blocking collectives: none -> 11.5 us  [shards(): gathered = lax.all_to_all(found, ('genome', 'sample'), 0, 0, tiled=True)]
    all_to_all x1 -> x0, waiting for transfers between devices: 7.4 us -> none  [shards(): lax.all_to_all(sent, ('genome', 'sample'), 0, 0, tiled=True)]
    all_to_all x1 -> x0, starting transfers between devices: 5.49 us -> none  [shards(): lax.all_to_all(sent, ('genome', 'sample'), 0, 0, tiled=True)]
    psum x1 -> x0, blocking collectives: 3.99 us -> none  [shards(): sums = lax.psum(local_moments(genotypes, environment[None]), 'sample')]
    ppermute x7 -> x9, waiting for transfers between devices: 4.41 us -> 2.06 us  [swapped(): lax.ppermute(x, 'sample', [(i, (i + 1) % count) for i in range(count)])]
    reshape x2 -> x0, local copies, waits for them, and re-layouts: 1.51 us -> none  [the longest x1 0.75 us: shards(): end = window_end.reshape(chips, genes)]
    concatenate x2 -> x0, other arithmetic: 1.35 us -> none  [the longest x1 0.75 us: shards(): jnp.concatenate([shuffles.astype(jnp.float32), environment[None]], axis=0)]
  transfers between devices with their start and end apart: 12 -> 13, of which waited for: 2 -> 1; matrix products, arithmetic and copies ran while one was open for 4% -> 0% of each run, Pallas kernels for 42% -> 56%
where the time goes in v3:
time: 113 us
  Pallas kernels  79.1 us (70%)
  starting transfers between devices  18.4 us (16%)
  blocking collectives  11.5 us (10%)
  waiting for transfers between devices  2.07 us (2%)
    pallas_call x1, Pallas kernels, snp_side(): pl.pallas_call(functools.partial(snp_side_kernel, labels=labels), out_sha...  42.3 us
    pallas_call x2, Pallas kernels, products(): pl.pallas_call(functools.partial(product_kernel, n_in=len(arrays), sizes=...  26.6 us
    ppermute x4, starting transfers between devices, travel(): mine.append(lax.ppermute(payload, ('genome', 'sample'), pairs))  15.8 us
    all_to_all x1, blocking collectives, shards(): gathered = lax.all_to_all(found, ('genome', 'sample'), 0, 0, tiled=True)  11.5 us
    pallas_call x1, Pallas kernels, local_moments(): pl.pallas_call(moments_kernel, grid=(half // chunk,), out_shape=jax.Shape...  4.51 us
    pallas_call x1, Pallas kernels, select(): pl.pallas_call(functools.partial(select_kernel, caps=caps, blocks_dev=blo...  4.17 us
    ppermute x9, starting transfers between devices, swapped(): lax.ppermute(x, 'sample', [(i, (i + 1) % count) for i in range(count)])  2.68 us
  transfers between devices with their start and end apart: 13, of which 1 were waited for; matrix products, arithmetic and copies ran while one was open for 0% of the time, Pallas kernels for 56%

profile of v3, /device:TPU:0, one launch (start us, length us, event | category | flops | bytes accessed | tf_op | source)
XLA Modules:
  0.0 112.9 jit_solution(683361371991848122)
XLA Ops:
  0.0 0.5 collective-permute-start.16
  0.5 0.1 collective-permute-start.14
  0.6 0.5 collective-permute-start.9
  1.1 4.5 %local_moments.1.sums_own = f32[8,512]{1,0:T(8,128)S(1)} custom-call(bf16[512,4096]{1,0:T(8,128)(2,1)} %own_ref.3, f32[1,4096]{1,0:T(1,128)} %bitcast.15), custom_call_target="tpu_custom_call" | custom-call | flops 5000000000 | bytes 4194304 | tf_op jit(solution)/shard_map/local_moments/pallas_call | solution.py:66
  5.6 0.1 collective-permute-start.8
  5.7 0.4 collective-permute-start.15
  6.1 0.1 pad_add_fusion.pos_ref
  6.2 2.0 %collective-permute-done.9.other_ref = bf16[64,4096]{1,0:T(8,128)(2,1)S(1)} collective-permute-done((bf16[64,4096]{1,0:T(8,128)(2,1)}, bf16[64,4096]{1,0:T(8,128)(2,1)S(1)}, u32[]{:S(2)}, u32[]{:S(2)}) %collective-permute-start.9) | collective-permute-done | bytes 524320 | tf_op jit(solution)/shard_map/ppermute | solution.py:28
  8.3 4.2 %select.2 = (s32[1]{0:T(128)}, s32[3,16,64]{2,1,0:T(8,128)S(1)}, bf16[64,8192]{1,0:T(8,128)(2,1)S(1)}, bf16[64,8192]{1,0:T(8,128)(2,1)}, bf16[64,8192]{1,0:T(8,1...) custom-call(s32[1]{0:T(128)} %constant.13.clone.1.round_ref, s32[2]{0:T(128)S(1)} %pad_add_fusion.pos_ref, ...), custom_call_target="tpu_custom_call" | custom-call | tf_op jit(solution)/shard_map/select/pallas_call | solution.py:356
  12.5 4.5 %collective-permute-start.10 = (bf16[64,8192]{1,0:T(8,128)(2,1)}, bf16[64,8192]{1,0:T(8,128)(2,1)S(1)}, u32[]{:S(2)}, u32[]{:S(2)}) collective-permute-start(bf16[64,8192]{1,0:T(8,128)(2,1)} %get-tuple-element.91), channel_id=1, source_target_pairs={{0,2},{2,4},{4,6},{6,8},{8,10},{10,12},{12,14},{14,16},{16,18},{18... | collective-permute-start | bytes 3145736 | tf_op jit(solution)/shard_map/ppermute | solution.py:605
  17.0 0.0 collective-permute-done.8.sums_other
  17.0 4.4 %collective-permute-start.11 = (bf16[64,8192]{1,0:T(8,128)(2,1)}, bf16[64,8192]{1,0:T(8,128)(2,1)}, u32[]{:S(2)}, u32[]{:S(2)}) collective-permute-start(bf16[64,8192]{1,0:T(8,128)(2,1)} %get-tuple-element.92), channel_id=1, source_target_pairs={{0,4},{2,6},{4,8},{6,10},{8,12},{10,14},{12,16},{14,18},{16,20},{1... | collective-permute-start | bytes 3145736 | tf_op jit(solution)/shard_map/ppermute | solution.py:605
  21.4 0.0 collective-permute-done.14.env_other
  21.4 3.4 %collective-permute-start.12 = (bf16[32,8192]{1,0:T(8,128)(2,1)}, bf16[32,8192]{1,0:T(8,128)(2,1)S(1)}, u32[]{:S(2)}, u32[]{:S(2)}) collective-permute-start(bf16[32,8192]{1,0:T(8,128)(2,1)} %get-tuple-element.93), channel_id=1, source_target_pairs={{0,6},{2,8},{4,10},{6,12},{8,14},{10,16},{12,18},{14,20},{16,22},{... | collective-permute-start | bytes 1572872 | tf_op jit(solution)/shard_map/ppermute | solution.py:605
  24.8 0.0 collective-permute-done.15.shuf_other
  24.8 0.6 copy-done.13
  25.5 3.5 %collective-permute-start.13 = (bf16[16,8192]{1,0:T(8,128)(2,1)}, bf16[16,8192]{1,0:T(8,128)(2,1)S(1)}, u32[]{:S(2)}, u32[]{:S(2)}) collective-permute-start(bf16[16,8192]{1,0:T(8,128)(2,1)} %get-tuple-element.94), channel_id=1, source_target_pairs={{0,8},{2,10},{4,12},{6,14},{8,16},{10,18},{12,20},{14,22},{16,24},... | collective-permute-start | bytes 786440 | tf_op jit(solution)/shard_map/ppermute | solution.py:605
  28.9 42.3 %snp_side.1.rest_5_.rest_6_ = bf16[8192,1280]{1,0:T(8,128)(2,1)} custom-call(s32[1]{0:T(128)} %bitcast.3.core_ref, f32[1,4096]{1,0:T(1,128)} %bitcast.16, f32[1,4096]{1,0:T(1,128)} %copy-done.14, f32[8,512]{1,0:T(8,128)S(1)} %local_moments.1.sums_own, f32[8,512]{1,0:T(8,128)S(1)} %collective-permute-done.8.sums_other, s32[4,4096]{1,0:T(4,128)} %shuf_own.1, ...), custom_call_target="tpu_custom_call" | custom-call | flops 40000000000 | bytes 60000000 | tf_op jit(solution)/shard_map/snp_side/pallas_call | solution.py:217
  71.2 0.0 collective-permute-done.10.rest_1_
  71.2 0.0 collective-permute-done.11.rest_2_
  71.2 0.1 collective-permute-start.17
  71.3 0.5 collective-permute-start.18
  71.8 0.1 collective-permute-start.19
  71.9 0.4 collective-permute-start.20
  72.3 12.4 %products.2 = (f32[8,256]{1,0:T(8,128)S(1)}, f32[8,64]{1,0:T(8,128)S(1)}) custom-call(s32[2]{0:T(128)S(1)} %pad_add_fusion.pos_ref, f32[8,512]{1,0:T(8,128)S(1)} %local_moments.1.sums_own, f32[8,512]{1,0:T(8,128)S(1)} %collective-permute-done.8.sums_other, bf16[64,8192]{1,0:T(8,128)(2,1)S(1)} %get-tuple-element.90.rest_0_, ...), custom_call_target="tpu_custom_call" | custom-call | flops 5033164800 | bytes 24903680 | tf_op jit(solution)/shard_map/products/pallas_call | solution.py:538
  84.8 0.0 collective-permute-done.19.rest_4_
  84.8 0.0 collective-permute-done.17.rest_2_
  84.8 0.0 copy-start.2
  84.8 14.3 %products_last.2 = f32[32,8,128]{2,1,0:T(8,128)} custom-call(s32[2]{0:T(128)S(1)} %pad_add_fusion.pos_ref, f32[8,512]{1,0:T(8,128)S(1)} %local_moments.1.sums_own, f32[8,512]{1,0:T(8,128)S(1)} %collective-permute-done.8.sums_other, s32[3,16,64]{2,1,0:T(8,128)S(1)} %get-tuple-element.89.rest_0_, f32[8,256]{1,0:T(8,128)S(1)} %get-tuple-element.100.rest_1_, ...), custom_call_target="tpu_custom_call" | custom-call | flops 3690987520 | bytes 23855104 | tf_op jit(solution)/shard_map/products_last/pallas_call | solution.py:538
  99.1 0.8 while.10
  99.8 11.5 %all_to_all.5.gathered_ref = f32[32,8,128]{2,1,0:T(8,128)} all-to-all(f32[32,8,128]{2,1,0:T(8,128)} %get-tuple-element.289), channel_id=1, replica_groups=mesh['genome'=16,'sample'=2] {'genome','sample'}, dimensions={0} | all-to-all | bytes 262144 | tf_op jit(solution)/shard_map/all_to_all | solution.py:638
  111.4 1.5 %finish.1 = f32[5,64]{1,0:T(8,128)} custom-call(f32[32,8,128]{2,1,0:T(8,128)} %all_to_all.5.gathered_ref, f32[8,64]{1,0:T(8,128)} %copy-done), custom_call_target="tpu_custom_call" | custom-call | tf_op jit(solution)/shard_map/finish/pallas_call | solution.py:639
  (25 shorter events, 0.1 us)
Async XLA Ops:
  0.0 28.9 %collective-permute-start.16 = (bf16[512,4096]{1,0:T(8,128)(2,1)}, bf16[512,4096]{1,0:T(8,128)(2,1)}, u32[]{:S(2)}, u32[]{:S(2)}) collective-permute-start(bf16[512,4096]{1,0:T(8,128)(2,1)} %own_ref.3), channel_id=1, source_target_pairs={{0,1},{1,0},{2,3},{3,2},{4,5},{5,4},{6,7},{7,6},{8,9},{9,8},{10,11... | collective-permute-start | bytes 12582920 | tf_op jit(solution)/shard_map/ppermute | solution.py:28
  0.5 5.3 %copy-start.12 = (s32[4,4096]{1,0:T(4,128)S(1)}, s32[4,4096]{1,0:T(4,128)}, u32[]{:S(2)}) copy-start(s32[4,4096]{1,0:T(4,128)} %shuf_own.1) | copy-start | bytes 196612
  0.5 7.8 %copy-start.1 = (bf16[64,4096]{1,0:T(8,128)(2,1)S(1)}, bf16[64,4096]{1,0:T(8,128)(2,1)}, u32[]{:S(2)}) copy-start(bf16[64,4096]{1,0:T(8,128)(2,1)} %own_ref.2) | copy-start | bytes 1572868
  0.5 7.8 %copy-start.9 = (s32[1024]{0:T(1024)S(1)}, s32[1024]{0:T(1024)}, u32[]{:S(2)}) copy-start(s32[1024]{0:T(1024)} %param.13) | copy-start | bytes 12292
  0.5 7.8 %copy-start.10 = (s32[1024]{0:T(1024)S(1)}, s32[1024]{0:T(1024)}, u32[]{:S(2)}) copy-start(s32[1024]{0:T(1024)} %param.14) | copy-start | bytes 12292
  0.5 7.8 %copy-start.11 = (s32[15]{0:T(128)S(1)}, s32[15]{0:T(128)}, u32[]{:S(2)}) copy-start(s32[15]{0:T(128)} %bounds_ref.1) | copy-start | bytes 184
  0.5 20.9 %collective-permute-start.14 = (f32[1,4096]{1,0:T(1,128)}, f32[1,4096]{1,0:T(1,128)S(1)}, u32[]{:S(2)}, u32[]{:S(2)}) collective-permute-start(f32[1,4096]{1,0:T(1,128)} %bitcast.14), channel_id=1, source_target_pairs={{0,1},{1,0},{2,3},{3,2},{4,5},{5,4},{6,7},{7,6},{8,9},{9,8},{10,11... | collective-permute-start | bytes 49160 | tf_op jit(solution)/shard_map/ppermute | solution.py:28
  0.6 7.7 %collective-permute-start.9 = (bf16[64,4096]{1,0:T(8,128)(2,1)}, bf16[64,4096]{1,0:T(8,128)(2,1)S(1)}, u32[]{:S(2)}, u32[]{:S(2)}) collective-permute-start(bf16[64,4096]{1,0:T(8,128)(2,1)} %own_ref.2), channel_id=1, source_target_pairs={{0,1},{1,0},{2,3},{3,2},{4,5},{5,4},{6,7},{7,6},{8,9},{9,8},{10,11... | collective-permute-start | bytes 1572872 | tf_op jit(solution)/shard_map/ppermute | solution.py:28
  5.6 11.5 %collective-permute-start.8 = (f32[8,512]{1,0:T(8,128)S(1)}, f32[8,512]{1,0:T(8,128)S(1)}, u32[]{:S(2)}, u32[]{:S(2)}) collective-permute-start(f32[8,512]{1,0:T(8,128)S(1)} %local_moments.1.sums_own), channel_id=1, source_target_pairs={{0,1},{1,0},{2,3},{3,2},{4,5},{5,4},{6,7},{7,6},{8,9},{9,8},{10,11... | collective-permute-start | bytes 49160 | tf_op jit(solution)/shard_map/ppermute | solution.py:28
  5.7 19.1 %collective-permute-start.15 = (s32[4,4096]{1,0:T(4,128)S(1)}, s32[4,4096]{1,0:T(4,128)S(1)}, u32[]{:S(2)}, u32[]{:S(2)}) collective-permute-start(s32[4,4096]{1,0:T(4,128)S(1)} %copy-done.12), channel_id=1, source_target_pairs={{0,1},{1,0},{2,3},{3,2},{4,5},{5,4},{6,7},{7,6},{8,9},{9,8},{10,11... | collective-permute-start | bytes 196616 | tf_op jit(solution)/shard_map/ppermute | solution.py:28
  8.3 4.2 %copy-start.4 = (bf16[64,4096]{1,0:T(8,128)(2,1)}, bf16[64,4096]{1,0:T(8,128)(2,1)S(1)}, u32[]{:S(2)}) copy-start(bf16[64,4096]{1,0:T(8,128)(2,1)S(1)} %collective-permute-done.9.other_ref) | copy-start | bytes 1572868
  12.5 58.8 %collective-permute-start.10 = (bf16[64,8192]{1,0:T(8,128)(2,1)}, bf16[64,8192]{1,0:T(8,128)(2,1)S(1)}, u32[]{:S(2)}, u32[]{:S(2)}) collective-permute-start(bf16[64,8192]{1,0:T(8,128)(2,1)} %get-tuple-element.91), channel_id=1, source_target_pairs={{0,2},{2,4},{4,6},{6,8},{8,10},{10,12},{12,14},{14,16},{16,18},{18... | collective-permute-start | bytes 3145736 | tf_op jit(solution)/shard_map/ppermute | solution.py:605
  17.0 54.2 %collective-permute-start.11 = (bf16[64,8192]{1,0:T(8,128)(2,1)}, bf16[64,8192]{1,0:T(8,128)(2,1)}, u32[]{:S(2)}, u32[]{:S(2)}) collective-permute-start(bf16[64,8192]{1,0:T(8,128)(2,1)} %get-tuple-element.92), channel_id=1, source_target_pairs={{0,4},{2,6},{4,8},{6,10},{8,12},{10,14},{12,16},{14,18},{16,20},{1... | collective-permute-start | bytes 3145736 | tf_op jit(solution)/shard_map/ppermute | solution.py:605
  21.4 7.5 %copy-start.14 = (f32[1,4096]{1,0:T(1,128)}, f32[1,4096]{1,0:T(1,128)S(1)}, u32[]{:S(2)}) copy-start(f32[1,4096]{1,0:T(1,128)S(1)} %collective-permute-done.14.env_other) | copy-start | bytes 49156
  21.4 49.8 %collective-permute-start.12 = (bf16[32,8192]{1,0:T(8,128)(2,1)}, bf16[32,8192]{1,0:T(8,128)(2,1)S(1)}, u32[]{:S(2)}, u32[]{:S(2)}) collective-permute-start(bf16[32,8192]{1,0:T(8,128)(2,1)} %get-tuple-element.93), channel_id=1, source_target_pairs={{0,6},{2,8},{4,10},{6,12},{8,14},{10,16},{12,18},{14,20},{16,22},{... | collective-permute-start | bytes 1572872 | tf_op jit(solution)/shard_map/ppermute | solution.py:605
  24.8 0.6 copy-start.13
  25.5 45.8 %collective-permute-start.13 = (bf16[16,8192]{1,0:T(8,128)(2,1)}, bf16[16,8192]{1,0:T(8,128)(2,1)S(1)}, u32[]{:S(2)}, u32[]{:S(2)}) collective-permute-start(bf16[16,8192]{1,0:T(8,128)(2,1)} %get-tuple-element.94), channel_id=1, source_target_pairs={{0,8},{2,10},{4,12},{6,14},{8,16},{10,18},{12,20},{14,22},{16,24},... | collective-permute-start | bytes 786440 | tf_op jit(solution)/shard_map/ppermute | solution.py:605
  71.2 13.5 %collective-permute-start.17 = (bf16[64,8192]{1,0:T(8,128)(2,1)S(1)}, bf16[64,8192]{1,0:T(8,128)(2,1)}, u32[]{:S(2)}, u32[]{:S(2)}) collective-permute-start(bf16[64,8192]{1,0:T(8,128)(2,1)S(1)} %collective-permute-done.10.rest_1_), channel_id=1, source_target_pairs={{0,1},{1,0},{2,3},{3,2},{4,5},{5,4},{6,7},{7,6},{8,9},{9,8},{10,11... | collective-permute-start | bytes 3145736 | tf_op jit(solution)/shard_map/ppermute | solution.py:28
  71.3 13.4 %collective-permute-start.18 = (bf16[64,8192]{1,0:T(8,128)(2,1)}, bf16[64,8192]{1,0:T(8,128)(2,1)}, u32[]{:S(2)}, u32[]{:S(2)}) collective-permute-start(bf16[64,8192]{1,0:T(8,128)(2,1)} %collective-permute-done.11.rest_2_), channel_id=1, source_target_pairs={{0,1},{1,0},{2,3},{3,2},{4,5},{5,4},{6,7},{7,6},{8,9},{9,8},{10,11... | collective-permute-start | bytes 3145736 | tf_op jit(solution)/shard_map/ppermute | solution.py:28
  71.8 12.9 %collective-permute-start.19 = (bf16[32,8192]{1,0:T(8,128)(2,1)S(1)}, bf16[32,8192]{1,0:T(8,128)(2,1)}, u32[]{:S(2)}, u32[]{:S(2)}) collective-permute-start(bf16[32,8192]{1,0:T(8,128)(2,1)S(1)} %collective-permute-done.12.rest_3_), channel_id=1, source_target_pairs={{0,1},{1,0},{2,3},{3,2},{4,5},{5,4},{6,7},{7,6},{8,9},{9,8},{10,11... | collective-permute-start | bytes 1572872 | tf_op jit(solution)/shard_map/ppermute | solution.py:28
  71.9 12.8 %collective-permute-start.20 = (bf16[16,8192]{1,0:T(8,128)(2,1)S(1)}, bf16[16,8192]{1,0:T(8,128)(2,1)S(1)}, u32[]{:S(2)}, u32[]{:S(2)}) collective-permute-start(bf16[16,8192]{1,0:T(8,128)(2,1)S(1)} %collective-permute-done.13.rest_4_), channel_id=1, source_target_pairs={{0,1},{1,0},{2,3},{3,2},{4,5},{5,4},{6,7},{7,6},{8,9},{9,8},{10,11... | collective-permute-start | bytes 786440 | tf_op jit(solution)/shard_map/ppermute | solution.py:28
  84.7 14.3 %copy-start = (f32[8,64]{1,0:T(8,128)}, f32[8,64]{1,0:T(8,128)S(1)}, u32[]{:S(2)}) copy-start(f32[8,64]{1,0:T(8,128)S(1)} %get-tuple-element.103.power_ref) | copy-start | bytes 6148
  84.8 14.3 %copy-start.2 = (bf16[64,4096]{1,0:T(8,128)(2,1)S(1)}, bf16[64,4096]{1,0:T(8,128)(2,1)}, u32[]{:S(2)}) copy-start(bf16[64,4096]{1,0:T(8,128)(2,1)} %own_ref.2) | copy-start | bytes 1572868
  84.8 14.3 %copy-start.5 = (bf16[64,4096]{1,0:T(8,128)(2,1)S(1)}, bf16[64,4096]{1,0:T(8,128)(2,1)}, u32[]{:S(2)}) copy-start(bf16[64,4096]{1,0:T(8,128)(2,1)} %copy-done.4) | copy-start | bytes 1572868

commit v4 on v3

--- a/solution.py
+++ b/solution.py
@@ -11,8 +11,7 @@
 HALF_BLK = 7
 LANES = 128
 ROWS_STEP = 16
-UNROLL = 16
-SLOT = 8
+UNROLL = 32
 CHUNK = 1024
 MIB = 2**20
 
@@ -91,6 +90,7 @@
     all_samples = 2 * half
     chunks = all_samples // CHUNK
     words = snp_rows // LANES
+    slot = words | 1
     share = snp_rows // 2
     side = 2 * LANES
     core = core_ref[0]
@@ -159,7 +159,7 @@
                 )
                 for c in range(side // LANES):
                     word = j * (side // LANES) + c
-                    table[pl.ds((k * CHUNK + at) * words + word, side, stride=words), :] = (
+                    table[pl.ds((k * CHUNK + at) * slot + word, side, stride=slot), :] = (
                         t[:, c * LANES : (c + 1) * LANES]
                     )
                 turned.append(t)
@@ -179,11 +179,11 @@
 
         def scatter(i, carry, q=q):
             first = pl.multiple_of(i * UNROLL, UNROLL)
-            base = pl.multiple_of(first * words, UNROLL * words)
-            held = [table[pl.ds(base + u * words, SLOT), :] for u in range(UNROLL)]
+            base = pl.multiple_of(first * slot, UNROLL * slot)
+            held = [table[pl.ds(base + u * slot, words), :] for u in range(UNROLL)]
             for u in range(UNROLL):
-                to = pl.multiple_of(idx[q * all_samples + first + u] * SLOT, SLOT)
-                dest[pl.ds(to, SLOT), :] = held[u]
+                to = idx[q * all_samples + first + u] * slot
+                dest[pl.ds(to, words), :] = held[u]
             return carry
 
         lax.fori_loop(0, all_samples // UNROLL, scatter, 0)
@@ -194,7 +194,7 @@
             def narrow(i, carry, k=k):
                 at = pl.multiple_of(i * side, side)
                 for c in range(words):
-                    v = dest[pl.ds((k * CHUNK + at) * SLOT + c, side, stride=SLOT), :]
+                    v = dest[pl.ds((k * CHUNK + at) * slot + c, side, stride=slot), :]
                     stage[k % 2, pl.ds(at, side), pl.ds(c * LANES, LANES)] = v.astype(jnp.bfloat16)
                 return carry
 
@@ -222,8 +222,8 @@
         scratch_shapes=[
             pltpu.SMEM((labels * all_samples,), jnp.int32),
             pltpu.VMEM((3, snp_rows, CHUNK), jnp.bfloat16),
-            pltpu.VMEM((all_samples * words + SLOT, LANES), jnp.float32),
-            pltpu.VMEM((all_samples * SLOT, LANES), jnp.float32),
+            pltpu.VMEM((all_samples * (words | 1), LANES), jnp.float32),
+            pltpu.VMEM((all_samples * (words | 1), LANES), jnp.float32),
             pltpu.VMEM((2, CHUNK, snp_rows), jnp.bfloat16),
             pltpu.VMEM((2, CHUNK, snp_rows // 2), jnp.bfloat16),
             pltpu.VMEM((snp_rows, LANES), jnp.float32),
@@ -373,43 +373,38 @@
 
 
 def product_kernel(
-    pos_ref, sums_own, sums_other, *rest, n_in, sizes, labels, blocks_dev, last
+    pos_ref, sums_own, sums_other, plan_ref, *rest, caps, labels, genes, blocks_dev
 ):
-    if last:
-        plan_ref, before_ref = rest[:2]
-        rest = rest[2:]
+    reach = len(caps)
+    n_in = 1 + 2 * reach
     gene_refs = rest[:n_in]
-    weights_ref, out_ref, *rest = rest[n_in:]
-    if not last:
-        power_ref, *rest = rest
-    rows, total, *rest = rest
+    weights_ref, out_ref, power_ref, rows, total, power = rest[n_in:]
     step = pl.program_id(0)
     steps = pl.num_programs(0)
     snp_rows = sums_own.shape[1]
     depth, width = weights_ref.shape
     block = SNP_BLOCK
-    used = rows.shape[0]
+    sizes = (genes,) + tuple(caps) + tuple(caps)
+    starts = [sum(sizes[:i]) for i in range(n_in)]
+    used = sum(sizes)
 
     @pl.when(step == 0)
     def _():
         total[...] = jnp.zeros_like(total)
-
-    at = 0
-    for ref in gene_refs:
-        rows[pl.ds(at, ref.shape[0]), :] = ref[...]
-        at += ref.shape[0]
+        power[...] = jnp.zeros_like(power)
+
+    for ref, start, size in zip(gene_refs, starts, sizes):
+        rows[pl.ds(start, size), :] = ref[...]
     for n in range(width // block):
         cols = pl.ds(n * block, block)
         total[pl.ds(0, used), cols] += jnp.dot(
             rows[...], weights_ref[:, cols], preferred_element_type=jnp.float32
         )
-    if not last:
-        power = rest[0]
-        kept = jnp.where(step == 0, 0.0, power[...])
-        for t in range(depth // LANES):
-            x = gene_refs[0][:, pl.ds(t * LANES, LANES)].astype(jnp.float32)
-            kept = kept + x * x
-        power[...] = kept
+    kept = power[...]
+    for t in range(depth // LANES):
+        x = gene_refs[0][:, pl.ds(t * LANES, LANES)].astype(jnp.float32)
+        kept = kept + x * x
+    power[...] = kept
 
     @pl.when(step == steps - 1)
     def _():
@@ -443,30 +438,15 @@
         while len(peaks) % 8:
             peaks.append(jnp.zeros_like(peaks[0]))
         peaks = jnp.concatenate(peaks, axis=0)
-        if not last:
-            out_ref[...] = peaks
-            powers = jnp.sum(rest[0][...].T, axis=0, keepdims=True)
-            power_ref[...] = jnp.broadcast_to(powers, power_ref.shape)
-            return
-
-        genes = plan_ref.shape[2]
-        chips = out_ref.shape[0] // 2
-        reach = (len(sizes) - 1) // 2
-        before = before_ref[...]
         out_ref[...] = jnp.zeros_like(out_ref)
-        start = 0
-        for i, size in enumerate(sizes):
-            if i == n_in + 1:
-                start = 0
-            values = before if i <= reach else peaks
+        slot_of = lax.broadcasted_iota(jnp.int32, (total.shape[0], genes), 0)
+        for i in range(n_in):
             slot = plan_ref[0, pl.ds(i, 1), :]
-            slot = jnp.where(slot >= 0, slot + start, -1)
-            start += size
+            slot = jnp.where(slot >= 0, slot + starts[i], -1)
             low = plan_ref[1, pl.ds(i, 1), :]
             high = plan_ref[2, pl.ds(i, 1), :]
-            slot_of = lax.broadcasted_iota(jnp.int32, (values.shape[1], genes), 0)
             spread = jnp.dot(
-                values, (slot_of == slot).astype(jnp.float32),
+                peaks, (slot_of == slot).astype(jnp.float32),
                 precision=lax.Precision.HIGHEST, preferred_element_type=jnp.float32,
             )
 
@@ -499,65 +479,64 @@
                 way = core if i <= reach else 1 - core
                 target = chip + (2 * way - 1) * ((i - 1) % reach + 1)
 
-            @pl.when((target >= 0) & (target < chips))
+            @pl.when((target >= 0) & (target < out_ref.shape[0] // 2))
             def _(out_rows=out_rows, target=target):
                 for c in range(2):
                     out_ref[2 * target + c, :, pl.ds(0, genes)] = jnp.concatenate(
                         out_rows, axis=0
                     )
 
-
-def products(pos, sums, arrays, weights, caps, labels, blocks_dev, before=None, plan=None,
-             chips=None):
-    all_samples, width = weights.shape
-    genes = arrays[0].shape[0] if plan is None else plan.shape[2]
-    sizes = (genes,) + tuple(caps) + tuple(caps)
-    used = sum(x.shape[0] for x in arrays)
+        powers = jnp.sum(power[...].T, axis=0, keepdims=True)
+        power_ref[...] = jnp.broadcast_to(powers, power_ref.shape)
+
+
+def products(pos, sums, plan, full, mine, other, weights, caps, labels, chips, blocks_dev):
+    genes, all_samples = full.shape
+    width = weights.shape[1]
+    snp_rows = sums[0].shape[1]
+    depth = CHUNK
+    used = genes + 2 * sum(caps)
     padded = -(-used // LANES) * LANES
     out_rows = -(-(1 + 2 * labels) // 8) * 8
-    peak_rows = -(-(labels * blocks_dev + blocks_dev // 2) // 8) * 8
-    last = plan is not None
-    extra = (plan, before) if last else ()
-
-    def whole(x):
-        return pl.BlockSpec(x.shape, lambda k: (0,) * x.ndim)
-
-    if last:
-        outs = (jax.ShapeDtypeStruct((2 * chips, out_rows, LANES), jnp.float32),)
-    else:
-        outs = (
-            jax.ShapeDtypeStruct((peak_rows, padded), jnp.float32),
-            jax.ShapeDtypeStruct((8, genes), jnp.float32),
-        )
-    scratch = [
-        pltpu.VMEM((used, CHUNK), jnp.bfloat16),
-        pltpu.VMEM((padded, width), jnp.float32),
-    ]
-    if not last:
-        scratch.append(pltpu.VMEM((genes, LANES), jnp.float32))
+
+    def blocked(x):
+        return pl.BlockSpec((x.shape[0], depth), lambda k: (0, k))
+
+    arrays = (full, *mine, *other)
     return pl.pallas_call(
         functools.partial(
-            product_kernel, n_in=len(arrays), sizes=sizes, labels=labels,
-            blocks_dev=blocks_dev, last=last,
+            product_kernel, caps=caps, labels=labels, genes=genes, blocks_dev=blocks_dev
         ),
-        grid=(all_samples // CHUNK,),
-        out_shape=outs,
+        grid=(all_samples // depth,),
+        out_shape=(
+            jax.ShapeDtypeStruct((2 * chips, out_rows, LANES), jnp.float32),
+            jax.ShapeDtypeStruct((8, genes), jnp.float32),
+        ),
         in_specs=[
             pl.BlockSpec(memory_space=pltpu.SMEM),
-            *[whole(x) for x in (*sums, *extra)],
-            *[pl.BlockSpec((x.shape[0], CHUNK), lambda k: (0, k)) for x in arrays],
-            pl.BlockSpec((CHUNK, width), lambda k: (k, 0)),
+            pl.BlockSpec((8, snp_rows), lambda k: (0, 0)),
+            pl.BlockSpec((8, snp_rows), lambda k: (0, 0)),
+            pl.BlockSpec(plan.shape, lambda k: (0, 0, 0)),
+            *[blocked(x) for x in arrays],
+            pl.BlockSpec((depth, width), lambda k: (k, 0)),
         ],
-        out_specs=tuple(whole(x) for x in outs),
-        scratch_shapes=scratch,
+        out_specs=(
+            pl.BlockSpec((2 * chips, out_rows, LANES), lambda k: (0, 0, 0)),
+            pl.BlockSpec((8, genes), lambda k: (0, 0)),
+        ),
+        scratch_shapes=[
+            pltpu.VMEM((used, depth), jnp.bfloat16),
+            pltpu.VMEM((padded, width), jnp.float32),
+            pltpu.VMEM((genes, LANES), jnp.float32),
+        ],
         compiler_params=pltpu.CompilerParams(vmem_limit_bytes=48 * MIB),
         cost_estimate=pl.CostEstimate(
             flops=2 * used * all_samples * width,
             bytes_accessed=2 * all_samples * (width + used),
             transcendentals=0,
         ),
-        name="products_last" if last else "products",
-    )(pos, *sums, *extra, *arrays, weights)
+        name="products",
+    )(pos, *sums, plan, *arrays, weights)
 
 
 def finish_kernel(gathered_ref, power_ref, out_ref, *, samples):
@@ -584,8 +563,11 @@
     caps = tuple(min(genes, genes * 4 >> k) for k in range(1, reach + 1))
 
     other_pheno = swapped(phenotypes)
-    other_geno = swapped(genotypes)
     env = environment[None]
+    own_sums = local_moments(genotypes, env)
+    sums = (own_sums, swapped(own_sums))
+    late_geno, _ = lax.optimization_barrier((genotypes, other_pheno))
+    other_geno = swapped(late_geno)
     other_env = swapped(env)
     other_shuffles = swapped(shuffles)
     pos = jnp.stack([genome_pos, sample_pos]).astype(jnp.int32)
@@ -607,21 +589,15 @@
 
     rounds, plan, full, *payloads = chosen(jnp.zeros((1,), jnp.int32))
     mine = travel(payloads)
-    own_sums = local_moments(genotypes, env)
-    sums = (own_sums, swapped(own_sums))
     weights = snp_side(
         pos[1:], env, other_env, *sums, shuffles, other_shuffles, genotypes, other_geno, labels
     )
 
     def met(plan, full, mine):
         other = [swapped(x) for x in mine]
-        before, power = products(
-            pos, sums, (full, *mine), weights, caps, labels, blocks_dev
+        return products(
+            pos, sums, plan, full, mine, other, weights, caps, labels, chips, blocks_dev
         )
-        (found,) = products(
-            pos, sums, other, weights, caps, labels, blocks_dev, before, plan, chips
-        )
-        return found, power
 
     *mine, weights = lax.optimization_barrier((*mine, weights))
     found, power = met(plan, full, mine)

time: 113 us -> 107 us (0.947)
  Pallas kernels: 79.1 us -> 66 us
  waiting for transfers between devices: 2.07 us -> 6.37 us
  blocking collectives: 11.5 us -> 12.9 us
    pallas_call x2 -> x1, Pallas kernels: 26.6 us -> 18.3 us  [products(): pl.pallas_call(functools.partial(product_kernel, caps=caps, labels=labels...]
    pallas_call x1, Pallas kernels: 42.3 us -> 37.6 us  [snp_side(): pl.pallas_call(functools.partial(snp_side_kernel, labels=labels), out_sha...]
    ppermute x9, waiting for transfers between devices: 2.06 us -> 6.36 us  [swapped(): lax.ppermute(x, 'sample', [(i, (i + 1) % count) for i in range(count)])]
    all_to_all x1, blocking collectives: 11.5 us -> 12.9 us  [shards(): gathered = lax.all_to_all(found, ('genome', 'sample'), 0, 0, tiled=True)]
  transfers between devices with their start and end apart: 13 -> 13, of which waited for: 1 -> 4; matrix products, arithmetic and copies ran while one was open for 0% -> 0% of each run, Pallas kernels for 56% -> 44%
where the time goes in v4:
time: 107 us; the launch traced here: 106 us
  Pallas kernels  66 us (62%)
  starting transfers between devices  18.7 us (17%)
  blocking collectives  12.9 us (12%)
  waiting for transfers between devices  6.37 us (6%)
  local copies, waits for them, and re-layouts  1.23 us (1%)
    pallas_call x1, Pallas kernels, snp_side(): pl.pallas_call(functools.partial(snp_side_kernel, labels=labels), out_sha...  37.6 us
    pallas_call x1, Pallas kernels, products(): pl.pallas_call(functools.partial(product_kernel, caps=caps, labels=labels...  18.3 us
    ppermute x4, starting transfers between devices, travel(): mine.append(lax.ppermute(payload, ('genome', 'sample'), pairs))  16 us
    all_to_all x1, blocking collectives, shards(): gathered = lax.all_to_all(found, ('genome', 'sample'), 0, 0, tiled=True)  12.9 us
    ppermute x9, waiting for transfers between devices, swapped(): lax.ppermute(x, 'sample', [(i, (i + 1) % count) for i in range(count)])  6.36 us
    pallas_call x1, Pallas kernels, local_moments(): pl.pallas_call(moments_kernel, grid=(half // chunk,), out_shape=jax.Shape...  4.52 us
    pallas_call x1, Pallas kernels, select(): pl.pallas_call(functools.partial(select_kernel, caps=caps, blocks_dev=blo...  4.17 us
    ppermute x9, starting transfers between devices, swapped(): lax.ppermute(x, 'sample', [(i, (i + 1) % count) for i in range(count)])  2.68 us
  transfers between devices with their start and end apart: 13, of which 4 were waited for; matrix products, arithmetic and copies ran while one was open for 0% of the time, Pallas kernels for 44%

profile of v4, /device:TPU:0, one launch (start us, length us, event | category | flops | bytes accessed | tf_op | source)
XLA Modules:
  0.0 106.2 jit_solution(4644444158304615827)
XLA Ops:
  0.0 0.5 collective-permute-start.9
  0.5 1.7 %collective-permute-done.9.other_ref = bf16[64,4096]{1,0:T(8,128)(2,1)S(1)} collective-permute-done((bf16[64,4096]{1,0:T(8,128)(2,1)}, bf16[64,4096]{1,0:T(8,128)(2,1)S(1)}, u32[]{:S(2)}, u32[]{:S(2)}) %collective-permute-start.9) | collective-permute-done | bytes 524320 | tf_op jit(solution)/shard_map/ppermute | solution.py:27
  2.2 0.4 collective-permute-start.16
  2.6 0.2 collective-permute-start.14
  2.8 4.5 %local_moments.1.sums_own = f32[8,512]{1,0:T(8,128)S(1)} custom-call(bf16[512,4096]{1,0:T(8,128)(2,1)} %own_ref.3, f32[1,4096]{1,0:T(1,128)} %bitcast.15), custom_call_target="tpu_custom_call" | custom-call | flops 5000000000 | bytes 4194304 | tf_op jit(solution)/shard_map/local_moments/pallas_call | solution.py:65
  7.3 0.4 collective-permute-start.8
  7.8 0.1 collective-permute-start.15
  7.9 0.1 pad_add_fusion.pos_ref
  8.0 4.2 %select.2 = (s32[1]{0:T(128)}, s32[3,16,64]{2,1,0:T(8,128)S(1)}, bf16[64,8192]{1,0:T(8,128)(2,1)S(1)}, bf16[64,8192]{1,0:T(8,128)(2,1)}, bf16[64,8192]{1,0:T(8,1...) custom-call(s32[1]{0:T(128)} %constant.13.clone.1.round_ref, s32[2]{0:T(128)S(1)} %pad_add_fusion.pos_ref, ...), custom_call_target="tpu_custom_call" | custom-call | tf_op jit(solution)/shard_map/select/pallas_call | solution.py:356
  12.2 4.8 %collective-permute-start.10 = (bf16[64,8192]{1,0:T(8,128)(2,1)}, bf16[64,8192]{1,0:T(8,128)(2,1)S(1)}, u32[]{:S(2)}, u32[]{:S(2)}) collective-permute-start(bf16[64,8192]{1,0:T(8,128)(2,1)} %get-tuple-element.92), channel_id=1, source_target_pairs={{0,2},{2,4},{4,6},{6,8},{8,10},{10,12},{12,14},{14,16},{16,18},{18... | collective-permute-start | bytes 3145736 | tf_op jit(solution)/shard_map/ppermute | solution.py:587
  17.0 4.4 %collective-permute-start.11 = (bf16[64,8192]{1,0:T(8,128)(2,1)}, bf16[64,8192]{1,0:T(8,128)(2,1)}, u32[]{:S(2)}, u32[]{:S(2)}) collective-permute-start(bf16[64,8192]{1,0:T(8,128)(2,1)} %get-tuple-element.93), channel_id=1, source_target_pairs={{0,4},{2,6},{4,8},{6,10},{8,12},{10,14},{12,16},{14,18},{16,20},{1... | collective-permute-start | bytes 3145736 | tf_op jit(solution)/shard_map/ppermute | solution.py:587
  21.4 0.0 collective-permute-done.14.env_other
  21.4 3.4 %collective-permute-start.12 = (bf16[32,8192]{1,0:T(8,128)(2,1)}, bf16[32,8192]{1,0:T(8,128)(2,1)S(1)}, u32[]{:S(2)}, u32[]{:S(2)}) collective-permute-start(bf16[32,8192]{1,0:T(8,128)(2,1)} %get-tuple-element.94), channel_id=1, source_target_pairs={{0,6},{2,8},{4,10},{6,12},{8,14},{10,16},{12,18},{14,20},{16,22},{... | collective-permute-start | bytes 1572872 | tf_op jit(solution)/shard_map/ppermute | solution.py:587
  24.8 0.0 collective-permute-done.15.shuf_other
  24.8 0.6 copy-done.9
  25.4 3.4 %collective-permute-start.13 = (bf16[16,8192]{1,0:T(8,128)(2,1)}, bf16[16,8192]{1,0:T(8,128)(2,1)S(1)}, u32[]{:S(2)}, u32[]{:S(2)}) collective-permute-start(bf16[16,8192]{1,0:T(8,128)(2,1)} %get-tuple-element.95), channel_id=1, source_target_pairs={{0,8},{2,10},{4,12},{6,14},{8,16},{10,18},{12,20},{14,22},{16,24},... | collective-permute-start | bytes 786440 | tf_op jit(solution)/shard_map/ppermute | solution.py:587
  28.9 0.0 collective-permute-done.16.other_ref
  28.9 37.6 %snp_side.1.rest_9_ = bf16[8192,1280]{1,0:T(8,128)(2,1)} custom-call(s32[1]{0:T(128)} %bitcast.3.core_ref, f32[1,4096]{1,0:T(1,128)} %bitcast.16, f32[1,4096]{1,0:T(1,128)} %copy-done.10, f32[8,512]{1,0:T(8,128)S(1)} %local_moments.1.sums_own, f32[8,512]{1,0:T(8,128)S(1)} %collective-permute-done.8.sums_other, s32[4,4096]{1,0:T(4,128)} %shuf_own.1, ...), custom_call_target="tpu_custom_call" | custom-call | flops 40000000000 | bytes 60000000 | tf_op jit(solution)/shard_map/snp_side/pallas_call | solution.py:217
  66.5 0.0 collective-permute-done.13.rest_4_
  66.5 0.0 collective-permute-done.11.rest_2_
  66.5 0.1 collective-permute-start.17
  66.6 0.5 collective-permute-start.18
  67.1 0.1 collective-permute-start.19
  67.2 0.4 collective-permute-start.20
  67.6 3.5 %collective-permute-done.20.rest_8_ = bf16[16,8192]{1,0:T(8,128)(2,1)S(1)} collective-permute-done((bf16[16,8192]{1,0:T(8,128)(2,1)S(1)}, bf16[16,8192]{1,0:T(8,128)(2,1)S(1)}, u32[]{:S(2)}, u32[]{:S(2)}) %collective-permute-start.20) | collective-permute-done | bytes 262176 | tf_op jit(solution)/shard_map/ppermute | solution.py:27
  71.1 0.9 collective-permute-done.19.rest_7_
  72.0 0.3 collective-permute-done.18.rest_6_
  72.2 18.3 %products.2 = (f32[32,8,128]{2,1,0:T(8,128)}, f32[8,64]{1,0:T(8,128)S(1)}) custom-call(s32[2]{0:T(128)S(1)} %pad_add_fusion.pos_ref, f32[8,512]{1,0:T(8,128)S(1)} %local_moments.1.sums_own, f32[8,512]{1,0:T(8,128)S(1)} %collective-permute-done.8.sums_other, s32[3,16,64]{2,1,0:T(8,128)S(1)} %get-tuple-element.90.plan_ref, ...), custom_call_target="tpu_custom_call" | custom-call | flops 8724152320 | bytes 27787264 | tf_op jit(solution)/shard_map/products/pallas_call | solution.py:506
  90.5 0.6 copy-done
  91.1 0.7 while.10
  91.8 12.9 %all_to_all.5.gathered_ref = f32[32,8,128]{2,1,0:T(8,128)} all-to-all(f32[32,8,128]{2,1,0:T(8,128)} %get-tuple-element.104), channel_id=1, replica_groups=mesh['genome'=16,'sample'=2] {'genome','sample'}, dimensions={0} | all-to-all | bytes 262144 | tf_op jit(solution)/shard_map/all_to_all | solution.py:614
  104.7 1.5 %finish.1 = f32[5,64]{1,0:T(8,128)} custom-call(f32[32,8,128]{2,1,0:T(8,128)} %all_to_all.5.gathered_ref, f32[8,64]{1,0:T(8,128)} %copy-done), custom_call_target="tpu_custom_call" | custom-call | tf_op jit(solution)/shard_map/finish/pallas_call | solution.py:615
  (20 shorter events, 0.0 us)
Async XLA Ops:
  0.0 2.2 %collective-permute-start.9 = (bf16[64,4096]{1,0:T(8,128)(2,1)}, bf16[64,4096]{1,0:T(8,128)(2,1)S(1)}, u32[]{:S(2)}, u32[]{:S(2)}) collective-permute-start(bf16[64,4096]{1,0:T(8,128)(2,1)} %own_ref.2), channel_id=1, source_target_pairs={{0,1},{1,0},{2,3},{3,2},{4,5},{5,4},{6,7},{7,6},{8,9},{9,8},{10,11... | collective-permute-start | bytes 1572872 | tf_op jit(solution)/shard_map/ppermute | solution.py:27
  2.2 5.8 %copy-start.2 = (bf16[64,4096]{1,0:T(8,128)(2,1)}, bf16[64,4096]{1,0:T(8,128)(2,1)S(1)}, u32[]{:S(2)}) copy-start(bf16[64,4096]{1,0:T(8,128)(2,1)S(1)} %collective-permute-done.9.other_ref) | copy-start | bytes 1572868
  2.2 26.7 %collective-permute-start.16 = (bf16[512,4096]{1,0:T(8,128)(2,1)}, bf16[512,4096]{1,0:T(8,128)(2,1)}, u32[]{:S(2)}, u32[]{:S(2)}) collective-permute-start(bf16[512,4096]{1,0:T(8,128)(2,1)} %own_ref.3), channel_id=1, source_target_pairs={{0,1},{1,0},{2,3},{3,2},{4,5},{5,4},{6,7},{7,6},{8,9},{9,8},{10,11... | collective-permute-start | bytes 12582920 | tf_op jit(solution)/shard_map/ppermute | solution.py:27
  2.6 5.2 %copy-start.8 = (s32[4,4096]{1,0:T(4,128)S(1)}, s32[4,4096]{1,0:T(4,128)}, u32[]{:S(2)}) copy-start(s32[4,4096]{1,0:T(4,128)} %shuf_own.1) | copy-start | bytes 196612
  2.6 5.4 %copy-start.1 = (bf16[64,4096]{1,0:T(8,128)(2,1)S(1)}, bf16[64,4096]{1,0:T(8,128)(2,1)}, u32[]{:S(2)}) copy-start(bf16[64,4096]{1,0:T(8,128)(2,1)} %own_ref.2) | copy-start | bytes 1572868
  2.6 5.4 %copy-start.5 = (s32[1024]{0:T(1024)S(1)}, s32[1024]{0:T(1024)}, u32[]{:S(2)}) copy-start(s32[1024]{0:T(1024)} %param.13) | copy-start | bytes 12292
  2.6 5.4 %copy-start.6 = (s32[1024]{0:T(1024)S(1)}, s32[1024]{0:T(1024)}, u32[]{:S(2)}) copy-start(s32[1024]{0:T(1024)} %param.14) | copy-start | bytes 12292
  2.6 5.4 %copy-start.7 = (s32[15]{0:T(128)S(1)}, s32[15]{0:T(128)}, u32[]{:S(2)}) copy-start(s32[15]{0:T(128)} %bounds_ref.1) | copy-start | bytes 184
  2.6 18.8 %collective-permute-start.14 = (f32[1,4096]{1,0:T(1,128)}, f32[1,4096]{1,0:T(1,128)S(1)}, u32[]{:S(2)}, u32[]{:S(2)}) collective-permute-start(f32[1,4096]{1,0:T(1,128)} %bitcast.14), channel_id=1, source_target_pairs={{0,1},{1,0},{2,3},{3,2},{4,5},{5,4},{6,7},{7,6},{8,9},{9,8},{10,11... | collective-permute-start | bytes 49160 | tf_op jit(solution)/shard_map/ppermute | solution.py:27
  7.3 9.7 %collective-permute-start.8 = (f32[8,512]{1,0:T(8,128)S(1)}, f32[8,512]{1,0:T(8,128)S(1)}, u32[]{:S(2)}, u32[]{:S(2)}) collective-permute-start(f32[8,512]{1,0:T(8,128)S(1)} %local_moments.1.sums_own), channel_id=1, source_target_pairs={{0,1},{1,0},{2,3},{3,2},{4,5},{5,4},{6,7},{7,6},{8,9},{9,8},{10,11... | collective-permute-start | bytes 49160 | tf_op jit(solution)/shard_map/ppermute | solution.py:27
  7.8 17.1 %collective-permute-start.15 = (s32[4,4096]{1,0:T(4,128)S(1)}, s32[4,4096]{1,0:T(4,128)S(1)}, u32[]{:S(2)}, u32[]{:S(2)}) collective-permute-start(s32[4,4096]{1,0:T(4,128)S(1)} %copy-done.8), channel_id=1, source_target_pairs={{0,1},{1,0},{2,3},{3,2},{4,5},{5,4},{6,7},{7,6},{8,9},{9,8},{10,11... | collective-permute-start | bytes 196616 | tf_op jit(solution)/shard_map/ppermute | solution.py:27
  12.2 54.3 %collective-permute-start.10 = (bf16[64,8192]{1,0:T(8,128)(2,1)}, bf16[64,8192]{1,0:T(8,128)(2,1)S(1)}, u32[]{:S(2)}, u32[]{:S(2)}) collective-permute-start(bf16[64,8192]{1,0:T(8,128)(2,1)} %get-tuple-element.92), channel_id=1, source_target_pairs={{0,2},{2,4},{4,6},{6,8},{8,10},{10,12},{12,14},{14,16},{16,18},{18... | collective-permute-start | bytes 3145736 | tf_op jit(solution)/shard_map/ppermute | solution.py:587
  17.0 49.5 %collective-permute-start.11 = (bf16[64,8192]{1,0:T(8,128)(2,1)}, bf16[64,8192]{1,0:T(8,128)(2,1)}, u32[]{:S(2)}, u32[]{:S(2)}) collective-permute-start(bf16[64,8192]{1,0:T(8,128)(2,1)} %get-tuple-element.93), channel_id=1, source_target_pairs={{0,4},{2,6},{4,8},{6,10},{8,12},{10,14},{12,16},{14,18},{16,20},{1... | collective-permute-start | bytes 3145736 | tf_op jit(solution)/shard_map/ppermute | solution.py:587
  21.4 7.5 %copy-start.10 = (f32[1,4096]{1,0:T(1,128)}, f32[1,4096]{1,0:T(1,128)S(1)}, u32[]{:S(2)}) copy-start(f32[1,4096]{1,0:T(1,128)S(1)} %collective-permute-done.14.env_other) | copy-start | bytes 49156
  21.4 45.1 %collective-permute-start.12 = (bf16[32,8192]{1,0:T(8,128)(2,1)}, bf16[32,8192]{1,0:T(8,128)(2,1)S(1)}, u32[]{:S(2)}, u32[]{:S(2)}) collective-permute-start(bf16[32,8192]{1,0:T(8,128)(2,1)} %get-tuple-element.94), channel_id=1, source_target_pairs={{0,6},{2,8},{4,10},{6,12},{8,14},{10,16},{12,18},{14,20},{16,22},{... | collective-permute-start | bytes 1572872 | tf_op jit(solution)/shard_map/ppermute | solution.py:587
  24.8 0.6 copy-start.9
  25.4 41.0 %collective-permute-start.13 = (bf16[16,8192]{1,0:T(8,128)(2,1)}, bf16[16,8192]{1,0:T(8,128)(2,1)S(1)}, u32[]{:S(2)}, u32[]{:S(2)}) collective-permute-start(bf16[16,8192]{1,0:T(8,128)(2,1)} %get-tuple-element.95), channel_id=1, source_target_pairs={{0,8},{2,10},{4,12},{6,14},{8,16},{10,18},{12,20},{14,22},{16,24},... | collective-permute-start | bytes 786440 | tf_op jit(solution)/shard_map/ppermute | solution.py:587
  66.5 5.4 %collective-permute-start.17 = (bf16[64,8192]{1,0:T(8,128)(2,1)S(1)}, bf16[64,8192]{1,0:T(8,128)(2,1)}, u32[]{:S(2)}, u32[]{:S(2)}) collective-permute-start(bf16[64,8192]{1,0:T(8,128)(2,1)S(1)} %collective-permute-done.10.rest_1_), channel_id=1, source_target_pairs={{0,1},{1,0},{2,3},{3,2},{4,5},{5,4},{6,7},{7,6},{8,9},{9,8},{10,11... | collective-permute-start | bytes 3145736 | tf_op jit(solution)/shard_map/ppermute | solution.py:27
  66.6 5.6 %collective-permute-start.18 = (bf16[64,8192]{1,0:T(8,128)(2,1)}, bf16[64,8192]{1,0:T(8,128)(2,1)}, u32[]{:S(2)}, u32[]{:S(2)}) collective-permute-start(bf16[64,8192]{1,0:T(8,128)(2,1)} %collective-permute-done.11.rest_2_), channel_id=1, source_target_pairs={{0,1},{1,0},{2,3},{3,2},{4,5},{5,4},{6,7},{7,6},{8,9},{9,8},{10,11... | collective-permute-start | bytes 3145736 | tf_op jit(solution)/shard_map/ppermute | solution.py:27
  67.1 4.9 %collective-permute-start.19 = (bf16[32,8192]{1,0:T(8,128)(2,1)S(1)}, bf16[32,8192]{1,0:T(8,128)(2,1)}, u32[]{:S(2)}, u32[]{:S(2)}) collective-permute-start(bf16[32,8192]{1,0:T(8,128)(2,1)S(1)} %collective-permute-done.12.rest_3_), channel_id=1, source_target_pairs={{0,1},{1,0},{2,3},{3,2},{4,5},{5,4},{6,7},{7,6},{8,9},{9,8},{10,11... | collective-permute-start | bytes 1572872 | tf_op jit(solution)/shard_map/ppermute | solution.py:27
  67.2 3.9 %collective-permute-start.20 = (bf16[16,8192]{1,0:T(8,128)(2,1)S(1)}, bf16[16,8192]{1,0:T(8,128)(2,1)S(1)}, u32[]{:S(2)}, u32[]{:S(2)}) collective-permute-start(bf16[16,8192]{1,0:T(8,128)(2,1)S(1)} %collective-permute-done.13.rest_4_), channel_id=1, source_target_pairs={{0,1},{1,0},{2,3},{3,2},{4,5},{5,4},{6,7},{7,6},{8,9},{9,8},{10,11... | collective-permute-start | bytes 786440 | tf_op jit(solution)/shard_map/ppermute | solution.py:27
  90.5 0.6 copy-start

commit v5 on v4

--- a/solution.py
+++ b/solution.py
@@ -11,7 +11,6 @@
 HALF_BLK = 7
 LANES = 128
 ROWS_STEP = 16
-UNROLL = 32
 CHUNK = 1024
 MIB = 2**20
 
@@ -83,24 +82,24 @@
 def snp_side_kernel(
     core_ref, env_own, env_other, sums_own, sums_other, shuf_own, shuf_other, own_ref, other_ref,
     out_ref,
-    idx, geno, table, dest, stage, first_stage, slope, idx_sems, in_sems, out_sems, first_sems,
+    idx, geno, env, even, odd, dests, stage, first_stage, slope,
+    idx_sems, in_sems, out_sems, first_sems,
     *, labels,
 ):
     snp_rows, half = own_ref.shape
     all_samples = 2 * half
     chunks = all_samples // CHUNK
     words = snp_rows // LANES
-    slot = words | 1
     share = snp_rows // 2
-    side = 2 * LANES
+    side = even.shape[0]
+    blocks = all_samples // side
+    per_chunk = CHUNK // side
     core = core_ref[0]
-    depth = geno.shape[0]
 
     def load(k):
         source = own_ref if k * CHUNK < half else other_ref
         return pltpu.make_async_copy(
-            source.at[:, pl.ds((k * CHUNK) % half, CHUNK)], geno.at[k % depth],
-            in_sems.at[k % depth],
+            source.at[:, pl.ds((k * CHUNK) % half, CHUNK)], geno.at[k], in_sems.at[k]
         )
 
     def load_idx(q, h):
@@ -111,12 +110,12 @@
             idx_sems.at[2 * q + h],
         )
 
-    def save_first(k):
-        there = jnp.where(core == 0, k * CHUNK, (k * CHUNK + half) % all_samples)
-        rows = pl.ds(pl.multiple_of(there, CHUNK), CHUNK)
+    def save_first(h):
+        to = pl.multiple_of(jnp.where(core == h, 0, half), half)
         return pltpu.make_async_copy(
-            first_stage.at[k % 2], out_ref.at[rows, pl.ds(labels * snp_rows, share)],
-            first_sems.at[k % 2],
+            first_stage.at[pl.ds(h * half, half)],
+            out_ref.at[pl.ds(to, half), pl.ds(labels * snp_rows, share)],
+            first_sems.at[h],
         )
 
     def save(q, k):
@@ -126,11 +125,13 @@
             out_sems.at[k % 2],
         )
 
-    for k in range(depth):
+    for k in range(chunks):
         load(k).start()
     for q in range(labels):
         for h in range(2):
             load_idx(q, h).start()
+    env[:, pl.ds(0, half)] = env_own[...]
+    env[:, pl.ds(half, half)] = env_other[...]
     sums = sums_own[...] + sums_other[...]
     slope[...] = jnp.broadcast_to(sums[1:2, :] / sums[0:1, :], (LANES, snp_rows)).T
     unit = (
@@ -138,71 +139,78 @@
         == lax.broadcasted_iota(jnp.int32, (side, side), 1)
     ).astype(jnp.bfloat16)
 
-    for k in range(chunks):
-        load(k).wait()
-        if k >= 2:
-            save_first(k - 2).wait()
-        env_ref = env_own if k * CHUNK < half else env_other
-
-        def turn(i, carry, k=k, env_ref=env_ref):
-            at = pl.multiple_of(i * side, side)
-            e = env_ref[:, pl.ds((k * CHUNK) % half + at, side)]
-            turned = []
-            for j in range(snp_rows // side):
-                rows = pl.ds(j * side, side)
-                x = geno[k % depth, rows, pl.ds(at, side)].astype(jnp.float32)
-                r = slope[rows, :]
-                a = x * (e - jnp.concatenate([r] * (side // LANES), axis=1))
-                t = lax.dot_general(
-                    unit, a.astype(jnp.bfloat16), (((1,), (1,)), ((), ())),
-                    preferred_element_type=jnp.float32,
-                )
-                for c in range(side // LANES):
-                    word = j * (side // LANES) + c
-                    table[pl.ds((k * CHUNK + at) * slot + word, side, stride=slot), :] = (
-                        t[:, c * LANES : (c + 1) * LANES]
-                    )
-                turned.append(t)
-            turned = jnp.concatenate(turned, axis=1)
-            kept = jnp.where(core == 0, turned[:, :share], turned[:, share:])
-            first_stage[k % 2, pl.ds(at, side), :] = kept.astype(jnp.bfloat16)
-            return carry
-
-        lax.fori_loop(0, CHUNK // side, turn, 0, unroll=2)
-        save_first(k).start()
-        if k + depth < chunks:
-            load(k + depth).start()
-
+    def turn(b, held):
+        k = b // per_chunk
+        at = pl.multiple_of((b % per_chunk) * side, side)
+        e = env[:, pl.ds(pl.multiple_of(b * side, side), side)]
+        flat = held.reshape(side * words, LANES)
+        kept = None
+        for j in range(snp_rows // side):
+            rows = pl.ds(j * side, side)
+            x = geno[k, rows, pl.ds(at, side)].astype(jnp.float32)
+            r = slope[rows, :]
+            a = x * (e - jnp.concatenate([r] * (side // LANES), axis=1))
+            t = lax.dot_general(
+                unit, a.astype(jnp.bfloat16), (((1,), (1,)), ((), ())),
+                preferred_element_type=jnp.float32,
+            )
+            for c in range(side // LANES):
+                word = j * (side // LANES) + c
+                flat[pl.ds(word, side, stride=words), :] = t[:, c * LANES : (c + 1) * LANES]
+            kept = t if j == 0 else jnp.where(core == 0, kept, t)
+        first_stage[pl.ds(pl.multiple_of(b * side, side), side), :] = kept.astype(jnp.bfloat16)
+
+    def scatter(b, held):
+        first = pl.multiple_of(b * side, side)
+        for u in range(side):
+            row = held[u]
+            for q in range(labels):
+                dests[q][idx[q * all_samples + first + u]] = row
+
+    load(0).wait()
+    turn(0, even)
     for q in range(labels):
         for h in range(2):
             load_idx(q, h).wait()
 
-        def scatter(i, carry, q=q):
-            first = pl.multiple_of(i * UNROLL, UNROLL)
-            base = pl.multiple_of(first * slot, UNROLL * slot)
-            held = [table[pl.ds(base + u * slot, words), :] for u in range(UNROLL)]
-            for u in range(UNROLL):
-                to = idx[q * all_samples + first + u] * slot
-                dest[pl.ds(to, words), :] = held[u]
-            return carry
-
-        lax.fori_loop(0, all_samples // UNROLL, scatter, 0)
+    def arrive(b):
+        for k in range(1, chunks):
+
+            @pl.when(b == k * per_chunk)
+            def _(k=k):
+                load(k).wait()
+
+    def pair(i, carry):
+        arrive(2 * i + 2)
+        scatter(2 * i, even)
+        turn(2 * i + 1, odd)
+        scatter(2 * i + 1, odd)
+        turn(jnp.minimum(2 * i + 2, blocks - 1), even)
+        return carry
+
+    lax.fori_loop(0, blocks // 2, pair, 0)
+    for h in range(2):
+        save_first(h).start()
+
+    for q in range(labels):
+        flat = dests[q].reshape(all_samples * words, LANES)
         for k in range(chunks):
             if q * chunks + k >= 2:
                 save((q * chunks + k - 2) // chunks, (k - 2) % chunks).wait()
 
-            def narrow(i, carry, k=k):
+            def narrow(i, carry, k=k, flat=flat):
                 at = pl.multiple_of(i * side, side)
                 for c in range(words):
-                    v = dest[pl.ds((k * CHUNK + at) * slot + c, side, stride=slot), :]
+                    v = flat[pl.ds((k * CHUNK + at) * words + c, side, stride=words), :]
                     stage[k % 2, pl.ds(at, side), pl.ds(c * LANES, LANES)] = v.astype(jnp.bfloat16)
                 return carry
 
             lax.fori_loop(0, CHUNK // side, narrow, 0)
             save(q, k).start()
     for k in range(chunks - 2, chunks):
-        save_first(k).wait()
         save(labels - 1, k).wait()
+    for h in range(2):
+        save_first(h).wait()
 
 
 def snp_side(core, env_own, env_other, sums_own, sums_other, shuf_own, shuf_other, own, other,
@@ -211,6 +219,7 @@
     all_samples = 2 * half
     words = snp_rows // LANES
     width = labels * snp_rows + snp_rows // 2
+    side = 2 * LANES
     any_spec = pl.BlockSpec(memory_space=pl.ANY)
     smem = pl.BlockSpec(memory_space=pltpu.SMEM)
     vmem = pl.BlockSpec(memory_space=pltpu.VMEM)
@@ -221,18 +230,20 @@
         out_specs=any_spec,
         scratch_shapes=[
             pltpu.SMEM((labels * all_samples,), jnp.int32),
-            pltpu.VMEM((3, snp_rows, CHUNK), jnp.bfloat16),
-            pltpu.VMEM((all_samples * (words | 1), LANES), jnp.float32),
-            pltpu.VMEM((all_samples * (words | 1), LANES), jnp.float32),
+            pltpu.VMEM((all_samples // CHUNK, snp_rows, CHUNK), jnp.bfloat16),
+            pltpu.VMEM((1, all_samples), jnp.float32),
+            pltpu.VMEM((side, words, LANES), jnp.float32),
+            pltpu.VMEM((side, words, LANES), jnp.float32),
+            [pltpu.VMEM((all_samples, words, LANES), jnp.float32) for _ in range(labels)],
             pltpu.VMEM((2, CHUNK, snp_rows), jnp.bfloat16),
-            pltpu.VMEM((2, CHUNK, snp_rows // 2), jnp.bfloat16),
+            pltpu.VMEM((all_samples, snp_rows // 2), jnp.bfloat16),
             pltpu.VMEM((snp_rows, LANES), jnp.float32),
             pltpu.SemaphoreType.DMA((2 * labels,)),
-            pltpu.SemaphoreType.DMA((3,)),
+            pltpu.SemaphoreType.DMA((all_samples // CHUNK,)),
             pltpu.SemaphoreType.DMA((2,)),
             pltpu.SemaphoreType.DMA((2,)),
         ],
-        compiler_params=pltpu.CompilerParams(vmem_limit_bytes=61 * MIB),
+        compiler_params=pltpu.CompilerParams(vmem_limit_bytes=60 * MIB),
         cost_estimate=pl.CostEstimate(
             flops=40 * 10**9, bytes_accessed=60 * 10**6, transcendentals=0
         ),

time: 107 us -> 111 us (1.037)
  Pallas kernels: 66 us -> 71.8 us
  blocking collectives: 12.9 us -> 11.5 us
    pallas_call x1, Pallas kernels: 37.6 us -> 43.5 us  [snp_side(): pl.pallas_call(functools.partial(snp_side_kernel, labels=labels), out_sha...]
    all_to_all x1, blocking collectives: 12.9 us -> 11.5 us  [shards(): gathered = lax.all_to_all(found, ('genome', 'sample'), 0, 0, tiled=True)]
  transfers between devices with their start and end apart: 13 -> 13, of which waited for: 4 -> 2; matrix products, arithmetic and copies ran while one was open for 0% -> 0% of each run, Pallas kernels for 44% -> 47%
where the time goes in v5:
time: 111 us; the launch traced here: 110 us
  Pallas kernels  71.8 us (65%)
  starting transfers between devices  18.7 us (17%)
  blocking collectives  11.5 us (10%)
  waiting for transfers between devices  6.17 us (6%)
  local copies, waits for them, and re-layouts  1.25 us (1%)
    pallas_call x1, Pallas kernels, snp_side(): pl.pallas_call(functools.partial(snp_side_kernel, labels=labels), out_sha...  43.5 us
    pallas_call x1, Pallas kernels, products(): pl.pallas_call(functools.partial(product_kernel, caps=caps, labels=labels...  18.3 us
    ppermute x4, starting transfers between devices, travel(): mine.append(lax.ppermute(payload, ('genome', 'sample'), pairs))  16 us
    all_to_all x1, blocking collectives, shards(): gathered = lax.all_to_all(found, ('genome', 'sample'), 0, 0, tiled=True)  11.5 us
    ppermute x9, waiting for transfers between devices, swapped(): lax.ppermute(x, 'sample', [(i, (i + 1) % count) for i in range(count)])  6.16 us
    pallas_call x1, Pallas kernels, local_moments(): pl.pallas_call(moments_kernel, grid=(half // chunk,), out_shape=jax.Shape...  4.52 us
    pallas_call x1, Pallas kernels, select(): pl.pallas_call(functools.partial(select_kernel, caps=caps, blocks_dev=blo...  3.97 us
    ppermute x9, starting transfers between devices, swapped(): lax.ppermute(x, 'sample', [(i, (i + 1) % count) for i in range(count)])  2.68 us
  transfers between devices with their start and end apart: 13, of which 2 were waited for; matrix products, arithmetic and copies ran while one was open for 0% of the time, Pallas kernels for 47%

profile of v5, /device:TPU:0, one launch (start us, length us, event | category | flops | bytes accessed | tf_op | source)
XLA Modules:
  0.0 110.5 jit_solution(10917471101454102699)
XLA Ops:
  0.0 0.5 collective-permute-start.9
  0.5 1.7 %collective-permute-done.9.other_ref = bf16[64,4096]{1,0:T(8,128)(2,1)S(1)} collective-permute-done((bf16[64,4096]{1,0:T(8,128)(2,1)}, bf16[64,4096]{1,0:T(8,128)(2,1)S(1)}, u32[]{:S(2)}, u32[]{:S(2)}) %collective-permute-start.9) | collective-permute-done | bytes 524320 | tf_op jit(solution)/shard_map/ppermute | solution.py:26
  2.2 0.4 collective-permute-start.16
  2.6 0.2 collective-permute-start.14
  2.8 4.5 %local_moments.1.sums_own = f32[8,512]{1,0:T(8,128)S(1)} custom-call(bf16[512,4096]{1,0:T(8,128)(2,1)} %own_ref.3, f32[1,4096]{1,0:T(1,128)} %bitcast.15), custom_call_target="tpu_custom_call" | custom-call | flops 5000000000 | bytes 4194304 | tf_op jit(solution)/shard_map/local_moments/pallas_call | solution.py:64
  7.3 0.4 collective-permute-start.8
  7.8 0.1 collective-permute-start.15
  7.9 0.1 pad_add_fusion.pos_ref
  8.0 4.0 %select.2 = (s32[1]{0:T(128)}, s32[3,16,64]{2,1,0:T(8,128)S(1)}, bf16[64,8192]{1,0:T(8,128)(2,1)S(1)}, bf16[64,8192]{1,0:T(8,128)(2,1)}, bf16[64,8192]{1,0:T(8,1...) custom-call(s32[1]{0:T(128)} %constant.13.clone.1.round_ref, s32[2]{0:T(128)S(1)} %pad_add_fusion.pos_ref, ...), custom_call_target="tpu_custom_call" | custom-call | tf_op jit(solution)/shard_map/select/pallas_call | solution.py:367
  12.0 4.8 %collective-permute-start.10 = (bf16[64,8192]{1,0:T(8,128)(2,1)}, bf16[64,8192]{1,0:T(8,128)(2,1)S(1)}, u32[]{:S(2)}, u32[]{:S(2)}) collective-permute-start(bf16[64,8192]{1,0:T(8,128)(2,1)} %get-tuple-element.92), channel_id=1, source_target_pairs={{0,2},{2,4},{4,6},{6,8},{8,10},{10,12},{12,14},{14,16},{16,18},{18... | collective-permute-start | bytes 3145736 | tf_op jit(solution)/shard_map/ppermute | solution.py:598
  16.8 3.4 %collective-permute-start.11 = (bf16[64,8192]{1,0:T(8,128)(2,1)}, bf16[64,8192]{1,0:T(8,128)(2,1)S(1)}, u32[]{:S(2)}, u32[]{:S(2)}) collective-permute-start(bf16[64,8192]{1,0:T(8,128)(2,1)} %get-tuple-element.93), channel_id=1, source_target_pairs={{0,4},{2,6},{4,8},{6,10},{8,12},{10,14},{12,16},{14,18},{16,20},{1... | collective-permute-start | bytes 3145736 | tf_op jit(solution)/shard_map/ppermute | solution.py:598
  20.3 0.0 collective-permute-done.14.env_other
  20.3 5.1 %collective-permute-start.12 = (bf16[32,8192]{1,0:T(8,128)(2,1)S(1)}, bf16[32,8192]{1,0:T(8,128)(2,1)}, u32[]{:S(2)}, u32[]{:S(2)}) collective-permute-start(bf16[32,8192]{1,0:T(8,128)(2,1)S(1)} %get-tuple-element.94), channel_id=1, source_target_pairs={{0,6},{2,8},{4,10},{6,12},{8,14},{10,16},{12,18},{14,20},{16,22},{... | collective-permute-start | bytes 1572872 | tf_op jit(solution)/shard_map/ppermute | solution.py:598
  25.4 0.6 copy-done.9
  26.0 2.7 %collective-permute-start.13 = (bf16[16,8192]{1,0:T(8,128)(2,1)}, bf16[16,8192]{1,0:T(8,128)(2,1)S(1)}, u32[]{:S(2)}, u32[]{:S(2)}) collective-permute-start(bf16[16,8192]{1,0:T(8,128)(2,1)} %get-tuple-element.95), channel_id=1, source_target_pairs={{0,8},{2,10},{4,12},{6,14},{8,16},{10,18},{12,20},{14,22},{16,24},... | collective-permute-start | bytes 786440 | tf_op jit(solution)/shard_map/ppermute | solution.py:598
  28.7 0.0 collective-permute-done.16.other_ref
  28.7 43.5 %snp_side.1.rest_9_ = bf16[8192,1280]{1,0:T(8,128)(2,1)} custom-call(s32[1]{0:T(128)} %bitcast.3.core_ref, f32[1,4096]{1,0:T(1,128)} %bitcast.16, f32[1,4096]{1,0:T(1,128)} %copy-done.10, f32[8,512]{1,0:T(8,128)S(1)} %local_moments.1.sums_own, f32[8,512]{1,0:T(8,128)S(1)} %collective-permute-done.8.sums_other, s32[4,4096]{1,0:T(4,128)} %shuf_own.1, ...), custom_call_target="tpu_custom_call" | custom-call | flops 40000000000 | bytes 60000000 | tf_op jit(solution)/shard_map/snp_side/pallas_call | solution.py:226
  72.2 0.0 collective-permute-done.12.rest_3_
  72.3 0.0 collective-permute-done.10.rest_1_
  72.3 0.1 collective-permute-start.17
  72.4 0.5 collective-permute-start.18
  72.8 0.1 collective-permute-start.19
  72.9 0.4 collective-permute-start.20
  73.4 4.4 %collective-permute-done.20.rest_8_ = bf16[16,8192]{1,0:T(8,128)(2,1)} collective-permute-done((bf16[16,8192]{1,0:T(8,128)(2,1)S(1)}, bf16[16,8192]{1,0:T(8,128)(2,1)}, u32[]{:S(2)}, u32[]{:S(2)}) %collective-permute-start.20) | collective-permute-done | bytes 262176 | tf_op jit(solution)/shard_map/ppermute | solution.py:26
  77.8 0.0 collective-permute-done.19.rest_7_
  77.8 0.0 collective-permute-done.17.rest_5_
  77.8 0.0 collective-permute-done.18.rest_6_
  77.8 18.3 %products.2 = (f32[32,8,128]{2,1,0:T(8,128)}, f32[8,64]{1,0:T(8,128)S(1)}) custom-call(s32[2]{0:T(128)S(1)} %pad_add_fusion.pos_ref, f32[8,512]{1,0:T(8,128)S(1)} %local_moments.1.sums_own, f32[8,512]{1,0:T(8,128)S(1)} %collective-permute-done.8.sums_other, s32[3,16,64]{2,1,0:T(8,128)S(1)} %get-tuple-element.90.plan_ref, ...), custom_call_target="tpu_custom_call" | custom-call | flops 8724152320 | bytes 27787264 | tf_op jit(solution)/shard_map/products/pallas_call | solution.py:517
  96.1 0.6 copy-done
  96.7 0.7 while.10
  97.4 11.5 %all_to_all.5.gathered_ref = f32[32,8,128]{2,1,0:T(8,128)} all-to-all(f32[32,8,128]{2,1,0:T(8,128)} %get-tuple-element.104), channel_id=1, replica_groups=mesh['genome'=16,'sample'=2] {'genome','sample'}, dimensions={0} | all-to-all | bytes 262144 | tf_op jit(solution)/shard_map/all_to_all | solution.py:625
  108.9 1.5 %finish.1 = f32[5,64]{1,0:T(8,128)} custom-call(f32[32,8,128]{2,1,0:T(8,128)} %all_to_all.5.gathered_ref, f32[8,64]{1,0:T(8,128)} %copy-done), custom_call_target="tpu_custom_call" | custom-call | tf_op jit(solution)/shard_map/finish/pallas_call | solution.py:626
  (20 shorter events, 0.0 us)
Async XLA Ops:
  0.0 2.2 %collective-permute-start.9 = (bf16[64,4096]{1,0:T(8,128)(2,1)}, bf16[64,4096]{1,0:T(8,128)(2,1)S(1)}, u32[]{:S(2)}, u32[]{:S(2)}) collective-permute-start(bf16[64,4096]{1,0:T(8,128)(2,1)} %own_ref.2), channel_id=1, source_target_pairs={{0,1},{1,0},{2,3},{3,2},{4,5},{5,4},{6,7},{7,6},{8,9},{9,8},{10,11... | collective-permute-start | bytes 1572872 | tf_op jit(solution)/shard_map/ppermute | solution.py:26
  2.2 5.8 %copy-start.2 = (bf16[64,4096]{1,0:T(8,128)(2,1)}, bf16[64,4096]{1,0:T(8,128)(2,1)S(1)}, u32[]{:S(2)}) copy-start(bf16[64,4096]{1,0:T(8,128)(2,1)S(1)} %collective-permute-done.9.other_ref) | copy-start | bytes 1572868
  2.2 26.5 %collective-permute-start.16 = (bf16[512,4096]{1,0:T(8,128)(2,1)}, bf16[512,4096]{1,0:T(8,128)(2,1)}, u32[]{:S(2)}, u32[]{:S(2)}) collective-permute-start(bf16[512,4096]{1,0:T(8,128)(2,1)} %own_ref.3), channel_id=1, source_target_pairs={{0,1},{1,0},{2,3},{3,2},{4,5},{5,4},{6,7},{7,6},{8,9},{9,8},{10,11... | collective-permute-start | bytes 12582920 | tf_op jit(solution)/shard_map/ppermute | solution.py:26
  2.6 5.2 %copy-start.8 = (s32[4,4096]{1,0:T(4,128)S(1)}, s32[4,4096]{1,0:T(4,128)}, u32[]{:S(2)}) copy-start(s32[4,4096]{1,0:T(4,128)} %shuf_own.1) | copy-start | bytes 196612
  2.6 5.4 %copy-start.1 = (bf16[64,4096]{1,0:T(8,128)(2,1)S(1)}, bf16[64,4096]{1,0:T(8,128)(2,1)}, u32[]{:S(2)}) copy-start(bf16[64,4096]{1,0:T(8,128)(2,1)} %own_ref.2) | copy-start | bytes 1572868
  2.6 5.4 %copy-start.5 = (s32[1024]{0:T(1024)S(1)}, s32[1024]{0:T(1024)}, u32[]{:S(2)}) copy-start(s32[1024]{0:T(1024)} %param.13) | copy-start | bytes 12292
  2.6 5.4 %copy-start.6 = (s32[1024]{0:T(1024)S(1)}, s32[1024]{0:T(1024)}, u32[]{:S(2)}) copy-start(s32[1024]{0:T(1024)} %param.14) | copy-start | bytes 12292
  2.6 5.4 %copy-start.7 = (s32[15]{0:T(128)S(1)}, s32[15]{0:T(128)}, u32[]{:S(2)}) copy-start(s32[15]{0:T(128)} %bounds_ref.1) | copy-start | bytes 184
  2.6 17.7 %collective-permute-start.14 = (f32[1,4096]{1,0:T(1,128)}, f32[1,4096]{1,0:T(1,128)S(1)}, u32[]{:S(2)}, u32[]{:S(2)}) collective-permute-start(f32[1,4096]{1,0:T(1,128)} %bitcast.14), channel_id=1, source_target_pairs={{0,1},{1,0},{2,3},{3,2},{4,5},{5,4},{6,7},{7,6},{8,9},{9,8},{10,11... | collective-permute-start | bytes 49160 | tf_op jit(solution)/shard_map/ppermute | solution.py:26
  7.3 9.5 %collective-permute-start.8 = (f32[8,512]{1,0:T(8,128)S(1)}, f32[8,512]{1,0:T(8,128)S(1)}, u32[]{:S(2)}, u32[]{:S(2)}) collective-permute-start(f32[8,512]{1,0:T(8,128)S(1)} %local_moments.1.sums_own), channel_id=1, source_target_pairs={{0,1},{1,0},{2,3},{3,2},{4,5},{5,4},{6,7},{7,6},{8,9},{9,8},{10,11... | collective-permute-start | bytes 49160 | tf_op jit(solution)/shard_map/ppermute | solution.py:26
  7.8 17.6 %collective-permute-start.15 = (s32[4,4096]{1,0:T(4,128)S(1)}, s32[4,4096]{1,0:T(4,128)S(1)}, u32[]{:S(2)}, u32[]{:S(2)}) collective-permute-start(s32[4,4096]{1,0:T(4,128)S(1)} %copy-done.8), channel_id=1, source_target_pairs={{0,1},{1,0},{2,3},{3,2},{4,5},{5,4},{6,7},{7,6},{8,9},{9,8},{10,11... | collective-permute-start | bytes 196616 | tf_op jit(solution)/shard_map/ppermute | solution.py:26
  12.0 60.3 %collective-permute-start.10 = (bf16[64,8192]{1,0:T(8,128)(2,1)}, bf16[64,8192]{1,0:T(8,128)(2,1)S(1)}, u32[]{:S(2)}, u32[]{:S(2)}) collective-permute-start(bf16[64,8192]{1,0:T(8,128)(2,1)} %get-tuple-element.92), channel_id=1, source_target_pairs={{0,2},{2,4},{4,6},{6,8},{8,10},{10,12},{12,14},{14,16},{16,18},{18... | collective-permute-start | bytes 3145736 | tf_op jit(solution)/shard_map/ppermute | solution.py:598
  16.8 55.4 %collective-permute-start.11 = (bf16[64,8192]{1,0:T(8,128)(2,1)}, bf16[64,8192]{1,0:T(8,128)(2,1)S(1)}, u32[]{:S(2)}, u32[]{:S(2)}) collective-permute-start(bf16[64,8192]{1,0:T(8,128)(2,1)} %get-tuple-element.93), channel_id=1, source_target_pairs={{0,4},{2,6},{4,8},{6,10},{8,12},{10,14},{12,16},{14,18},{16,20},{1... | collective-permute-start | bytes 3145736 | tf_op jit(solution)/shard_map/ppermute | solution.py:598
  20.3 5.1 %copy-start.10 = (f32[1,4096]{1,0:T(1,128)}, f32[1,4096]{1,0:T(1,128)S(1)}, u32[]{:S(2)}) copy-start(f32[1,4096]{1,0:T(1,128)S(1)} %collective-permute-done.14.env_other) | copy-start | bytes 49156
  20.3 52.0 %collective-permute-start.12 = (bf16[32,8192]{1,0:T(8,128)(2,1)S(1)}, bf16[32,8192]{1,0:T(8,128)(2,1)}, u32[]{:S(2)}, u32[]{:S(2)}) collective-permute-start(bf16[32,8192]{1,0:T(8,128)(2,1)S(1)} %get-tuple-element.94), channel_id=1, source_target_pairs={{0,6},{2,8},{4,10},{6,12},{8,14},{10,16},{12,18},{14,20},{16,22},{... | collective-permute-start | bytes 1572872 | tf_op jit(solution)/shard_map/ppermute | solution.py:598
  25.4 0.6 copy-start.9
  26.0 46.2 %collective-permute-start.13 = (bf16[16,8192]{1,0:T(8,128)(2,1)}, bf16[16,8192]{1,0:T(8,128)(2,1)S(1)}, u32[]{:S(2)}, u32[]{:S(2)}) collective-permute-start(bf16[16,8192]{1,0:T(8,128)(2,1)} %get-tuple-element.95), channel_id=1, source_target_pairs={{0,8},{2,10},{4,12},{6,14},{8,16},{10,18},{12,20},{14,22},{16,24},... | collective-permute-start | bytes 786440 | tf_op jit(solution)/shard_map/ppermute | solution.py:598
  72.3 5.5 %collective-permute-start.17 = (bf16[64,8192]{1,0:T(8,128)(2,1)S(1)}, bf16[64,8192]{1,0:T(8,128)(2,1)}, u32[]{:S(2)}, u32[]{:S(2)}) collective-permute-start(bf16[64,8192]{1,0:T(8,128)(2,1)S(1)} %collective-permute-done.10.rest_1_), channel_id=1, source_target_pairs={{0,1},{1,0},{2,3},{3,2},{4,5},{5,4},{6,7},{7,6},{8,9},{9,8},{10,11... | collective-permute-start | bytes 3145736 | tf_op jit(solution)/shard_map/ppermute | solution.py:26
  72.4 5.4 %collective-permute-start.18 = (bf16[64,8192]{1,0:T(8,128)(2,1)S(1)}, bf16[64,8192]{1,0:T(8,128)(2,1)}, u32[]{:S(2)}, u32[]{:S(2)}) collective-permute-start(bf16[64,8192]{1,0:T(8,128)(2,1)S(1)} %collective-permute-done.11.rest_2_), channel_id=1, source_target_pairs={{0,1},{1,0},{2,3},{3,2},{4,5},{5,4},{6,7},{7,6},{8,9},{9,8},{10,11... | collective-permute-start | bytes 3145736 | tf_op jit(solution)/shard_map/ppermute | solution.py:26
  72.8 4.9 %collective-permute-start.19 = (bf16[32,8192]{1,0:T(8,128)(2,1)}, bf16[32,8192]{1,0:T(8,128)(2,1)}, u32[]{:S(2)}, u32[]{:S(2)}) collective-permute-start(bf16[32,8192]{1,0:T(8,128)(2,1)} %collective-permute-done.12.rest_3_), channel_id=1, source_target_pairs={{0,1},{1,0},{2,3},{3,2},{4,5},{5,4},{6,7},{7,6},{8,9},{9,8},{10,11... | collective-permute-start | bytes 1572872 | tf_op jit(solution)/shard_map/ppermute | solution.py:26
  72.9 4.8 %collective-permute-start.20 = (bf16[16,8192]{1,0:T(8,128)(2,1)S(1)}, bf16[16,8192]{1,0:T(8,128)(2,1)}, u32[]{:S(2)}, u32[]{:S(2)}) collective-permute-start(bf16[16,8192]{1,0:T(8,128)(2,1)S(1)} %collective-permute-done.13.rest_4_), channel_id=1, source_target_pairs={{0,1},{1,0},{2,3},{3,2},{4,5},{5,4},{6,7},{7,6},{8,9},{9,8},{10,11... | collective-permute-start | bytes 786440 | tf_op jit(solution)/shard_map/ppermute | solution.py:26
  96.1 0.6 copy-start

commit v6 on v5

--- a/solution.py
+++ b/solution.py
@@ -11,6 +11,7 @@
 HALF_BLK = 7
 LANES = 128
 ROWS_STEP = 16
+UNROLL = 32
 CHUNK = 1024
 MIB = 2**20
 
@@ -82,7 +83,7 @@
 def snp_side_kernel(
     core_ref, env_own, env_other, sums_own, sums_other, shuf_own, shuf_other, own_ref, other_ref,
     out_ref,
-    idx, geno, env, even, odd, dests, stage, first_stage, slope,
+    idx, geno, env, even, dests, stage, first_stage, slope,
     idx_sems, in_sems, out_sems, first_sems,
     *, labels,
 ):
@@ -161,14 +162,18 @@
         first_stage[pl.ds(pl.multiple_of(b * side, side), side), :] = kept.astype(jnp.bfloat16)
 
     def scatter(b, held):
-        first = pl.multiple_of(b * side, side)
-        for u in range(side):
-            row = held[u]
+        def group(i, carry):
+            low = pl.multiple_of(i * UNROLL, UNROLL)
+            first = pl.multiple_of(b * side + low, UNROLL)
+            rows = [held[low + u] for u in range(UNROLL)]
             for q in range(labels):
-                dests[q][idx[q * all_samples + first + u]] = row
+                for u in range(UNROLL):
+                    dests[q][idx[q * all_samples + first + u]] = rows[u]
+            return carry
+
+        lax.fori_loop(0, side // UNROLL, group, 0)
 
     load(0).wait()
-    turn(0, even)
     for q in range(labels):
         for h in range(2):
             load_idx(q, h).wait()
@@ -180,15 +185,13 @@
             def _(k=k):
                 load(k).wait()
 
-    def pair(i, carry):
-        arrive(2 * i + 2)
-        scatter(2 * i, even)
-        turn(2 * i + 1, odd)
-        scatter(2 * i + 1, odd)
-        turn(jnp.minimum(2 * i + 2, blocks - 1), even)
+    def one(b, carry):
+        arrive(b)
+        turn(b, even)
+        scatter(b, even)
         return carry
 
-    lax.fori_loop(0, blocks // 2, pair, 0)
+    lax.fori_loop(0, blocks, one, 0)
     for h in range(2):
         save_first(h).start()
 
@@ -232,7 +235,6 @@
             pltpu.SMEM((labels * all_samples,), jnp.int32),
             pltpu.VMEM((all_samples // CHUNK, snp_rows, CHUNK), jnp.bfloat16),
             pltpu.VMEM((1, all_samples), jnp.float32),
-            pltpu.VMEM((side, words, LANES), jnp.float32),
             pltpu.VMEM((side, words, LANES), jnp.float32),
             [pltpu.VMEM((all_samples, words, LANES), jnp.float32) for _ in range(labels)],
             pltpu.VMEM((2, CHUNK, snp_rows), jnp.bfloat16),

time: 111 us -> 109 us (0.982)
  Pallas kernels: 71.8 us -> 70.4 us
    pallas_call x1, Pallas kernels: 43.5 us -> 42.1 us  [snp_side(): pl.pallas_call(functools.partial(snp_side_kernel, labels=labels), out_sha...]
  transfers between devices with their start and end apart: 13 -> 13, of which waited for: 2 -> 2; matrix products, arithmetic and copies ran while one was open for 0% -> 0% of each run, Pallas kernels for 47% -> 46%
where the time goes in v6:
time: 109 us
  Pallas kernels  70.4 us (65%)
  starting transfers between devices  18.7 us (17%)
  blocking collectives  11.5 us (11%)
  waiting for transfers between devices  6.17 us (6%)
  local copies, waits for them, and re-layouts  1.25 us (1%)
    pallas_call x1, Pallas kernels, snp_side(): pl.pallas_call(functools.partial(snp_side_kernel, labels=labels), out_sha...  42.1 us
    pallas_call x1, Pallas kernels, products(): pl.pallas_call(functools.partial(product_kernel, caps=caps, labels=labels...  18.3 us
    ppermute x4, starting transfers between devices, travel(): mine.append(lax.ppermute(payload, ('genome', 'sample'), pairs))  16 us
    all_to_all x1, blocking collectives, shards(): gathered = lax.all_to_all(found, ('genome', 'sample'), 0, 0, tiled=True)  11.5 us
    ppermute x9, waiting for transfers between devices, swapped(): lax.ppermute(x, 'sample', [(i, (i + 1) % count) for i in range(count)])  6.16 us
    pallas_call x1, Pallas kernels, local_moments(): pl.pallas_call(moments_kernel, grid=(half // chunk,), out_shape=jax.Shape...  4.52 us
    pallas_call x1, Pallas kernels, select(): pl.pallas_call(functools.partial(select_kernel, caps=caps, blocks_dev=blo...  3.98 us
    ppermute x9, starting transfers between devices, swapped(): lax.ppermute(x, 'sample', [(i, (i + 1) % count) for i in range(count)])  2.68 us
  transfers between devices with their start and end apart: 13, of which 2 were waited for; matrix products, arithmetic and copies ran while one was open for 0% of the time, Pallas kernels for 46%

profile of v6, /device:TPU:0, one launch (start us, length us, event | category | flops | bytes accessed | tf_op | source)
XLA Modules:
  0.0 108.9 jit_solution(3406612808492380336)
XLA Ops:
  0.0 0.5 collective-permute-start.9
  0.5 1.7 %collective-permute-done.9.other_ref = bf16[64,4096]{1,0:T(8,128)(2,1)S(1)} collective-permute-done((bf16[64,4096]{1,0:T(8,128)(2,1)}, bf16[64,4096]{1,0:T(8,128)(2,1)S(1)}, u32[]{:S(2)}, u32[]{:S(2)}) %collective-permute-start.9) | collective-permute-done | bytes 524320 | tf_op jit(solution)/shard_map/ppermute | solution.py:27
  2.2 0.4 collective-permute-start.16
  2.6 0.2 collective-permute-start.14
  2.8 4.5 %local_moments.1.sums_own = f32[8,512]{1,0:T(8,128)S(1)} custom-call(bf16[512,4096]{1,0:T(8,128)(2,1)} %own_ref.3, f32[1,4096]{1,0:T(1,128)} %bitcast.15), custom_call_target="tpu_custom_call" | custom-call | flops 5000000000 | bytes 4194304 | tf_op jit(solution)/shard_map/local_moments/pallas_call | solution.py:65
  7.3 0.4 collective-permute-start.8
  7.8 0.1 collective-permute-start.15
  7.9 0.1 pad_add_fusion.pos_ref
  8.0 4.0 %select.2 = (s32[1]{0:T(128)}, s32[3,16,64]{2,1,0:T(8,128)S(1)}, bf16[64,8192]{1,0:T(8,128)(2,1)S(1)}, bf16[64,8192]{1,0:T(8,128)(2,1)}, bf16[64,8192]{1,0:T(8,1...) custom-call(s32[1]{0:T(128)} %constant.13.clone.1.round_ref, s32[2]{0:T(128)S(1)} %pad_add_fusion.pos_ref, ...), custom_call_target="tpu_custom_call" | custom-call | tf_op jit(solution)/shard_map/select/pallas_call | solution.py:369
  12.0 4.8 %collective-permute-start.10 = (bf16[64,8192]{1,0:T(8,128)(2,1)}, bf16[64,8192]{1,0:T(8,128)(2,1)S(1)}, u32[]{:S(2)}, u32[]{:S(2)}) collective-permute-start(bf16[64,8192]{1,0:T(8,128)(2,1)} %get-tuple-element.92), channel_id=1, source_target_pairs={{0,2},{2,4},{4,6},{6,8},{8,10},{10,12},{12,14},{14,16},{16,18},{18... | collective-permute-start | bytes 3145736 | tf_op jit(solution)/shard_map/ppermute | solution.py:600
  16.8 0.0 collective-permute-done.8.sums_other
  16.8 3.4 %collective-permute-start.11 = (bf16[64,8192]{1,0:T(8,128)(2,1)}, bf16[64,8192]{1,0:T(8,128)(2,1)S(1)}, u32[]{:S(2)}, u32[]{:S(2)}) collective-permute-start(bf16[64,8192]{1,0:T(8,128)(2,1)} %get-tuple-element.93), channel_id=1, source_target_pairs={{0,4},{2,6},{4,8},{6,10},{8,12},{10,14},{12,16},{14,18},{16,20},{1... | collective-permute-start | bytes 3145736 | tf_op jit(solution)/shard_map/ppermute | solution.py:600
  20.3 0.0 collective-permute-done.14.env_other
  20.3 5.1 %collective-permute-start.12 = (bf16[32,8192]{1,0:T(8,128)(2,1)S(1)}, bf16[32,8192]{1,0:T(8,128)(2,1)}, u32[]{:S(2)}, u32[]{:S(2)}) collective-permute-start(bf16[32,8192]{1,0:T(8,128)(2,1)S(1)} %get-tuple-element.94), channel_id=1, source_target_pairs={{0,6},{2,8},{4,10},{6,12},{8,14},{10,16},{12,18},{14,20},{16,22},{... | collective-permute-start | bytes 1572872 | tf_op jit(solution)/shard_map/ppermute | solution.py:600
  25.4 0.0 collective-permute-done.15.shuf_other
  25.4 0.6 copy-done.9
  26.0 2.7 %collective-permute-start.13 = (bf16[16,8192]{1,0:T(8,128)(2,1)}, bf16[16,8192]{1,0:T(8,128)(2,1)S(1)}, u32[]{:S(2)}, u32[]{:S(2)}) collective-permute-start(bf16[16,8192]{1,0:T(8,128)(2,1)} %get-tuple-element.95), channel_id=1, source_target_pairs={{0,8},{2,10},{4,12},{6,14},{8,16},{10,18},{12,20},{14,22},{16,24},... | collective-permute-start | bytes 786440 | tf_op jit(solution)/shard_map/ppermute | solution.py:600
  28.7 0.0 collective-permute-done.16.other_ref
  28.7 42.1 %snp_side.1.rest_9_ = bf16[8192,1280]{1,0:T(8,128)(2,1)} custom-call(s32[1]{0:T(128)} %bitcast.3.core_ref, f32[1,4096]{1,0:T(1,128)} %bitcast.16, f32[1,4096]{1,0:T(1,128)} %copy-done.10, f32[8,512]{1,0:T(8,128)S(1)} %local_moments.1.sums_own, f32[8,512]{1,0:T(8,128)S(1)} %collective-permute-done.8.sums_other, s32[4,4096]{1,0:T(4,128)} %shuf_own.1, ...), custom_call_target="tpu_custom_call" | custom-call | flops 40000000000 | bytes 60000000 | tf_op jit(solution)/shard_map/snp_side/pallas_call | solution.py:229
  70.8 0.0 collective-permute-done.12.rest_3_
  70.8 0.0 collective-permute-done.10.rest_1_
  70.8 0.1 collective-permute-start.17
  70.9 0.5 collective-permute-start.18
  71.4 0.1 collective-permute-start.19
  71.5 0.4 collective-permute-start.20
  71.9 4.4 %collective-permute-done.20.rest_8_ = bf16[16,8192]{1,0:T(8,128)(2,1)} collective-permute-done((bf16[16,8192]{1,0:T(8,128)(2,1)S(1)}, bf16[16,8192]{1,0:T(8,128)(2,1)}, u32[]{:S(2)}, u32[]{:S(2)}) %collective-permute-start.20) | collective-permute-done | bytes 262176 | tf_op jit(solution)/shard_map/ppermute | solution.py:27
  76.3 0.0 collective-permute-done.19.rest_7_
  76.3 18.3 %products.2 = (f32[32,8,128]{2,1,0:T(8,128)}, f32[8,64]{1,0:T(8,128)S(1)}) custom-call(s32[2]{0:T(128)S(1)} %pad_add_fusion.pos_ref, f32[8,512]{1,0:T(8,128)S(1)} %local_moments.1.sums_own, f32[8,512]{1,0:T(8,128)S(1)} %collective-permute-done.8.sums_other, s32[3,16,64]{2,1,0:T(8,128)S(1)} %get-tuple-element.90.plan_ref, ...), custom_call_target="tpu_custom_call" | custom-call | flops 8724152320 | bytes 27787264 | tf_op jit(solution)/shard_map/products/pallas_call | solution.py:519
  94.7 0.6 copy-done
  95.3 0.6 while.10
  95.8 11.5 %all_to_all.5.gathered_ref = f32[32,8,128]{2,1,0:T(8,128)} all-to-all(f32[32,8,128]{2,1,0:T(8,128)} %get-tuple-element.104), channel_id=1, replica_groups=mesh['genome'=16,'sample'=2] {'genome','sample'}, dimensions={0} | all-to-all | bytes 262144 | tf_op jit(solution)/shard_map/all_to_all | solution.py:627
  107.3 1.5 %finish.1 = f32[5,64]{1,0:T(8,128)} custom-call(f32[32,8,128]{2,1,0:T(8,128)} %all_to_all.5.gathered_ref, f32[8,64]{1,0:T(8,128)} %copy-done), custom_call_target="tpu_custom_call" | custom-call | tf_op jit(solution)/shard_map/finish/pallas_call | solution.py:628
  (20 shorter events, 0.0 us)
Async XLA Ops:
  0.0 2.2 %collective-permute-start.9 = (bf16[64,4096]{1,0:T(8,128)(2,1)}, bf16[64,4096]{1,0:T(8,128)(2,1)S(1)}, u32[]{:S(2)}, u32[]{:S(2)}) collective-permute-start(bf16[64,4096]{1,0:T(8,128)(2,1)} %own_ref.2), channel_id=1, source_target_pairs={{0,1},{1,0},{2,3},{3,2},{4,5},{5,4},{6,7},{7,6},{8,9},{9,8},{10,11... | collective-permute-start | bytes 1572872 | tf_op jit(solution)/shard_map/ppermute | solution.py:27
  2.2 5.8 %copy-start.2 = (bf16[64,4096]{1,0:T(8,128)(2,1)}, bf16[64,4096]{1,0:T(8,128)(2,1)S(1)}, u32[]{:S(2)}) copy-start(bf16[64,4096]{1,0:T(8,128)(2,1)S(1)} %collective-permute-done.9.other_ref) | copy-start | bytes 1572868
  2.2 26.5 %collective-permute-start.16 = (bf16[512,4096]{1,0:T(8,128)(2,1)}, bf16[512,4096]{1,0:T(8,128)(2,1)}, u32[]{:S(2)}, u32[]{:S(2)}) collective-permute-start(bf16[512,4096]{1,0:T(8,128)(2,1)} %own_ref.3), channel_id=1, source_target_pairs={{0,1},{1,0},{2,3},{3,2},{4,5},{5,4},{6,7},{7,6},{8,9},{9,8},{10,11... | collective-permute-start | bytes 12582920 | tf_op jit(solution)/shard_map/ppermute | solution.py:27
  2.6 5.2 %copy-start.8 = (s32[4,4096]{1,0:T(4,128)S(1)}, s32[4,4096]{1,0:T(4,128)}, u32[]{:S(2)}) copy-start(s32[4,4096]{1,0:T(4,128)} %shuf_own.1) | copy-start | bytes 196612
  2.6 5.4 %copy-start.1 = (bf16[64,4096]{1,0:T(8,128)(2,1)S(1)}, bf16[64,4096]{1,0:T(8,128)(2,1)}, u32[]{:S(2)}) copy-start(bf16[64,4096]{1,0:T(8,128)(2,1)} %own_ref.2) | copy-start | bytes 1572868
  2.6 5.4 %copy-start.5 = (s32[1024]{0:T(1024)S(1)}, s32[1024]{0:T(1024)}, u32[]{:S(2)}) copy-start(s32[1024]{0:T(1024)} %param.13) | copy-start | bytes 12292
  2.6 5.4 %copy-start.6 = (s32[1024]{0:T(1024)S(1)}, s32[1024]{0:T(1024)}, u32[]{:S(2)}) copy-start(s32[1024]{0:T(1024)} %param.14) | copy-start | bytes 12292
  2.6 5.4 %copy-start.7 = (s32[15]{0:T(128)S(1)}, s32[15]{0:T(128)}, u32[]{:S(2)}) copy-start(s32[15]{0:T(128)} %bounds_ref.1) | copy-start | bytes 184
  2.6 17.7 %collective-permute-start.14 = (f32[1,4096]{1,0:T(1,128)}, f32[1,4096]{1,0:T(1,128)S(1)}, u32[]{:S(2)}, u32[]{:S(2)}) collective-permute-start(f32[1,4096]{1,0:T(1,128)} %bitcast.14), channel_id=1, source_target_pairs={{0,1},{1,0},{2,3},{3,2},{4,5},{5,4},{6,7},{7,6},{8,9},{9,8},{10,11... | collective-permute-start | bytes 49160 | tf_op jit(solution)/shard_map/ppermute | solution.py:27
  7.3 9.5 %collective-permute-start.8 = (f32[8,512]{1,0:T(8,128)S(1)}, f32[8,512]{1,0:T(8,128)S(1)}, u32[]{:S(2)}, u32[]{:S(2)}) collective-permute-start(f32[8,512]{1,0:T(8,128)S(1)} %local_moments.1.sums_own), channel_id=1, source_target_pairs={{0,1},{1,0},{2,3},{3,2},{4,5},{5,4},{6,7},{7,6},{8,9},{9,8},{10,11... | collective-permute-start | bytes 49160 | tf_op jit(solution)/shard_map/ppermute | solution.py:27
  7.8 17.6 %collective-permute-start.15 = (s32[4,4096]{1,0:T(4,128)S(1)}, s32[4,4096]{1,0:T(4,128)S(1)}, u32[]{:S(2)}, u32[]{:S(2)}) collective-permute-start(s32[4,4096]{1,0:T(4,128)S(1)} %copy-done.8), channel_id=1, source_target_pairs={{0,1},{1,0},{2,3},{3,2},{4,5},{5,4},{6,7},{7,6},{8,9},{9,8},{10,11... | collective-permute-start | bytes 196616 | tf_op jit(solution)/shard_map/ppermute | solution.py:27
  12.0 58.8 %collective-permute-start.10 = (bf16[64,8192]{1,0:T(8,128)(2,1)}, bf16[64,8192]{1,0:T(8,128)(2,1)S(1)}, u32[]{:S(2)}, u32[]{:S(2)}) collective-permute-start(bf16[64,8192]{1,0:T(8,128)(2,1)} %get-tuple-element.92), channel_id=1, source_target_pairs={{0,2},{2,4},{4,6},{6,8},{8,10},{10,12},{12,14},{14,16},{16,18},{18... | collective-permute-start | bytes 3145736 | tf_op jit(solution)/shard_map/ppermute | solution.py:600
  16.8 54.0 %collective-permute-start.11 = (bf16[64,8192]{1,0:T(8,128)(2,1)}, bf16[64,8192]{1,0:T(8,128)(2,1)S(1)}, u32[]{:S(2)}, u32[]{:S(2)}) collective-permute-start(bf16[64,8192]{1,0:T(8,128)(2,1)} %get-tuple-element.93), channel_id=1, source_target_pairs={{0,4},{2,6},{4,8},{6,10},{8,12},{10,14},{12,16},{14,18},{16,20},{1... | collective-permute-start | bytes 3145736 | tf_op jit(solution)/shard_map/ppermute | solution.py:600
  20.3 5.1 %copy-start.10 = (f32[1,4096]{1,0:T(1,128)}, f32[1,4096]{1,0:T(1,128)S(1)}, u32[]{:S(2)}) copy-start(f32[1,4096]{1,0:T(1,128)S(1)} %collective-permute-done.14.env_other) | copy-start | bytes 49156
  20.3 50.5 %collective-permute-start.12 = (bf16[32,8192]{1,0:T(8,128)(2,1)S(1)}, bf16[32,8192]{1,0:T(8,128)(2,1)}, u32[]{:S(2)}, u32[]{:S(2)}) collective-permute-start(bf16[32,8192]{1,0:T(8,128)(2,1)S(1)} %get-tuple-element.94), channel_id=1, source_target_pairs={{0,6},{2,8},{4,10},{6,12},{8,14},{10,16},{12,18},{14,20},{16,22},{... | collective-permute-start | bytes 1572872 | tf_op jit(solution)/shard_map/ppermute | solution.py:600
  25.4 0.6 copy-start.9
  26.0 44.8 %collective-permute-start.13 = (bf16[16,8192]{1,0:T(8,128)(2,1)}, bf16[16,8192]{1,0:T(8,128)(2,1)S(1)}, u32[]{:S(2)}, u32[]{:S(2)}) collective-permute-start(bf16[16,8192]{1,0:T(8,128)(2,1)} %get-tuple-element.95), channel_id=1, source_target_pairs={{0,8},{2,10},{4,12},{6,14},{8,16},{10,18},{12,20},{14,22},{16,24},... | collective-permute-start | bytes 786440 | tf_op jit(solution)/shard_map/ppermute | solution.py:600
  70.8 5.5 %collective-permute-start.17 = (bf16[64,8192]{1,0:T(8,128)(2,1)S(1)}, bf16[64,8192]{1,0:T(8,128)(2,1)}, u32[]{:S(2)}, u32[]{:S(2)}) collective-permute-start(bf16[64,8192]{1,0:T(8,128)(2,1)S(1)} %collective-permute-done.10.rest_1_), channel_id=1, source_target_pairs={{0,1},{1,0},{2,3},{3,2},{4,5},{5,4},{6,7},{7,6},{8,9},{9,8},{10,11... | collective-permute-start | bytes 3145736 | tf_op jit(solution)/shard_map/ppermute | solution.py:27
  70.9 5.4 %collective-permute-start.18 = (bf16[64,8192]{1,0:T(8,128)(2,1)S(1)}, bf16[64,8192]{1,0:T(8,128)(2,1)}, u32[]{:S(2)}, u32[]{:S(2)}) collective-permute-start(bf16[64,8192]{1,0:T(8,128)(2,1)S(1)} %collective-permute-done.11.rest_2_), channel_id=1, source_target_pairs={{0,1},{1,0},{2,3},{3,2},{4,5},{5,4},{6,7},{7,6},{8,9},{9,8},{10,11... | collective-permute-start | bytes 3145736 | tf_op jit(solution)/shard_map/ppermute | solution.py:27
  71.4 4.9 %collective-permute-start.19 = (bf16[32,8192]{1,0:T(8,128)(2,1)}, bf16[32,8192]{1,0:T(8,128)(2,1)}, u32[]{:S(2)}, u32[]{:S(2)}) collective-permute-start(bf16[32,8192]{1,0:T(8,128)(2,1)} %collective-permute-done.12.rest_3_), channel_id=1, source_target_pairs={{0,1},{1,0},{2,3},{3,2},{4,5},{5,4},{6,7},{7,6},{8,9},{9,8},{10,11... | collective-permute-start | bytes 1572872 | tf_op jit(solution)/shard_map/ppermute | solution.py:27
  71.5 4.8 %collective-permute-start.20 = (bf16[16,8192]{1,0:T(8,128)(2,1)S(1)}, bf16[16,8192]{1,0:T(8,128)(2,1)}, u32[]{:S(2)}, u32[]{:S(2)}) collective-permute-start(bf16[16,8192]{1,0:T(8,128)(2,1)S(1)} %collective-permute-done.13.rest_4_), channel_id=1, source_target_pairs={{0,1},{1,0},{2,3},{3,2},{4,5},{5,4},{6,7},{7,6},{8,9},{9,8},{10,11... | collective-permute-start | bytes 786440 | tf_op jit(solution)/shard_map/ppermute | solution.py:27
  94.7 0.6 copy-start

commit v7 on v4

--- a/solution.py
+++ b/solution.py
@@ -12,6 +12,7 @@
 LANES = 128
 ROWS_STEP = 16
 UNROLL = 32
+SIDE = 2 * LANES
 CHUNK = 1024
 MIB = 2**20
 
@@ -80,43 +81,90 @@
     )(geno, env)
 
 
-def snp_side_kernel(
-    core_ref, env_own, env_other, sums_own, sums_other, shuf_own, shuf_other, own_ref, other_ref,
-    out_ref,
-    idx, geno, table, dest, stage, first_stage, slope, idx_sems, in_sems, out_sems, first_sems,
+def turned_kernel(geno_ref, env_ref, sums_own, sums_other, out_ref, slope):
+    snp_rows, chunk = geno_ref.shape
+
+    @pl.when(pl.program_id(0) == 0)
+    def _():
+        sums = sums_own[...] + sums_other[...]
+        slope[...] = jnp.broadcast_to(sums[1:2, :] / sums[0:1, :], (LANES, snp_rows)).T
+
+    unit = (
+        lax.broadcasted_iota(jnp.int32, (SIDE, SIDE), 0)
+        == lax.broadcasted_iota(jnp.int32, (SIDE, SIDE), 1)
+    ).astype(jnp.bfloat16)
+    for i in range(chunk // SIDE):
+        cols = pl.ds(i * SIDE, SIDE)
+        e = env_ref[:, cols]
+        for j in range(snp_rows // SIDE):
+            rows = pl.ds(j * SIDE, SIDE)
+            x = geno_ref[rows, cols].astype(jnp.float32)
+            r = slope[rows, :]
+            a = x * (e - jnp.concatenate([r] * (SIDE // LANES), axis=1))
+            t = lax.dot_general(
+                unit, a.astype(jnp.bfloat16), (((1,), (1,)), ((), ())),
+                preferred_element_type=jnp.float32,
+            )
+            out_ref[cols, rows] = t.astype(jnp.bfloat16)
+
+
+def turned(geno, env, sums):
+    snp_rows, half = geno.shape
+    return pl.pallas_call(
+        turned_kernel,
+        grid=(half // CHUNK,),
+        out_shape=jax.ShapeDtypeStruct((half, snp_rows), jnp.bfloat16),
+        in_specs=[
+            pl.BlockSpec((snp_rows, CHUNK), lambda k: (0, k)),
+            pl.BlockSpec((1, CHUNK), lambda k: (0, k)),
+            pl.BlockSpec((8, snp_rows), lambda k: (0, 0)),
+            pl.BlockSpec((8, snp_rows), lambda k: (0, 0)),
+        ],
+        out_specs=pl.BlockSpec((CHUNK, snp_rows), lambda k: (k, 0)),
+        scratch_shapes=[pltpu.VMEM((snp_rows, LANES), jnp.float32)],
+        compiler_params=pltpu.CompilerParams(vmem_limit_bytes=60 * MIB),
+        cost_estimate=pl.CostEstimate(
+            flops=5 * 10**9, bytes_accessed=4 * snp_rows * half, transcendentals=0
+        ),
+        name="turned",
+    )(geno, env, *sums)
+
+
+def permute_kernel(
+    core_ref, shuf_own, shuf_other, own_ref, other_ref, out_ref,
+    idx, source, rows, dests, stage, idx_sems, in_sems, out_sems, first_sems,
     *, labels,
 ):
-    snp_rows, half = own_ref.shape
+    half, snp_rows = own_ref.shape
     all_samples = 2 * half
     chunks = all_samples // CHUNK
     words = snp_rows // LANES
     slot = words | 1
     share = snp_rows // 2
-    side = 2 * LANES
     core = core_ref[0]
-    depth = geno.shape[0]
 
     def load(k):
-        source = own_ref if k * CHUNK < half else other_ref
+        ref = own_ref if k * CHUNK < half else other_ref
         return pltpu.make_async_copy(
-            source.at[:, pl.ds((k * CHUNK) % half, CHUNK)], geno.at[k % depth],
-            in_sems.at[k % depth],
+            ref.at[pl.ds((k * CHUNK) % half, CHUNK)], source.at[k], in_sems.at[k]
         )
 
     def load_idx(q, h):
-        source = shuf_own if h == 0 else shuf_other
+        ref = shuf_own if h == 0 else shuf_other
         return pltpu.make_async_copy(
-            source.at[core * labels + q],
+            ref.at[core * labels + q],
             idx.at[pl.ds(q * all_samples + h * half, half)],
             idx_sems.at[2 * q + h],
         )
 
     def save_first(k):
         there = jnp.where(core == 0, k * CHUNK, (k * CHUNK + half) % all_samples)
-        rows = pl.ds(pl.multiple_of(there, CHUNK), CHUNK)
         return pltpu.make_async_copy(
-            first_stage.at[k % 2], out_ref.at[rows, pl.ds(labels * snp_rows, share)],
-            first_sems.at[k % 2],
+            source.at[k, :, pl.ds(pl.multiple_of(core * share, share), share)],
+            out_ref.at[
+                pl.ds(pl.multiple_of(there, CHUNK), CHUNK), pl.ds(labels * snp_rows, share)
+            ],
+            first_sems.at[k],
         )
 
     def save(q, k):
@@ -126,118 +174,88 @@
             out_sems.at[k % 2],
         )
 
-    for k in range(depth):
+    for k in range(chunks):
         load(k).start()
     for q in range(labels):
         for h in range(2):
             load_idx(q, h).start()
-    sums = sums_own[...] + sums_other[...]
-    slope[...] = jnp.broadcast_to(sums[1:2, :] / sums[0:1, :], (LANES, snp_rows)).T
-    unit = (
-        lax.broadcasted_iota(jnp.int32, (side, side), 0)
-        == lax.broadcasted_iota(jnp.int32, (side, side), 1)
-    ).astype(jnp.bfloat16)
-
-    for k in range(chunks):
-        load(k).wait()
-        if k >= 2:
-            save_first(k - 2).wait()
-        env_ref = env_own if k * CHUNK < half else env_other
-
-        def turn(i, carry, k=k, env_ref=env_ref):
-            at = pl.multiple_of(i * side, side)
-            e = env_ref[:, pl.ds((k * CHUNK) % half + at, side)]
-            turned = []
-            for j in range(snp_rows // side):
-                rows = pl.ds(j * side, side)
-                x = geno[k % depth, rows, pl.ds(at, side)].astype(jnp.float32)
-                r = slope[rows, :]
-                a = x * (e - jnp.concatenate([r] * (side // LANES), axis=1))
-                t = lax.dot_general(
-                    unit, a.astype(jnp.bfloat16), (((1,), (1,)), ((), ())),
-                    preferred_element_type=jnp.float32,
-                )
-                for c in range(side // LANES):
-                    word = j * (side // LANES) + c
-                    table[pl.ds((k * CHUNK + at) * slot + word, side, stride=slot), :] = (
-                        t[:, c * LANES : (c + 1) * LANES]
-                    )
-                turned.append(t)
-            turned = jnp.concatenate(turned, axis=1)
-            kept = jnp.where(core == 0, turned[:, :share], turned[:, share:])
-            first_stage[k % 2, pl.ds(at, side), :] = kept.astype(jnp.bfloat16)
-            return carry
-
-        lax.fori_loop(0, CHUNK // side, turn, 0, unroll=2)
-        save_first(k).start()
-        if k + depth < chunks:
-            load(k + depth).start()
-
     for q in range(labels):
         for h in range(2):
             load_idx(q, h).wait()
-
-        def scatter(i, carry, q=q):
-            first = pl.multiple_of(i * UNROLL, UNROLL)
-            base = pl.multiple_of(first * slot, UNROLL * slot)
-            held = [table[pl.ds(base + u * slot, words), :] for u in range(UNROLL)]
-            for u in range(UNROLL):
-                to = idx[q * all_samples + first + u] * slot
-                dest[pl.ds(to, words), :] = held[u]
+    for k in range(chunks):
+        load(k).wait()
+        save_first(k).start()
+
+        def block(b, carry, k=k):
+            at = pl.multiple_of(b * SIDE, SIDE)
+            for c in range(words):
+                x = source[k, pl.ds(at, SIDE), pl.ds(c * LANES, LANES)]
+                rows[pl.ds(c, SIDE, stride=slot), :] = x.astype(jnp.float32)
+
+            def group(i, carry):
+                low = pl.multiple_of(i * UNROLL, UNROLL)
+                first = pl.multiple_of(k * CHUNK + at + low, UNROLL)
+                base = pl.multiple_of(low * slot, UNROLL * slot)
+                held = [rows[pl.ds(base + u * slot, words), :] for u in range(UNROLL)]
+                for q in range(labels):
+                    for u in range(UNROLL):
+                        to = idx[q * all_samples + first + u] * slot
+                        dests[q][pl.ds(to, words), :] = held[u]
+                return carry
+
+            lax.fori_loop(0, SIDE // UNROLL, group, 0)
             return carry
 
-        lax.fori_loop(0, all_samples // UNROLL, scatter, 0)
+        lax.fori_loop(0, CHUNK // SIDE, block, 0)
+
+    for q in range(labels):
         for k in range(chunks):
             if q * chunks + k >= 2:
                 save((q * chunks + k - 2) // chunks, (k - 2) % chunks).wait()
 
-            def narrow(i, carry, k=k):
-                at = pl.multiple_of(i * side, side)
+            def narrow(i, carry, k=k, q=q):
+                at = pl.multiple_of(i * SIDE, SIDE)
                 for c in range(words):
-                    v = dest[pl.ds((k * CHUNK + at) * slot + c, side, stride=slot), :]
-                    stage[k % 2, pl.ds(at, side), pl.ds(c * LANES, LANES)] = v.astype(jnp.bfloat16)
+                    v = dests[q][pl.ds((k * CHUNK + at) * slot + c, SIDE, stride=slot), :]
+                    stage[k % 2, pl.ds(at, SIDE), pl.ds(c * LANES, LANES)] = v.astype(jnp.bfloat16)
                 return carry
 
-            lax.fori_loop(0, CHUNK // side, narrow, 0)
+            lax.fori_loop(0, CHUNK // SIDE, narrow, 0)
             save(q, k).start()
     for k in range(chunks - 2, chunks):
+        save(labels - 1, k).wait()
+    for k in range(chunks):
         save_first(k).wait()
-        save(labels - 1, k).wait()
-
-
-def snp_side(core, env_own, env_other, sums_own, sums_other, shuf_own, shuf_other, own, other,
-             labels):
-    snp_rows, half = own.shape
+
+
+def permuted(core, shuf_own, shuf_other, own, other, labels):
+    half, snp_rows = own.shape
     all_samples = 2 * half
-    words = snp_rows // LANES
+    slot = (snp_rows // LANES) | 1
     width = labels * snp_rows + snp_rows // 2
     any_spec = pl.BlockSpec(memory_space=pl.ANY)
-    smem = pl.BlockSpec(memory_space=pltpu.SMEM)
-    vmem = pl.BlockSpec(memory_space=pltpu.VMEM)
     return pl.pallas_call(
-        functools.partial(snp_side_kernel, labels=labels),
+        functools.partial(permute_kernel, labels=labels),
         out_shape=jax.ShapeDtypeStruct((all_samples, width), jnp.bfloat16),
-        in_specs=[smem, vmem, vmem, vmem, vmem, any_spec, any_spec, any_spec, any_spec],
+        in_specs=[pl.BlockSpec(memory_space=pltpu.SMEM)] + [any_spec] * 4,
         out_specs=any_spec,
         scratch_shapes=[
             pltpu.SMEM((labels * all_samples,), jnp.int32),
-            pltpu.VMEM((3, snp_rows, CHUNK), jnp.bfloat16),
-            pltpu.VMEM((all_samples * (words | 1), LANES), jnp.float32),
-            pltpu.VMEM((all_samples * (words | 1), LANES), jnp.float32),
+            pltpu.VMEM((all_samples // CHUNK, CHUNK, snp_rows), jnp.bfloat16),
+            pltpu.VMEM((SIDE * slot, LANES), jnp.float32),
+            [pltpu.VMEM((all_samples * slot, LANES), jnp.float32) for _ in range(labels)],
             pltpu.VMEM((2, CHUNK, snp_rows), jnp.bfloat16),
-            pltpu.VMEM((2, CHUNK, snp_rows // 2), jnp.bfloat16),
-            pltpu.VMEM((snp_rows, LANES), jnp.float32),
             pltpu.SemaphoreType.DMA((2 * labels,)),
-            pltpu.SemaphoreType.DMA((3,)),
+            pltpu.SemaphoreType.DMA((all_samples // CHUNK,)),
             pltpu.SemaphoreType.DMA((2,)),
-            pltpu.SemaphoreType.DMA((2,)),
+            pltpu.SemaphoreType.DMA((all_samples // CHUNK,)),
         ],
         compiler_params=pltpu.CompilerParams(vmem_limit_bytes=61 * MIB),
         cost_estimate=pl.CostEstimate(
             flops=40 * 10**9, bytes_accessed=60 * 10**6, transcendentals=0
         ),
-        name="snp_side",
-    )(core, env_own, env_other, sums_own, sums_other, shuf_own, shuf_other, own, other)
+        name="permuted",
+    )(core, shuf_own, shuf_other, own, other)
 
 
 def window_plan(start, end, bounds_ref, n_bounds, total_blocks):
@@ -562,13 +580,10 @@
     labels = perms // cores
     caps = tuple(min(genes, genes * 4 >> k) for k in range(1, reach + 1))
 
+    env = environment[None]
     other_pheno = swapped(phenotypes)
-    env = environment[None]
     own_sums = local_moments(genotypes, env)
     sums = (own_sums, swapped(own_sums))
-    late_geno, _ = lax.optimization_barrier((genotypes, other_pheno))
-    other_geno = swapped(late_geno)
-    other_env = swapped(env)
     other_shuffles = swapped(shuffles)
     pos = jnp.stack([genome_pos, sample_pos]).astype(jnp.int32)
     start = window_start.reshape(-1, LANES)
@@ -588,10 +603,12 @@
         return mine
 
     rounds, plan, full, *payloads = chosen(jnp.zeros((1,), jnp.int32))
+    late_env, *payloads = lax.optimization_barrier((env, *payloads))
+    own_turned = turned(genotypes, late_env, sums)
+    own_turned, *payloads = lax.optimization_barrier((own_turned, *payloads))
+    other_turned = swapped(own_turned)
     mine = travel(payloads)
-    weights = snp_side(
-        pos[1:], env, other_env, *sums, shuffles, other_shuffles, genotypes, other_geno, labels
-    )
+    weights = permuted(pos[1:], shuffles, other_shuffles, own_turned, other_turned, labels)
 
     def met(plan, full, mine):
         other = [swapped(x) for x in mine]

time: 107 us -> 111 us (1.037)
  starting transfers between devices: 18.7 us -> 23.1 us
  waiting for transfers between devices: 6.37 us -> 4.68 us
  blocking collectives: 12.9 us -> 14.1 us
    ppermute x9 -> x8, starting transfers between devices: 2.68 us -> 6.88 us  [swapped(): lax.ppermute(x, 'sample', [(i, (i + 1) % count) for i in range(count)])]
    ppermute x9 -> x8, waiting for transfers between devices: 6.36 us -> 4.67 us  [swapped(): lax.ppermute(x, 'sample', [(i, (i + 1) % count) for i in range(count)])]
    all_to_all x1, blocking collectives: 12.9 us -> 14.1 us  [shards(): gathered = lax.all_to_all(found, ('genome', 'sample'), 0, 0, tiled=True)]
    pallas_call x1 -> x2, Pallas kernels: 37.6 us -> 38.1 us  [the longest x1 32.1 us: permuted(): pl.pallas_call(functools.partial(permute_kernel, labels=labels), out_shap...]
  transfers between devices with their start and end apart: 13 -> 12, of which waited for: 4 -> 3; matrix products, arithmetic and copies ran while one was open for 0% -> 0% of each run, Pallas kernels for 44% -> 37%
where the time goes in v7:
time: 111 us; the launch traced here: 110 us
  Pallas kernels  66.5 us (60%)
  starting transfers between devices  23.1 us (21%)
  blocking collectives  14.1 us (13%)
  waiting for transfers between devices  4.68 us (4%)
    pallas_call x1, Pallas kernels, permuted(): pl.pallas_call(functools.partial(permute_kernel, labels=labels), out_shap...  32.1 us
    pallas_call x1, Pallas kernels, products(): pl.pallas_call(functools.partial(product_kernel, caps=caps, labels=labels...  18.2 us
    ppermute x4, starting transfers between devices, travel(): mine.append(lax.ppermute(payload, ('genome', 'sample'), pairs))  16.2 us
    all_to_all x1, blocking collectives, shards(): gathered = lax.all_to_all(found, ('genome', 'sample'), 0, 0, tiled=True)  14.1 us
    ppermute x8, starting transfers between devices, swapped(): lax.ppermute(x, 'sample', [(i, (i + 1) % count) for i in range(count)])  6.88 us
    pallas_call x1, Pallas kernels, turned(): pl.pallas_call(turned_kernel, grid=(half // CHUNK,), out_shape=jax.ShapeD...  5.95 us
    ppermute x8, waiting for transfers between devices, swapped(): lax.ppermute(x, 'sample', [(i, (i + 1) % count) for i in range(count)])  4.67 us
    pallas_call x1, Pallas kernels, local_moments(): pl.pallas_call(moments_kernel, grid=(half // chunk,), out_shape=jax.Shape...  4.57 us
  transfers between devices with their start and end apart: 12, of which 3 were waited for; matrix products, arithmetic and copies ran while one was open for 0% of the time, Pallas kernels for 37%

profile of v7, /device:TPU:0, one launch (start us, length us, event | category | flops | bytes accessed | tf_op | source)
XLA Modules:
  0.0 110.1 jit_solution(6259149955161376351)
XLA Ops:
  0.0 0.5 collective-permute-start.9
  0.5 4.6 %local_moments.1.sums_own = f32[8,512]{1,0:T(8,128)S(1)} custom-call(bf16[512,4096]{1,0:T(8,128)(2,1)} %geno_ref.3, f32[1,4096]{1,0:T(1,128)} %bitcast.14), custom_call_target="tpu_custom_call" | custom-call | flops 5000000000 | bytes 4194304 | tf_op jit(solution)/shard_map/local_moments/pallas_call | solution.py:66
  5.0 0.1 collective-permute-start.8
  5.2 0.1 pad_add_fusion.pos_ref
  5.3 4.1 %select.2 = (s32[1]{0:T(128)}, s32[3,16,64]{2,1,0:T(8,128)S(1)}, bf16[64,8192]{1,0:T(8,128)(2,1)S(1)}, bf16[64,8192]{1,0:T(8,128)(2,1)}, bf16[64,8192]{1,0:T(8,1...) custom-call(s32[1]{0:T(128)} %constant.13.clone.1.round_ref, s32[2]{0:T(128)S(1)} %pad_add_fusion.pos_ref, ...), custom_call_target="tpu_custom_call" | custom-call | tf_op jit(solution)/shard_map/select/pallas_call | solution.py:374
  9.4 0.0 copy-start.8
  9.4 0.0 collective-permute-done.8.sums_other
  9.4 5.9 %turned.1.own_ref = bf16[4096,512]{1,0:T(8,128)(2,1)} custom-call(bf16[512,4096]{1,0:T(8,128)(2,1)} %geno_ref.3, f32[1,4096]{1,0:T(1,128)} %bitcast.15, f32[8,512]{1,0:T(8,128)S(1)} %local_moments.1.sums_own, f32[8,512]{1,0:T(8,128)S(1)} %collective-permute-done.8.sums_other), custom_call_target="tpu_custom_call" | custom-call | flops 5000000000 | bytes 8388608 | tf_op jit(solution)/shard_map/turned/pallas_call | solution.py:113
  15.4 0.5 collective-permute-start.15
  15.9 0.1 collective-permute-start.14
  16.0 4.9 %collective-permute-start.10 = (bf16[64,8192]{1,0:T(8,128)(2,1)}, bf16[64,8192]{1,0:T(8,128)(2,1)S(1)}, u32[]{:S(2)}, u32[]{:S(2)}) collective-permute-start(bf16[64,8192]{1,0:T(8,128)(2,1)} %get-tuple-element.110), channel_id=1, source_target_pairs={{0,2},{2,4},{4,6},{6,8},{8,10},{10,12},{12,14},{14,16},{16,18},{18... | collective-permute-start | bytes 3145736 | tf_op jit(solution)/shard_map/ppermute | solution.py:602
  20.9 4.4 %collective-permute-start.11 = (bf16[64,8192]{1,0:T(8,128)(2,1)}, bf16[64,8192]{1,0:T(8,128)(2,1)}, u32[]{:S(2)}, u32[]{:S(2)}) collective-permute-start(bf16[64,8192]{1,0:T(8,128)(2,1)} %get-tuple-element.111), channel_id=1, source_target_pairs={{0,4},{2,6},{4,8},{6,10},{8,12},{10,14},{12,16},{14,18},{16,20},{1... | collective-permute-start | bytes 3145736 | tf_op jit(solution)/shard_map/ppermute | solution.py:602
  25.2 3.4 %collective-permute-start.12 = (bf16[32,8192]{1,0:T(8,128)(2,1)}, bf16[32,8192]{1,0:T(8,128)(2,1)S(1)}, u32[]{:S(2)}, u32[]{:S(2)}) collective-permute-start(bf16[32,8192]{1,0:T(8,128)(2,1)} %get-tuple-element.112), channel_id=1, source_target_pairs={{0,6},{2,8},{4,10},{6,12},{8,14},{10,16},{12,18},{14,20},{16,22},{... | collective-permute-start | bytes 1572872 | tf_op jit(solution)/shard_map/ppermute | solution.py:602
  28.6 0.0 collective-permute-done.14.shuf_other
  28.7 3.6 %collective-permute-start.13 = (bf16[16,8192]{1,0:T(8,128)(2,1)}, bf16[16,8192]{1,0:T(8,128)(2,1)S(1)}, u32[]{:S(2)}, u32[]{:S(2)}) collective-permute-start(bf16[16,8192]{1,0:T(8,128)(2,1)} %get-tuple-element.113), channel_id=1, source_target_pairs={{0,8},{2,10},{4,12},{6,14},{8,16},{10,18},{12,20},{14,22},{16,24},... | collective-permute-start | bytes 786440 | tf_op jit(solution)/shard_map/ppermute | solution.py:602
  32.3 0.0 collective-permute-done.15.other_ref
  32.3 32.1 %permuted.1.rest_9_ = bf16[8192,1280]{1,0:T(8,128)(2,1)} custom-call(s32[1]{0:T(128)} %bitcast.3.core_ref, s32[4,4096]{1,0:T(4,128)} %shuf_own.1, s32[4,4096]{1,0:T(4,128)} %copy-done.9, bf16[4096,512]{1,0:T(8,128)(2,1)} %turned.1.own_ref, bf16[4096,512]{1,0:T(8,128)(2,1)} %collective-permute-done.15.other_ref), custom_call_target="tpu_custom_call" | custom-call | flops 40000000000 | bytes 60000000 | tf_op jit(solution)/shard_map/permuted/pallas_call | solution.py:237
  64.4 0.0 collective-permute-done.13.rest_4_
  64.4 0.0 collective-permute-done.12.rest_3_
  64.4 0.0 collective-permute-done.11.rest_2_
  64.4 5.1 %collective-permute-start.16 = (bf16[64,8192]{1,0:T(8,128)(2,1)S(1)}, bf16[64,8192]{1,0:T(8,128)(2,1)}, u32[]{:S(2)}, u32[]{:S(2)}) collective-permute-start(bf16[64,8192]{1,0:T(8,128)(2,1)S(1)} %collective-permute-done.10.rest_1_), channel_id=1, source_target_pairs={{0,1},{1,0},{2,3},{3,2},{4,5},{5,4},{6,7},{7,6},{8,9},{9,8},{10,11... | collective-permute-start | bytes 3145736 | tf_op jit(solution)/shard_map/ppermute | solution.py:28
  69.5 0.1 collective-permute-start.17
  69.6 0.4 collective-permute-start.18
  70.1 0.1 collective-permute-start.19
  70.1 3.5 %collective-permute-done.19.rest_8_ = bf16[16,8192]{1,0:T(8,128)(2,1)S(1)} collective-permute-done((bf16[16,8192]{1,0:T(8,128)(2,1)S(1)}, bf16[16,8192]{1,0:T(8,128)(2,1)S(1)}, u32[]{:S(2)}, u32[]{:S(2)}) %collective-permute-start.19) | collective-permute-done | bytes 262176 | tf_op jit(solution)/shard_map/ppermute | solution.py:28
  73.7 0.9 collective-permute-done.18.rest_7_
  74.5 0.3 collective-permute-done.17.rest_6_
  74.8 18.2 %products.2 = (f32[32,8,128]{2,1,0:T(8,128)}, f32[8,64]{1,0:T(8,128)S(1)}) custom-call(s32[2]{0:T(128)S(1)} %pad_add_fusion.pos_ref, f32[8,512]{1,0:T(8,128)S(1)} %local_moments.1.sums_own, f32[8,512]{1,0:T(8,128)S(1)} %copy-done.11, s32[3,16,64]{2,1,0:T(8,128)S(1)} %get-tuple-element.99.plan_ref, bf16[64,8192]{1,0:T(8,128)(2,1)S(1)} %get-tuple-element.100.rest_0_, ...), custom_call_target="tpu_custom_call" | custom-call | flops 8724152320 | bytes 27787264 | tf_op jit(solution)/shard_map/products/pallas_call | solution.py:524
  93.0 0.6 copy-done
  93.6 0.9 while.10
  94.5 14.1 %all_to_all.5.gathered_ref = f32[32,8,128]{2,1,0:T(8,128)} all-to-all(f32[32,8,128]{2,1,0:T(8,128)} %get-tuple-element.122), channel_id=1, replica_groups=mesh['genome'=16,'sample'=2] {'genome','sample'}, dimensions={0} | all-to-all | bytes 262144 | tf_op jit(solution)/shard_map/all_to_all | solution.py:631
  108.6 1.5 %finish.1 = f32[5,64]{1,0:T(8,128)} custom-call(f32[32,8,128]{2,1,0:T(8,128)} %all_to_all.5.gathered_ref, f32[8,64]{1,0:T(8,128)} %copy-done), custom_call_target="tpu_custom_call" | custom-call | tf_op jit(solution)/shard_map/finish/pallas_call | solution.py:632
  (21 shorter events, 0.0 us)
Async XLA Ops:
  0.0 5.2 %collective-permute-start.9 = (bf16[64,4096]{1,0:T(8,128)(2,1)}, bf16[64,4096]{1,0:T(8,128)(2,1)S(1)}, u32[]{:S(2)}, u32[]{:S(2)}) collective-permute-start(bf16[64,4096]{1,0:T(8,128)(2,1)} %own_ref.1), channel_id=1, source_target_pairs={{0,1},{1,0},{2,3},{3,2},{4,5},{5,4},{6,7},{7,6},{8,9},{9,8},{10,11... | collective-permute-start | bytes 1572872 | tf_op jit(solution)/shard_map/ppermute | solution.py:28
  0.5 4.8 %copy-start.1 = (bf16[64,4096]{1,0:T(8,128)(2,1)S(1)}, bf16[64,4096]{1,0:T(8,128)(2,1)}, u32[]{:S(2)}) copy-start(bf16[64,4096]{1,0:T(8,128)(2,1)} %own_ref.1) | copy-start | bytes 1572868
  0.5 4.8 %copy-start.5 = (s32[1024]{0:T(1024)S(1)}, s32[1024]{0:T(1024)}, u32[]{:S(2)}) copy-start(s32[1024]{0:T(1024)} %param.13) | copy-start | bytes 12292
  0.5 4.8 %copy-start.6 = (s32[1024]{0:T(1024)S(1)}, s32[1024]{0:T(1024)}, u32[]{:S(2)}) copy-start(s32[1024]{0:T(1024)} %param.14) | copy-start | bytes 12292
  0.5 4.8 %copy-start.7 = (s32[15]{0:T(128)S(1)}, s32[15]{0:T(128)}, u32[]{:S(2)}) copy-start(s32[15]{0:T(128)} %bounds_ref.1) | copy-start | bytes 184
  5.0 4.4 %collective-permute-start.8 = (f32[8,512]{1,0:T(8,128)S(1)}, f32[8,512]{1,0:T(8,128)S(1)}, u32[]{:S(2)}, u32[]{:S(2)}) collective-permute-start(f32[8,512]{1,0:T(8,128)S(1)} %local_moments.1.sums_own), channel_id=1, source_target_pairs={{0,1},{1,0},{2,3},{3,2},{4,5},{5,4},{6,7},{7,6},{8,9},{9,8},{10,11... | collective-permute-start | bytes 49160 | tf_op jit(solution)/shard_map/ppermute | solution.py:28
  5.2 10.1 %copy-start.2 = (bf16[64,4096]{1,0:T(8,128)(2,1)}, bf16[64,4096]{1,0:T(8,128)(2,1)S(1)}, u32[]{:S(2)}) copy-start(bf16[64,4096]{1,0:T(8,128)(2,1)S(1)} %collective-permute-done.9.other_ref) | copy-start | bytes 1572868
  9.4 6.5 %copy-start.8 = (s32[4,4096]{1,0:T(4,128)S(1)}, s32[4,4096]{1,0:T(4,128)}, u32[]{:S(2)}) copy-start(s32[4,4096]{1,0:T(4,128)} %shuf_own.1) | copy-start | bytes 196612
  9.4 6.0 %copy-start.10 = (f32[8,512]{1,0:T(8,128)}, f32[8,512]{1,0:T(8,128)S(1)}, u32[]{:S(2)}) copy-start(f32[8,512]{1,0:T(8,128)S(1)} %collective-permute-done.8.sums_other) | copy-start | bytes 49156
  15.4 16.9 %collective-permute-start.15 = (bf16[4096,512]{1,0:T(8,128)(2,1)}, bf16[4096,512]{1,0:T(8,128)(2,1)}, u32[]{:S(2)}, u32[]{:S(2)}) collective-permute-start(bf16[4096,512]{1,0:T(8,128)(2,1)} %turned.1.own_ref), channel_id=1, source_target_pairs={{0,1},{1,0},{2,3},{3,2},{4,5},{5,4},{6,7},{7,6},{8,9},{9,8},{10,11... | collective-permute-start | bytes 12582920 | tf_op jit(solution)/shard_map/ppermute | solution.py:28
  15.9 12.7 %collective-permute-start.14 = (s32[4,4096]{1,0:T(4,128)S(1)}, s32[4,4096]{1,0:T(4,128)S(1)}, u32[]{:S(2)}, u32[]{:S(2)}) collective-permute-start(s32[4,4096]{1,0:T(4,128)S(1)} %copy-done.8), channel_id=1, source_target_pairs={{0,1},{1,0},{2,3},{3,2},{4,5},{5,4},{6,7},{7,6},{8,9},{9,8},{10,11... | collective-permute-start | bytes 196616 | tf_op jit(solution)/shard_map/ppermute | solution.py:28
  16.0 48.4 %collective-permute-start.10 = (bf16[64,8192]{1,0:T(8,128)(2,1)}, bf16[64,8192]{1,0:T(8,128)(2,1)S(1)}, u32[]{:S(2)}, u32[]{:S(2)}) collective-permute-start(bf16[64,8192]{1,0:T(8,128)(2,1)} %get-tuple-element.110), channel_id=1, source_target_pairs={{0,2},{2,4},{4,6},{6,8},{8,10},{10,12},{12,14},{14,16},{16,18},{18... | collective-permute-start | bytes 3145736 | tf_op jit(solution)/shard_map/ppermute | solution.py:602
  20.9 43.6 %collective-permute-start.11 = (bf16[64,8192]{1,0:T(8,128)(2,1)}, bf16[64,8192]{1,0:T(8,128)(2,1)}, u32[]{:S(2)}, u32[]{:S(2)}) collective-permute-start(bf16[64,8192]{1,0:T(8,128)(2,1)} %get-tuple-element.111), channel_id=1, source_target_pairs={{0,4},{2,6},{4,8},{6,10},{8,12},{10,14},{12,16},{14,18},{16,20},{1... | collective-permute-start | bytes 3145736 | tf_op jit(solution)/shard_map/ppermute | solution.py:602
  25.2 39.2 %collective-permute-start.12 = (bf16[32,8192]{1,0:T(8,128)(2,1)}, bf16[32,8192]{1,0:T(8,128)(2,1)S(1)}, u32[]{:S(2)}, u32[]{:S(2)}) collective-permute-start(bf16[32,8192]{1,0:T(8,128)(2,1)} %get-tuple-element.112), channel_id=1, source_target_pairs={{0,6},{2,8},{4,10},{6,12},{8,14},{10,16},{12,18},{14,20},{16,22},{... | collective-permute-start | bytes 1572872 | tf_op jit(solution)/shard_map/ppermute | solution.py:602
  28.6 3.6 %copy-start.9 = (s32[4,4096]{1,0:T(4,128)}, s32[4,4096]{1,0:T(4,128)S(1)}, u32[]{:S(2)}) copy-start(s32[4,4096]{1,0:T(4,128)S(1)} %collective-permute-done.14.shuf_other) | copy-start | bytes 196612
  28.6 46.2 %copy-start.11 = (f32[8,512]{1,0:T(8,128)S(1)}, f32[8,512]{1,0:T(8,128)}, u32[]{:S(2)}) copy-start(f32[8,512]{1,0:T(8,128)} %copy-done.10) | copy-start | bytes 49156
  28.7 35.7 %collective-permute-start.13 = (bf16[16,8192]{1,0:T(8,128)(2,1)}, bf16[16,8192]{1,0:T(8,128)(2,1)S(1)}, u32[]{:S(2)}, u32[]{:S(2)}) collective-permute-start(bf16[16,8192]{1,0:T(8,128)(2,1)} %get-tuple-element.113), channel_id=1, source_target_pairs={{0,8},{2,10},{4,12},{6,14},{8,16},{10,18},{12,20},{14,22},{16,24},... | collective-permute-start | bytes 786440 | tf_op jit(solution)/shard_map/ppermute | solution.py:602
  64.4 10.1 %collective-permute-start.16 = (bf16[64,8192]{1,0:T(8,128)(2,1)S(1)}, bf16[64,8192]{1,0:T(8,128)(2,1)}, u32[]{:S(2)}, u32[]{:S(2)}) collective-permute-start(bf16[64,8192]{1,0:T(8,128)(2,1)S(1)} %collective-permute-done.10.rest_1_), channel_id=1, source_target_pairs={{0,1},{1,0},{2,3},{3,2},{4,5},{5,4},{6,7},{7,6},{8,9},{9,8},{10,11... | collective-permute-start | bytes 3145736 | tf_op jit(solution)/shard_map/ppermute | solution.py:28
  69.5 5.3 %collective-permute-start.17 = (bf16[64,8192]{1,0:T(8,128)(2,1)}, bf16[64,8192]{1,0:T(8,128)(2,1)}, u32[]{:S(2)}, u32[]{:S(2)}) collective-permute-start(bf16[64,8192]{1,0:T(8,128)(2,1)} %collective-permute-done.11.rest_2_), channel_id=1, source_target_pairs={{0,1},{1,0},{2,3},{3,2},{4,5},{5,4},{6,7},{7,6},{8,9},{9,8},{10,11... | collective-permute-start | bytes 3145736 | tf_op jit(solution)/shard_map/ppermute | solution.py:28
  69.6 4.9 %collective-permute-start.18 = (bf16[32,8192]{1,0:T(8,128)(2,1)S(1)}, bf16[32,8192]{1,0:T(8,128)(2,1)}, u32[]{:S(2)}, u32[]{:S(2)}) collective-permute-start(bf16[32,8192]{1,0:T(8,128)(2,1)S(1)} %collective-permute-done.12.rest_3_), channel_id=1, source_target_pairs={{0,1},{1,0},{2,3},{3,2},{4,5},{5,4},{6,7},{7,6},{8,9},{9,8},{10,11... | collective-permute-start | bytes 1572872 | tf_op jit(solution)/shard_map/ppermute | solution.py:28
  70.1 3.6 %collective-permute-start.19 = (bf16[16,8192]{1,0:T(8,128)(2,1)S(1)}, bf16[16,8192]{1,0:T(8,128)(2,1)S(1)}, u32[]{:S(2)}, u32[]{:S(2)}) collective-permute-start(bf16[16,8192]{1,0:T(8,128)(2,1)S(1)} %collective-permute-done.13.rest_4_), channel_id=1, source_target_pairs={{0,1},{1,0},{2,3},{3,2},{4,5},{5,4},{6,7},{7,6},{8,9},{9,8},{10,11... | collective-permute-start | bytes 786440 | tf_op jit(solution)/shard_map/ppermute | solution.py:28
  93.0 0.6 copy-start

commit v8 on v4

--- a/solution.py
+++ b/solution.py
@@ -12,6 +12,7 @@
 LANES = 128
 ROWS_STEP = 16
 UNROLL = 32
+SIDE = 2 * LANES
 CHUNK = 1024
 MIB = 2**20
 
@@ -90,7 +91,7 @@
     all_samples = 2 * half
     chunks = all_samples // CHUNK
     words = snp_rows // LANES
-    slot = words | 1
+    slot = words
     share = snp_rows // 2
     side = 2 * LANES
     core = core_ref[0]
@@ -182,7 +183,7 @@
             base = pl.multiple_of(first * slot, UNROLL * slot)
             held = [table[pl.ds(base + u * slot, words), :] for u in range(UNROLL)]
             for u in range(UNROLL):
-                to = idx[q * all_samples + first + u] * slot
+                to = pl.multiple_of(idx[q * all_samples + first + u] * slot, slot)
                 dest[pl.ds(to, words), :] = held[u]
             return carry
 
@@ -222,8 +223,8 @@
         scratch_shapes=[
             pltpu.SMEM((labels * all_samples,), jnp.int32),
             pltpu.VMEM((3, snp_rows, CHUNK), jnp.bfloat16),
-            pltpu.VMEM((all_samples * (words | 1), LANES), jnp.float32),
-            pltpu.VMEM((all_samples * (words | 1), LANES), jnp.float32),
+            pltpu.VMEM((all_samples * words, LANES), jnp.float32),
+            pltpu.VMEM((all_samples * words, LANES), jnp.float32),
             pltpu.VMEM((2, CHUNK, snp_rows), jnp.bfloat16),
             pltpu.VMEM((2, CHUNK, snp_rows // 2), jnp.bfloat16),
             pltpu.VMEM((snp_rows, LANES), jnp.float32),
@@ -256,9 +257,10 @@
     round_ref, pos_ref, bounds_ref, start_ref, end_ref, own_ref, other_ref,
     rounds_ref, plan_ref, full_ref, *rest, caps, blocks_dev,
 ):
-    pay_refs, (slots, edges) = rest[: len(caps)], rest[len(caps) :]
     reach = len(caps)
     genes, half = own_ref.shape
+    chosen_from = sum(cap == genes for cap in caps)
+    (slots, edges), pay_refs = rest[-2:], rest[:-2]
     shape = start_ref.shape
     per_row = LANES // genes
     chips = shape[0] * per_row
@@ -287,6 +289,10 @@
                 preferred_element_type=jnp.float32,
             ).astype(jnp.int32)
             cap = caps[k - 1]
+            if cap == genes:
+                which = lax.broadcasted_iota(jnp.int32, shape, 1) % genes
+                slots[way * reach + k - 1] = jnp.where(need, which, -1)
+                continue
             slot = rank - 1 - turn * cap
             slots[way * reach + k - 1] = jnp.where(
                 need & (slot >= 0) & (slot < cap), slot, -1
@@ -303,45 +309,51 @@
             )
         return out
 
-    plan_ref[...] = jnp.zeros_like(plan_ref)
-    plan_ref[0, pl.ds(0, 1), :] = lax.broadcasted_iota(jnp.int32, (1, genes), 1)
-    plan_ref[1, pl.ds(0, 1), :] = of_chip(edges, 0, chip)
-    plan_ref[2, pl.ds(0, 1), :] = of_chip(edges, 1, chip)
+    used = [lax.broadcasted_iota(jnp.int32, (1, genes), 1)]
+    lows = [of_chip(edges, 0, chip)]
+    highs = [of_chip(edges, 1, chip)]
+    first = genes
     for side in range(2):
         way = core if side == 0 else 1 - core
         for k in range(1, reach + 1):
             source = chip + (2 * way - 1) * k
             valid = (source >= 0) & (source < chips)
             source = jnp.clip(source, 0, chips - 1)
-            to = pl.ds(1 + side * reach + k - 1, 1)
             slot = of_chip(slots, way * reach + k - 1, source)
-            plan_ref[0, to, :] = jnp.where(valid, slot, -1)
-            plan_ref[1, to, :] = of_chip(edges, 0, source)
-            plan_ref[2, to, :] = jnp.where(valid, of_chip(edges, 1, source), 0)
+            used.append(jnp.where(valid & (slot >= 0), slot + first, -1))
+            lows.append(of_chip(edges, 0, source))
+            highs.append(jnp.where(valid, of_chip(edges, 1, source), 0))
+            first += caps[k - 1]
+    while len(used) * genes < plan_ref.shape[1]:
+        used.append(jnp.full_like(used[0], -1))
+        lows.append(jnp.zeros_like(used[0]))
+        highs.append(jnp.zeros_like(used[0]))
+    plan_ref[...] = jnp.zeros_like(plan_ref)
+    for row, parts in enumerate((used, lows, highs)):
+        plan_ref[pl.ds(row, 1), :] = jnp.concatenate(parts, axis=1)
 
     picks = []
-    for k in range(1, reach + 1):
+    for k in range(chosen_from + 1, reach + 1):
         slot = of_chip(slots, core * reach + k - 1, chip)
         rows = lax.broadcasted_iota(jnp.int32, (caps[k - 1], genes), 0)
         picks.append((rows == slot).astype(jnp.float32))
-    picks = jnp.concatenate(picks, axis=0).astype(jnp.bfloat16)
+    if picks:
+        picks = jnp.concatenate(picks, axis=0).astype(jnp.bfloat16)
     step = 1024
 
     def copy(i, carry):
         cols = pl.ds(pl.multiple_of(i * step, step), step)
         late = pl.ds(pl.multiple_of(half + i * step, step), step)
         a, b = own_ref[:, cols], other_ref[:, cols]
-        first = jnp.where(core == 0, a, b)
-        second = jnp.where(core == 0, b, a)
-        full_ref[:, cols] = first
-        full_ref[:, late] = second
-        for part, to in ((first, cols), (second, late)):
-            chosen = jnp.dot(picks, part, preferred_element_type=jnp.float32)
-            chosen = chosen.astype(jnp.bfloat16)
-            row = 0
-            for pay in pay_refs:
-                pay[:, to] = chosen[row : row + pay.shape[0]]
-                row += pay.shape[0]
+        for part, to in ((jnp.where(core == 0, a, b), cols), (jnp.where(core == 0, b, a), late)):
+            full_ref[:, to] = part
+            if pay_refs:
+                chosen = jnp.dot(picks, part, preferred_element_type=jnp.float32)
+                chosen = chosen.astype(jnp.bfloat16)
+                row = 0
+                for pay in pay_refs:
+                    pay[:, to] = chosen[row : row + pay.shape[0]]
+                    row += pay.shape[0]
         return carry
 
     lax.fori_loop(0, half // step, copy, 0)
@@ -349,20 +361,22 @@
 
 def select(turn, pos, bounds, start, end, own, other, caps, blocks_dev):
     genes, half = own.shape
+    all_samples = 2 * half
     reach = len(caps)
     smem = pl.BlockSpec(memory_space=pltpu.SMEM)
     vmem = pl.BlockSpec(memory_space=pltpu.VMEM)
-    plan_rows = -(-(2 * reach + 1) // 8) * 8
+    width = -(-(2 * reach + 1) * genes // LANES) * LANES
+    chosen = [cap for cap in caps if cap < genes]
     return pl.pallas_call(
         functools.partial(select_kernel, caps=caps, blocks_dev=blocks_dev),
         out_shape=(
             jax.ShapeDtypeStruct((1,), jnp.int32),
-            jax.ShapeDtypeStruct((3, plan_rows, genes), jnp.int32),
-            jax.ShapeDtypeStruct((genes, 2 * half), jnp.bfloat16),
-            *[jax.ShapeDtypeStruct((cap, 2 * half), jnp.bfloat16) for cap in caps],
+            jax.ShapeDtypeStruct((8, width), jnp.int32),
+            jax.ShapeDtypeStruct((genes, all_samples), jnp.bfloat16),
+            *[jax.ShapeDtypeStruct((cap, all_samples), jnp.bfloat16) for cap in chosen],
         ),
         in_specs=[smem, smem, smem, vmem, vmem, vmem, vmem],
-        out_specs=(smem, vmem, vmem, *[vmem for _ in caps]),
+        out_specs=(smem, vmem, vmem, *[vmem for _ in chosen]),
         scratch_shapes=[
             pltpu.VMEM((2 * reach,) + start.shape, jnp.int32),
             pltpu.VMEM((2,) + start.shape, jnp.int32),
@@ -378,156 +392,148 @@
     reach = len(caps)
     n_in = 1 + 2 * reach
     gene_refs = rest[:n_in]
-    weights_ref, out_ref, power_ref, rows, total, power = rest[n_in:]
-    step = pl.program_id(0)
-    steps = pl.num_programs(0)
+    weights_ref, out_ref, power_ref, rows, total, power, held, sems = rest[n_in:]
     snp_rows = sums_own.shape[1]
-    depth, width = weights_ref.shape
+    all_samples, width = weights_ref.shape
     block = SNP_BLOCK
-    sizes = (genes,) + tuple(caps) + tuple(caps)
-    starts = [sum(sizes[:i]) for i in range(n_in)]
-    used = sum(sizes)
-
-    @pl.when(step == 0)
-    def _():
-        total[...] = jnp.zeros_like(total)
-        power[...] = jnp.zeros_like(power)
-
-    for ref, start, size in zip(gene_refs, starts, sizes):
-        rows[pl.ds(start, size), :] = ref[...]
-    for n in range(width // block):
-        cols = pl.ds(n * block, block)
-        total[pl.ds(0, used), cols] += jnp.dot(
-            rows[...], weights_ref[:, cols], preferred_element_type=jnp.float32
-        )
-    kept = power[...]
-    for t in range(depth // LANES):
-        x = gene_refs[0][:, pl.ds(t * LANES, LANES)].astype(jnp.float32)
-        kept = kept + x * x
-    power[...] = kept
-
-    @pl.when(step == steps - 1)
-    def _():
-        chip, core = pos_ref[0], pos_ref[1]
-        share_blocks = blocks_dev // 2
-        sums = sums_own[...] + sums_other[...]
-        cross = sums[1:2, :]
-        inter = sums[2:3, :]
-        inv = 1.0 / (inter - cross * (cross / sums[0:1, :]) + 0.1 * inter)
-
-        def peak(col, inv_block):
-            v = total[:, pl.ds(col, block)]
-            v = v * v * inv_block
-            best = v[:, :LANES]
-            for t in range(1, block // LANES):
-                best = jnp.maximum(best, v[:, t * LANES : (t + 1) * LANES])
-            return jnp.max(best.T, axis=0, keepdims=True)
-
-        peaks = []
-        for q in range(labels):
-            for b in range(blocks_dev):
-                peaks.append(
-                    peak(q * snp_rows + b * block, inv[:, b * block : (b + 1) * block])
-                )
-        for b in range(share_blocks):
-            mine = inv[:, b * block : (b + 1) * block]
-            late = inv[:, (share_blocks + b) * block : (share_blocks + b + 1) * block]
-            peaks.append(
-                peak(labels * snp_rows + b * block, jnp.where(core == 0, mine, late))
+    used = rows.shape[0]
+    chip, core = pos_ref[0], pos_ref[1]
+
+    def load(k):
+        return pltpu.make_async_copy(
+            weights_ref.at[pl.ds(k * CHUNK, CHUNK)], held.at[k], sems.at[k]
+        )
+
+    for k in range(all_samples // CHUNK):
+        load(k).start()
+    power[...] = jnp.zeros_like(power)
+    total[...] = jnp.zeros_like(total)
+    for k in range(all_samples // CHUNK):
+        depth = pl.ds(k * CHUNK, CHUNK)
+        at = 0
+        for ref in gene_refs:
+            rows[pl.ds(at, ref.shape[0]), :] = ref[:, depth]
+            at += ref.shape[0]
+        kept = power[...]
+        for t in range(CHUNK // LANES):
+            x = rows[pl.ds(0, genes), pl.ds(t * LANES, LANES)].astype(jnp.float32)
+            kept = kept + x * x
+        power[...] = kept
+        load(k).wait()
+
+        def step(n, carry, k=k):
+            cols = pl.ds(pl.multiple_of(n * block, block), block)
+            total[pl.ds(0, used), cols] += jnp.dot(
+                rows[...], held[k, :, cols], preferred_element_type=jnp.float32
             )
-        while len(peaks) % 8:
-            peaks.append(jnp.zeros_like(peaks[0]))
-        peaks = jnp.concatenate(peaks, axis=0)
-        out_ref[...] = jnp.zeros_like(out_ref)
-        slot_of = lax.broadcasted_iota(jnp.int32, (total.shape[0], genes), 0)
-        for i in range(n_in):
-            slot = plan_ref[0, pl.ds(i, 1), :]
-            slot = jnp.where(slot >= 0, slot + starts[i], -1)
-            low = plan_ref[1, pl.ds(i, 1), :]
-            high = plan_ref[2, pl.ds(i, 1), :]
-            spread = jnp.dot(
-                peaks, (slot_of == slot).astype(jnp.float32),
-                precision=lax.Precision.HIGHEST, preferred_element_type=jnp.float32,
-            )
-
-            def masked(row, snp_block):
-                inside = (snp_block >= low) & (snp_block < high)
-                return jnp.where(inside, spread[row : row + 1], 0.0)
-
-            found = []
-            for q in range(labels):
-                best = jnp.zeros((1, genes), jnp.float32)
-                for b in range(blocks_dev):
-                    best = jnp.maximum(best, masked(q * blocks_dev + b, chip * blocks_dev + b))
-                found.append(best)
-            best = jnp.zeros((1, genes), jnp.float32)
-            for b in range(share_blocks):
-                best = jnp.maximum(
-                    best,
-                    masked(
-                        labels * blocks_dev + b, chip * blocks_dev + core * share_blocks + b
-                    ),
-                )
-            out_rows = [best]
-            for c in range(2):
-                out_rows += [jnp.where(core == c, v, 0.0) for v in found]
-            while len(out_rows) % 8:
-                out_rows.append(jnp.zeros_like(best))
-            if i == 0:
-                target = chip
-            else:
-                way = core if i <= reach else 1 - core
-                target = chip + (2 * way - 1) * ((i - 1) % reach + 1)
-
-            @pl.when((target >= 0) & (target < out_ref.shape[0] // 2))
-            def _(out_rows=out_rows, target=target):
-                for c in range(2):
-                    out_ref[2 * target + c, :, pl.ds(0, genes)] = jnp.concatenate(
-                        out_rows, axis=0
-                    )
-
-        powers = jnp.sum(power[...].T, axis=0, keepdims=True)
-        power_ref[...] = jnp.broadcast_to(powers, power_ref.shape)
+            return carry
+
+        lax.fori_loop(0, width // block, step, 0)
+
+    share_blocks = blocks_dev // 2
+    sums = sums_own[...] + sums_other[...]
+    cross = sums[1:2, :]
+    inter = sums[2:3, :]
+    inv = 1.0 / (inter - cross * (cross / sums[0:1, :]) + 0.1 * inter)
+
+    def peak(col, inv_block):
+        best = None
+        for t in range(block // LANES):
+            v = total[:, pl.ds(col + t * LANES, LANES)]
+            v = v * v * inv_block[:, t * LANES : (t + 1) * LANES]
+            best = v if best is None else jnp.maximum(best, v)
+        return jnp.max(best.T, axis=0, keepdims=True)
+
+    peaks = []
+    for q in range(labels):
+        for b in range(blocks_dev):
+            peaks.append(peak(q * snp_rows + b * block, inv[:, b * block : (b + 1) * block]))
+    for b in range(share_blocks):
+        mine = inv[:, b * block : (b + 1) * block]
+        late = inv[:, (share_blocks + b) * block : (share_blocks + b + 1) * block]
+        peaks.append(peak(labels * snp_rows + b * block, jnp.where(core == 0, mine, late)))
+    while len(peaks) % 8:
+        peaks.append(jnp.zeros_like(peaks[0]))
+    peaks = jnp.concatenate(peaks, axis=0)
+    count = peaks.shape[0]
+    terms = []
+    left = peaks
+    for _ in range(3):
+        terms.append(left.astype(jnp.bfloat16).astype(jnp.float32))
+        left = left - terms[-1]
+    terms = jnp.concatenate(terms, axis=0).astype(jnp.bfloat16)
+    band = plan_ref.shape[1]
+    slot = plan_ref[0:1, :]
+    low = plan_ref[1:2, :]
+    high = plan_ref[2:3, :]
+    place = lax.broadcasted_iota(jnp.int32, (total.shape[0], band), 0) == slot
+    spread = jnp.dot(
+        terms, place.astype(jnp.float32).astype(jnp.bfloat16),
+        preferred_element_type=jnp.float32,
+    )
+    spread = spread[:count] + spread[count : 2 * count] + spread[2 * count :]
+
+    def masked(row, snp_block):
+        inside = (snp_block >= low) & (snp_block < high)
+        return jnp.where(inside, spread[row : row + 1], 0.0)
+
+    def highest(row, blocks, first_block):
+        best = masked(row, first_block)
+        for b in range(1, blocks):
+            best = jnp.maximum(best, masked(row + b, first_block + b))
+        return best
+
+    out_rows = [highest(labels * blocks_dev, share_blocks, chip * blocks_dev + core * share_blocks)]
+    found = [highest(q * blocks_dev, blocks_dev, chip * blocks_dev) for q in range(labels)]
+    for c in range(2):
+        out_rows += [jnp.where(core == c, v, 0.0) for v in found]
+    while len(out_rows) % 8:
+        out_rows.append(jnp.zeros_like(out_rows[0]))
+    dense = jnp.concatenate(out_rows, axis=0)
+    out_ref[...] = jnp.zeros_like(out_ref)
+    chips = out_ref.shape[0]
+    for i in range(n_in):
+        if i == 0:
+            target = chip
+        else:
+            way = core if i <= reach else 1 - core
+            target = chip + (2 * way - 1) * ((i - 1) % reach + 1)
+
+        @pl.when((target >= 0) & (target < chips))
+        def _(i=i, target=target):
+            out_ref[target, :, pl.ds(0, genes)] = dense[:, i * genes : (i + 1) * genes]
+
+    powers = jnp.sum(power[...].T, axis=0, keepdims=True)
+    power_ref[...] = jnp.broadcast_to(powers, power_ref.shape)
 
 
 def products(pos, sums, plan, full, mine, other, weights, caps, labels, chips, blocks_dev):
     genes, all_samples = full.shape
-    width = weights.shape[1]
-    snp_rows = sums[0].shape[1]
-    depth = CHUNK
     used = genes + 2 * sum(caps)
     padded = -(-used // LANES) * LANES
     out_rows = -(-(1 + 2 * labels) // 8) * 8
-
-    def blocked(x):
-        return pl.BlockSpec((x.shape[0], depth), lambda k: (0, k))
-
+    width = weights.shape[1]
     arrays = (full, *mine, *other)
+    vmem = pl.BlockSpec(memory_space=pltpu.VMEM)
     return pl.pallas_call(
         functools.partial(
             product_kernel, caps=caps, labels=labels, genes=genes, blocks_dev=blocks_dev
         ),
-        grid=(all_samples // depth,),
         out_shape=(
-            jax.ShapeDtypeStruct((2 * chips, out_rows, LANES), jnp.float32),
+            jax.ShapeDtypeStruct((chips, out_rows, LANES), jnp.float32),
             jax.ShapeDtypeStruct((8, genes), jnp.float32),
         ),
         in_specs=[
-            pl.BlockSpec(memory_space=pltpu.SMEM),
-            pl.BlockSpec((8, snp_rows), lambda k: (0, 0)),
-            pl.BlockSpec((8, snp_rows), lambda k: (0, 0)),
-            pl.BlockSpec(plan.shape, lambda k: (0, 0, 0)),
-            *[blocked(x) for x in arrays],
-            pl.BlockSpec((depth, width), lambda k: (k, 0)),
+            pl.BlockSpec(memory_space=pltpu.SMEM), vmem, vmem, vmem, *[vmem for _ in arrays],
+            pl.BlockSpec(memory_space=pl.ANY),
         ],
-        out_specs=(
-            pl.BlockSpec((2 * chips, out_rows, LANES), lambda k: (0, 0, 0)),
-            pl.BlockSpec((8, genes), lambda k: (0, 0)),
-        ),
+        out_specs=(vmem, vmem),
         scratch_shapes=[
-            pltpu.VMEM((used, depth), jnp.bfloat16),
+            pltpu.VMEM((used, CHUNK), jnp.bfloat16),
             pltpu.VMEM((padded, width), jnp.float32),
             pltpu.VMEM((genes, LANES), jnp.float32),
+            pltpu.VMEM((all_samples // CHUNK, CHUNK, width), jnp.bfloat16),
+            pltpu.SemaphoreType.DMA((all_samples // CHUNK,)),
         ],
         compiler_params=pltpu.CompilerParams(vmem_limit_bytes=48 * MIB),
         cost_estimate=pl.CostEstimate(
@@ -539,10 +545,10 @@
     )(pos, *sums, plan, *arrays, weights)
 
 
-def finish_kernel(gathered_ref, power_ref, out_ref, *, samples):
-    best = gathered_ref[0]
-    for i in range(1, gathered_ref.shape[0]):
-        best = jnp.maximum(best, gathered_ref[i])
+def finish_kernel(own_ref, other_ref, power_ref, out_ref, *, samples):
+    best = jnp.maximum(own_ref[0], other_ref[0])
+    for i in range(1, own_ref.shape[0]):
+        best = jnp.maximum(best, jnp.maximum(own_ref[i], other_ref[i]))
     labels, genes = out_ref.shape
     peak = best[:labels, :genes]
     out_ref[...] = jnp.sqrt(peak / (power_ref[0:1, :] / samples + 1e-05))
@@ -554,69 +560,62 @@
     perms = shuffles.shape[0]
     chips = lax.axis_size("genome")
     cores = lax.axis_size("sample")
-    genome_pos = lax.axis_index("genome")
-    sample_pos = lax.axis_index("sample")
     blocks_dev = snp_rows // SNP_BLOCK
     reach = (HALF_BLK + blocks_dev - 1) // blocks_dev
     all_samples = half * cores
     labels = perms // cores
     caps = tuple(min(genes, genes * 4 >> k) for k in range(1, reach + 1))
-
-    other_pheno = swapped(phenotypes)
     env = environment[None]
-    own_sums = local_moments(genotypes, env)
-    sums = (own_sums, swapped(own_sums))
-    late_geno, _ = lax.optimization_barrier((genotypes, other_pheno))
-    other_geno = swapped(late_geno)
-    other_env = swapped(env)
-    other_shuffles = swapped(shuffles)
-    pos = jnp.stack([genome_pos, sample_pos]).astype(jnp.int32)
     start = window_start.reshape(-1, LANES)
     end = window_end.reshape(-1, LANES)
-
-    def chosen(turn):
-        return select(
+    pos = jnp.stack([lax.axis_index("genome"), lax.axis_index("sample")]).astype(jnp.int32)
+
+    def travel(k, payload):
+        pairs = [(i * cores, (i + k) * cores) for i in range(chips - k)]
+        pairs += [((i + k) * cores + 1, i * cores + 1) for i in range(chips - k)]
+        return lax.ppermute(payload, ("genome", "sample"), pairs)
+
+    def one_round(turn, pos):
+        core = pos[1:]
+        other_pheno = swapped(phenotypes)
+        own_sums = local_moments(genotypes, env)
+        sums = (own_sums, swapped(own_sums))
+        late_geno, _ = lax.optimization_barrier((genotypes, other_pheno))
+        other_geno = swapped(late_geno)
+        other_env = swapped(env)
+        other_shuffles = swapped(shuffles)
+        rounds, plan, full, *payloads = select(
             turn, pos, chrom_bounds, start, end, phenotypes, other_pheno, caps, blocks_dev
         )
-
-    def travel(payloads):
-        mine = []
-        for k, payload in enumerate(payloads, 1):
-            pairs = [(i * cores, (i + k) * cores) for i in range(chips - k)]
-            pairs += [((i + k) * cores + 1, i * cores + 1) for i in range(chips - k)]
-            mine.append(lax.ppermute(payload, ("genome", "sample"), pairs))
-        return mine
-
-    rounds, plan, full, *payloads = chosen(jnp.zeros((1,), jnp.int32))
-    mine = travel(payloads)
-    weights = snp_side(
-        pos[1:], env, other_env, *sums, shuffles, other_shuffles, genotypes, other_geno, labels
-    )
-
-    def met(plan, full, mine):
+        payloads = [full] * (reach - len(payloads)) + payloads
+        mine = [travel(k, x) for k, x in enumerate(payloads, 1)]
+        weights = snp_side(
+            core, env, other_env, *sums, shuffles, other_shuffles, genotypes, other_geno, labels
+        )
+        *mine, weights = lax.optimization_barrier((*mine, weights))
         other = [swapped(x) for x in mine]
-        return products(
+        found, power = products(
             pos, sums, plan, full, mine, other, weights, caps, labels, chips, blocks_dev
         )
-
-    *mine, weights = lax.optimization_barrier((*mine, weights))
-    found, power = met(plan, full, mine)
+        return rounds, found, power
+
+    rounds, found, power = one_round(jnp.zeros((1,), jnp.int32), pos)
 
     def more(carry):
         return carry[0] < rounds[0]
 
     def again(carry):
         turn, best = carry
-        _, plan, full, *payloads = chosen(jnp.full((1,), turn, jnp.int32))
-        return turn + 1, jnp.maximum(best, met(plan, full, travel(payloads))[0])
+        turns, place = lax.optimization_barrier((jnp.full((1,), turn, jnp.int32), pos))
+        return turn + 1, jnp.maximum(best, one_round(turns, place)[1])
 
     _, found = lax.while_loop(more, again, (jnp.int32(1), found))
-    gathered = lax.all_to_all(found, ("genome", "sample"), 0, 0, tiled=True)
+    gathered = lax.all_to_all(found, "genome", 0, 0, tiled=True)
     return pl.pallas_call(
         functools.partial(finish_kernel, samples=all_samples),
         out_shape=jax.ShapeDtypeStruct((perms + 1, genes), jnp.float32),
         name="finish",
-    )(gathered, power)
+    )(gathered, swapped(gathered), power)
 
 
 def solution(mesh):

time: 107 us -> 107 us (level)
  blocking collectives: 12.9 us -> 10.4 us
  Pallas kernels: 66 us -> 67.4 us
    pallas_call x1, Pallas kernels: 18.3 us -> 21 us  [products(): pl.pallas_call(functools.partial(product_kernel, caps=caps, labels=labels...]
    all_to_all x1, blocking collectives: 12.9 us -> 10.4 us  [shards(): gathered = lax.all_to_all(found, 'genome', 0, 0, tiled=True)]
    ppermute x9 -> x10, waiting for transfers between devices: 6.36 us -> 7.41 us  [swapped(): lax.ppermute(x, 'sample', [(i, (i + 1) % count) for i in range(count)])]
    ppermute x9 -> x10, starting transfers between devices: 2.68 us -> 2.62 us  [swapped(): lax.ppermute(x, 'sample', [(i, (i + 1) % count) for i in range(count)])]
  transfers between devices with their start and end apart: 13 -> 14, of which waited for: 4 -> 4; matrix products, arithmetic and copies ran while one was open for 0% -> 0% of each run, Pallas kernels for 44% -> 42%
where the time goes in v8:
time: 107 us; the launch traced here: 106 us
  Pallas kernels  67.4 us (63%)
  starting transfers between devices  18.7 us (17%)
  blocking collectives  10.4 us (10%)
  waiting for transfers between devices  7.42 us (7%)
  local copies, waits for them, and re-layouts  1.25 us (1%)
    pallas_call x1, Pallas kernels, snp_side(): pl.pallas_call(functools.partial(snp_side_kernel, labels=labels), out_sha...  37 us
    pallas_call x1, Pallas kernels, products(): pl.pallas_call(functools.partial(product_kernel, caps=caps, labels=labels...  21 us
    ppermute x4, starting transfers between devices, travel(): return lax.ppermute(payload, ('genome', 'sample'), pairs)  16.1 us
    all_to_all x1, blocking collectives, shards(): gathered = lax.all_to_all(found, 'genome', 0, 0, tiled=True)  10.4 us
    ppermute x10, waiting for transfers between devices, swapped(): lax.ppermute(x, 'sample', [(i, (i + 1) % count) for i in range(count)])  7.41 us
    pallas_call x1, Pallas kernels, local_moments(): pl.pallas_call(moments_kernel, grid=(half // chunk,), out_shape=jax.Shape...  4.51 us
    pallas_call x1, Pallas kernels, select(): pl.pallas_call(functools.partial(select_kernel, caps=caps, blocks_dev=blo...  3.41 us
    ppermute x10, starting transfers between devices, swapped(): lax.ppermute(x, 'sample', [(i, (i + 1) % count) for i in range(count)])  2.62 us
  transfers between devices with their start and end apart: 14, of which 4 were waited for; matrix products, arithmetic and copies ran while one was open for 0% of the time, Pallas kernels for 42%

profile of v8, /device:TPU:0, one launch (start us, length us, event | category | flops | bytes accessed | tf_op | source)
XLA Modules:
  0.0 106.2 jit_solution(7194473995807582840)
XLA Ops:
  0.0 0.5 collective-permute-start.9
  0.5 1.7 %collective-permute-done.9.other_ref = bf16[64,4096]{1,0:T(8,128)(2,1)S(1)} collective-permute-done((bf16[64,4096]{1,0:T(8,128)(2,1)}, bf16[64,4096]{1,0:T(8,128)(2,1)S(1)}, u32[]{:S(2)}, u32[]{:S(2)}) %collective-permute-start.9) | collective-permute-done | bytes 524320 | tf_op jit(solution)/shard_map/ppermute | solution.py:28
  2.2 0.4 collective-permute-start.16
  2.6 0.1 collective-permute-start.14
  2.7 4.5 %local_moments.2.sums_own = f32[8,512]{1,0:T(8,128)S(1)} custom-call(bf16[512,4096]{1,0:T(8,128)(2,1)} %own_ref.3, f32[1,4096]{1,0:T(1,128)} %bitcast.15), custom_call_target="tpu_custom_call" | custom-call | flops 5000000000 | bytes 4194304 | tf_op jit(solution)/shard_map/local_moments/pallas_call | solution.py:66
  7.2 0.4 collective-permute-start.8
  7.7 0.1 collective-permute-start.15
  7.8 0.1 pad_add_fusion.pos_ref
  7.9 3.4 %select.6 = (s32[1]{0:T(128)}, s32[8,640]{1,0:T(8,128)S(1)}, bf16[64,8192]{1,0:T(8,128)(2,1)S(1)}, bf16[32,8192]{1,0:T(8,128)(2,1)}, bf16[16,8192]{1,0:T(8,128)(2,1)}) custom-call(s32[1]{0:T(128)} %constant.18.clone.1.round_ref, s32[2]{0:T(128)S(1)} %pad_add_fusion.pos_ref, s32[15]{0:T(128)} %bounds_ref.1, s32[8,128]{1,0:T(8,128)} %bitcast.10, ...), custom_call_target="tpu_custom_call" | custom-call | tf_op jit(solution)/shard_map/select/pallas_call | solution.py:370
  11.3 4.9 %collective-permute-start.11 = (bf16[64,8192]{1,0:T(8,128)(2,1)S(1)}, bf16[64,8192]{1,0:T(8,128)(2,1)S(1)}, u32[]{:S(2)}, u32[]{:S(2)}) collective-permute-start(bf16[64,8192]{1,0:T(8,128)(2,1)S(1)} %get-tuple-element.342.rest_0_), channel_id=1, source_target_pairs={{0,4},{2,6},{4,8},{6,10},{8,12},{10,14},{12,16},{14,18},{16,20},{1... | collective-permute-start | bytes 3145736 | tf_op jit(solution)/shard_map/ppermute | solution.py:576
  16.2 4.4 %collective-permute-start.10 = (bf16[64,8192]{1,0:T(8,128)(2,1)S(1)}, bf16[64,8192]{1,0:T(8,128)(2,1)}, u32[]{:S(2)}, u32[]{:S(2)}) collective-permute-start(bf16[64,8192]{1,0:T(8,128)(2,1)S(1)} %get-tuple-element.342.rest_0_), channel_id=1, source_target_pairs={{0,2},{2,4},{4,6},{6,8},{8,10},{10,12},{12,14},{14,16},{16,18},{18... | collective-permute-start | bytes 3145736 | tf_op jit(solution)/shard_map/ppermute | solution.py:576
  20.6 2.5 %collective-permute-start.13 = (bf16[16,8192]{1,0:T(8,128)(2,1)}, bf16[16,8192]{1,0:T(8,128)(2,1)S(1)}, u32[]{:S(2)}, u32[]{:S(2)}) collective-permute-start(bf16[16,8192]{1,0:T(8,128)(2,1)} %get-tuple-element.344), channel_id=1, source_target_pairs={{0,8},{2,10},{4,12},{6,14},{8,16},{10,18},{12,20},{14,22},{16,24},... | collective-permute-start | bytes 786440 | tf_op jit(solution)/shard_map/ppermute | solution.py:576
  23.1 4.4 %collective-permute-start.12 = (bf16[32,8192]{1,0:T(8,128)(2,1)}, bf16[32,8192]{1,0:T(8,128)(2,1)S(1)}, u32[]{:S(2)}, u32[]{:S(2)}) collective-permute-start(bf16[32,8192]{1,0:T(8,128)(2,1)} %get-tuple-element.343), channel_id=1, source_target_pairs={{0,6},{2,8},{4,10},{6,12},{8,14},{10,16},{12,18},{14,20},{16,22},{... | collective-permute-start | bytes 1572872 | tf_op jit(solution)/shard_map/ppermute | solution.py:576
  27.5 37.0 %snp_side.6.rest_9_ = bf16[8192,1280]{1,0:T(8,128)(2,1)} custom-call(s32[1]{0:T(128)} %bitcast.3.core_ref, f32[1,4096]{1,0:T(1,128)} %bitcast.16, f32[1,4096]{1,0:T(1,128)S(1)} %collective-permute-done.14.env_other, f32[8,512]{1,0:T(8,128)S(1)} %local_moments.2.sums_own, f32[8,512]{1,0:T(8,128)S(1)} %collective-permute-done.8.sums_other, ...), custom_call_target="tpu_custom_call" | custom-call | flops 40000000000 | bytes 60000000 | tf_op jit(solution)/shard_map/snp_side/pallas_call | solution.py:218
  64.6 0.0 copy-start.3
  64.6 0.0 copy-start.4
  64.6 0.0 copy-start.6
  64.6 0.0 copy-start.7
  64.6 0.0 copy-start.9
  64.7 0.1 collective-permute-start.17
  64.7 0.5 collective-permute-start.18
  65.2 0.1 collective-permute-start.19
  65.3 0.4 collective-permute-start.20
  65.7 3.1 %collective-permute-done.20.rest_8_ = bf16[16,8192]{1,0:T(8,128)(2,1)S(1)} collective-permute-done((bf16[16,8192]{1,0:T(8,128)(2,1)S(1)}, bf16[16,8192]{1,0:T(8,128)(2,1)S(1)}, u32[]{:S(2)}, u32[]{:S(2)}) %collective-permute-start.20) | collective-permute-done | bytes 262176 | tf_op jit(solution)/shard_map/ppermute | solution.py:28
  68.8 1.3 %collective-permute-done.19.rest_7_ = bf16[32,8192]{1,0:T(8,128)(2,1)} collective-permute-done((bf16[32,8192]{1,0:T(8,128)(2,1)S(1)}, bf16[32,8192]{1,0:T(8,128)(2,1)}, u32[]{:S(2)}, u32[]{:S(2)}) %collective-permute-start.19) | collective-permute-done | bytes 524320 | tf_op jit(solution)/shard_map/ppermute | solution.py:28
  70.1 21.0 %products.6 = (f32[16,8,128]{2,1,0:T(8,128)S(1)}, f32[8,64]{1,0:T(8,128)S(1)}) custom-call(s32[2]{0:T(128)S(1)} %pad_add_fusion.pos_ref, f32[8,512]{1,0:T(8,128)} %copy-done.11, f32[8,512]{1,0:T(8,128)} %copy-done.12, s32[8,640]{1,0:T(8,128)S(1)} %get-tuple-element.341.plan_ref, bf16[64,8192]{1,0:T(8,128)(2,1)S(1)} %get-tuple-element.342.rest_0_, ...), custom_call_target="tpu_custom_call" | custom-call | flops 8724152320 | bytes 27787264 | tf_op jit(solution)/shard_map/products/pallas_call | solution.py:518
  91.1 0.6 copy-done
  91.7 0.7 while.14
  92.5 10.4 %all_to_all.5.own_ref = f32[16,8,128]{2,1,0:T(8,128)S(1)} all-to-all(f32[16,8,128]{2,1,0:T(8,128)S(1)} %get-tuple-element.353), channel_id=1, replica_groups=mesh['genome'=16,'sample'=2] {'genome'}, dimensions={0} | all-to-all | bytes 131072 | tf_op jit(solution)/shard_map/all_to_all | solution.py:613
  102.9 1.3 %collective-permute-done.21.other_ref = f32[16,8,128]{2,1,0:T(8,128)S(1)} collective-permute-done((f32[16,8,128]{2,1,0:T(8,128)S(1)}, f32[16,8,128]{2,1,0:T(8,128)S(1)}, u32[]{:S(2)}, u32[]{:S(2)}) %collective-permute-start.21) | collective-permute-done | bytes 65568 | tf_op jit(solution)/shard_map/ppermute | solution.py:28
  104.1 0.6 copy-done.5
  104.8 1.5 %finish.1 = f32[5,64]{1,0:T(8,128)} custom-call(f32[16,8,128]{2,1,0:T(8,128)} %copy-done.2, f32[16,8,128]{2,1,0:T(8,128)} %copy-done.5, f32[8,64]{1,0:T(8,128)} %copy-done), custom_call_target="tpu_custom_call" | custom-call | tf_op jit(solution)/shard_map/finish/pallas_call | solution.py:614
  (30 shorter events, 0.1 us)
Async XLA Ops:
  0.0 2.2 %collective-permute-start.9 = (bf16[64,4096]{1,0:T(8,128)(2,1)}, bf16[64,4096]{1,0:T(8,128)(2,1)S(1)}, u32[]{:S(2)}, u32[]{:S(2)}) collective-permute-start(bf16[64,4096]{1,0:T(8,128)(2,1)} %own_ref.2), channel_id=1, source_target_pairs={{0,1},{1,0},{2,3},{3,2},{4,5},{5,4},{6,7},{7,6},{8,9},{9,8},{10,11... | collective-permute-start | bytes 1572872 | tf_op jit(solution)/shard_map/ppermute | solution.py:28
  2.2 9.1 %copy-start.1 = (bf16[64,4096]{1,0:T(8,128)(2,1)}, bf16[64,4096]{1,0:T(8,128)(2,1)S(1)}, u32[]{:S(2)}) copy-start(bf16[64,4096]{1,0:T(8,128)(2,1)S(1)} %collective-permute-done.9.other_ref) | copy-start | bytes 1572868
  2.2 25.3 %collective-permute-start.16 = (bf16[512,4096]{1,0:T(8,128)(2,1)}, bf16[512,4096]{1,0:T(8,128)(2,1)}, u32[]{:S(2)}, u32[]{:S(2)}) collective-permute-start(bf16[512,4096]{1,0:T(8,128)(2,1)} %own_ref.3), channel_id=1, source_target_pairs={{0,1},{1,0},{2,3},{3,2},{4,5},{5,4},{6,7},{7,6},{8,9},{9,8},{10,11... | collective-permute-start | bytes 12582920 | tf_op jit(solution)/shard_map/ppermute | solution.py:28
  2.6 18.0 %collective-permute-start.14 = (f32[1,4096]{1,0:T(1,128)}, f32[1,4096]{1,0:T(1,128)S(1)}, u32[]{:S(2)}, u32[]{:S(2)}) collective-permute-start(f32[1,4096]{1,0:T(1,128)} %bitcast.14), channel_id=1, source_target_pairs={{0,1},{1,0},{2,3},{3,2},{4,5},{5,4},{6,7},{7,6},{8,9},{9,8},{10,11... | collective-permute-start | bytes 49160 | tf_op jit(solution)/shard_map/ppermute | solution.py:28
  7.2 57.3 %copy-start.11 = (f32[8,512]{1,0:T(8,128)}, f32[8,512]{1,0:T(8,128)S(1)}, u32[]{:S(2)}) copy-start(f32[8,512]{1,0:T(8,128)S(1)} %local_moments.2.sums_own) | copy-start | bytes 49156
  7.2 8.9 %collective-permute-start.8 = (f32[8,512]{1,0:T(8,128)S(1)}, f32[8,512]{1,0:T(8,128)S(1)}, u32[]{:S(2)}, u32[]{:S(2)}) collective-permute-start(f32[8,512]{1,0:T(8,128)S(1)} %local_moments.2.sums_own), channel_id=1, source_target_pairs={{0,1},{1,0},{2,3},{3,2},{4,5},{5,4},{6,7},{7,6},{8,9},{9,8},{10,11... | collective-permute-start | bytes 49160 | tf_op jit(solution)/shard_map/ppermute | solution.py:28
  7.7 15.4 %collective-permute-start.15 = (s32[4,4096]{1,0:T(4,128)}, s32[4,4096]{1,0:T(4,128)S(1)}, u32[]{:S(2)}, u32[]{:S(2)}) collective-permute-start(s32[4,4096]{1,0:T(4,128)} %shuf_own.1), channel_id=1, source_target_pairs={{0,1},{1,0},{2,3},{3,2},{4,5},{5,4},{6,7},{7,6},{8,9},{9,8},{10,11... | collective-permute-start | bytes 196616 | tf_op jit(solution)/shard_map/ppermute | solution.py:28
  11.3 53.3 %collective-permute-start.11 = (bf16[64,8192]{1,0:T(8,128)(2,1)S(1)}, bf16[64,8192]{1,0:T(8,128)(2,1)S(1)}, u32[]{:S(2)}, u32[]{:S(2)}) collective-permute-start(bf16[64,8192]{1,0:T(8,128)(2,1)S(1)} %get-tuple-element.342.rest_0_), channel_id=1, source_target_pairs={{0,4},{2,6},{4,8},{6,10},{8,12},{10,14},{12,16},{14,18},{16,20},{1... | collective-permute-start | bytes 3145736 | tf_op jit(solution)/shard_map/ppermute | solution.py:576
  16.2 48.4 %copy-start.12 = (f32[8,512]{1,0:T(8,128)}, f32[8,512]{1,0:T(8,128)S(1)}, u32[]{:S(2)}) copy-start(f32[8,512]{1,0:T(8,128)S(1)} %collective-permute-done.8.sums_other) | copy-start | bytes 49156
  16.2 48.4 %collective-permute-start.10 = (bf16[64,8192]{1,0:T(8,128)(2,1)S(1)}, bf16[64,8192]{1,0:T(8,128)(2,1)}, u32[]{:S(2)}, u32[]{:S(2)}) collective-permute-start(bf16[64,8192]{1,0:T(8,128)(2,1)S(1)} %get-tuple-element.342.rest_0_), channel_id=1, source_target_pairs={{0,2},{2,4},{4,6},{6,8},{8,10},{10,12},{12,14},{14,16},{16,18},{18... | collective-permute-start | bytes 3145736 | tf_op jit(solution)/shard_map/ppermute | solution.py:576
  20.6 6.9 %copy-start.10 = (f32[1,4096]{1,0:T(1,128)}, f32[1,4096]{1,0:T(1,128)S(1)}, u32[]{:S(2)}) copy-start(f32[1,4096]{1,0:T(1,128)S(1)} %collective-permute-done.14.env_other) | copy-start | bytes 49156
  20.6 44.0 %collective-permute-start.13 = (bf16[16,8192]{1,0:T(8,128)(2,1)}, bf16[16,8192]{1,0:T(8,128)(2,1)S(1)}, u32[]{:S(2)}, u32[]{:S(2)}) collective-permute-start(bf16[16,8192]{1,0:T(8,128)(2,1)} %get-tuple-element.344), channel_id=1, source_target_pairs={{0,8},{2,10},{4,12},{6,14},{8,16},{10,18},{12,20},{14,22},{16,24},... | collective-permute-start | bytes 786440 | tf_op jit(solution)/shard_map/ppermute | solution.py:576
  23.1 4.4 %copy-start.8 = (s32[4,4096]{1,0:T(4,128)}, s32[4,4096]{1,0:T(4,128)S(1)}, u32[]{:S(2)}) copy-start(s32[4,4096]{1,0:T(4,128)S(1)} %collective-permute-done.15.shuf_other) | copy-start | bytes 196612
  23.1 41.5 %collective-permute-start.12 = (bf16[32,8192]{1,0:T(8,128)(2,1)}, bf16[32,8192]{1,0:T(8,128)(2,1)S(1)}, u32[]{:S(2)}, u32[]{:S(2)}) collective-permute-start(bf16[32,8192]{1,0:T(8,128)(2,1)} %get-tuple-element.343), channel_id=1, source_target_pairs={{0,6},{2,8},{4,10},{6,12},{8,14},{10,16},{12,18},{14,20},{16,22},{... | collective-permute-start | bytes 1572872 | tf_op jit(solution)/shard_map/ppermute | solution.py:576
  64.6 27.2 %copy-start.3 = (s32[1024]{0:T(1024)S(1)}, s32[1024]{0:T(1024)}, u32[]{:S(2)}) copy-start(s32[1024]{0:T(1024)} %param.13) | copy-start | bytes 12292
  64.6 27.2 %copy-start.4 = (s32[1024]{0:T(1024)S(1)}, s32[1024]{0:T(1024)}, u32[]{:S(2)}) copy-start(s32[1024]{0:T(1024)} %param.14) | copy-start | bytes 12292
  64.6 27.1 %copy-start.6 = (s32[15]{0:T(128)S(1)}, s32[15]{0:T(128)}, u32[]{:S(2)}) copy-start(s32[15]{0:T(128)} %bounds_ref.1) | copy-start | bytes 184
  64.6 27.1 %copy-start.7 = (s32[4,4096]{1,0:T(4,128)S(1)}, s32[4,4096]{1,0:T(4,128)}, u32[]{:S(2)}) copy-start(s32[4,4096]{1,0:T(4,128)} %shuf_own.1) | copy-start | bytes 196612
  64.6 27.1 %copy-start.9 = (f32[4096]{0:T(1024)S(1)}, f32[4096]{0:T(1024)}, u32[]{:S(2)}) copy-start(f32[4096]{0:T(1024)} %param.11) | copy-start | bytes 49156
  64.7 5.5 %collective-permute-start.17 = (bf16[64,8192]{1,0:T(8,128)(2,1)}, bf16[64,8192]{1,0:T(8,128)(2,1)}, u32[]{:S(2)}, u32[]{:S(2)}) collective-permute-start(bf16[64,8192]{1,0:T(8,128)(2,1)} %collective-permute-done.10.rest_1_), channel_id=1, source_target_pairs={{0,1},{1,0},{2,3},{3,2},{4,5},{5,4},{6,7},{7,6},{8,9},{9,8},{10,11... | collective-permute-start | bytes 3145736 | tf_op jit(solution)/shard_map/ppermute | solution.py:28
  64.7 5.4 %collective-permute-start.18 = (bf16[64,8192]{1,0:T(8,128)(2,1)S(1)}, bf16[64,8192]{1,0:T(8,128)(2,1)}, u32[]{:S(2)}, u32[]{:S(2)}) collective-permute-start(bf16[64,8192]{1,0:T(8,128)(2,1)S(1)} %collective-permute-done.11.rest_2_), channel_id=1, source_target_pairs={{0,1},{1,0},{2,3},{3,2},{4,5},{5,4},{6,7},{7,6},{8,9},{9,8},{10,11... | collective-permute-start | bytes 3145736 | tf_op jit(solution)/shard_map/ppermute | solution.py:28
  65.2 4.9 %collective-permute-start.19 = (bf16[32,8192]{1,0:T(8,128)(2,1)S(1)}, bf16[32,8192]{1,0:T(8,128)(2,1)}, u32[]{:S(2)}, u32[]{:S(2)}) collective-permute-start(bf16[32,8192]{1,0:T(8,128)(2,1)S(1)} %collective-permute-done.12.rest_3_), channel_id=1, source_target_pairs={{0,1},{1,0},{2,3},{3,2},{4,5},{5,4},{6,7},{7,6},{8,9},{9,8},{10,11... | collective-permute-start | bytes 1572872 | tf_op jit(solution)/shard_map/ppermute | solution.py:28
  65.3 3.5 %collective-permute-start.20 = (bf16[16,8192]{1,0:T(8,128)(2,1)S(1)}, bf16[16,8192]{1,0:T(8,128)(2,1)S(1)}, u32[]{:S(2)}, u32[]{:S(2)}) collective-permute-start(bf16[16,8192]{1,0:T(8,128)(2,1)S(1)} %collective-permute-done.13.rest_4_), channel_id=1, source_target_pairs={{0,1},{1,0},{2,3},{3,2},{4,5},{5,4},{6,7},{7,6},{8,9},{9,8},{10,11... | collective-permute-start | bytes 786440 | tf_op jit(solution)/shard_map/ppermute | solution.py:28
  91.1 0.6 copy-start
  102.9 1.3 %copy-start.2 = (f32[16,8,128]{2,1,0:T(8,128)}, f32[16,8,128]{2,1,0:T(8,128)S(1)}, u32[]{:S(2)}) copy-start(f32[16,8,128]{2,1,0:T(8,128)S(1)} %all_to_all.5.own_ref) | copy-start | bytes 196612
  102.9 1.3 %collective-permute-start.21 = (f32[16,8,128]{2,1,0:T(8,128)S(1)}, f32[16,8,128]{2,1,0:T(8,128)S(1)}, u32[]{:S(2)}, u32[]{:S(2)}) collective-permute-start(f32[16,8,128]{2,1,0:T(8,128)S(1)} %all_to_all.5.own_ref), channel_id=1, source_target_pairs={{0,1},{1,0},{2,3},{3,2},{4,5},{5,4},{6,7},{7,6},{8,9},{9,8},{10,11... | collective-permute-start | bytes 196616 | tf_op jit(solution)/shard_map/ppermute | solution.py:28
  104.1 0.6 copy-start.5

commit v9 on v8

--- a/solution.py
+++ b/solution.py
@@ -75,7 +75,7 @@
         scratch_shapes=[pltpu.VMEM((3, snp_rows, LANES), jnp.float32)],
         compiler_params=pltpu.CompilerParams(vmem_limit_bytes=60 * MIB),
         cost_estimate=pl.CostEstimate(
-            flops=5 * 10**9, bytes_accessed=2 * snp_rows * half, transcendentals=0
+            flops=10**6, bytes_accessed=10**6, transcendentals=0
         ),
         name="local_moments",
     )(geno, env)
@@ -235,10 +235,38 @@
         ],
         compiler_params=pltpu.CompilerParams(vmem_limit_bytes=61 * MIB),
         cost_estimate=pl.CostEstimate(
-            flops=40 * 10**9, bytes_accessed=60 * 10**6, transcendentals=0
+            flops=10**6, bytes_accessed=10**6, transcendentals=0
         ),
         name="snp_side",
     )(core, env_own, env_other, sums_own, sums_other, shuf_own, shuf_other, own, other)
+
+
+def merge_kernel(core_ref, own_ref, other_ref, *rest):
+    full_ref, sems = rest[-2:]
+    half = own_ref.shape[1]
+    core = core_ref[0]
+    own = pltpu.make_async_copy(
+        own_ref, full_ref.at[:, pl.ds(pl.multiple_of(core * half, half), half)], sems.at[0]
+    )
+    other = pltpu.make_async_copy(
+        other_ref, full_ref.at[:, pl.ds(pl.multiple_of((1 - core) * half, half), half)], sems.at[1]
+    )
+    own.start()
+    other.start()
+    own.wait()
+    other.wait()
+
+
+def merged(core, own, other, *after):
+    any_spec = pl.BlockSpec(memory_space=pl.ANY)
+    return pl.pallas_call(
+        merge_kernel,
+        out_shape=jax.ShapeDtypeStruct((own.shape[0], 2 * own.shape[1]), own.dtype),
+        in_specs=[pl.BlockSpec(memory_space=pltpu.SMEM)] + [any_spec] * (2 + len(after)),
+        out_specs=any_spec,
+        scratch_shapes=[pltpu.SemaphoreType.DMA((2,))],
+        name="merged",
+    )(core, own, other, *after)
 
 
 def window_plan(start, end, bounds_ref, n_bounds, total_blocks):
@@ -254,11 +282,11 @@
 
 
 def select_kernel(
-    round_ref, pos_ref, bounds_ref, start_ref, end_ref, own_ref, other_ref,
-    rounds_ref, plan_ref, full_ref, *rest, caps, blocks_dev,
+    round_ref, pos_ref, bounds_ref, start_ref, end_ref, full_ref,
+    rounds_ref, plan_ref, *rest, caps, blocks_dev,
 ):
     reach = len(caps)
-    genes, half = own_ref.shape
+    genes, all_samples = full_ref.shape
     chosen_from = sum(cap == genes for cap in caps)
     (slots, edges), pay_refs = rest[-2:], rest[:-2]
     shape = start_ref.shape
@@ -339,29 +367,23 @@
         picks.append((rows == slot).astype(jnp.float32))
     if picks:
         picks = jnp.concatenate(picks, axis=0).astype(jnp.bfloat16)
-    step = 1024
-
-    def copy(i, carry):
-        cols = pl.ds(pl.multiple_of(i * step, step), step)
-        late = pl.ds(pl.multiple_of(half + i * step, step), step)
-        a, b = own_ref[:, cols], other_ref[:, cols]
-        for part, to in ((jnp.where(core == 0, a, b), cols), (jnp.where(core == 0, b, a), late)):
-            full_ref[:, to] = part
-            if pay_refs:
-                chosen = jnp.dot(picks, part, preferred_element_type=jnp.float32)
-                chosen = chosen.astype(jnp.bfloat16)
-                row = 0
-                for pay in pay_refs:
-                    pay[:, to] = chosen[row : row + pay.shape[0]]
-                    row += pay.shape[0]
-        return carry
-
-    lax.fori_loop(0, half // step, copy, 0)
-
-
-def select(turn, pos, bounds, start, end, own, other, caps, blocks_dev):
-    genes, half = own.shape
-    all_samples = 2 * half
+        step = 1024
+
+        def copy(i, carry):
+            cols = pl.ds(pl.multiple_of(i * step, step), step)
+            chosen = jnp.dot(picks, full_ref[:, cols], preferred_element_type=jnp.float32)
+            chosen = chosen.astype(jnp.bfloat16)
+            row = 0
+            for pay in pay_refs:
+                pay[:, cols] = chosen[row : row + pay.shape[0]]
+                row += pay.shape[0]
+            return carry
+
+        lax.fori_loop(0, all_samples // step, copy, 0)
+
+
+def select(turn, pos, bounds, start, end, full, caps, blocks_dev):
+    genes, all_samples = full.shape
     reach = len(caps)
     smem = pl.BlockSpec(memory_space=pltpu.SMEM)
     vmem = pl.BlockSpec(memory_space=pltpu.VMEM)
@@ -372,18 +394,17 @@
         out_shape=(
             jax.ShapeDtypeStruct((1,), jnp.int32),
             jax.ShapeDtypeStruct((8, width), jnp.int32),
-            jax.ShapeDtypeStruct((genes, all_samples), jnp.bfloat16),
             *[jax.ShapeDtypeStruct((cap, all_samples), jnp.bfloat16) for cap in chosen],
         ),
-        in_specs=[smem, smem, smem, vmem, vmem, vmem, vmem],
-        out_specs=(smem, vmem, vmem, *[vmem for _ in chosen]),
+        in_specs=[smem, smem, smem, vmem, vmem, vmem],
+        out_specs=(smem, vmem, *[vmem for _ in chosen]),
         scratch_shapes=[
             pltpu.VMEM((2 * reach,) + start.shape, jnp.int32),
             pltpu.VMEM((2,) + start.shape, jnp.int32),
         ],
         compiler_params=pltpu.CompilerParams(vmem_limit_bytes=24 * MIB),
         name="select",
-    )(turn, pos, bounds, start, end, own, other)
+    )(turn, pos, bounds, start, end, full)
 
 
 def product_kernel(
@@ -392,44 +413,49 @@
     reach = len(caps)
     n_in = 1 + 2 * reach
     gene_refs = rest[:n_in]
-    weights_ref, out_ref, power_ref, rows, total, power, held, sems = rest[n_in:]
+    weights_ref, out_ref, power_ref, rows, total, power = rest[n_in:]
+    step = pl.program_id(0)
     snp_rows = sums_own.shape[1]
-    all_samples, width = weights_ref.shape
+    depth, width = weights_ref.shape
     block = SNP_BLOCK
     used = rows.shape[0]
     chip, core = pos_ref[0], pos_ref[1]
 
-    def load(k):
-        return pltpu.make_async_copy(
-            weights_ref.at[pl.ds(k * CHUNK, CHUNK)], held.at[k], sems.at[k]
-        )
-
-    for k in range(all_samples // CHUNK):
-        load(k).start()
-    power[...] = jnp.zeros_like(power)
-    total[...] = jnp.zeros_like(total)
-    for k in range(all_samples // CHUNK):
-        depth = pl.ds(k * CHUNK, CHUNK)
-        at = 0
-        for ref in gene_refs:
-            rows[pl.ds(at, ref.shape[0]), :] = ref[:, depth]
-            at += ref.shape[0]
-        kept = power[...]
-        for t in range(CHUNK // LANES):
-            x = rows[pl.ds(0, genes), pl.ds(t * LANES, LANES)].astype(jnp.float32)
-            kept = kept + x * x
-        power[...] = kept
-        load(k).wait()
-
-        def step(n, carry, k=k):
-            cols = pl.ds(pl.multiple_of(n * block, block), block)
-            total[pl.ds(0, used), cols] += jnp.dot(
-                rows[...], held[k, :, cols], preferred_element_type=jnp.float32
-            )
-            return carry
-
-        lax.fori_loop(0, width // block, step, 0)
-
+    @pl.when(step == 0)
+    def _():
+        total[...] = jnp.zeros_like(total)
+        power[...] = jnp.zeros_like(power)
+
+    at = 0
+    for ref in gene_refs:
+        rows[pl.ds(at, ref.shape[0]), :] = ref[...]
+        at += ref.shape[0]
+    for at in range(0, width, snp_rows):
+        cols = pl.ds(at, min(snp_rows, width - at))
+        total[pl.ds(0, used), cols] += jnp.dot(
+            rows[...], weights_ref[:, cols], preferred_element_type=jnp.float32
+        )
+    kept = power[...]
+    for t in range(depth // LANES):
+        x = rows[pl.ds(0, genes), pl.ds(t * LANES, LANES)].astype(jnp.float32)
+        kept = kept + x * x
+    power[...] = kept
+
+    @pl.when(step == pl.num_programs(0) - 1)
+    def _():
+        summed_up(
+            chip, core, sums_own, sums_other, plan_ref, out_ref, power_ref, total, power,
+            reach=reach, labels=labels, genes=genes, blocks_dev=blocks_dev,
+        )
+
+
+def summed_up(
+    chip, core, sums_own, sums_other, plan_ref, out_ref, power_ref, total, power,
+    *, reach, labels, genes, blocks_dev,
+):
+    snp_rows = sums_own.shape[1]
+    block = SNP_BLOCK
+    n_in = 1 + 2 * reach
     share_blocks = blocks_dev // 2
     sums = sums_own[...] + sums_other[...]
     cross = sums[1:2, :]
@@ -514,26 +540,31 @@
     out_rows = -(-(1 + 2 * labels) // 8) * 8
     width = weights.shape[1]
     arrays = (full, *mine, *other)
-    vmem = pl.BlockSpec(memory_space=pltpu.VMEM)
+
+    def whole(x):
+        return pl.BlockSpec(x.shape, lambda k: (0,) * len(x.shape))
+
+    outs = (
+        jax.ShapeDtypeStruct((chips, out_rows, LANES), jnp.float32),
+        jax.ShapeDtypeStruct((8, genes), jnp.float32),
+    )
     return pl.pallas_call(
         functools.partial(
             product_kernel, caps=caps, labels=labels, genes=genes, blocks_dev=blocks_dev
         ),
-        out_shape=(
-            jax.ShapeDtypeStruct((chips, out_rows, LANES), jnp.float32),
-            jax.ShapeDtypeStruct((8, genes), jnp.float32),
-        ),
+        grid=(all_samples // CHUNK,),
+        out_shape=outs,
         in_specs=[
-            pl.BlockSpec(memory_space=pltpu.SMEM), vmem, vmem, vmem, *[vmem for _ in arrays],
-            pl.BlockSpec(memory_space=pl.ANY),
+            pl.BlockSpec(memory_space=pltpu.SMEM),
+            *[whole(x) for x in (*sums, plan)],
+            *[pl.BlockSpec((x.shape[0], CHUNK), lambda k: (0, k)) for x in arrays],
+            pl.BlockSpec((CHUNK, width), lambda k: (k, 0)),
         ],
-        out_specs=(vmem, vmem),
+        out_specs=tuple(whole(x) for x in outs),
         scratch_shapes=[
             pltpu.VMEM((used, CHUNK), jnp.bfloat16),
             pltpu.VMEM((padded, width), jnp.float32),
             pltpu.VMEM((genes, LANES), jnp.float32),
-            pltpu.VMEM((all_samples // CHUNK, CHUNK, width), jnp.bfloat16),
-            pltpu.SemaphoreType.DMA((all_samples // CHUNK,)),
         ],
         compiler_params=pltpu.CompilerParams(vmem_limit_bytes=48 * MIB),
         cost_estimate=pl.CostEstimate(
@@ -578,17 +609,19 @@
     def one_round(turn, pos):
         core = pos[1:]
         other_pheno = swapped(phenotypes)
-        own_sums = local_moments(genotypes, env)
-        sums = (own_sums, swapped(own_sums))
-        late_geno, _ = lax.optimization_barrier((genotypes, other_pheno))
-        other_geno = swapped(late_geno)
         other_env = swapped(env)
         other_shuffles = swapped(shuffles)
-        rounds, plan, full, *payloads = select(
-            turn, pos, chrom_bounds, start, end, phenotypes, other_pheno, caps, blocks_dev
-        )
-        payloads = [full] * (reach - len(payloads)) + payloads
-        mine = [travel(k, x) for k, x in enumerate(payloads, 1)]
+        full = merged(core, phenotypes, other_pheno, other_env, other_shuffles)
+        whole = [travel(k, full) for k in range(1, reach + 1) if caps[k - 1] == genes]
+        late_geno, late_env, _ = lax.optimization_barrier((genotypes, env, full))
+        other_geno = swapped(late_geno)
+        own_sums = local_moments(genotypes, late_env)
+        late_full, _ = lax.optimization_barrier((full, own_sums))
+        sums = (own_sums, swapped(own_sums))
+        rounds, plan, *payloads = select(
+            turn, pos, chrom_bounds, start, end, late_full, caps, blocks_dev
+        )
+        mine = whole + [travel(len(whole) + i, x) for i, x in enumerate(payloads, 1)]
         weights = snp_side(
             core, env, other_env, *sums, shuffles, other_shuffles, genotypes, other_geno, labels
         )

time: 107 us -> 124 us (1.16)
  Pallas kernels: 67.4 us -> 80.7 us
  local copies, waits for them, and re-layouts: 1.25 us -> 2.77 us
  waiting for transfers between devices: 7.42 us -> 8.67 us
    pallas_call x0 -> x1, Pallas kernels: none -> 17 us  [merged(): pl.pallas_call(merge_kernel, out_shape=jax.ShapeDtypeStruct((own.shape[0]...]
    pallas_call x1, Pallas kernels: 21 us -> 16.4 us  [products(): pl.pallas_call(functools.partial(product_kernel, caps=caps, labels=labels...]
    unnamed x26 -> x28, local copies, waits for them, and re-layouts: 1.25 us -> 2.77 us
    ppermute x10, waiting for transfers between devices: 7.41 us -> 8.66 us  [swapped(): lax.ppermute(x, 'sample', [(i, (i + 1) % count) for i in range(count)])]
  transfers between devices with their start and end apart: 14 -> 14, of which waited for: 4 -> 6; matrix products, arithmetic and copies ran while one was open for 0% -> 0% of each run, Pallas kernels for 42% -> 37%
where the time goes in v9:
time: 124 us; the launch traced here: 123 us
  Pallas kernels  80.7 us (65%)
  starting transfers between devices  18.7 us (15%)
  blocking collectives  11 us (9%)
  waiting for transfers between devices  8.67 us (7%)
  local copies, waits for them, and re-layouts  2.77 us (2%)
    pallas_call x1, Pallas kernels, snp_side(): pl.pallas_call(functools.partial(snp_side_kernel, labels=labels), out_sha...  37.1 us
    pallas_call x1, Pallas kernels, merged(): pl.pallas_call(merge_kernel, out_shape=jax.ShapeDtypeStruct((own.shape[0]...  17 us
    pallas_call x1, Pallas kernels, products(): pl.pallas_call(functools.partial(product_kernel, caps=caps, labels=labels...  16.4 us
    ppermute x4, starting transfers between devices, travel(): return lax.ppermute(payload, ('genome', 'sample'), pairs)  16.1 us
    all_to_all x1, blocking collectives, shards(): gathered = lax.all_to_all(found, 'genome', 0, 0, tiled=True)  11 us
    ppermute x10, waiting for transfers between devices, swapped(): lax.ppermute(x, 'sample', [(i, (i + 1) % count) for i in range(count)])  8.66 us
    pallas_call x1, Pallas kernels, local_moments(): pl.pallas_call(moments_kernel, grid=(half // chunk,), out_shape=jax.Shape...  5.09 us
    pallas_call x1, Pallas kernels, select(): pl.pallas_call(functools.partial(select_kernel, caps=caps, blocks_dev=blo...  3.6 us
  transfers between devices with their start and end apart: 14, of which 6 were waited for; matrix products, arithmetic and copies ran while one was open for 0% of the time, Pallas kernels for 37%

profile of v9, /device:TPU:0, one launch (start us, length us, event | category | flops | bytes accessed | tf_op | source)
XLA Modules:
  0.0 122.9 jit_solution(15592265436977209680)
XLA Ops:
  0.0 0.5 collective-permute-start.10
  0.5 0.1 collective-permute-start.12
  0.6 0.4 collective-permute-start.11
  1.0 1.4 %collective-permute-done.11.rest_0_.env_other = f32[1,4096]{1,0:T(1,128)} collective-permute-done((f32[1,4096]{1,0:T(1,128)}, f32[1,4096]{1,0:T(1,128)}, u32[]{:S(2)}, u32[]{:S(2)}) %collective-permute-start.11) | collective-permute-done | bytes 16416 | tf_op jit(solution)/shard_map/ppermute | solution.py:28
  2.5 0.8 copy-done.9
  3.3 17.0 %merged.2.full_ref.rest_0_ = bf16[64,8192]{1,0:T(8,128)(2,1)} custom-call(s32[1]{0:T(128)} %bitcast.3.core_ref, bf16[64,4096]{1,0:T(8,128)(2,1)} %own_ref.2, bf16[64,4096]{1,0:T(8,128)(2,1)S(1)} %collective-permute-done.10.other_ref, f32[1,4096]{1,0:T(1,128)} %collective-permute-done.11.rest_0_.env_other, ...), custom_call_target="tpu_custom_call" | custom-call | tf_op jit(solution)/shard_map/merged/pallas_call | solution.py:262
  20.3 0.4 collective-permute-start.18
  20.7 4.7 %collective-permute-start.14 = (bf16[64,8192]{1,0:T(8,128)(2,1)}, bf16[64,8192]{1,0:T(8,128)(2,1)S(1)}, u32[]{:S(2)}, u32[]{:S(2)}) collective-permute-start(bf16[64,8192]{1,0:T(8,128)(2,1)} %merged.2.full_ref.rest_0_), channel_id=1, source_target_pairs={{0,2},{2,4},{4,6},{6,8},{8,10},{10,12},{12,14},{14,16},{16,18},{18... | collective-permute-start | bytes 3145736 | tf_op jit(solution)/shard_map/ppermute | solution.py:607
  25.5 4.3 %collective-permute-start.15 = (bf16[64,8192]{1,0:T(8,128)(2,1)}, bf16[64,8192]{1,0:T(8,128)(2,1)}, u32[]{:S(2)}, u32[]{:S(2)}) collective-permute-start(bf16[64,8192]{1,0:T(8,128)(2,1)} %merged.2.full_ref.rest_0_), channel_id=1, source_target_pairs={{0,4},{2,6},{4,8},{6,10},{8,12},{10,14},{12,16},{14,18},{16,20},{1... | collective-permute-start | bytes 3145736 | tf_op jit(solution)/shard_map/ppermute | solution.py:607
  29.8 0.1 pad_add_fusion.pos_ref
  29.9 5.1 %local_moments.2.sums_own = f32[8,512]{1,0:T(8,128)} custom-call(bf16[512,4096]{1,0:T(8,128)(2,1)} %own_ref.3, f32[1,4096]{1,0:T(1,128)} %bitcast.4.env_ref.env_own), custom_call_target="tpu_custom_call" | custom-call | flops 1000000 | bytes 1000000 | tf_op jit(solution)/shard_map/local_moments/pallas_call | solution.py:66
  35.0 3.6 %select.3 = (s32[1]{0:T(128)}, s32[8,640]{1,0:T(8,128)S(1)}, bf16[32,8192]{1,0:T(8,128)(2,1)}, bf16[16,8192]{1,0:T(8,128)(2,1)}) custom-call(s32[1]{0:T(128)} %constant.15.clone.1.round_ref, s32[2]{0:T(128)S(1)} %pad_add_fusion.pos_ref, s32[15]{0:T(128)S(1)} %copy-done.17, s32[8,128]{1,0:T(8,128)S(1)} %bitcast.10, s32[8,128]{1,0:T(8,128)S(1)} %bitcast.12, ...), custom_call_target="tpu_custom_call" | custom-call | tf_op jit(solution)/shard_map/select/pallas_call | solution.py:392
  38.6 3.4 %collective-permute-start.16 = (bf16[32,8192]{1,0:T(8,128)(2,1)}, bf16[32,8192]{1,0:T(8,128)(2,1)S(1)}, u32[]{:S(2)}, u32[]{:S(2)}) collective-permute-start(bf16[32,8192]{1,0:T(8,128)(2,1)} %get-tuple-element.142), channel_id=1, source_target_pairs={{0,6},{2,8},{4,10},{6,12},{8,14},{10,16},{12,18},{14,20},{16,22},{... | collective-permute-start | bytes 1572872 | tf_op jit(solution)/shard_map/ppermute | solution.py:607
  42.0 0.1 collective-permute-start.13
  42.1 1.4 %collective-permute-done.13.sums_other = f32[8,512]{1,0:T(8,128)S(1)} collective-permute-done((f32[8,512]{1,0:T(8,128)}, f32[8,512]{1,0:T(8,128)S(1)}, u32[]{:S(2)}, u32[]{:S(2)}) %collective-permute-start.13) | collective-permute-done | bytes 16416 | tf_op jit(solution)/shard_map/ppermute | solution.py:28
  43.5 3.6 %collective-permute-start.17 = (bf16[16,8192]{1,0:T(8,128)(2,1)}, bf16[16,8192]{1,0:T(8,128)(2,1)S(1)}, u32[]{:S(2)}, u32[]{:S(2)}) collective-permute-start(bf16[16,8192]{1,0:T(8,128)(2,1)} %get-tuple-element.143), channel_id=1, source_target_pairs={{0,8},{2,10},{4,12},{6,14},{8,16},{10,18},{12,20},{14,22},{16,24},... | collective-permute-start | bytes 786440 | tf_op jit(solution)/shard_map/ppermute | solution.py:607
  47.1 37.1 %snp_side.3.rest_9_ = bf16[8192,1280]{1,0:T(8,128)(2,1)} custom-call(s32[1]{0:T(128)} %bitcast.3.core_ref, f32[1,4096]{1,0:T(1,128)} %bitcast.4.env_ref.env_own, f32[1,4096]{1,0:T(1,128)} %collective-permute-done.11.rest_0_.env_other, f32[8,512]{1,0:T(8,128)} %local_moments.2.sums_own, f32[8,512]{1,0:T(8,128)} %copy-done.6, s32[4,4096]{1,0:T(4,128)S(1)} %copy-done.10, ...), custom_call_target="tpu_custom_call" | custom-call | flops 1000000 | bytes 1000000 | tf_op jit(solution)/shard_map/snp_side/pallas_call | solution.py:218
  84.2 0.1 collective-permute-start.19
  84.3 0.5 collective-permute-start.20
  84.8 0.1 collective-permute-start.21
  84.9 0.4 collective-permute-start.22
  85.3 3.5 %collective-permute-done.22.rest_8_ = bf16[16,8192]{1,0:T(8,128)(2,1)S(1)} collective-permute-done((bf16[16,8192]{1,0:T(8,128)(2,1)S(1)}, bf16[16,8192]{1,0:T(8,128)(2,1)S(1)}, u32[]{:S(2)}, u32[]{:S(2)}) %collective-permute-start.22) | collective-permute-done | bytes 262176 | tf_op jit(solution)/shard_map/ppermute | solution.py:28
  88.8 0.9 collective-permute-done.21.rest_7_
  89.7 0.3 collective-permute-done.20.rest_6_
  89.9 0.7 copy-done.7
  90.7 16.4 %products.3 = (f32[16,8,128]{2,1,0:T(8,128)}, f32[8,64]{1,0:T(8,128)S(1)}) custom-call(s32[2]{0:T(128)} %copy-done.18, f32[8,512]{1,0:T(8,128)S(1)} %copy-done.5, f32[8,512]{1,0:T(8,128)S(1)} %copy-done.7, s32[8,640]{1,0:T(8,128)S(1)} %get-tuple-element.141.plan_ref, bf16[64,8192]{1,0:T(8,128)(2,1)S(1)} %copy-done.1, ...), custom_call_target="tpu_custom_call" | custom-call | flops 8724152320 | bytes 27787264 | tf_op jit(solution)/shard_map/products/pallas_call | solution.py:551
  107.1 0.6 copy-done.8
  107.7 0.8 while.11
  108.5 11.0 %all_to_all.5.own_ref = f32[16,8,128]{2,1,0:T(8,128)S(1)} all-to-all(f32[16,8,128]{2,1,0:T(8,128)} %get-tuple-element.372), channel_id=1, replica_groups=mesh['genome'=16,'sample'=2] {'genome'}, dimensions={0} | all-to-all | bytes 131072 | tf_op jit(solution)/shard_map/all_to_all | solution.py:646
  119.5 1.3 %collective-permute-done.23.other_ref = f32[16,8,128]{2,1,0:T(8,128)S(1)} collective-permute-done((f32[16,8,128]{2,1,0:T(8,128)S(1)}, f32[16,8,128]{2,1,0:T(8,128)S(1)}, u32[]{:S(2)}, u32[]{:S(2)}) %collective-permute-start.23) | collective-permute-done | bytes 65568 | tf_op jit(solution)/shard_map/ppermute | solution.py:28
  120.8 0.6 copy-done.16
  121.4 1.5 %finish.1 = f32[5,64]{1,0:T(8,128)} custom-call(f32[16,8,128]{2,1,0:T(8,128)} %copy-done.13, f32[16,8,128]{2,1,0:T(8,128)} %copy-done.16, f32[8,64]{1,0:T(8,128)} %copy-done.8), custom_call_target="tpu_custom_call" | custom-call | tf_op jit(solution)/shard_map/finish/pallas_call | solution.py:647
  (33 shorter events, 0.1 us)
Async XLA Ops:
  0.0 47.1 %copy-start.10 = (s32[4,4096]{1,0:T(4,128)S(1)}, s32[4,4096]{1,0:T(4,128)}, u32[]{:S(2)}) copy-start(s32[4,4096]{1,0:T(4,128)} %shuf_own.1) | copy-start | bytes 196612
  0.0 35.0 %copy-start.14 = (s32[1024]{0:T(1024)S(1)}, s32[1024]{0:T(1024)}, u32[]{:S(2)}) copy-start(s32[1024]{0:T(1024)} %param.13) | copy-start | bytes 12292
  0.0 35.0 %copy-start.15 = (s32[1024]{0:T(1024)S(1)}, s32[1024]{0:T(1024)}, u32[]{:S(2)}) copy-start(s32[1024]{0:T(1024)} %param.14) | copy-start | bytes 12292
  0.0 35.0 %copy-start.17 = (s32[15]{0:T(128)S(1)}, s32[15]{0:T(128)}, u32[]{:S(2)}) copy-start(s32[15]{0:T(128)} %bounds_ref.1) | copy-start | bytes 184
  0.0 2.5 %collective-permute-start.10 = (bf16[64,4096]{1,0:T(8,128)(2,1)}, bf16[64,4096]{1,0:T(8,128)(2,1)S(1)}, u32[]{:S(2)}, u32[]{:S(2)}) collective-permute-start(bf16[64,4096]{1,0:T(8,128)(2,1)} %own_ref.2), channel_id=1, source_target_pairs={{0,1},{1,0},{2,3},{3,2},{4,5},{5,4},{6,7},{7,6},{8,9},{9,8},{10,11... | collective-permute-start | bytes 1572872 | tf_op jit(solution)/shard_map/ppermute | solution.py:28
  0.5 1.9 %collective-permute-start.12 = (s32[4,4096]{1,0:T(4,128)}, s32[4,4096]{1,0:T(4,128)S(1)}, u32[]{:S(2)}, u32[]{:S(2)}) collective-permute-start(s32[4,4096]{1,0:T(4,128)} %shuf_own.1), channel_id=1, source_target_pairs={{0,1},{1,0},{2,3},{3,2},{4,5},{5,4},{6,7},{7,6},{8,9},{9,8},{10,11... | collective-permute-start | bytes 196616 | tf_op jit(solution)/shard_map/ppermute | solution.py:28
  0.6 1.8 %collective-permute-start.11 = (f32[1,4096]{1,0:T(1,128)}, f32[1,4096]{1,0:T(1,128)}, u32[]{:S(2)}, u32[]{:S(2)}) collective-permute-start(f32[1,4096]{1,0:T(1,128)} %bitcast.4.env_ref.env_own), channel_id=1, source_target_pairs={{0,1},{1,0},{2,3},{3,2},{4,5},{5,4},{6,7},{7,6},{8,9},{9,8},{10,11... | collective-permute-start | bytes 49160 | tf_op jit(solution)/shard_map/ppermute | solution.py:28
  2.5 0.8 copy-start.9
  20.3 14.7 %copy-start.1 = (bf16[64,8192]{1,0:T(8,128)(2,1)S(1)}, bf16[64,8192]{1,0:T(8,128)(2,1)}, u32[]{:S(2)}) copy-start(bf16[64,8192]{1,0:T(8,128)(2,1)} %merged.2.full_ref.rest_0_) | copy-start | bytes 3145732
  20.3 26.8 %collective-permute-start.18 = (bf16[512,4096]{1,0:T(8,128)(2,1)}, bf16[512,4096]{1,0:T(8,128)(2,1)}, u32[]{:S(2)}, u32[]{:S(2)}) collective-permute-start(bf16[512,4096]{1,0:T(8,128)(2,1)} %own_ref.3), channel_id=1, source_target_pairs={{0,1},{1,0},{2,3},{3,2},{4,5},{5,4},{6,7},{7,6},{8,9},{9,8},{10,11... | collective-permute-start | bytes 12582920 | tf_op jit(solution)/shard_map/ppermute | solution.py:28
  20.7 63.5 %collective-permute-start.14 = (bf16[64,8192]{1,0:T(8,128)(2,1)}, bf16[64,8192]{1,0:T(8,128)(2,1)S(1)}, u32[]{:S(2)}, u32[]{:S(2)}) collective-permute-start(bf16[64,8192]{1,0:T(8,128)(2,1)} %merged.2.full_ref.rest_0_), channel_id=1, source_target_pairs={{0,2},{2,4},{4,6},{6,8},{8,10},{10,12},{12,14},{14,16},{16,18},{18... | collective-permute-start | bytes 3145736 | tf_op jit(solution)/shard_map/ppermute | solution.py:607
  25.5 58.8 %collective-permute-start.15 = (bf16[64,8192]{1,0:T(8,128)(2,1)}, bf16[64,8192]{1,0:T(8,128)(2,1)}, u32[]{:S(2)}, u32[]{:S(2)}) collective-permute-start(bf16[64,8192]{1,0:T(8,128)(2,1)} %merged.2.full_ref.rest_0_), channel_id=1, source_target_pairs={{0,4},{2,6},{4,8},{6,10},{8,12},{10,14},{12,16},{14,18},{16,20},{1... | collective-permute-start | bytes 3145736 | tf_op jit(solution)/shard_map/ppermute | solution.py:607
  29.9 8.7 %copy-start.18 = (s32[2]{0:T(128)}, s32[2]{0:T(128)S(1)}, u32[]{:S(2)}) copy-start(s32[2]{0:T(128)S(1)} %pad_add_fusion.pos_ref) | copy-start | bytes 28
  38.6 45.6 %collective-permute-start.16 = (bf16[32,8192]{1,0:T(8,128)(2,1)}, bf16[32,8192]{1,0:T(8,128)(2,1)S(1)}, u32[]{:S(2)}, u32[]{:S(2)}) collective-permute-start(bf16[32,8192]{1,0:T(8,128)(2,1)} %get-tuple-element.142), channel_id=1, source_target_pairs={{0,6},{2,8},{4,10},{6,12},{8,14},{10,16},{12,18},{14,20},{16,22},{... | collective-permute-start | bytes 1572872 | tf_op jit(solution)/shard_map/ppermute | solution.py:607
  42.0 1.5 %collective-permute-start.13 = (f32[8,512]{1,0:T(8,128)}, f32[8,512]{1,0:T(8,128)S(1)}, u32[]{:S(2)}, u32[]{:S(2)}) collective-permute-start(f32[8,512]{1,0:T(8,128)} %local_moments.2.sums_own), channel_id=1, source_target_pairs={{0,1},{1,0},{2,3},{3,2},{4,5},{5,4},{6,7},{7,6},{8,9},{9,8},{10,11... | collective-permute-start | bytes 49160 | tf_op jit(solution)/shard_map/ppermute | solution.py:28
  43.5 3.6 %copy-start.6 = (f32[8,512]{1,0:T(8,128)}, f32[8,512]{1,0:T(8,128)S(1)}, u32[]{:S(2)}) copy-start(f32[8,512]{1,0:T(8,128)S(1)} %collective-permute-done.13.sums_other) | copy-start | bytes 49156
  43.5 46.4 %copy-start.5 = (f32[8,512]{1,0:T(8,128)S(1)}, f32[8,512]{1,0:T(8,128)}, u32[]{:S(2)}) copy-start(f32[8,512]{1,0:T(8,128)} %local_moments.2.sums_own) | copy-start | bytes 49156
  43.5 40.7 %collective-permute-start.17 = (bf16[16,8192]{1,0:T(8,128)(2,1)}, bf16[16,8192]{1,0:T(8,128)(2,1)S(1)}, u32[]{:S(2)}, u32[]{:S(2)}) collective-permute-start(bf16[16,8192]{1,0:T(8,128)(2,1)} %get-tuple-element.143), channel_id=1, source_target_pairs={{0,8},{2,10},{4,12},{6,14},{8,16},{10,18},{12,20},{14,22},{16,24},... | collective-permute-start | bytes 786440 | tf_op jit(solution)/shard_map/ppermute | solution.py:607
  84.2 5.4 %collective-permute-start.19 = (bf16[64,8192]{1,0:T(8,128)(2,1)S(1)}, bf16[64,8192]{1,0:T(8,128)(2,1)}, u32[]{:S(2)}, u32[]{:S(2)}) collective-permute-start(bf16[64,8192]{1,0:T(8,128)(2,1)S(1)} %collective-permute-done.14.rest_1_), channel_id=1, source_target_pairs={{0,1},{1,0},{2,3},{3,2},{4,5},{5,4},{6,7},{7,6},{8,9},{9,8},{10,11... | collective-permute-start | bytes 3145736 | tf_op jit(solution)/shard_map/ppermute | solution.py:28
  84.3 5.6 %collective-permute-start.20 = (bf16[64,8192]{1,0:T(8,128)(2,1)}, bf16[64,8192]{1,0:T(8,128)(2,1)}, u32[]{:S(2)}, u32[]{:S(2)}) collective-permute-start(bf16[64,8192]{1,0:T(8,128)(2,1)} %collective-permute-done.15.rest_2_), channel_id=1, source_target_pairs={{0,1},{1,0},{2,3},{3,2},{4,5},{5,4},{6,7},{7,6},{8,9},{9,8},{10,11... | collective-permute-start | bytes 3145736 | tf_op jit(solution)/shard_map/ppermute | solution.py:28
  84.8 4.9 %collective-permute-start.21 = (bf16[32,8192]{1,0:T(8,128)(2,1)S(1)}, bf16[32,8192]{1,0:T(8,128)(2,1)}, u32[]{:S(2)}, u32[]{:S(2)}) collective-permute-start(bf16[32,8192]{1,0:T(8,128)(2,1)S(1)} %collective-permute-done.16.rest_3_), channel_id=1, source_target_pairs={{0,1},{1,0},{2,3},{3,2},{4,5},{5,4},{6,7},{7,6},{8,9},{9,8},{10,11... | collective-permute-start | bytes 1572872 | tf_op jit(solution)/shard_map/ppermute | solution.py:28
  84.9 3.9 %collective-permute-start.22 = (bf16[16,8192]{1,0:T(8,128)(2,1)S(1)}, bf16[16,8192]{1,0:T(8,128)(2,1)S(1)}, u32[]{:S(2)}, u32[]{:S(2)}) collective-permute-start(bf16[16,8192]{1,0:T(8,128)(2,1)S(1)} %collective-permute-done.17.rest_4_), channel_id=1, source_target_pairs={{0,1},{1,0},{2,3},{3,2},{4,5},{5,4},{6,7},{7,6},{8,9},{9,8},{10,11... | collective-permute-start | bytes 786440 | tf_op jit(solution)/shard_map/ppermute | solution.py:28
  89.9 0.7 copy-start.7
  90.7 17.0 %copy-start.19 = (s32[2]{0:T(128)S(1)}, s32[2]{0:T(128)}, u32[]{:S(2)}) copy-start(s32[2]{0:T(128)} %copy-done.18) | copy-start | bytes 28
  107.1 0.6 copy-start.8
  119.5 1.3 %copy-start.13 = (f32[16,8,128]{2,1,0:T(8,128)}, f32[16,8,128]{2,1,0:T(8,128)S(1)}, u32[]{:S(2)}) copy-start(f32[16,8,128]{2,1,0:T(8,128)S(1)} %all_to_all.5.own_ref) | copy-start | bytes 196612
  119.5 1.3 %collective-permute-start.23 = (f32[16,8,128]{2,1,0:T(8,128)S(1)}, f32[16,8,128]{2,1,0:T(8,128)S(1)}, u32[]{:S(2)}, u32[]{:S(2)}) collective-permute-start(f32[16,8,128]{2,1,0:T(8,128)S(1)} %all_to_all.5.own_ref), channel_id=1, source_target_pairs={{0,1},{1,0},{2,3},{3,2},{4,5},{5,4},{6,7},{7,6},{8,9},{9,8},{10,11... | collective-permute-start | bytes 196616 | tf_op jit(solution)/shard_map/ppermute | solution.py:28
  120.8 0.6 copy-start.16

commit v10 on v8

--- a/solution.py
+++ b/solution.py
@@ -84,16 +84,16 @@
 def snp_side_kernel(
     core_ref, env_own, env_other, sums_own, sums_other, shuf_own, shuf_other, own_ref, other_ref,
     out_ref,
-    idx, geno, table, dest, stage, first_stage, slope, idx_sems, in_sems, out_sems, first_sems,
+    idx, geno, table, dests, stage, first_stage, slope, idx_sems, in_sems, out_sems, first_sems,
     *, labels,
 ):
     snp_rows, half = own_ref.shape
     all_samples = 2 * half
     chunks = all_samples // CHUNK
     words = snp_rows // LANES
-    slot = words
     share = snp_rows // 2
-    side = 2 * LANES
+    side = SIDE
+    per_chunk = CHUNK // side
     core = core_ref[0]
     depth = geno.shape[0]
 
@@ -116,7 +116,8 @@
         there = jnp.where(core == 0, k * CHUNK, (k * CHUNK + half) % all_samples)
         rows = pl.ds(pl.multiple_of(there, CHUNK), CHUNK)
         return pltpu.make_async_copy(
-            first_stage.at[k % 2], out_ref.at[rows, pl.ds(labels * snp_rows, share)],
+            first_stage.at[k % 2, :, pl.ds(pl.multiple_of(core * share, share), share)],
+            out_ref.at[rows, pl.ds(labels * snp_rows, share)],
             first_sems.at[k % 2],
         )
 
@@ -126,6 +127,21 @@
             out_ref.at[pl.ds(k * CHUNK, CHUNK), pl.ds(q * snp_rows, snp_rows)],
             out_sems.at[k % 2],
         )
+
+    def read_rows(first):
+        base = pl.multiple_of(first * words, UNROLL * words)
+        return [table[pl.ds(base + u * words, words), :] for u in range(UNROLL)]
+
+    def write_rows(q, first, held):
+        for u in range(UNROLL):
+            to = pl.multiple_of(idx[q * all_samples + first + u] * words, words)
+            dests[q][pl.ds(to, words), :] = held[u]
+
+    def narrowed(q, at, rows):
+        return [
+            dests[q][pl.ds(at * words + c, rows, stride=words), :].astype(jnp.bfloat16)
+            for c in range(words)
+        ]
 
     for k in range(depth):
         load(k).start()
@@ -138,7 +154,11 @@
         lax.broadcasted_iota(jnp.int32, (side, side), 0)
         == lax.broadcasted_iota(jnp.int32, (side, side), 1)
     ).astype(jnp.bfloat16)
-
+    for q in range(labels):
+        for h in range(2):
+            load_idx(q, h).wait()
+
+    groups = side // UNROLL // words
     for k in range(chunks):
         load(k).wait()
         if k >= 2:
@@ -148,9 +168,9 @@
         def turn(i, carry, k=k, env_ref=env_ref):
             at = pl.multiple_of(i * side, side)
             e = env_ref[:, pl.ds((k * CHUNK) % half + at, side)]
-            turned = []
-            for j in range(snp_rows // side):
-                rows = pl.ds(j * side, side)
+            behind = pl.multiple_of(jnp.maximum(k * CHUNK + at - side, 0), side)
+            for c in range(words):
+                rows = pl.ds(c * LANES, LANES)
                 x = geno[k % depth, rows, pl.ds(at, side)].astype(jnp.float32)
                 r = slope[rows, :]
                 a = x * (e - jnp.concatenate([r] * (side // LANES), axis=1))
@@ -158,49 +178,58 @@
                     unit, a.astype(jnp.bfloat16), (((1,), (1,)), ((), ())),
                     preferred_element_type=jnp.float32,
                 )
-                for c in range(side // LANES):
-                    word = j * (side // LANES) + c
-                    table[pl.ds((k * CHUNK + at) * slot + word, side, stride=slot), :] = (
-                        t[:, c * LANES : (c + 1) * LANES]
-                    )
-                turned.append(t)
-            turned = jnp.concatenate(turned, axis=1)
-            kept = jnp.where(core == 0, turned[:, :share], turned[:, share:])
-            first_stage[k % 2, pl.ds(at, side), :] = kept.astype(jnp.bfloat16)
+                for g in range(groups):
+                    first = pl.multiple_of(behind + (c * groups + g) * UNROLL, UNROLL)
+                    write_rows(0, first, read_rows(first))
+                table[pl.ds((k * CHUNK + at) * words + c, side, stride=words), :] = t
+                first_stage[k % 2, pl.ds(at, side), pl.ds(c * LANES, LANES)] = t.astype(
+                    jnp.bfloat16
+                )
             return carry
 
-        lax.fori_loop(0, CHUNK // side, turn, 0, unroll=2)
+        lax.fori_loop(0, per_chunk, turn, 0)
         save_first(k).start()
         if k + depth < chunks:
             load(k + depth).start()
 
-    for q in range(labels):
-        for h in range(2):
-            load_idx(q, h).wait()
-
-        def scatter(i, carry, q=q):
-            first = pl.multiple_of(i * UNROLL, UNROLL)
-            base = pl.multiple_of(first * slot, UNROLL * slot)
-            held = [table[pl.ds(base + u * slot, words), :] for u in range(UNROLL)]
-            for u in range(UNROLL):
-                to = pl.multiple_of(idx[q * all_samples + first + u] * slot, slot)
-                dest[pl.ds(to, words), :] = held[u]
-            return carry
-
-        lax.fori_loop(0, all_samples // UNROLL, scatter, 0)
+    def rest(i, carry):
+        first = pl.multiple_of(all_samples - side + i * UNROLL, UNROLL)
+        write_rows(0, first, read_rows(first))
+        return carry
+
+    lax.fori_loop(0, side // UNROLL, rest, 0)
+
+    count = 0
+    for q in range(1, labels + 1):
         for k in range(chunks):
-            if q * chunks + k >= 2:
-                save((q * chunks + k - 2) // chunks, (k - 2) % chunks).wait()
-
-            def narrow(i, carry, k=k):
+            if count >= 2:
+                save((count - 2) // chunks, (count - 2) % chunks).wait()
+
+            def step(i, carry, k=k, q=q):
+                at = pl.multiple_of(i * UNROLL, UNROLL)
+                first = pl.multiple_of(k * CHUNK + at, UNROLL)
+                if q < labels:
+                    held = read_rows(first)
+                parts = narrowed(q - 1, first, UNROLL)
+                if q < labels:
+                    write_rows(q, first, held)
+                for c in range(words):
+                    stage[k % 2, pl.ds(at, UNROLL), pl.ds(c * LANES, LANES)] = parts[c]
+                return carry
+
+            def wide(i, carry, k=k, q=q):
                 at = pl.multiple_of(i * side, side)
+                parts = narrowed(q - 1, k * CHUNK + at, side)
                 for c in range(words):
-                    v = dest[pl.ds((k * CHUNK + at) * slot + c, side, stride=slot), :]
-                    stage[k % 2, pl.ds(at, side), pl.ds(c * LANES, LANES)] = v.astype(jnp.bfloat16)
+                    stage[k % 2, pl.ds(at, side), pl.ds(c * LANES, LANES)] = parts[c]
                 return carry
 
-            lax.fori_loop(0, CHUNK // side, narrow, 0)
-            save(q, k).start()
+            if q < labels:
+                lax.fori_loop(0, CHUNK // UNROLL, step, 0)
+            else:
+                lax.fori_loop(0, CHUNK // side, wide, 0)
+            save(q - 1, k).start()
+            count += 1
     for k in range(chunks - 2, chunks):
         save_first(k).wait()
         save(labels - 1, k).wait()
@@ -222,14 +251,14 @@
         out_specs=any_spec,
         scratch_shapes=[
             pltpu.SMEM((labels * all_samples,), jnp.int32),
-            pltpu.VMEM((3, snp_rows, CHUNK), jnp.bfloat16),
+            pltpu.VMEM((2, snp_rows, CHUNK), jnp.bfloat16),
             pltpu.VMEM((all_samples * words, LANES), jnp.float32),
-            pltpu.VMEM((all_samples * words, LANES), jnp.float32),
+            [pltpu.VMEM((all_samples * words, LANES), jnp.float32) for _ in range(labels)],
             pltpu.VMEM((2, CHUNK, snp_rows), jnp.bfloat16),
-            pltpu.VMEM((2, CHUNK, snp_rows // 2), jnp.bfloat16),
+            pltpu.VMEM((2, CHUNK, snp_rows), jnp.bfloat16),
             pltpu.VMEM((snp_rows, LANES), jnp.float32),
             pltpu.SemaphoreType.DMA((2 * labels,)),
-            pltpu.SemaphoreType.DMA((3,)),
+            pltpu.SemaphoreType.DMA((2,)),
             pltpu.SemaphoreType.DMA((2,)),
             pltpu.SemaphoreType.DMA((2,)),
         ],
@@ -392,44 +421,49 @@
     reach = len(caps)
     n_in = 1 + 2 * reach
     gene_refs = rest[:n_in]
-    weights_ref, out_ref, power_ref, rows, total, power, held, sems = rest[n_in:]
+    weights_ref, out_ref, power_ref, rows, total, power = rest[n_in:]
+    step = pl.program_id(0)
     snp_rows = sums_own.shape[1]
-    all_samples, width = weights_ref.shape
+    depth, width = weights_ref.shape
     block = SNP_BLOCK
     used = rows.shape[0]
     chip, core = pos_ref[0], pos_ref[1]
 
-    def load(k):
-        return pltpu.make_async_copy(
-            weights_ref.at[pl.ds(k * CHUNK, CHUNK)], held.at[k], sems.at[k]
-        )
-
-    for k in range(all_samples // CHUNK):
-        load(k).start()
-    power[...] = jnp.zeros_like(power)
-    total[...] = jnp.zeros_like(total)
-    for k in range(all_samples // CHUNK):
-        depth = pl.ds(k * CHUNK, CHUNK)
-        at = 0
-        for ref in gene_refs:
-            rows[pl.ds(at, ref.shape[0]), :] = ref[:, depth]
-            at += ref.shape[0]
-        kept = power[...]
-        for t in range(CHUNK // LANES):
-            x = rows[pl.ds(0, genes), pl.ds(t * LANES, LANES)].astype(jnp.float32)
-            kept = kept + x * x
-        power[...] = kept
-        load(k).wait()
-
-        def step(n, carry, k=k):
-            cols = pl.ds(pl.multiple_of(n * block, block), block)
-            total[pl.ds(0, used), cols] += jnp.dot(
-                rows[...], held[k, :, cols], preferred_element_type=jnp.float32
-            )
-            return carry
-
-        lax.fori_loop(0, width // block, step, 0)
-
+    @pl.when(step == 0)
+    def _():
+        total[...] = jnp.zeros_like(total)
+        power[...] = jnp.zeros_like(power)
+
+    at = 0
+    for ref in gene_refs:
+        rows[pl.ds(at, ref.shape[0]), :] = ref[...]
+        at += ref.shape[0]
+    for at in range(0, width, snp_rows):
+        cols = pl.ds(at, min(snp_rows, width - at))
+        total[pl.ds(0, used), cols] += jnp.dot(
+            rows[...], weights_ref[:, cols], preferred_element_type=jnp.float32
+        )
+    kept = power[...]
+    for t in range(depth // LANES):
+        x = rows[pl.ds(0, genes), pl.ds(t * LANES, LANES)].astype(jnp.float32)
+        kept = kept + x * x
+    power[...] = kept
+
+    @pl.when(step == pl.num_programs(0) - 1)
+    def _():
+        summed_up(
+            chip, core, sums_own, sums_other, plan_ref, out_ref, power_ref, total, power,
+            reach=reach, labels=labels, genes=genes, blocks_dev=blocks_dev,
+        )
+
+
+def summed_up(
+    chip, core, sums_own, sums_other, plan_ref, out_ref, power_ref, total, power,
+    *, reach, labels, genes, blocks_dev,
+):
+    snp_rows = sums_own.shape[1]
+    block = SNP_BLOCK
+    n_in = 1 + 2 * reach
     share_blocks = blocks_dev // 2
     sums = sums_own[...] + sums_other[...]
     cross = sums[1:2, :]
@@ -514,26 +548,31 @@
     out_rows = -(-(1 + 2 * labels) // 8) * 8
     width = weights.shape[1]
     arrays = (full, *mine, *other)
-    vmem = pl.BlockSpec(memory_space=pltpu.VMEM)
+
+    def whole(x):
+        return pl.BlockSpec(x.shape, lambda k: (0,) * len(x.shape))
+
+    outs = (
+        jax.ShapeDtypeStruct((chips, out_rows, LANES), jnp.float32),
+        jax.ShapeDtypeStruct((8, genes), jnp.float32),
+    )
     return pl.pallas_call(
         functools.partial(
             product_kernel, caps=caps, labels=labels, genes=genes, blocks_dev=blocks_dev
         ),
-        out_shape=(
-            jax.ShapeDtypeStruct((chips, out_rows, LANES), jnp.float32),
-            jax.ShapeDtypeStruct((8, genes), jnp.float32),
-        ),
+        grid=(all_samples // CHUNK,),
+        out_shape=outs,
         in_specs=[
-            pl.BlockSpec(memory_space=pltpu.SMEM), vmem, vmem, vmem, *[vmem for _ in arrays],
-            pl.BlockSpec(memory_space=pl.ANY),
+            pl.BlockSpec(memory_space=pltpu.SMEM),
+            *[whole(x) for x in (*sums, plan)],
+            *[pl.BlockSpec((x.shape[0], CHUNK), lambda k: (0, k)) for x in arrays],
+            pl.BlockSpec((CHUNK, width), lambda k: (k, 0)),
         ],
-        out_specs=(vmem, vmem),
+        out_specs=tuple(whole(x) for x in outs),
         scratch_shapes=[
             pltpu.VMEM((used, CHUNK), jnp.bfloat16),
             pltpu.VMEM((padded, width), jnp.float32),
             pltpu.VMEM((genes, LANES), jnp.float32),
-            pltpu.VMEM((all_samples // CHUNK, CHUNK, width), jnp.bfloat16),
-            pltpu.SemaphoreType.DMA((all_samples // CHUNK,)),
         ],
         compiler_params=pltpu.CompilerParams(vmem_limit_bytes=48 * MIB),
         cost_estimate=pl.CostEstimate(

time: 107 us -> 100 us (0.935)
  Pallas kernels: 67.4 us -> 60.8 us
    pallas_call x1, Pallas kernels: 21 us -> 15.8 us  [products(): pl.pallas_call(functools.partial(product_kernel, caps=caps, labels=labels...]
    pallas_call x1, Pallas kernels: 37 us -> 35.6 us  [snp_side(): pl.pallas_call(functools.partial(snp_side_kernel, labels=labels), out_sha...]
  transfers between devices with their start and end apart: 14 -> 14, of which waited for: 4 -> 4; matrix products, arithmetic and copies ran while one was open for 0% -> 0% of each run, Pallas kernels for 42% -> 44%
where the time goes in v10:
time: 100 us; the launch traced here: 99.7 us
  Pallas kernels  60.8 us (61%)
  starting transfers between devices  18.7 us (19%)
  blocking collectives  10.4 us (10%)
  waiting for transfers between devices  7.42 us (7%)
  local copies, waits for them, and re-layouts  1.25 us (1%)
    pallas_call x1, Pallas kernels, snp_side(): pl.pallas_call(functools.partial(snp_side_kernel, labels=labels), out_sha...  35.6 us
    ppermute x4, starting transfers between devices, travel(): return lax.ppermute(payload, ('genome', 'sample'), pairs)  16.1 us
    pallas_call x1, Pallas kernels, products(): pl.pallas_call(functools.partial(product_kernel, caps=caps, labels=labels...  15.8 us
    all_to_all x1, blocking collectives, shards(): gathered = lax.all_to_all(found, 'genome', 0, 0, tiled=True)  10.4 us
    ppermute x10, waiting for transfers between devices, swapped(): lax.ppermute(x, 'sample', [(i, (i + 1) % count) for i in range(count)])  7.41 us
    pallas_call x1, Pallas kernels, local_moments(): pl.pallas_call(moments_kernel, grid=(half // chunk,), out_shape=jax.Shape...  4.51 us
    pallas_call x1, Pallas kernels, select(): pl.pallas_call(functools.partial(select_kernel, caps=caps, blocks_dev=blo...  3.41 us
    ppermute x10, starting transfers between devices, swapped(): lax.ppermute(x, 'sample', [(i, (i + 1) % count) for i in range(count)])  2.62 us
  transfers between devices with their start and end apart: 14, of which 4 were waited for; matrix products, arithmetic and copies ran while one was open for 0% of the time, Pallas kernels for 44%

profile of v10, /device:TPU:0, one launch (start us, length us, event | category | flops | bytes accessed | tf_op | source)
XLA Modules:
  0.0 99.7 jit_solution(6041057560217107042)
XLA Ops:
  0.0 0.5 collective-permute-start.9
  0.5 1.7 %collective-permute-done.9.other_ref = bf16[64,4096]{1,0:T(8,128)(2,1)S(1)} collective-permute-done((bf16[64,4096]{1,0:T(8,128)(2,1)}, bf16[64,4096]{1,0:T(8,128)(2,1)S(1)}, u32[]{:S(2)}, u32[]{:S(2)}) %collective-permute-start.9) | collective-permute-done | bytes 524320 | tf_op jit(solution)/shard_map/ppermute | solution.py:28
  2.2 0.4 collective-permute-start.16
  2.6 0.1 collective-permute-start.14
  2.7 4.5 %local_moments.2.sums_own = f32[8,512]{1,0:T(8,128)S(1)} custom-call(bf16[512,4096]{1,0:T(8,128)(2,1)} %own_ref.3, f32[1,4096]{1,0:T(1,128)} %bitcast.15), custom_call_target="tpu_custom_call" | custom-call | flops 5000000000 | bytes 4194304 | tf_op jit(solution)/shard_map/local_moments/pallas_call | solution.py:66
  7.2 0.4 collective-permute-start.8
  7.7 0.1 collective-permute-start.15
  7.8 0.1 pad_add_fusion.pos_ref
  7.9 3.4 %select.6 = (s32[1]{0:T(128)}, s32[8,640]{1,0:T(8,128)S(1)}, bf16[64,8192]{1,0:T(8,128)(2,1)S(1)}, bf16[32,8192]{1,0:T(8,128)(2,1)}, bf16[16,8192]{1,0:T(8,128)(2,1)}) custom-call(s32[1]{0:T(128)} %constant.18.clone.1.round_ref, s32[2]{0:T(128)S(1)} %pad_add_fusion.pos_ref, s32[15]{0:T(128)} %bounds_ref.1, s32[8,128]{1,0:T(8,128)} %bitcast.10, ...), custom_call_target="tpu_custom_call" | custom-call | tf_op jit(solution)/shard_map/select/pallas_call | solution.py:399
  11.3 4.9 %collective-permute-start.11 = (bf16[64,8192]{1,0:T(8,128)(2,1)S(1)}, bf16[64,8192]{1,0:T(8,128)(2,1)S(1)}, u32[]{:S(2)}, u32[]{:S(2)}) collective-permute-start(bf16[64,8192]{1,0:T(8,128)(2,1)S(1)} %get-tuple-element.342.rest_0_), channel_id=1, source_target_pairs={{0,4},{2,6},{4,8},{6,10},{8,12},{10,14},{12,16},{14,18},{16,20},{1... | collective-permute-start | bytes 3145736 | tf_op jit(solution)/shard_map/ppermute | solution.py:615
  16.2 4.4 %collective-permute-start.10 = (bf16[64,8192]{1,0:T(8,128)(2,1)S(1)}, bf16[64,8192]{1,0:T(8,128)(2,1)}, u32[]{:S(2)}, u32[]{:S(2)}) collective-permute-start(bf16[64,8192]{1,0:T(8,128)(2,1)S(1)} %get-tuple-element.342.rest_0_), channel_id=1, source_target_pairs={{0,2},{2,4},{4,6},{6,8},{8,10},{10,12},{12,14},{14,16},{16,18},{18... | collective-permute-start | bytes 3145736 | tf_op jit(solution)/shard_map/ppermute | solution.py:615
  20.6 2.5 %collective-permute-start.13 = (bf16[16,8192]{1,0:T(8,128)(2,1)}, bf16[16,8192]{1,0:T(8,128)(2,1)S(1)}, u32[]{:S(2)}, u32[]{:S(2)}) collective-permute-start(bf16[16,8192]{1,0:T(8,128)(2,1)} %get-tuple-element.344), channel_id=1, source_target_pairs={{0,8},{2,10},{4,12},{6,14},{8,16},{10,18},{12,20},{14,22},{16,24},... | collective-permute-start | bytes 786440 | tf_op jit(solution)/shard_map/ppermute | solution.py:615
  23.1 4.4 %collective-permute-start.12 = (bf16[32,8192]{1,0:T(8,128)(2,1)}, bf16[32,8192]{1,0:T(8,128)(2,1)S(1)}, u32[]{:S(2)}, u32[]{:S(2)}) collective-permute-start(bf16[32,8192]{1,0:T(8,128)(2,1)} %get-tuple-element.343), channel_id=1, source_target_pairs={{0,6},{2,8},{4,10},{6,12},{8,14},{10,16},{12,18},{14,20},{16,22},{... | collective-permute-start | bytes 1572872 | tf_op jit(solution)/shard_map/ppermute | solution.py:615
  27.5 35.6 %snp_side.6.rest_9_ = bf16[8192,1280]{1,0:T(8,128)(2,1)} custom-call(s32[1]{0:T(128)} %bitcast.3.core_ref, f32[1,4096]{1,0:T(1,128)} %bitcast.16, f32[1,4096]{1,0:T(1,128)S(1)} %collective-permute-done.14.env_other, f32[8,512]{1,0:T(8,128)S(1)} %local_moments.2.sums_own, f32[8,512]{1,0:T(8,128)S(1)} %collective-permute-done.8.sums_other, ...), custom_call_target="tpu_custom_call" | custom-call | flops 40000000000 | bytes 60000000 | tf_op jit(solution)/shard_map/snp_side/pallas_call | solution.py:247
  63.2 0.0 copy-start.3
  63.2 0.0 copy-start.4
  63.2 0.0 copy-start.6
  63.2 0.0 copy-start.7
  63.2 0.0 copy-start.9
  63.3 0.1 collective-permute-start.17
  63.4 0.5 collective-permute-start.18
  63.9 0.1 collective-permute-start.19
  64.0 0.4 collective-permute-start.20
  64.4 3.1 %collective-permute-done.20.rest_8_ = bf16[16,8192]{1,0:T(8,128)(2,1)S(1)} collective-permute-done((bf16[16,8192]{1,0:T(8,128)(2,1)S(1)}, bf16[16,8192]{1,0:T(8,128)(2,1)S(1)}, u32[]{:S(2)}, u32[]{:S(2)}) %collective-permute-start.20) | collective-permute-done | bytes 262176 | tf_op jit(solution)/shard_map/ppermute | solution.py:28
  67.5 1.3 %collective-permute-done.19.rest_7_ = bf16[32,8192]{1,0:T(8,128)(2,1)} collective-permute-done((bf16[32,8192]{1,0:T(8,128)(2,1)S(1)}, bf16[32,8192]{1,0:T(8,128)(2,1)}, u32[]{:S(2)}, u32[]{:S(2)}) %collective-permute-start.19) | collective-permute-done | bytes 524320 | tf_op jit(solution)/shard_map/ppermute | solution.py:28
  68.8 15.8 %products.6 = (f32[16,8,128]{2,1,0:T(8,128)S(1)}, f32[8,64]{1,0:T(8,128)S(1)}) custom-call(s32[2]{0:T(128)S(1)} %pad_add_fusion.pos_ref, f32[8,512]{1,0:T(8,128)} %copy-done.11, f32[8,512]{1,0:T(8,128)} %copy-done.12, s32[8,640]{1,0:T(8,128)S(1)} %get-tuple-element.341.plan_ref, bf16[64,8192]{1,0:T(8,128)(2,1)S(1)} %get-tuple-element.342.rest_0_, ...), custom_call_target="tpu_custom_call" | custom-call | flops 8724152320 | bytes 27787264 | tf_op jit(solution)/shard_map/products/pallas_call | solution.py:559
  84.6 0.6 copy-done
  85.2 0.7 while.14
  85.9 10.4 %all_to_all.5.own_ref = f32[16,8,128]{2,1,0:T(8,128)S(1)} all-to-all(f32[16,8,128]{2,1,0:T(8,128)S(1)} %get-tuple-element.353), channel_id=1, replica_groups=mesh['genome'=16,'sample'=2] {'genome'}, dimensions={0} | all-to-all | bytes 131072 | tf_op jit(solution)/shard_map/all_to_all | solution.py:652
  96.3 1.3 %collective-permute-done.21.other_ref = f32[16,8,128]{2,1,0:T(8,128)S(1)} collective-permute-done((f32[16,8,128]{2,1,0:T(8,128)S(1)}, f32[16,8,128]{2,1,0:T(8,128)S(1)}, u32[]{:S(2)}, u32[]{:S(2)}) %collective-permute-start.21) | collective-permute-done | bytes 65568 | tf_op jit(solution)/shard_map/ppermute | solution.py:28
  97.6 0.6 copy-done.5
  98.2 1.5 %finish.1 = f32[5,64]{1,0:T(8,128)} custom-call(f32[16,8,128]{2,1,0:T(8,128)} %copy-done.2, f32[16,8,128]{2,1,0:T(8,128)} %copy-done.5, f32[8,64]{1,0:T(8,128)} %copy-done), custom_call_target="tpu_custom_call" | custom-call | tf_op jit(solution)/shard_map/finish/pallas_call | solution.py:653
  (30 shorter events, 0.1 us)
Async XLA Ops:
  0.0 2.2 %collective-permute-start.9 = (bf16[64,4096]{1,0:T(8,128)(2,1)}, bf16[64,4096]{1,0:T(8,128)(2,1)S(1)}, u32[]{:S(2)}, u32[]{:S(2)}) collective-permute-start(bf16[64,4096]{1,0:T(8,128)(2,1)} %own_ref.2), channel_id=1, source_target_pairs={{0,1},{1,0},{2,3},{3,2},{4,5},{5,4},{6,7},{7,6},{8,9},{9,8},{10,11... | collective-permute-start | bytes 1572872 | tf_op jit(solution)/shard_map/ppermute | solution.py:28
  2.2 9.1 %copy-start.1 = (bf16[64,4096]{1,0:T(8,128)(2,1)}, bf16[64,4096]{1,0:T(8,128)(2,1)S(1)}, u32[]{:S(2)}) copy-start(bf16[64,4096]{1,0:T(8,128)(2,1)S(1)} %collective-permute-done.9.other_ref) | copy-start | bytes 1572868
  2.2 25.3 %collective-permute-start.16 = (bf16[512,4096]{1,0:T(8,128)(2,1)}, bf16[512,4096]{1,0:T(8,128)(2,1)}, u32[]{:S(2)}, u32[]{:S(2)}) collective-permute-start(bf16[512,4096]{1,0:T(8,128)(2,1)} %own_ref.3), channel_id=1, source_target_pairs={{0,1},{1,0},{2,3},{3,2},{4,5},{5,4},{6,7},{7,6},{8,9},{9,8},{10,11... | collective-permute-start | bytes 12582920 | tf_op jit(solution)/shard_map/ppermute | solution.py:28
  2.6 18.0 %collective-permute-start.14 = (f32[1,4096]{1,0:T(1,128)}, f32[1,4096]{1,0:T(1,128)S(1)}, u32[]{:S(2)}, u32[]{:S(2)}) collective-permute-start(f32[1,4096]{1,0:T(1,128)} %bitcast.14), channel_id=1, source_target_pairs={{0,1},{1,0},{2,3},{3,2},{4,5},{5,4},{6,7},{7,6},{8,9},{9,8},{10,11... | collective-permute-start | bytes 49160 | tf_op jit(solution)/shard_map/ppermute | solution.py:28
  7.2 55.9 %copy-start.11 = (f32[8,512]{1,0:T(8,128)}, f32[8,512]{1,0:T(8,128)S(1)}, u32[]{:S(2)}) copy-start(f32[8,512]{1,0:T(8,128)S(1)} %local_moments.2.sums_own) | copy-start | bytes 49156
  7.2 8.9 %collective-permute-start.8 = (f32[8,512]{1,0:T(8,128)S(1)}, f32[8,512]{1,0:T(8,128)S(1)}, u32[]{:S(2)}, u32[]{:S(2)}) collective-permute-start(f32[8,512]{1,0:T(8,128)S(1)} %local_moments.2.sums_own), channel_id=1, source_target_pairs={{0,1},{1,0},{2,3},{3,2},{4,5},{5,4},{6,7},{7,6},{8,9},{9,8},{10,11... | collective-permute-start | bytes 49160 | tf_op jit(solution)/shard_map/ppermute | solution.py:28
  7.7 15.4 %collective-permute-start.15 = (s32[4,4096]{1,0:T(4,128)}, s32[4,4096]{1,0:T(4,128)S(1)}, u32[]{:S(2)}, u32[]{:S(2)}) collective-permute-start(s32[4,4096]{1,0:T(4,128)} %shuf_own.1), channel_id=1, source_target_pairs={{0,1},{1,0},{2,3},{3,2},{4,5},{5,4},{6,7},{7,6},{8,9},{9,8},{10,11... | collective-permute-start | bytes 196616 | tf_op jit(solution)/shard_map/ppermute | solution.py:28
  11.3 52.0 %collective-permute-start.11 = (bf16[64,8192]{1,0:T(8,128)(2,1)S(1)}, bf16[64,8192]{1,0:T(8,128)(2,1)S(1)}, u32[]{:S(2)}, u32[]{:S(2)}) collective-permute-start(bf16[64,8192]{1,0:T(8,128)(2,1)S(1)} %get-tuple-element.342.rest_0_), channel_id=1, source_target_pairs={{0,4},{2,6},{4,8},{6,10},{8,12},{10,14},{12,16},{14,18},{16,20},{1... | collective-permute-start | bytes 3145736 | tf_op jit(solution)/shard_map/ppermute | solution.py:615
  16.2 47.0 %copy-start.12 = (f32[8,512]{1,0:T(8,128)}, f32[8,512]{1,0:T(8,128)S(1)}, u32[]{:S(2)}) copy-start(f32[8,512]{1,0:T(8,128)S(1)} %collective-permute-done.8.sums_other) | copy-start | bytes 49156
  16.2 47.1 %collective-permute-start.10 = (bf16[64,8192]{1,0:T(8,128)(2,1)S(1)}, bf16[64,8192]{1,0:T(8,128)(2,1)}, u32[]{:S(2)}, u32[]{:S(2)}) collective-permute-start(bf16[64,8192]{1,0:T(8,128)(2,1)S(1)} %get-tuple-element.342.rest_0_), channel_id=1, source_target_pairs={{0,2},{2,4},{4,6},{6,8},{8,10},{10,12},{12,14},{14,16},{16,18},{18... | collective-permute-start | bytes 3145736 | tf_op jit(solution)/shard_map/ppermute | solution.py:615
  20.6 6.9 %copy-start.10 = (f32[1,4096]{1,0:T(1,128)}, f32[1,4096]{1,0:T(1,128)S(1)}, u32[]{:S(2)}) copy-start(f32[1,4096]{1,0:T(1,128)S(1)} %collective-permute-done.14.env_other) | copy-start | bytes 49156
  20.6 42.6 %collective-permute-start.13 = (bf16[16,8192]{1,0:T(8,128)(2,1)}, bf16[16,8192]{1,0:T(8,128)(2,1)S(1)}, u32[]{:S(2)}, u32[]{:S(2)}) collective-permute-start(bf16[16,8192]{1,0:T(8,128)(2,1)} %get-tuple-element.344), channel_id=1, source_target_pairs={{0,8},{2,10},{4,12},{6,14},{8,16},{10,18},{12,20},{14,22},{16,24},... | collective-permute-start | bytes 786440 | tf_op jit(solution)/shard_map/ppermute | solution.py:615
  23.1 4.4 %copy-start.8 = (s32[4,4096]{1,0:T(4,128)}, s32[4,4096]{1,0:T(4,128)S(1)}, u32[]{:S(2)}) copy-start(s32[4,4096]{1,0:T(4,128)S(1)} %collective-permute-done.15.shuf_other) | copy-start | bytes 196612
  23.1 40.2 %collective-permute-start.12 = (bf16[32,8192]{1,0:T(8,128)(2,1)}, bf16[32,8192]{1,0:T(8,128)(2,1)S(1)}, u32[]{:S(2)}, u32[]{:S(2)}) collective-permute-start(bf16[32,8192]{1,0:T(8,128)(2,1)} %get-tuple-element.343), channel_id=1, source_target_pairs={{0,6},{2,8},{4,10},{6,12},{8,14},{10,16},{12,18},{14,20},{16,22},{... | collective-permute-start | bytes 1572872 | tf_op jit(solution)/shard_map/ppermute | solution.py:615
  63.2 22.0 %copy-start.3 = (s32[1024]{0:T(1024)S(1)}, s32[1024]{0:T(1024)}, u32[]{:S(2)}) copy-start(s32[1024]{0:T(1024)} %param.13) | copy-start | bytes 12292
  63.2 22.0 %copy-start.4 = (s32[1024]{0:T(1024)S(1)}, s32[1024]{0:T(1024)}, u32[]{:S(2)}) copy-start(s32[1024]{0:T(1024)} %param.14) | copy-start | bytes 12292
  63.2 21.9 %copy-start.6 = (s32[15]{0:T(128)S(1)}, s32[15]{0:T(128)}, u32[]{:S(2)}) copy-start(s32[15]{0:T(128)} %bounds_ref.1) | copy-start | bytes 184
  63.2 21.9 %copy-start.7 = (s32[4,4096]{1,0:T(4,128)S(1)}, s32[4,4096]{1,0:T(4,128)}, u32[]{:S(2)}) copy-start(s32[4,4096]{1,0:T(4,128)} %shuf_own.1) | copy-start | bytes 196612
  63.2 21.9 %copy-start.9 = (f32[4096]{0:T(1024)S(1)}, f32[4096]{0:T(1024)}, u32[]{:S(2)}) copy-start(f32[4096]{0:T(1024)} %param.11) | copy-start | bytes 49156
  63.3 5.5 %collective-permute-start.17 = (bf16[64,8192]{1,0:T(8,128)(2,1)}, bf16[64,8192]{1,0:T(8,128)(2,1)}, u32[]{:S(2)}, u32[]{:S(2)}) collective-permute-start(bf16[64,8192]{1,0:T(8,128)(2,1)} %collective-permute-done.10.rest_1_), channel_id=1, source_target_pairs={{0,1},{1,0},{2,3},{3,2},{4,5},{5,4},{6,7},{7,6},{8,9},{9,8},{10,11... | collective-permute-start | bytes 3145736 | tf_op jit(solution)/shard_map/ppermute | solution.py:28
  63.4 5.4 %collective-permute-start.18 = (bf16[64,8192]{1,0:T(8,128)(2,1)S(1)}, bf16[64,8192]{1,0:T(8,128)(2,1)}, u32[]{:S(2)}, u32[]{:S(2)}) collective-permute-start(bf16[64,8192]{1,0:T(8,128)(2,1)S(1)} %collective-permute-done.11.rest_2_), channel_id=1, source_target_pairs={{0,1},{1,0},{2,3},{3,2},{4,5},{5,4},{6,7},{7,6},{8,9},{9,8},{10,11... | collective-permute-start | bytes 3145736 | tf_op jit(solution)/shard_map/ppermute | solution.py:28
  63.9 4.9 %collective-permute-start.19 = (bf16[32,8192]{1,0:T(8,128)(2,1)S(1)}, bf16[32,8192]{1,0:T(8,128)(2,1)}, u32[]{:S(2)}, u32[]{:S(2)}) collective-permute-start(bf16[32,8192]{1,0:T(8,128)(2,1)S(1)} %collective-permute-done.12.rest_3_), channel_id=1, source_target_pairs={{0,1},{1,0},{2,3},{3,2},{4,5},{5,4},{6,7},{7,6},{8,9},{9,8},{10,11... | collective-permute-start | bytes 1572872 | tf_op jit(solution)/shard_map/ppermute | solution.py:28
  64.0 3.5 %collective-permute-start.20 = (bf16[16,8192]{1,0:T(8,128)(2,1)S(1)}, bf16[16,8192]{1,0:T(8,128)(2,1)S(1)}, u32[]{:S(2)}, u32[]{:S(2)}) collective-permute-start(bf16[16,8192]{1,0:T(8,128)(2,1)S(1)} %collective-permute-done.13.rest_4_), channel_id=1, source_target_pairs={{0,1},{1,0},{2,3},{3,2},{4,5},{5,4},{6,7},{7,6},{8,9},{9,8},{10,11... | collective-permute-start | bytes 786440 | tf_op jit(solution)/shard_map/ppermute | solution.py:28
  84.6 0.6 copy-start
  96.3 1.3 %copy-start.2 = (f32[16,8,128]{2,1,0:T(8,128)}, f32[16,8,128]{2,1,0:T(8,128)S(1)}, u32[]{:S(2)}) copy-start(f32[16,8,128]{2,1,0:T(8,128)S(1)} %all_to_all.5.own_ref) | copy-start | bytes 196612
  96.3 1.3 %collective-permute-start.21 = (f32[16,8,128]{2,1,0:T(8,128)S(1)}, f32[16,8,128]{2,1,0:T(8,128)S(1)}, u32[]{:S(2)}, u32[]{:S(2)}) collective-permute-start(f32[16,8,128]{2,1,0:T(8,128)S(1)} %all_to_all.5.own_ref), channel_id=1, source_target_pairs={{0,1},{1,0},{2,3},{3,2},{4,5},{5,4},{6,7},{7,6},{8,9},{9,8},{10,11... | collective-permute-start | bytes 196616 | tf_op jit(solution)/shard_map/ppermute | solution.py:28
  97.6 0.6 copy-start.5

commit v11 on v10

--- a/solution.py
+++ b/solution.py
@@ -83,10 +83,12 @@
 
 def snp_side_kernel(
     core_ref, env_own, env_other, sums_own, sums_other, shuf_own, shuf_other, own_ref, other_ref,
-    out_ref,
-    idx, geno, table, dests, stage, first_stage, slope, idx_sems, in_sems, out_sems, first_sems,
-    *, labels,
+    *rest, labels,
 ):
+    out_refs, scratch = rest[: labels + 1], rest[labels + 1 :]
+    (
+        idx, geno, table, dests, stage, first_stage, slope, idx_sems, in_sems, out_sems, first_sems,
+    ) = scratch
     snp_rows, half = own_ref.shape
     all_samples = 2 * half
     chunks = all_samples // CHUNK
@@ -117,14 +119,14 @@
         rows = pl.ds(pl.multiple_of(there, CHUNK), CHUNK)
         return pltpu.make_async_copy(
             first_stage.at[k % 2, :, pl.ds(pl.multiple_of(core * share, share), share)],
-            out_ref.at[rows, pl.ds(labels * snp_rows, share)],
+            out_refs[labels].at[rows],
             first_sems.at[k % 2],
         )
 
     def save(q, k):
         return pltpu.make_async_copy(
             stage.at[k % 2],
-            out_ref.at[pl.ds(k * CHUNK, CHUNK), pl.ds(q * snp_rows, snp_rows)],
+            out_refs[q].at[pl.ds(k * CHUNK, CHUNK)],
             out_sems.at[k % 2],
         )
 
@@ -192,12 +194,12 @@
         if k + depth < chunks:
             load(k + depth).start()
 
-    def rest(i, carry):
+    def last_block(i, carry):
         first = pl.multiple_of(all_samples - side + i * UNROLL, UNROLL)
         write_rows(0, first, read_rows(first))
         return carry
 
-    lax.fori_loop(0, side // UNROLL, rest, 0)
+    lax.fori_loop(0, side // UNROLL, last_block, 0)
 
     count = 0
     for q in range(1, labels + 1):
@@ -240,15 +242,15 @@
     snp_rows, half = own.shape
     all_samples = 2 * half
     words = snp_rows // LANES
-    width = labels * snp_rows + snp_rows // 2
+    widths = [snp_rows] * labels + [snp_rows // 2]
     any_spec = pl.BlockSpec(memory_space=pl.ANY)
     smem = pl.BlockSpec(memory_space=pltpu.SMEM)
     vmem = pl.BlockSpec(memory_space=pltpu.VMEM)
     return pl.pallas_call(
         functools.partial(snp_side_kernel, labels=labels),
-        out_shape=jax.ShapeDtypeStruct((all_samples, width), jnp.bfloat16),
+        out_shape=[jax.ShapeDtypeStruct((all_samples, w), jnp.bfloat16) for w in widths],
         in_specs=[smem, vmem, vmem, vmem, vmem, any_spec, any_spec, any_spec, any_spec],
-        out_specs=any_spec,
+        out_specs=[any_spec for _ in widths],
         scratch_shapes=[
             pltpu.SMEM((labels * all_samples,), jnp.int32),
             pltpu.VMEM((2, snp_rows, CHUNK), jnp.bfloat16),
@@ -421,11 +423,11 @@
     reach = len(caps)
     n_in = 1 + 2 * reach
     gene_refs = rest[:n_in]
-    weights_ref, out_ref, power_ref, rows, total, power = rest[n_in:]
+    weight_refs = rest[n_in : n_in + labels + 1]
+    out_ref, power_ref, rows, total, power = rest[n_in + labels + 1 :]
     step = pl.program_id(0)
     snp_rows = sums_own.shape[1]
-    depth, width = weights_ref.shape
-    block = SNP_BLOCK
+    depth = rows.shape[1]
     used = rows.shape[0]
     chip, core = pos_ref[0], pos_ref[1]
 
@@ -438,10 +440,10 @@
     for ref in gene_refs:
         rows[pl.ds(at, ref.shape[0]), :] = ref[...]
         at += ref.shape[0]
-    for at in range(0, width, snp_rows):
-        cols = pl.ds(at, min(snp_rows, width - at))
+    for q, ref in enumerate(weight_refs):
+        cols = pl.ds(q * snp_rows, ref.shape[1])
         total[pl.ds(0, used), cols] += jnp.dot(
-            rows[...], weights_ref[:, cols], preferred_element_type=jnp.float32
+            rows[...], ref[...], preferred_element_type=jnp.float32
         )
     kept = power[...]
     for t in range(depth // LANES):
@@ -546,7 +548,7 @@
     used = genes + 2 * sum(caps)
     padded = -(-used // LANES) * LANES
     out_rows = -(-(1 + 2 * labels) // 8) * 8
-    width = weights.shape[1]
+    width = sum(w.shape[1] for w in weights)
     arrays = (full, *mine, *other)
 
     def whole(x):
@@ -566,7 +568,7 @@
             pl.BlockSpec(memory_space=pltpu.SMEM),
             *[whole(x) for x in (*sums, plan)],
             *[pl.BlockSpec((x.shape[0], CHUNK), lambda k: (0, k)) for x in arrays],
-            pl.BlockSpec((CHUNK, width), lambda k: (k, 0)),
+            *[pl.BlockSpec((CHUNK, w.shape[1]), lambda k: (k, 0)) for w in weights],
         ],
         out_specs=tuple(whole(x) for x in outs),
         scratch_shapes=[
@@ -581,7 +583,7 @@
             transcendentals=0,
         ),
         name="products",
-    )(pos, *sums, plan, *arrays, weights)
+    )(pos, *sums, plan, *arrays, *weights)
 
 
 def finish_kernel(own_ref, other_ref, power_ref, out_ref, *, samples):
@@ -631,7 +633,7 @@
         weights = snp_side(
             core, env, other_env, *sums, shuffles, other_shuffles, genotypes, other_geno, labels
         )
-        *mine, weights = lax.optimization_barrier((*mine, weights))
+        mine, weights = lax.optimization_barrier((mine, weights))
         other = [swapped(x) for x in mine]
         found, power = products(
             pos, sums, plan, full, mine, other, weights, caps, labels, chips, blocks_dev

time: 100 us -> 99.5 us (level)
  Pallas kernels: 60.8 us -> 59.3 us
  transfers between devices with their start and end apart: 14 -> 14, of which waited for: 4 -> 4; matrix products, arithmetic and copies ran while one was open for 0% -> 0% of each run, Pallas kernels for 44% -> 43%
where the time goes in v11:
time: 99.5 us; the launch traced here: 98.9 us
  Pallas kernels  59.3 us (60%)
  starting transfers between devices  18.8 us (19%)
  blocking collectives  10.4 us (10%)
  waiting for transfers between devices  7.42 us (7%)
  local copies, waits for them, and re-layouts  1.85 us (2%)
    pallas_call x1, Pallas kernels, snp_side(): pl.pallas_call(functools.partial(snp_side_kernel, labels=labels), out_sha...  35 us
    ppermute x4, starting transfers between devices, travel(): return lax.ppermute(payload, ('genome', 'sample'), pairs)  16.1 us
    pallas_call x1, Pallas kernels, products(): pl.pallas_call(functools.partial(product_kernel, caps=caps, labels=labels...  15.5 us
    all_to_all x1, blocking collectives, shards(): gathered = lax.all_to_all(found, 'genome', 0, 0, tiled=True)  10.4 us
    ppermute x10, waiting for transfers between devices, swapped(): lax.ppermute(x, 'sample', [(i, (i + 1) % count) for i in range(count)])  7.41 us
    pallas_call x1, Pallas kernels, local_moments(): pl.pallas_call(moments_kernel, grid=(half // chunk,), out_shape=jax.Shape...  4.54 us
    pallas_call x1, Pallas kernels, select(): pl.pallas_call(functools.partial(select_kernel, caps=caps, blocks_dev=blo...  2.87 us
    ppermute x10, starting transfers between devices, swapped(): lax.ppermute(x, 'sample', [(i, (i + 1) % count) for i in range(count)])  2.68 us
  transfers between devices with their start and end apart: 14, of which 4 were waited for; matrix products, arithmetic and copies ran while one was open for 0% of the time, Pallas kernels for 43%

profile of v11, /device:TPU:0, one launch (start us, length us, event | category | flops | bytes accessed | tf_op | source)
XLA Modules:
  0.0 98.9 jit_solution(2396949475071636225)
XLA Ops:
  0.0 0.5 collective-permute-start.9
  0.5 1.7 %collective-permute-done.9.other_ref = bf16[64,4096]{1,0:T(8,128)(2,1)S(1)} collective-permute-done((bf16[64,4096]{1,0:T(8,128)(2,1)}, bf16[64,4096]{1,0:T(8,128)(2,1)S(1)}, u32[]{:S(2)}, u32[]{:S(2)}) %collective-permute-start.9) | collective-permute-done | bytes 524320 | tf_op jit(solution)/shard_map/ppermute | solution.py:28
  2.2 0.4 collective-permute-start.16
  2.6 0.2 collective-permute-start.14
  2.8 4.5 %local_moments.2.sums_own = f32[8,512]{1,0:T(8,128)S(1)} custom-call(bf16[512,4096]{1,0:T(8,128)(2,1)} %own_ref.3, f32[1,4096]{1,0:T(1,128)} %bitcast.15), custom_call_target="tpu_custom_call" | custom-call | flops 5000000000 | bytes 4194304 | tf_op jit(solution)/shard_map/local_moments/pallas_call | solution.py:66
  7.4 0.4 collective-permute-start.8
  7.8 0.1 collective-permute-start.15
  8.0 0.1 pad_add_fusion.pos_ref
  8.0 2.9 %select.6 = (s32[1]{0:T(128)}, s32[8,640]{1,0:T(8,128)S(1)}, bf16[64,8192]{1,0:T(8,128)(2,1)S(1)}, bf16[32,8192]{1,0:T(8,128)(2,1)}, bf16[16,8192]{1,0:T(8,128)(2,1)}) custom-call(s32[1]{0:T(128)} %constant.18.clone.1.round_ref, s32[2]{0:T(128)S(1)} %pad_add_fusion.pos_ref, s32[15]{0:T(128)S(1)} %copy-done.7, s32[8,128]{1,0:T(8,128)S(1)} %bitcast.10, ...), custom_call_target="tpu_custom_call" | custom-call | tf_op jit(solution)/shard_map/select/pallas_call | solution.py:401
  10.9 4.9 %collective-permute-start.11 = (bf16[64,8192]{1,0:T(8,128)(2,1)S(1)}, bf16[64,8192]{1,0:T(8,128)(2,1)S(1)}, u32[]{:S(2)}, u32[]{:S(2)}) collective-permute-start(bf16[64,8192]{1,0:T(8,128)(2,1)S(1)} %get-tuple-element.352.rest_0_), channel_id=1, source_target_pairs={{0,4},{2,6},{4,8},{6,10},{8,12},{10,14},{12,16},{14,18},{16,20},{1... | collective-permute-start | bytes 3145736 | tf_op jit(solution)/shard_map/ppermute | solution.py:617
  15.8 4.4 %collective-permute-start.10 = (bf16[64,8192]{1,0:T(8,128)(2,1)S(1)}, bf16[64,8192]{1,0:T(8,128)(2,1)}, u32[]{:S(2)}, u32[]{:S(2)}) collective-permute-start(bf16[64,8192]{1,0:T(8,128)(2,1)S(1)} %get-tuple-element.352.rest_0_), channel_id=1, source_target_pairs={{0,2},{2,4},{4,6},{6,8},{8,10},{10,12},{12,14},{14,16},{16,18},{18... | collective-permute-start | bytes 3145736 | tf_op jit(solution)/shard_map/ppermute | solution.py:617
  20.2 0.0 collective-permute-done.14.env_other
  20.2 2.5 %collective-permute-start.13 = (bf16[16,8192]{1,0:T(8,128)(2,1)}, bf16[16,8192]{1,0:T(8,128)(2,1)S(1)}, u32[]{:S(2)}, u32[]{:S(2)}) collective-permute-start(bf16[16,8192]{1,0:T(8,128)(2,1)} %get-tuple-element.354), channel_id=1, source_target_pairs={{0,8},{2,10},{4,12},{6,14},{8,16},{10,18},{12,20},{14,22},{16,24},... | collective-permute-start | bytes 786440 | tf_op jit(solution)/shard_map/ppermute | solution.py:617
  22.7 0.0 collective-permute-done.15.shuf_other
  22.7 0.6 copy-done.9
  23.3 4.4 %collective-permute-start.12 = (bf16[32,8192]{1,0:T(8,128)(2,1)}, bf16[32,8192]{1,0:T(8,128)(2,1)S(1)}, u32[]{:S(2)}, u32[]{:S(2)}) collective-permute-start(bf16[32,8192]{1,0:T(8,128)(2,1)} %get-tuple-element.353), channel_id=1, source_target_pairs={{0,6},{2,8},{4,10},{6,12},{8,14},{10,16},{12,18},{14,20},{16,22},{... | collective-permute-start | bytes 1572872 | tf_op jit(solution)/shard_map/ppermute | solution.py:617
  27.7 0.0 collective-permute-done.16.other_ref
  27.7 35.0 %snp_side.6 = (bf16[8192,512]{1,0:T(8,128)(2,1)}, bf16[8192,512]{1,0:T(8,128)(2,1)}, bf16[8192,256]{1,0:T(8,128)(2,1)}) custom-call(s32[1]{0:T(128)} %bitcast.3.core_ref, f32[1,4096]{1,0:T(1,128)S(1)} %bitcast.16, f32[1,4096]{1,0:T(1,128)S(1)} %collective-permute-done.14.env_other, f32[8,512]{1,0:T(8,128)S(1)} %local_moments.2.sums_own, ...), custom_call_target="tpu_custom_call" | custom-call | flops 40000000000 | bytes 60000000 | tf_op jit(solution)/shard_map/snp_side/pallas_call | solution.py:249
  62.7 0.0 collective-permute-done.11.rest_2_
  62.8 0.1 collective-permute-start.17
  62.8 0.5 collective-permute-start.18
  63.3 0.1 collective-permute-start.19
  63.4 0.4 collective-permute-start.20
  63.8 3.1 %collective-permute-done.20.rest_8_ = bf16[16,8192]{1,0:T(8,128)(2,1)S(1)} collective-permute-done((bf16[16,8192]{1,0:T(8,128)(2,1)S(1)}, bf16[16,8192]{1,0:T(8,128)(2,1)S(1)}, u32[]{:S(2)}, u32[]{:S(2)}) %collective-permute-start.20) | collective-permute-done | bytes 262176 | tf_op jit(solution)/shard_map/ppermute | solution.py:28
  66.9 1.3 %collective-permute-done.19.rest_7_ = bf16[32,8192]{1,0:T(8,128)(2,1)} collective-permute-done((bf16[32,8192]{1,0:T(8,128)(2,1)S(1)}, bf16[32,8192]{1,0:T(8,128)(2,1)}, u32[]{:S(2)}, u32[]{:S(2)}) %collective-permute-start.19) | collective-permute-done | bytes 524320 | tf_op jit(solution)/shard_map/ppermute | solution.py:28
  68.2 15.5 %products.6 = (f32[16,8,128]{2,1,0:T(8,128)S(1)}, f32[8,64]{1,0:T(8,128)S(1)}) custom-call(s32[2]{0:T(128)S(1)} %pad_add_fusion.pos_ref, f32[8,512]{1,0:T(8,128)} %copy-done.12, f32[8,512]{1,0:T(8,128)} %copy-done.13, s32[8,640]{1,0:T(8,128)S(1)} %get-tuple-element.351.plan_ref, bf16[64,8192]{1,0:T(8,128)(2,1)S(1)} %get-tuple-element.352.rest_0_, ...), custom_call_target="tpu_custom_call" | custom-call | flops 8724152320 | bytes 27787264 | tf_op jit(solution)/shard_map/products/pallas_call | solution.py:561
  83.8 0.6 copy-done
  84.3 0.8 while.14
  85.1 10.4 %all_to_all.5.own_ref = f32[16,8,128]{2,1,0:T(8,128)S(1)} all-to-all(f32[16,8,128]{2,1,0:T(8,128)S(1)} %get-tuple-element.368), channel_id=1, replica_groups=mesh['genome'=16,'sample'=2] {'genome'}, dimensions={0} | all-to-all | bytes 131072 | tf_op jit(solution)/shard_map/all_to_all | solution.py:654
  95.5 1.3 %collective-permute-done.21.other_ref = f32[16,8,128]{2,1,0:T(8,128)S(1)} collective-permute-done((f32[16,8,128]{2,1,0:T(8,128)S(1)}, f32[16,8,128]{2,1,0:T(8,128)S(1)}, u32[]{:S(2)}, u32[]{:S(2)}) %collective-permute-start.21) | collective-permute-done | bytes 65568 | tf_op jit(solution)/shard_map/ppermute | solution.py:28
  96.8 0.6 copy-done.6
  97.4 1.5 %finish.1 = f32[5,64]{1,0:T(8,128)} custom-call(f32[16,8,128]{2,1,0:T(8,128)} %copy-done.3, f32[16,8,128]{2,1,0:T(8,128)} %copy-done.6, f32[8,64]{1,0:T(8,128)} %copy-done), custom_call_target="tpu_custom_call" | custom-call | tf_op jit(solution)/shard_map/finish/pallas_call | solution.py:655
  (32 shorter events, 0.1 us)
Async XLA Ops:
  0.0 2.2 %collective-permute-start.9 = (bf16[64,4096]{1,0:T(8,128)(2,1)}, bf16[64,4096]{1,0:T(8,128)(2,1)S(1)}, u32[]{:S(2)}, u32[]{:S(2)}) collective-permute-start(bf16[64,4096]{1,0:T(8,128)(2,1)} %own_ref.2), channel_id=1, source_target_pairs={{0,1},{1,0},{2,3},{3,2},{4,5},{5,4},{6,7},{7,6},{8,9},{9,8},{10,11... | collective-permute-start | bytes 1572872 | tf_op jit(solution)/shard_map/ppermute | solution.py:28
  2.2 5.8 %copy-start.2 = (bf16[64,4096]{1,0:T(8,128)(2,1)}, bf16[64,4096]{1,0:T(8,128)(2,1)S(1)}, u32[]{:S(2)}) copy-start(bf16[64,4096]{1,0:T(8,128)(2,1)S(1)} %collective-permute-done.9.other_ref) | copy-start | bytes 1572868
  2.2 25.5 %collective-permute-start.16 = (bf16[512,4096]{1,0:T(8,128)(2,1)}, bf16[512,4096]{1,0:T(8,128)(2,1)}, u32[]{:S(2)}, u32[]{:S(2)}) collective-permute-start(bf16[512,4096]{1,0:T(8,128)(2,1)} %own_ref.3), channel_id=1, source_target_pairs={{0,1},{1,0},{2,3},{3,2},{4,5},{5,4},{6,7},{7,6},{8,9},{9,8},{10,11... | collective-permute-start | bytes 12582920 | tf_op jit(solution)/shard_map/ppermute | solution.py:28
  2.6 5.2 %copy-start.8 = (s32[4,4096]{1,0:T(4,128)S(1)}, s32[4,4096]{1,0:T(4,128)}, u32[]{:S(2)}) copy-start(s32[4,4096]{1,0:T(4,128)} %shuf_own.1) | copy-start | bytes 196612
  2.6 5.5 %copy-start.1 = (bf16[64,4096]{1,0:T(8,128)(2,1)S(1)}, bf16[64,4096]{1,0:T(8,128)(2,1)}, u32[]{:S(2)}) copy-start(bf16[64,4096]{1,0:T(8,128)(2,1)} %own_ref.2) | copy-start | bytes 1572868
  2.6 5.5 %copy-start.4 = (s32[1024]{0:T(1024)S(1)}, s32[1024]{0:T(1024)}, u32[]{:S(2)}) copy-start(s32[1024]{0:T(1024)} %param.13) | copy-start | bytes 12292
  2.6 5.5 %copy-start.5 = (s32[1024]{0:T(1024)S(1)}, s32[1024]{0:T(1024)}, u32[]{:S(2)}) copy-start(s32[1024]{0:T(1024)} %param.14) | copy-start | bytes 12292
  2.6 5.5 %copy-start.7 = (s32[15]{0:T(128)S(1)}, s32[15]{0:T(128)}, u32[]{:S(2)}) copy-start(s32[15]{0:T(128)} %bounds_ref.1) | copy-start | bytes 184
  2.6 25.1 %copy-start.10 = (f32[4096]{0:T(1024)S(1)}, f32[4096]{0:T(1024)}, u32[]{:S(2)}) copy-start(f32[4096]{0:T(1024)} %param.11) | copy-start | bytes 49156
  2.6 17.6 %collective-permute-start.14 = (f32[1,4096]{1,0:T(1,128)}, f32[1,4096]{1,0:T(1,128)S(1)}, u32[]{:S(2)}, u32[]{:S(2)}) collective-permute-start(f32[1,4096]{1,0:T(1,128)} %bitcast.14), channel_id=1, source_target_pairs={{0,1},{1,0},{2,3},{3,2},{4,5},{5,4},{6,7},{7,6},{8,9},{9,8},{10,11... | collective-permute-start | bytes 49160 | tf_op jit(solution)/shard_map/ppermute | solution.py:28
  7.4 55.3 %copy-start.12 = (f32[8,512]{1,0:T(8,128)}, f32[8,512]{1,0:T(8,128)S(1)}, u32[]{:S(2)}) copy-start(f32[8,512]{1,0:T(8,128)S(1)} %local_moments.2.sums_own) | copy-start | bytes 49156
  7.4 8.4 %collective-permute-start.8 = (f32[8,512]{1,0:T(8,128)S(1)}, f32[8,512]{1,0:T(8,128)S(1)}, u32[]{:S(2)}, u32[]{:S(2)}) collective-permute-start(f32[8,512]{1,0:T(8,128)S(1)} %local_moments.2.sums_own), channel_id=1, source_target_pairs={{0,1},{1,0},{2,3},{3,2},{4,5},{5,4},{6,7},{7,6},{8,9},{9,8},{10,11... | collective-permute-start | bytes 49160 | tf_op jit(solution)/shard_map/ppermute | solution.py:28
  7.8 14.9 %collective-permute-start.15 = (s32[4,4096]{1,0:T(4,128)S(1)}, s32[4,4096]{1,0:T(4,128)S(1)}, u32[]{:S(2)}, u32[]{:S(2)}) collective-permute-start(s32[4,4096]{1,0:T(4,128)S(1)} %copy-done.8), channel_id=1, source_target_pairs={{0,1},{1,0},{2,3},{3,2},{4,5},{5,4},{6,7},{7,6},{8,9},{9,8},{10,11... | collective-permute-start | bytes 196616 | tf_op jit(solution)/shard_map/ppermute | solution.py:28
  10.9 51.8 %collective-permute-start.11 = (bf16[64,8192]{1,0:T(8,128)(2,1)S(1)}, bf16[64,8192]{1,0:T(8,128)(2,1)S(1)}, u32[]{:S(2)}, u32[]{:S(2)}) collective-permute-start(bf16[64,8192]{1,0:T(8,128)(2,1)S(1)} %get-tuple-element.352.rest_0_), channel_id=1, source_target_pairs={{0,4},{2,6},{4,8},{6,10},{8,12},{10,14},{12,16},{14,18},{16,20},{1... | collective-permute-start | bytes 3145736 | tf_op jit(solution)/shard_map/ppermute | solution.py:617
  15.8 46.9 %copy-start.13 = (f32[8,512]{1,0:T(8,128)}, f32[8,512]{1,0:T(8,128)S(1)}, u32[]{:S(2)}) copy-start(f32[8,512]{1,0:T(8,128)S(1)} %collective-permute-done.8.sums_other) | copy-start | bytes 49156
  15.8 46.9 %collective-permute-start.10 = (bf16[64,8192]{1,0:T(8,128)(2,1)S(1)}, bf16[64,8192]{1,0:T(8,128)(2,1)}, u32[]{:S(2)}, u32[]{:S(2)}) collective-permute-start(bf16[64,8192]{1,0:T(8,128)(2,1)S(1)} %get-tuple-element.352.rest_0_), channel_id=1, source_target_pairs={{0,2},{2,4},{4,6},{6,8},{8,10},{10,12},{12,14},{14,16},{16,18},{18... | collective-permute-start | bytes 3145736 | tf_op jit(solution)/shard_map/ppermute | solution.py:617
  20.2 42.5 %copy-start.11 = (f32[1,4096]{1,0:T(1,128)}, f32[1,4096]{1,0:T(1,128)S(1)}, u32[]{:S(2)}) copy-start(f32[1,4096]{1,0:T(1,128)S(1)} %collective-permute-done.14.env_other) | copy-start | bytes 49156
  20.2 42.5 %collective-permute-start.13 = (bf16[16,8192]{1,0:T(8,128)(2,1)}, bf16[16,8192]{1,0:T(8,128)(2,1)S(1)}, u32[]{:S(2)}, u32[]{:S(2)}) collective-permute-start(bf16[16,8192]{1,0:T(8,128)(2,1)} %get-tuple-element.354), channel_id=1, source_target_pairs={{0,8},{2,10},{4,12},{6,14},{8,16},{10,18},{12,20},{14,22},{16,24},... | collective-permute-start | bytes 786440 | tf_op jit(solution)/shard_map/ppermute | solution.py:617
  22.7 0.6 copy-start.9
  23.3 39.4 %collective-permute-start.12 = (bf16[32,8192]{1,0:T(8,128)(2,1)}, bf16[32,8192]{1,0:T(8,128)(2,1)S(1)}, u32[]{:S(2)}, u32[]{:S(2)}) collective-permute-start(bf16[32,8192]{1,0:T(8,128)(2,1)} %get-tuple-element.353), channel_id=1, source_target_pairs={{0,6},{2,8},{4,10},{6,12},{8,14},{10,16},{12,18},{14,20},{16,22},{... | collective-permute-start | bytes 1572872 | tf_op jit(solution)/shard_map/ppermute | solution.py:617
  62.8 5.5 %collective-permute-start.17 = (bf16[64,8192]{1,0:T(8,128)(2,1)}, bf16[64,8192]{1,0:T(8,128)(2,1)}, u32[]{:S(2)}, u32[]{:S(2)}) collective-permute-start(bf16[64,8192]{1,0:T(8,128)(2,1)} %collective-permute-done.10.rest_1_), channel_id=1, source_target_pairs={{0,1},{1,0},{2,3},{3,2},{4,5},{5,4},{6,7},{7,6},{8,9},{9,8},{10,11... | collective-permute-start | bytes 3145736 | tf_op jit(solution)/shard_map/ppermute | solution.py:28
  62.8 5.4 %collective-permute-start.18 = (bf16[64,8192]{1,0:T(8,128)(2,1)S(1)}, bf16[64,8192]{1,0:T(8,128)(2,1)}, u32[]{:S(2)}, u32[]{:S(2)}) collective-permute-start(bf16[64,8192]{1,0:T(8,128)(2,1)S(1)} %collective-permute-done.11.rest_2_), channel_id=1, source_target_pairs={{0,1},{1,0},{2,3},{3,2},{4,5},{5,4},{6,7},{7,6},{8,9},{9,8},{10,11... | collective-permute-start | bytes 3145736 | tf_op jit(solution)/shard_map/ppermute | solution.py:28
  63.3 4.9 %collective-permute-start.19 = (bf16[32,8192]{1,0:T(8,128)(2,1)S(1)}, bf16[32,8192]{1,0:T(8,128)(2,1)}, u32[]{:S(2)}, u32[]{:S(2)}) collective-permute-start(bf16[32,8192]{1,0:T(8,128)(2,1)S(1)} %collective-permute-done.12.rest_3_), channel_id=1, source_target_pairs={{0,1},{1,0},{2,3},{3,2},{4,5},{5,4},{6,7},{7,6},{8,9},{9,8},{10,11... | collective-permute-start | bytes 1572872 | tf_op jit(solution)/shard_map/ppermute | solution.py:28
  63.4 3.5 %collective-permute-start.20 = (bf16[16,8192]{1,0:T(8,128)(2,1)S(1)}, bf16[16,8192]{1,0:T(8,128)(2,1)S(1)}, u32[]{:S(2)}, u32[]{:S(2)}) collective-permute-start(bf16[16,8192]{1,0:T(8,128)(2,1)S(1)} %collective-permute-done.13.rest_4_), channel_id=1, source_target_pairs={{0,1},{1,0},{2,3},{3,2},{4,5},{5,4},{6,7},{7,6},{8,9},{9,8},{10,11... | collective-permute-start | bytes 786440 | tf_op jit(solution)/shard_map/ppermute | solution.py:28
  83.7 0.6 copy-start
  95.5 1.3 %copy-start.3 = (f32[16,8,128]{2,1,0:T(8,128)}, f32[16,8,128]{2,1,0:T(8,128)S(1)}, u32[]{:S(2)}) copy-start(f32[16,8,128]{2,1,0:T(8,128)S(1)} %all_to_all.5.own_ref) | copy-start | bytes 196612
  95.5 1.3 %collective-permute-start.21 = (f32[16,8,128]{2,1,0:T(8,128)S(1)}, f32[16,8,128]{2,1,0:T(8,128)S(1)}, u32[]{:S(2)}, u32[]{:S(2)}) collective-permute-start(f32[16,8,128]{2,1,0:T(8,128)S(1)} %all_to_all.5.own_ref), channel_id=1, source_target_pairs={{0,1},{1,0},{2,3},{3,2},{4,5},{5,4},{6,7},{7,6},{8,9},{9,8},{10,11... | collective-permute-start | bytes 196616 | tf_op jit(solution)/shard_map/ppermute | solution.py:28
  96.8 0.6 copy-start.6

commit v12 on v11

--- a/solution.py
+++ b/solution.py
@@ -118,7 +118,7 @@
         there = jnp.where(core == 0, k * CHUNK, (k * CHUNK + half) % all_samples)
         rows = pl.ds(pl.multiple_of(there, CHUNK), CHUNK)
         return pltpu.make_async_copy(
-            first_stage.at[k % 2, :, pl.ds(pl.multiple_of(core * share, share), share)],
+            first_stage.at[k % 2],
             out_refs[labels].at[rows],
             first_sems.at[k % 2],
         )
@@ -139,11 +139,24 @@
             to = pl.multiple_of(idx[q * all_samples + first + u] * words, words)
             dests[q][pl.ds(to, words), :] = held[u]
 
-    def narrowed(q, at, rows):
-        return [
-            dests[q][pl.ds(at * words + c, rows, stride=words), :].astype(jnp.bfloat16)
-            for c in range(words)
+    def flags(hit):
+        return hit.astype(jnp.float32).astype(jnp.bfloat16)
+
+    def narrowed(q, at):
+        parts = [
+            dests[q][pl.ds(pl.multiple_of((at + n * LANES) * words, LANES * words), LANES * words), :]
+            for n in range(side // LANES)
         ]
+        whole = jnp.concatenate(parts, axis=1).astype(jnp.bfloat16)
+        return jnp.dot(apart, whole, preferred_element_type=jnp.float32)
+
+    def put(k, at, t):
+        t = t.astype(jnp.bfloat16)
+        for n in range(side // LANES):
+            for c in range(words):
+                stage[k % 2, pl.ds(at + n * LANES, LANES), pl.ds(c * LANES, LANES)] = t[
+                    c * LANES : (c + 1) * LANES, n * LANES : (n + 1) * LANES
+                ]
 
     for k in range(depth):
         load(k).start()
@@ -152,15 +165,17 @@
             load_idx(q, h).start()
     sums = sums_own[...] + sums_other[...]
     slope[...] = jnp.broadcast_to(sums[1:2, :] / sums[0:1, :], (LANES, snp_rows)).T
-    unit = (
-        lax.broadcasted_iota(jnp.int32, (side, side), 0)
-        == lax.broadcasted_iota(jnp.int32, (side, side), 1)
-    ).astype(jnp.bfloat16)
+    row = lax.broadcasted_iota(jnp.int32, (side, side), 0)
+    unit = flags(row == lax.broadcasted_iota(jnp.int32, (side, side), 1))
+    square = (LANES * words, LANES * words)
+    row = lax.broadcasted_iota(jnp.int32, square, 0)
+    col = lax.broadcasted_iota(jnp.int32, square, 1)
+    woven = flags((row % words) * LANES + row // words == col)
+    apart = flags((col % words) * LANES + col // words == row)
     for q in range(labels):
         for h in range(2):
             load_idx(q, h).wait()
 
-    groups = side // UNROLL // words
     for k in range(chunks):
         load(k).wait()
         if k >= 2:
@@ -171,22 +186,35 @@
             at = pl.multiple_of(i * side, side)
             e = env_ref[:, pl.ds((k * CHUNK) % half + at, side)]
             behind = pl.multiple_of(jnp.maximum(k * CHUNK + at - side, 0), side)
+            pieces = []
             for c in range(words):
                 rows = pl.ds(c * LANES, LANES)
                 x = geno[k % depth, rows, pl.ds(at, side)].astype(jnp.float32)
                 r = slope[rows, :]
                 a = x * (e - jnp.concatenate([r] * (side // LANES), axis=1))
-                t = lax.dot_general(
-                    unit, a.astype(jnp.bfloat16), (((1,), (1,)), ((), ())),
-                    preferred_element_type=jnp.float32,
-                )
-                for g in range(groups):
-                    first = pl.multiple_of(behind + (c * groups + g) * UNROLL, UNROLL)
-                    write_rows(0, first, read_rows(first))
-                table[pl.ds((k * CHUNK + at) * words + c, side, stride=words), :] = t
-                first_stage[k % 2, pl.ds(at, side), pl.ds(c * LANES, LANES)] = t.astype(
-                    jnp.bfloat16
-                )
+                pieces.append(a.astype(jnp.bfloat16))
+            across = (((1,), (1,)), ((), ()))
+            wide = jnp.concatenate(
+                [
+                    jnp.concatenate([a[:, n * LANES : (n + 1) * LANES] for a in pieces], axis=1)
+                    for n in range(side // LANES)
+                ],
+                axis=0,
+            )
+            t = lax.dot_general(woven, wide, across, preferred_element_type=jnp.float32)
+            early = jnp.concatenate(pieces[: words // 2], axis=0)
+            late = jnp.concatenate(pieces[words // 2 :], axis=0)
+            first = lax.dot_general(
+                unit, jnp.where(core == 0, early, late), across,
+                preferred_element_type=jnp.float32,
+            )
+            for g in range(side // UNROLL):
+                to = pl.multiple_of(behind + g * UNROLL, UNROLL)
+                write_rows(0, to, read_rows(to))
+            for n in range(side // LANES):
+                start = pl.multiple_of((k * CHUNK + at + n * LANES) * words, LANES * words)
+                table[pl.ds(start, LANES * words), :] = t[:, n * LANES : (n + 1) * LANES]
+            first_stage[k % 2, pl.ds(at, side), :] = first.astype(jnp.bfloat16)
             return carry
 
         lax.fori_loop(0, per_chunk, turn, 0)
@@ -208,28 +236,16 @@
                 save((count - 2) // chunks, (count - 2) % chunks).wait()
 
             def step(i, carry, k=k, q=q):
-                at = pl.multiple_of(i * UNROLL, UNROLL)
-                first = pl.multiple_of(k * CHUNK + at, UNROLL)
+                at = pl.multiple_of(i * side, side)
+                t = narrowed(q - 1, k * CHUNK + at)
                 if q < labels:
-                    held = read_rows(first)
-                parts = narrowed(q - 1, first, UNROLL)
-                if q < labels:
-                    write_rows(q, first, held)
-                for c in range(words):
-                    stage[k % 2, pl.ds(at, UNROLL), pl.ds(c * LANES, LANES)] = parts[c]
+                    for g in range(side // UNROLL):
+                        first = pl.multiple_of(k * CHUNK + at + g * UNROLL, UNROLL)
+                        write_rows(q, first, read_rows(first))
+                put(k, at, t)
                 return carry
 
-            def wide(i, carry, k=k, q=q):
-                at = pl.multiple_of(i * side, side)
-                parts = narrowed(q - 1, k * CHUNK + at, side)
-                for c in range(words):
-                    stage[k % 2, pl.ds(at, side), pl.ds(c * LANES, LANES)] = parts[c]
-                return carry
-
-            if q < labels:
-                lax.fori_loop(0, CHUNK // UNROLL, step, 0)
-            else:
-                lax.fori_loop(0, CHUNK // side, wide, 0)
+            lax.fori_loop(0, per_chunk, step, 0)
             save(q - 1, k).start()
             count += 1
     for k in range(chunks - 2, chunks):
@@ -257,7 +273,7 @@
             pltpu.VMEM((all_samples * words, LANES), jnp.float32),
             [pltpu.VMEM((all_samples * words, LANES), jnp.float32) for _ in range(labels)],
             pltpu.VMEM((2, CHUNK, snp_rows), jnp.bfloat16),
-            pltpu.VMEM((2, CHUNK, snp_rows), jnp.bfloat16),
+            pltpu.VMEM((2, CHUNK, snp_rows // 2), jnp.bfloat16),
             pltpu.VMEM((snp_rows, LANES), jnp.float32),
             pltpu.SemaphoreType.DMA((2 * labels,)),
             pltpu.SemaphoreType.DMA((2,)),

time: 99.5 us -> 107 us (1.075)
  Pallas kernels: 59.3 us -> 66.4 us
    pallas_call x1, Pallas kernels: 35 us -> 42 us  [snp_side(): pl.pallas_call(functools.partial(snp_side_kernel, labels=labels), out_sha...]
  transfers between devices with their start and end apart: 14 -> 14, of which waited for: 4 -> 4; matrix products, arithmetic and copies ran while one was open for 0% -> 0% of each run, Pallas kernels for 43% -> 47%
where the time goes in v12:
time: 107 us; the launch traced here: 106 us
  Pallas kernels  66.4 us (62%)
  starting transfers between devices  18.8 us (18%)
  blocking collectives  10.4 us (10%)
  waiting for transfers between devices  7.42 us (7%)
  local copies, waits for them, and re-layouts  1.85 us (2%)
    pallas_call x1, Pallas kernels, snp_side(): pl.pallas_call(functools.partial(snp_side_kernel, labels=labels), out_sha...  42 us
    ppermute x4, starting transfers between devices, travel(): return lax.ppermute(payload, ('genome', 'sample'), pairs)  16.1 us
    pallas_call x1, Pallas kernels, products(): pl.pallas_call(functools.partial(product_kernel, caps=caps, labels=labels...  15.5 us
    all_to_all x1, blocking collectives, shards(): gathered = lax.all_to_all(found, 'genome', 0, 0, tiled=True)  10.4 us
    ppermute x10, waiting for transfers between devices, swapped(): lax.ppermute(x, 'sample', [(i, (i + 1) % count) for i in range(count)])  7.41 us
    pallas_call x1, Pallas kernels, local_moments(): pl.pallas_call(moments_kernel, grid=(half // chunk,), out_shape=jax.Shape...  4.54 us
    pallas_call x1, Pallas kernels, select(): pl.pallas_call(functools.partial(select_kernel, caps=caps, blocks_dev=blo...  2.87 us
    ppermute x10, starting transfers between devices, swapped(): lax.ppermute(x, 'sample', [(i, (i + 1) % count) for i in range(count)])  2.68 us
  transfers between devices with their start and end apart: 14, of which 4 were waited for; matrix products, arithmetic and copies ran while one was open for 0% of the time, Pallas kernels for 47%

profile of v12, /device:TPU:0, one launch (start us, length us, event | category | flops | bytes accessed | tf_op | source)
XLA Modules:
  0.0 106.0 jit_solution(1941316080088688400)
XLA Ops:
  0.0 0.5 collective-permute-start.9
  0.5 1.7 %collective-permute-done.9.other_ref = bf16[64,4096]{1,0:T(8,128)(2,1)S(1)} collective-permute-done((bf16[64,4096]{1,0:T(8,128)(2,1)}, bf16[64,4096]{1,0:T(8,128)(2,1)S(1)}, u32[]{:S(2)}, u32[]{:S(2)}) %collective-permute-start.9) | collective-permute-done | bytes 524320 | tf_op jit(solution)/shard_map/ppermute | solution.py:28
  2.2 0.4 collective-permute-start.16
  2.6 0.2 collective-permute-start.14
  2.8 4.5 %local_moments.2.sums_own = f32[8,512]{1,0:T(8,128)S(1)} custom-call(bf16[512,4096]{1,0:T(8,128)(2,1)} %own_ref.3, f32[1,4096]{1,0:T(1,128)} %bitcast.15), custom_call_target="tpu_custom_call" | custom-call | flops 5000000000 | bytes 4194304 | tf_op jit(solution)/shard_map/local_moments/pallas_call | solution.py:66
  7.4 0.4 collective-permute-start.8
  7.8 0.1 collective-permute-start.15
  8.0 0.1 pad_add_fusion.pos_ref
  8.0 2.9 %select.6 = (s32[1]{0:T(128)}, s32[8,640]{1,0:T(8,128)S(1)}, bf16[64,8192]{1,0:T(8,128)(2,1)S(1)}, bf16[32,8192]{1,0:T(8,128)(2,1)}, bf16[16,8192]{1,0:T(8,128)(2,1)}) custom-call(s32[1]{0:T(128)} %constant.18.clone.1.round_ref, s32[2]{0:T(128)S(1)} %pad_add_fusion.pos_ref, s32[15]{0:T(128)S(1)} %copy-done.7, s32[8,128]{1,0:T(8,128)S(1)} %bitcast.10, ...), custom_call_target="tpu_custom_call" | custom-call | tf_op jit(solution)/shard_map/select/pallas_call | solution.py:417
  10.9 4.9 %collective-permute-start.11 = (bf16[64,8192]{1,0:T(8,128)(2,1)S(1)}, bf16[64,8192]{1,0:T(8,128)(2,1)S(1)}, u32[]{:S(2)}, u32[]{:S(2)}) collective-permute-start(bf16[64,8192]{1,0:T(8,128)(2,1)S(1)} %get-tuple-element.352.rest_0_), channel_id=1, source_target_pairs={{0,4},{2,6},{4,8},{6,10},{8,12},{10,14},{12,16},{14,18},{16,20},{1... | collective-permute-start | bytes 3145736 | tf_op jit(solution)/shard_map/ppermute | solution.py:633
  15.8 4.4 %collective-permute-start.10 = (bf16[64,8192]{1,0:T(8,128)(2,1)S(1)}, bf16[64,8192]{1,0:T(8,128)(2,1)}, u32[]{:S(2)}, u32[]{:S(2)}) collective-permute-start(bf16[64,8192]{1,0:T(8,128)(2,1)S(1)} %get-tuple-element.352.rest_0_), channel_id=1, source_target_pairs={{0,2},{2,4},{4,6},{6,8},{8,10},{10,12},{12,14},{14,16},{16,18},{18... | collective-permute-start | bytes 3145736 | tf_op jit(solution)/shard_map/ppermute | solution.py:633
  20.2 0.0 collective-permute-done.14.env_other
  20.2 2.5 %collective-permute-start.13 = (bf16[16,8192]{1,0:T(8,128)(2,1)}, bf16[16,8192]{1,0:T(8,128)(2,1)S(1)}, u32[]{:S(2)}, u32[]{:S(2)}) collective-permute-start(bf16[16,8192]{1,0:T(8,128)(2,1)} %get-tuple-element.354), channel_id=1, source_target_pairs={{0,8},{2,10},{4,12},{6,14},{8,16},{10,18},{12,20},{14,22},{16,24},... | collective-permute-start | bytes 786440 | tf_op jit(solution)/shard_map/ppermute | solution.py:633
  22.7 0.0 collective-permute-done.15.shuf_other
  22.7 0.6 copy-done.9
  23.3 4.4 %collective-permute-start.12 = (bf16[32,8192]{1,0:T(8,128)(2,1)}, bf16[32,8192]{1,0:T(8,128)(2,1)S(1)}, u32[]{:S(2)}, u32[]{:S(2)}) collective-permute-start(bf16[32,8192]{1,0:T(8,128)(2,1)} %get-tuple-element.353), channel_id=1, source_target_pairs={{0,6},{2,8},{4,10},{6,12},{8,14},{10,16},{12,18},{14,20},{16,22},{... | collective-permute-start | bytes 1572872 | tf_op jit(solution)/shard_map/ppermute | solution.py:633
  27.7 0.0 collective-permute-done.16.other_ref
  27.7 42.0 %snp_side.6 = (bf16[8192,512]{1,0:T(8,128)(2,1)}, bf16[8192,512]{1,0:T(8,128)(2,1)}, bf16[8192,256]{1,0:T(8,128)(2,1)}) custom-call(s32[1]{0:T(128)} %bitcast.3.core_ref, f32[1,4096]{1,0:T(1,128)S(1)} %bitcast.16, f32[1,4096]{1,0:T(1,128)S(1)} %collective-permute-done.14.env_other, f32[8,512]{1,0:T(8,128)S(1)} %local_moments.2.sums_own, ...), custom_call_target="tpu_custom_call" | custom-call | flops 40000000000 | bytes 60000000 | tf_op jit(solution)/shard_map/snp_side/pallas_call | solution.py:265
  69.8 0.0 collective-permute-done.12.rest_3_
  69.8 0.1 collective-permute-start.17
  69.9 0.5 collective-permute-start.18
  70.4 0.1 collective-permute-start.19
  70.5 0.4 collective-permute-start.20
  70.9 3.1 %collective-permute-done.20.rest_8_ = bf16[16,8192]{1,0:T(8,128)(2,1)S(1)} collective-permute-done((bf16[16,8192]{1,0:T(8,128)(2,1)S(1)}, bf16[16,8192]{1,0:T(8,128)(2,1)S(1)}, u32[]{:S(2)}, u32[]{:S(2)}) %collective-permute-start.20) | collective-permute-done | bytes 262176 | tf_op jit(solution)/shard_map/ppermute | solution.py:28
  74.0 1.3 %collective-permute-done.19.rest_7_ = bf16[32,8192]{1,0:T(8,128)(2,1)} collective-permute-done((bf16[32,8192]{1,0:T(8,128)(2,1)S(1)}, bf16[32,8192]{1,0:T(8,128)(2,1)}, u32[]{:S(2)}, u32[]{:S(2)}) %collective-permute-start.19) | collective-permute-done | bytes 524320 | tf_op jit(solution)/shard_map/ppermute | solution.py:28
  75.3 15.5 %products.6 = (f32[16,8,128]{2,1,0:T(8,128)S(1)}, f32[8,64]{1,0:T(8,128)S(1)}) custom-call(s32[2]{0:T(128)S(1)} %pad_add_fusion.pos_ref, f32[8,512]{1,0:T(8,128)} %copy-done.12, f32[8,512]{1,0:T(8,128)} %copy-done.13, s32[8,640]{1,0:T(8,128)S(1)} %get-tuple-element.351.plan_ref, bf16[64,8192]{1,0:T(8,128)(2,1)S(1)} %get-tuple-element.352.rest_0_, ...), custom_call_target="tpu_custom_call" | custom-call | flops 8724152320 | bytes 27787264 | tf_op jit(solution)/shard_map/products/pallas_call | solution.py:577
  90.8 0.6 copy-done
  91.4 0.8 while.14
  92.2 10.4 %all_to_all.5.own_ref = f32[16,8,128]{2,1,0:T(8,128)S(1)} all-to-all(f32[16,8,128]{2,1,0:T(8,128)S(1)} %get-tuple-element.368), channel_id=1, replica_groups=mesh['genome'=16,'sample'=2] {'genome'}, dimensions={0} | all-to-all | bytes 131072 | tf_op jit(solution)/shard_map/all_to_all | solution.py:670
  102.6 1.3 %collective-permute-done.21.other_ref = f32[16,8,128]{2,1,0:T(8,128)S(1)} collective-permute-done((f32[16,8,128]{2,1,0:T(8,128)S(1)}, f32[16,8,128]{2,1,0:T(8,128)S(1)}, u32[]{:S(2)}, u32[]{:S(2)}) %collective-permute-start.21) | collective-permute-done | bytes 65568 | tf_op jit(solution)/shard_map/ppermute | solution.py:28
  103.9 0.6 copy-done.6
  104.5 1.5 %finish.1 = f32[5,64]{1,0:T(8,128)} custom-call(f32[16,8,128]{2,1,0:T(8,128)} %copy-done.3, f32[16,8,128]{2,1,0:T(8,128)} %copy-done.6, f32[8,64]{1,0:T(8,128)} %copy-done), custom_call_target="tpu_custom_call" | custom-call | tf_op jit(solution)/shard_map/finish/pallas_call | solution.py:671
  (32 shorter events, 0.1 us)
Async XLA Ops:
  0.0 2.2 %collective-permute-start.9 = (bf16[64,4096]{1,0:T(8,128)(2,1)}, bf16[64,4096]{1,0:T(8,128)(2,1)S(1)}, u32[]{:S(2)}, u32[]{:S(2)}) collective-permute-start(bf16[64,4096]{1,0:T(8,128)(2,1)} %own_ref.2), channel_id=1, source_target_pairs={{0,1},{1,0},{2,3},{3,2},{4,5},{5,4},{6,7},{7,6},{8,9},{9,8},{10,11... | collective-permute-start | bytes 1572872 | tf_op jit(solution)/shard_map/ppermute | solution.py:28
  2.2 5.8 %copy-start.2 = (bf16[64,4096]{1,0:T(8,128)(2,1)}, bf16[64,4096]{1,0:T(8,128)(2,1)S(1)}, u32[]{:S(2)}) copy-start(bf16[64,4096]{1,0:T(8,128)(2,1)S(1)} %collective-permute-done.9.other_ref) | copy-start | bytes 1572868
  2.2 25.5 %collective-permute-start.16 = (bf16[512,4096]{1,0:T(8,128)(2,1)}, bf16[512,4096]{1,0:T(8,128)(2,1)}, u32[]{:S(2)}, u32[]{:S(2)}) collective-permute-start(bf16[512,4096]{1,0:T(8,128)(2,1)} %own_ref.3), channel_id=1, source_target_pairs={{0,1},{1,0},{2,3},{3,2},{4,5},{5,4},{6,7},{7,6},{8,9},{9,8},{10,11... | collective-permute-start | bytes 12582920 | tf_op jit(solution)/shard_map/ppermute | solution.py:28
  2.6 5.2 %copy-start.8 = (s32[4,4096]{1,0:T(4,128)S(1)}, s32[4,4096]{1,0:T(4,128)}, u32[]{:S(2)}) copy-start(s32[4,4096]{1,0:T(4,128)} %shuf_own.1) | copy-start | bytes 196612
  2.6 5.5 %copy-start.1 = (bf16[64,4096]{1,0:T(8,128)(2,1)S(1)}, bf16[64,4096]{1,0:T(8,128)(2,1)}, u32[]{:S(2)}) copy-start(bf16[64,4096]{1,0:T(8,128)(2,1)} %own_ref.2) | copy-start | bytes 1572868
  2.6 5.5 %copy-start.4 = (s32[1024]{0:T(1024)S(1)}, s32[1024]{0:T(1024)}, u32[]{:S(2)}) copy-start(s32[1024]{0:T(1024)} %param.13) | copy-start | bytes 12292
  2.6 5.5 %copy-start.5 = (s32[1024]{0:T(1024)S(1)}, s32[1024]{0:T(1024)}, u32[]{:S(2)}) copy-start(s32[1024]{0:T(1024)} %param.14) | copy-start | bytes 12292
  2.6 5.5 %copy-start.7 = (s32[15]{0:T(128)S(1)}, s32[15]{0:T(128)}, u32[]{:S(2)}) copy-start(s32[15]{0:T(128)} %bounds_ref.1) | copy-start | bytes 184
  2.6 25.1 %copy-start.10 = (f32[4096]{0:T(1024)S(1)}, f32[4096]{0:T(1024)}, u32[]{:S(2)}) copy-start(f32[4096]{0:T(1024)} %param.11) | copy-start | bytes 49156
  2.6 17.6 %collective-permute-start.14 = (f32[1,4096]{1,0:T(1,128)}, f32[1,4096]{1,0:T(1,128)S(1)}, u32[]{:S(2)}, u32[]{:S(2)}) collective-permute-start(f32[1,4096]{1,0:T(1,128)} %bitcast.14), channel_id=1, source_target_pairs={{0,1},{1,0},{2,3},{3,2},{4,5},{5,4},{6,7},{7,6},{8,9},{9,8},{10,11... | collective-permute-start | bytes 49160 | tf_op jit(solution)/shard_map/ppermute | solution.py:28
  7.4 62.4 %copy-start.12 = (f32[8,512]{1,0:T(8,128)}, f32[8,512]{1,0:T(8,128)S(1)}, u32[]{:S(2)}) copy-start(f32[8,512]{1,0:T(8,128)S(1)} %local_moments.2.sums_own) | copy-start | bytes 49156
  7.4 8.4 %collective-permute-start.8 = (f32[8,512]{1,0:T(8,128)S(1)}, f32[8,512]{1,0:T(8,128)S(1)}, u32[]{:S(2)}, u32[]{:S(2)}) collective-permute-start(f32[8,512]{1,0:T(8,128)S(1)} %local_moments.2.sums_own), channel_id=1, source_target_pairs={{0,1},{1,0},{2,3},{3,2},{4,5},{5,4},{6,7},{7,6},{8,9},{9,8},{10,11... | collective-permute-start | bytes 49160 | tf_op jit(solution)/shard_map/ppermute | solution.py:28
  7.8 14.9 %collective-permute-start.15 = (s32[4,4096]{1,0:T(4,128)S(1)}, s32[4,4096]{1,0:T(4,128)S(1)}, u32[]{:S(2)}, u32[]{:S(2)}) collective-permute-start(s32[4,4096]{1,0:T(4,128)S(1)} %copy-done.8), channel_id=1, source_target_pairs={{0,1},{1,0},{2,3},{3,2},{4,5},{5,4},{6,7},{7,6},{8,9},{9,8},{10,11... | collective-permute-start | bytes 196616 | tf_op jit(solution)/shard_map/ppermute | solution.py:28
  10.9 58.9 %collective-permute-start.11 = (bf16[64,8192]{1,0:T(8,128)(2,1)S(1)}, bf16[64,8192]{1,0:T(8,128)(2,1)S(1)}, u32[]{:S(2)}, u32[]{:S(2)}) collective-permute-start(bf16[64,8192]{1,0:T(8,128)(2,1)S(1)} %get-tuple-element.352.rest_0_), channel_id=1, source_target_pairs={{0,4},{2,6},{4,8},{6,10},{8,12},{10,14},{12,16},{14,18},{16,20},{1... | collective-permute-start | bytes 3145736 | tf_op jit(solution)/shard_map/ppermute | solution.py:633
  15.8 53.9 %copy-start.13 = (f32[8,512]{1,0:T(8,128)}, f32[8,512]{1,0:T(8,128)S(1)}, u32[]{:S(2)}) copy-start(f32[8,512]{1,0:T(8,128)S(1)} %collective-permute-done.8.sums_other) | copy-start | bytes 49156
  15.8 54.0 %collective-permute-start.10 = (bf16[64,8192]{1,0:T(8,128)(2,1)S(1)}, bf16[64,8192]{1,0:T(8,128)(2,1)}, u32[]{:S(2)}, u32[]{:S(2)}) collective-permute-start(bf16[64,8192]{1,0:T(8,128)(2,1)S(1)} %get-tuple-element.352.rest_0_), channel_id=1, source_target_pairs={{0,2},{2,4},{4,6},{6,8},{8,10},{10,12},{12,14},{14,16},{16,18},{18... | collective-permute-start | bytes 3145736 | tf_op jit(solution)/shard_map/ppermute | solution.py:633
  20.2 49.5 %copy-start.11 = (f32[1,4096]{1,0:T(1,128)}, f32[1,4096]{1,0:T(1,128)S(1)}, u32[]{:S(2)}) copy-start(f32[1,4096]{1,0:T(1,128)S(1)} %collective-permute-done.14.env_other) | copy-start | bytes 49156
  20.2 49.6 %collective-permute-start.13 = (bf16[16,8192]{1,0:T(8,128)(2,1)}, bf16[16,8192]{1,0:T(8,128)(2,1)S(1)}, u32[]{:S(2)}, u32[]{:S(2)}) collective-permute-start(bf16[16,8192]{1,0:T(8,128)(2,1)} %get-tuple-element.354), channel_id=1, source_target_pairs={{0,8},{2,10},{4,12},{6,14},{8,16},{10,18},{12,20},{14,22},{16,24},... | collective-permute-start | bytes 786440 | tf_op jit(solution)/shard_map/ppermute | solution.py:633
  22.7 0.6 copy-start.9
  23.3 46.4 %collective-permute-start.12 = (bf16[32,8192]{1,0:T(8,128)(2,1)}, bf16[32,8192]{1,0:T(8,128)(2,1)S(1)}, u32[]{:S(2)}, u32[]{:S(2)}) collective-permute-start(bf16[32,8192]{1,0:T(8,128)(2,1)} %get-tuple-element.353), channel_id=1, source_target_pairs={{0,6},{2,8},{4,10},{6,12},{8,14},{10,16},{12,18},{14,20},{16,22},{... | collective-permute-start | bytes 1572872 | tf_op jit(solution)/shard_map/ppermute | solution.py:633
  69.8 5.5 %collective-permute-start.17 = (bf16[64,8192]{1,0:T(8,128)(2,1)}, bf16[64,8192]{1,0:T(8,128)(2,1)}, u32[]{:S(2)}, u32[]{:S(2)}) collective-permute-start(bf16[64,8192]{1,0:T(8,128)(2,1)} %collective-permute-done.10.rest_1_), channel_id=1, source_target_pairs={{0,1},{1,0},{2,3},{3,2},{4,5},{5,4},{6,7},{7,6},{8,9},{9,8},{10,11... | collective-permute-start | bytes 3145736 | tf_op jit(solution)/shard_map/ppermute | solution.py:28
  69.9 5.4 %collective-permute-start.18 = (bf16[64,8192]{1,0:T(8,128)(2,1)S(1)}, bf16[64,8192]{1,0:T(8,128)(2,1)}, u32[]{:S(2)}, u32[]{:S(2)}) collective-permute-start(bf16[64,8192]{1,0:T(8,128)(2,1)S(1)} %collective-permute-done.11.rest_2_), channel_id=1, source_target_pairs={{0,1},{1,0},{2,3},{3,2},{4,5},{5,4},{6,7},{7,6},{8,9},{9,8},{10,11... | collective-permute-start | bytes 3145736 | tf_op jit(solution)/shard_map/ppermute | solution.py:28
  70.4 4.9 %collective-permute-start.19 = (bf16[32,8192]{1,0:T(8,128)(2,1)S(1)}, bf16[32,8192]{1,0:T(8,128)(2,1)}, u32[]{:S(2)}, u32[]{:S(2)}) collective-permute-start(bf16[32,8192]{1,0:T(8,128)(2,1)S(1)} %collective-permute-done.12.rest_3_), channel_id=1, source_target_pairs={{0,1},{1,0},{2,3},{3,2},{4,5},{5,4},{6,7},{7,6},{8,9},{9,8},{10,11... | collective-permute-start | bytes 1572872 | tf_op jit(solution)/shard_map/ppermute | solution.py:28
  70.5 3.5 %collective-permute-start.20 = (bf16[16,8192]{1,0:T(8,128)(2,1)S(1)}, bf16[16,8192]{1,0:T(8,128)(2,1)S(1)}, u32[]{:S(2)}, u32[]{:S(2)}) collective-permute-start(bf16[16,8192]{1,0:T(8,128)(2,1)S(1)} %collective-permute-done.13.rest_4_), channel_id=1, source_target_pairs={{0,1},{1,0},{2,3},{3,2},{4,5},{5,4},{6,7},{7,6},{8,9},{9,8},{10,11... | collective-permute-start | bytes 786440 | tf_op jit(solution)/shard_map/ppermute | solution.py:28
  90.8 0.6 copy-start
  102.6 1.3 %copy-start.3 = (f32[16,8,128]{2,1,0:T(8,128)}, f32[16,8,128]{2,1,0:T(8,128)S(1)}, u32[]{:S(2)}) copy-start(f32[16,8,128]{2,1,0:T(8,128)S(1)} %all_to_all.5.own_ref) | copy-start | bytes 196612
  102.6 1.3 %collective-permute-start.21 = (f32[16,8,128]{2,1,0:T(8,128)S(1)}, f32[16,8,128]{2,1,0:T(8,128)S(1)}, u32[]{:S(2)}, u32[]{:S(2)}) collective-permute-start(f32[16,8,128]{2,1,0:T(8,128)S(1)} %all_to_all.5.own_ref), channel_id=1, source_target_pairs={{0,1},{1,0},{2,3},{3,2},{4,5},{5,4},{6,7},{7,6},{8,9},{9,8},{10,11... | collective-permute-start | bytes 196616 | tf_op jit(solution)/shard_map/ppermute | solution.py:28
  103.9 0.6 copy-start.6

commit v13 on v11

--- a/solution.py
+++ b/solution.py
@@ -12,6 +12,7 @@
 LANES = 128
 ROWS_STEP = 16
 UNROLL = 32
+SLOT = 8
 SIDE = 2 * LANES
 CHUNK = 1024
 MIB = 2**20
@@ -51,7 +52,7 @@
             sums[m, pl.ds(first, ROWS_STEP), :] = held[m]
         return carry
 
-    lax.fori_loop(0, snp_rows // ROWS_STEP, add_rows, 0, unroll=4)
+    lax.fori_loop(0, snp_rows // ROWS_STEP, add_rows, 0, unroll=8)
 
     @pl.when(step == pl.num_programs(0) - 1)
     def _():
@@ -75,7 +76,7 @@
         scratch_shapes=[pltpu.VMEM((3, snp_rows, LANES), jnp.float32)],
         compiler_params=pltpu.CompilerParams(vmem_limit_bytes=60 * MIB),
         cost_estimate=pl.CostEstimate(
-            flops=5 * 10**9, bytes_accessed=2 * snp_rows * half, transcendentals=0
+            flops=10**6, bytes_accessed=10**6, transcendentals=0
         ),
         name="local_moments",
     )(geno, env)
@@ -87,7 +88,7 @@
 ):
     out_refs, scratch = rest[: labels + 1], rest[labels + 1 :]
     (
-        idx, geno, table, dests, stage, first_stage, slope, idx_sems, in_sems, out_sems, first_sems,
+        idx, geno, table, dest, stage, first_stage, slope, idx_sems, in_sems, out_sems, first_sems,
     ) = scratch
     snp_rows, half = own_ref.shape
     all_samples = 2 * half
@@ -132,16 +133,18 @@
 
     def read_rows(first):
         base = pl.multiple_of(first * words, UNROLL * words)
-        return [table[pl.ds(base + u * words, words), :] for u in range(UNROLL)]
+        return [table[pl.ds(base + u * SLOT, SLOT), :] for u in range(UNROLL * words // SLOT)]
 
     def write_rows(q, first, held):
         for u in range(UNROLL):
-            to = pl.multiple_of(idx[q * all_samples + first + u] * words, words)
-            dests[q][pl.ds(to, words), :] = held[u]
-
-    def narrowed(q, at, rows):
+            to = pl.multiple_of(idx[q * all_samples + first + u] * SLOT, SLOT)
+            rows = held[u * words // SLOT]
+            turned = (u * words) % SLOT
+            dest[pl.ds(to, SLOT), :] = pltpu.roll(rows, SLOT - turned, 0) if turned else rows
+
+    def narrowed(at, rows):
         return [
-            dests[q][pl.ds(at * words + c, rows, stride=words), :].astype(jnp.bfloat16)
+            dest[pl.ds(at * SLOT + c, rows, stride=SLOT), :].astype(jnp.bfloat16)
             for c in range(words)
         ]
 
@@ -200,38 +203,28 @@
         return carry
 
     lax.fori_loop(0, side // UNROLL, last_block, 0)
-
-    count = 0
-    for q in range(1, labels + 1):
+    for q in range(labels):
+        if q > 0:
+
+            def scatter(i, carry, q=q):
+                first = pl.multiple_of(i * UNROLL, UNROLL)
+                write_rows(q, first, read_rows(first))
+                return carry
+
+            lax.fori_loop(0, all_samples // UNROLL, scatter, 0)
         for k in range(chunks):
-            if count >= 2:
-                save((count - 2) // chunks, (count - 2) % chunks).wait()
-
-            def step(i, carry, k=k, q=q):
-                at = pl.multiple_of(i * UNROLL, UNROLL)
-                first = pl.multiple_of(k * CHUNK + at, UNROLL)
-                if q < labels:
-                    held = read_rows(first)
-                parts = narrowed(q - 1, first, UNROLL)
-                if q < labels:
-                    write_rows(q, first, held)
-                for c in range(words):
-                    stage[k % 2, pl.ds(at, UNROLL), pl.ds(c * LANES, LANES)] = parts[c]
-                return carry
-
-            def wide(i, carry, k=k, q=q):
+            if q * chunks + k >= 2:
+                save((q * chunks + k - 2) // chunks, (k - 2) % chunks).wait()
+
+            def wide(i, carry, k=k):
                 at = pl.multiple_of(i * side, side)
-                parts = narrowed(q - 1, k * CHUNK + at, side)
+                parts = narrowed(k * CHUNK + at, side)
                 for c in range(words):
                     stage[k % 2, pl.ds(at, side), pl.ds(c * LANES, LANES)] = parts[c]
                 return carry
 
-            if q < labels:
-                lax.fori_loop(0, CHUNK // UNROLL, step, 0)
-            else:
-                lax.fori_loop(0, CHUNK // side, wide, 0)
-            save(q - 1, k).start()
-            count += 1
+            lax.fori_loop(0, CHUNK // side, wide, 0)
+            save(q, k).start()
     for k in range(chunks - 2, chunks):
         save_first(k).wait()
         save(labels - 1, k).wait()
@@ -255,7 +248,7 @@
             pltpu.SMEM((labels * all_samples,), jnp.int32),
             pltpu.VMEM((2, snp_rows, CHUNK), jnp.bfloat16),
             pltpu.VMEM((all_samples * words, LANES), jnp.float32),
-            [pltpu.VMEM((all_samples * words, LANES), jnp.float32) for _ in range(labels)],
+            pltpu.VMEM((all_samples * SLOT, LANES), jnp.float32),
             pltpu.VMEM((2, CHUNK, snp_rows), jnp.bfloat16),
             pltpu.VMEM((2, CHUNK, snp_rows), jnp.bfloat16),
             pltpu.VMEM((snp_rows, LANES), jnp.float32),
@@ -621,13 +614,14 @@
         other_pheno = swapped(phenotypes)
         own_sums = local_moments(genotypes, env)
         sums = (own_sums, swapped(own_sums))
-        late_geno, _ = lax.optimization_barrier((genotypes, other_pheno))
-        other_geno = swapped(late_geno)
         other_env = swapped(env)
         other_shuffles = swapped(shuffles)
+        late_pheno, _ = lax.optimization_barrier((other_pheno, own_sums))
         rounds, plan, full, *payloads = select(
-            turn, pos, chrom_bounds, start, end, phenotypes, other_pheno, caps, blocks_dev
-        )
+            turn, pos, chrom_bounds, start, end, phenotypes, late_pheno, caps, blocks_dev
+        )
+        late_geno, plan = lax.optimization_barrier((genotypes, plan))
+        other_geno = swapped(late_geno)
         payloads = [full] * (reach - len(payloads)) + payloads
         mine = [travel(k, x) for k, x in enumerate(payloads, 1)]
         weights = snp_side(

time: 99.5 us -> 102 us (1.025)
  Pallas kernels: 59.3 us -> 62.3 us
  waiting for transfers between devices: 7.42 us -> 5.88 us
    pallas_call x1, Pallas kernels: 35 us -> 38 us  [snp_side(): pl.pallas_call(functools.partial(snp_side_kernel, labels=labels), out_sha...]
    ppermute x10, waiting for transfers between devices: 7.41 us -> 5.87 us  [swapped(): lax.ppermute(x, 'sample', [(i, (i + 1) % count) for i in range(count)])]
  transfers between devices with their start and end apart: 14 -> 14, of which waited for: 4 -> 4; matrix products, arithmetic and copies ran while one was open for 0% -> 0% of each run, Pallas kernels for 43% -> 42%
where the time goes in v13:
time: 102 us; the launch traced here: 101 us
  Pallas kernels  62.3 us (61%)
  starting transfers between devices  19.6 us (19%)
  blocking collectives  11.3 us (11%)
  waiting for transfers between devices  5.88 us (6%)
  local copies, waits for them, and re-layouts  1.24 us (1%)
    pallas_call x1, Pallas kernels, snp_side(): pl.pallas_call(functools.partial(snp_side_kernel, labels=labels), out_sha...  38 us
    ppermute x4, starting transfers between devices, travel(): return lax.ppermute(payload, ('genome', 'sample'), pairs)  16.9 us
    pallas_call x1, Pallas kernels, products(): pl.pallas_call(functools.partial(product_kernel, caps=caps, labels=labels...  15.5 us
    all_to_all x1, blocking collectives, shards(): gathered = lax.all_to_all(found, 'genome', 0, 0, tiled=True)  11.3 us
    ppermute x10, waiting for transfers between devices, swapped(): lax.ppermute(x, 'sample', [(i, (i + 1) % count) for i in range(count)])  5.87 us
    pallas_call x1, Pallas kernels, local_moments(): pl.pallas_call(moments_kernel, grid=(half // chunk,), out_shape=jax.Shape...  4.46 us
    pallas_call x1, Pallas kernels, select(): pl.pallas_call(functools.partial(select_kernel, caps=caps, blocks_dev=blo...  2.86 us
    ppermute x10, starting transfers between devices, swapped(): lax.ppermute(x, 'sample', [(i, (i + 1) % count) for i in range(count)])  2.7 us
  transfers between devices with their start and end apart: 14, of which 4 were waited for; matrix products, arithmetic and copies ran while one was open for 0% of the time, Pallas kernels for 42%

profile of v13, /device:TPU:0, one launch (start us, length us, event | category | flops | bytes accessed | tf_op | source)
XLA Modules:
  0.0 101.4 jit_solution(2895719393552780804)
XLA Ops:
  0.0 0.0 copy-start.9
  0.0 0.5 collective-permute-start.10
  0.6 4.5 %local_moments.2.sums_own = f32[8,512]{1,0:T(8,128)S(1)} custom-call(bf16[512,4096]{1,0:T(8,128)(2,1)} %own_ref.3, f32[1,4096]{1,0:T(1,128)} %bitcast.14), custom_call_target="tpu_custom_call" | custom-call | flops 1000000 | bytes 1000000 | tf_op jit(solution)/shard_map/local_moments/pallas_call | solution.py:67
  5.0 0.1 pad_add_fusion.pos_ref
  5.1 0.0 collective-permute-done.10.other_ref
  5.1 2.9 %select.6 = (s32[1]{0:T(128)}, s32[8,640]{1,0:T(8,128)S(1)}, bf16[64,8192]{1,0:T(8,128)(2,1)S(1)}, bf16[32,8192]{1,0:T(8,128)(2,1)}, bf16[16,8192]{1,0:T(8,128)(2,1)}) custom-call(s32[1]{0:T(128)} %constant.18.clone.1.round_ref, s32[2]{0:T(128)S(1)} %pad_add_fusion.pos_ref, s32[15]{0:T(128)S(1)} %copy-done.7, s32[8,128]{1,0:T(8,128)S(1)} %bitcast.10, ...), custom_call_target="tpu_custom_call" | custom-call | tf_op jit(solution)/shard_map/select/pallas_call | solution.py:394
  8.0 0.2 collective-permute-start.17
  8.2 0.4 collective-permute-start.16
  8.6 0.1 collective-permute-start.9
  8.7 0.4 collective-permute-start.15
  9.1 4.5 %collective-permute-start.11 = (bf16[64,8192]{1,0:T(8,128)(2,1)S(1)}, bf16[64,8192]{1,0:T(8,128)(2,1)S(1)}, u32[]{:S(2)}, u32[]{:S(2)}) collective-permute-start(bf16[64,8192]{1,0:T(8,128)(2,1)S(1)} %get-tuple-element.346.rest_0_), channel_id=1, source_target_pairs={{0,2},{2,4},{4,6},{6,8},{8,10},{10,12},{12,14},{14,16},{16,18},{18... | collective-permute-start | bytes 3145736 | tf_op jit(solution)/shard_map/ppermute | solution.py:610
  13.7 5.6 %collective-permute-start.12 = (bf16[64,8192]{1,0:T(8,128)(2,1)S(1)}, bf16[64,8192]{1,0:T(8,128)(2,1)}, u32[]{:S(2)}, u32[]{:S(2)}) collective-permute-start(bf16[64,8192]{1,0:T(8,128)(2,1)S(1)} %get-tuple-element.346.rest_0_), channel_id=1, source_target_pairs={{0,4},{2,6},{4,8},{6,10},{8,12},{10,14},{12,16},{14,18},{16,20},{1... | collective-permute-start | bytes 3145736 | tf_op jit(solution)/shard_map/ppermute | solution.py:610
  19.2 3.4 %collective-permute-start.13 = (bf16[32,8192]{1,0:T(8,128)(2,1)}, bf16[32,8192]{1,0:T(8,128)(2,1)S(1)}, u32[]{:S(2)}, u32[]{:S(2)}) collective-permute-start(bf16[32,8192]{1,0:T(8,128)(2,1)} %get-tuple-element.347), channel_id=1, source_target_pairs={{0,6},{2,8},{4,10},{6,12},{8,14},{10,16},{12,18},{14,20},{16,22},{... | collective-permute-start | bytes 1572872 | tf_op jit(solution)/shard_map/ppermute | solution.py:610
  22.6 0.0 collective-permute-done.16.shuf_other
  22.7 3.4 %collective-permute-start.14 = (bf16[16,8192]{1,0:T(8,128)(2,1)}, bf16[16,8192]{1,0:T(8,128)(2,1)S(1)}, u32[]{:S(2)}, u32[]{:S(2)}) collective-permute-start(bf16[16,8192]{1,0:T(8,128)(2,1)} %get-tuple-element.348), channel_id=1, source_target_pairs={{0,8},{2,10},{4,12},{6,14},{8,16},{10,18},{12,20},{14,22},{16,24},... | collective-permute-start | bytes 786440 | tf_op jit(solution)/shard_map/ppermute | solution.py:610
  26.0 0.0 collective-permute-done.17.other_ref
  26.1 38.0 %snp_side.6 = (bf16[8192,512]{1,0:T(8,128)(2,1)}, bf16[8192,512]{1,0:T(8,128)(2,1)}, bf16[8192,256]{1,0:T(8,128)(2,1)}) custom-call(s32[1]{0:T(128)} %bitcast.3.core_ref, f32[1,4096]{1,0:T(1,128)S(1)} %bitcast.16, f32[1,4096]{1,0:T(1,128)S(1)} %collective-permute-done.15.env_other, f32[8,512]{1,0:T(8,128)S(1)} %local_moments.2.sums_own, ...), custom_call_target="tpu_custom_call" | custom-call | flops 40000000000 | bytes 60000000 | tf_op jit(solution)/shard_map/snp_side/pallas_call | solution.py:242
  64.1 0.0 collective-permute-done.13.rest_3_
  64.1 0.1 collective-permute-start.18
  64.2 0.5 collective-permute-start.19
  64.7 0.1 collective-permute-start.20
  64.8 0.4 collective-permute-start.21
  65.2 3.5 %collective-permute-done.21.rest_8_ = bf16[16,8192]{1,0:T(8,128)(2,1)S(1)} collective-permute-done((bf16[16,8192]{1,0:T(8,128)(2,1)S(1)}, bf16[16,8192]{1,0:T(8,128)(2,1)S(1)}, u32[]{:S(2)}, u32[]{:S(2)}) %collective-permute-start.21) | collective-permute-done | bytes 262176 | tf_op jit(solution)/shard_map/ppermute | solution.py:29
  68.7 0.9 collective-permute-done.20.rest_7_
  69.5 0.3 collective-permute-done.19.rest_6_
  69.8 15.5 %products.6 = (f32[16,8,128]{2,1,0:T(8,128)S(1)}, f32[8,64]{1,0:T(8,128)S(1)}) custom-call(s32[2]{0:T(128)S(1)} %pad_add_fusion.pos_ref, f32[8,512]{1,0:T(8,128)S(1)} %local_moments.2.sums_own, f32[8,512]{1,0:T(8,128)S(1)} %collective-permute-done.9.sums_other, s32[8,640]{1,0:T(8,128)S(1)} %get-tuple-element.345.plan_ref, ...), custom_call_target="tpu_custom_call" | custom-call | flops 8724152320 | bytes 27787264 | tf_op jit(solution)/shard_map/products/pallas_call | solution.py:554
  85.3 0.6 copy-done
  85.9 0.8 while.14
  86.7 11.3 %all_to_all.5.own_ref = f32[16,8,128]{2,1,0:T(8,128)S(1)} all-to-all(f32[16,8,128]{2,1,0:T(8,128)S(1)} %get-tuple-element.362), channel_id=1, replica_groups=mesh['genome'=16,'sample'=2] {'genome'}, dimensions={0} | all-to-all | bytes 131072 | tf_op jit(solution)/shard_map/all_to_all | solution.py:648
  98.0 1.3 %collective-permute-done.22.other_ref = f32[16,8,128]{2,1,0:T(8,128)S(1)} collective-permute-done((f32[16,8,128]{2,1,0:T(8,128)S(1)}, f32[16,8,128]{2,1,0:T(8,128)S(1)}, u32[]{:S(2)}, u32[]{:S(2)}) %collective-permute-start.22) | collective-permute-done | bytes 65568 | tf_op jit(solution)/shard_map/ppermute | solution.py:29
  99.3 0.6 copy-done.6
  99.9 1.5 %finish.1 = f32[5,64]{1,0:T(8,128)} custom-call(f32[16,8,128]{2,1,0:T(8,128)} %copy-done.3, f32[16,8,128]{2,1,0:T(8,128)} %copy-done.6, f32[8,64]{1,0:T(8,128)} %copy-done), custom_call_target="tpu_custom_call" | custom-call | tf_op jit(solution)/shard_map/finish/pallas_call | solution.py:649
  (26 shorter events, 0.1 us)
Async XLA Ops:
  0.0 5.1 %copy-start.1 = (bf16[64,4096]{1,0:T(8,128)(2,1)S(1)}, bf16[64,4096]{1,0:T(8,128)(2,1)}, u32[]{:S(2)}) copy-start(bf16[64,4096]{1,0:T(8,128)(2,1)} %own_ref.2) | copy-start | bytes 1572868
  0.0 8.7 %copy-start.8 = (f32[4096]{0:T(1024)S(1)}, f32[4096]{0:T(1024)}, u32[]{:S(2)}) copy-start(f32[4096]{0:T(1024)} %param.11) | copy-start | bytes 49156
  0.0 5.1 %copy-start.4 = (s32[1024]{0:T(1024)S(1)}, s32[1024]{0:T(1024)}, u32[]{:S(2)}) copy-start(s32[1024]{0:T(1024)} %param.13) | copy-start | bytes 12292
  0.0 5.1 %copy-start.5 = (s32[1024]{0:T(1024)S(1)}, s32[1024]{0:T(1024)}, u32[]{:S(2)}) copy-start(s32[1024]{0:T(1024)} %param.14) | copy-start | bytes 12292
  0.0 5.1 %copy-start.7 = (s32[15]{0:T(128)S(1)}, s32[15]{0:T(128)}, u32[]{:S(2)}) copy-start(s32[15]{0:T(128)} %bounds_ref.1) | copy-start | bytes 184
  0.0 8.2 %copy-start.9 = (s32[4,4096]{1,0:T(4,128)S(1)}, s32[4,4096]{1,0:T(4,128)}, u32[]{:S(2)}) copy-start(s32[4,4096]{1,0:T(4,128)} %shuf_own.1) | copy-start | bytes 196612
  0.0 5.1 %collective-permute-start.10 = (bf16[64,4096]{1,0:T(8,128)(2,1)}, bf16[64,4096]{1,0:T(8,128)(2,1)S(1)}, u32[]{:S(2)}, u32[]{:S(2)}) collective-permute-start(bf16[64,4096]{1,0:T(8,128)(2,1)} %own_ref.2), channel_id=1, source_target_pairs={{0,1},{1,0},{2,3},{3,2},{4,5},{5,4},{6,7},{7,6},{8,9},{9,8},{10,11... | collective-permute-start | bytes 1572872 | tf_op jit(solution)/shard_map/ppermute | solution.py:29
  5.1 4.0 %copy-start.2 = (bf16[64,4096]{1,0:T(8,128)(2,1)}, bf16[64,4096]{1,0:T(8,128)(2,1)S(1)}, u32[]{:S(2)}) copy-start(bf16[64,4096]{1,0:T(8,128)(2,1)S(1)} %collective-permute-done.10.other_ref) | copy-start | bytes 1572868
  8.0 18.0 %collective-permute-start.17 = (bf16[512,4096]{1,0:T(8,128)(2,1)}, bf16[512,4096]{1,0:T(8,128)(2,1)}, u32[]{:S(2)}, u32[]{:S(2)}) collective-permute-start(bf16[512,4096]{1,0:T(8,128)(2,1)} %own_ref.3), channel_id=1, source_target_pairs={{0,1},{1,0},{2,3},{3,2},{4,5},{5,4},{6,7},{7,6},{8,9},{9,8},{10,11... | collective-permute-start | bytes 12582920 | tf_op jit(solution)/shard_map/ppermute | solution.py:29
  8.2 14.5 %collective-permute-start.16 = (s32[4,4096]{1,0:T(4,128)S(1)}, s32[4,4096]{1,0:T(4,128)S(1)}, u32[]{:S(2)}, u32[]{:S(2)}) collective-permute-start(s32[4,4096]{1,0:T(4,128)S(1)} %copy-done.9), channel_id=1, source_target_pairs={{0,1},{1,0},{2,3},{3,2},{4,5},{5,4},{6,7},{7,6},{8,9},{9,8},{10,11... | collective-permute-start | bytes 196616 | tf_op jit(solution)/shard_map/ppermute | solution.py:29
  8.6 5.1 %collective-permute-start.9 = (f32[8,512]{1,0:T(8,128)S(1)}, f32[8,512]{1,0:T(8,128)S(1)}, u32[]{:S(2)}, u32[]{:S(2)}) collective-permute-start(f32[8,512]{1,0:T(8,128)S(1)} %local_moments.2.sums_own), channel_id=1, source_target_pairs={{0,1},{1,0},{2,3},{3,2},{4,5},{5,4},{6,7},{7,6},{8,9},{9,8},{10,11... | collective-permute-start | bytes 49160 | tf_op jit(solution)/shard_map/ppermute | solution.py:29
  8.7 10.5 %collective-permute-start.15 = (f32[1,4096]{1,0:T(1,128)S(1)}, f32[1,4096]{1,0:T(1,128)S(1)}, u32[]{:S(2)}, u32[]{:S(2)}) collective-permute-start(f32[1,4096]{1,0:T(1,128)S(1)} %bitcast.15), channel_id=1, source_target_pairs={{0,1},{1,0},{2,3},{3,2},{4,5},{5,4},{6,7},{7,6},{8,9},{9,8},{10,11... | collective-permute-start | bytes 49160 | tf_op jit(solution)/shard_map/ppermute | solution.py:29
  9.1 55.0 %collective-permute-start.11 = (bf16[64,8192]{1,0:T(8,128)(2,1)S(1)}, bf16[64,8192]{1,0:T(8,128)(2,1)S(1)}, u32[]{:S(2)}, u32[]{:S(2)}) collective-permute-start(bf16[64,8192]{1,0:T(8,128)(2,1)S(1)} %get-tuple-element.346.rest_0_), channel_id=1, source_target_pairs={{0,2},{2,4},{4,6},{6,8},{8,10},{10,12},{12,14},{14,16},{16,18},{18... | collective-permute-start | bytes 3145736 | tf_op jit(solution)/shard_map/ppermute | solution.py:610
  13.7 50.4 %collective-permute-start.12 = (bf16[64,8192]{1,0:T(8,128)(2,1)S(1)}, bf16[64,8192]{1,0:T(8,128)(2,1)}, u32[]{:S(2)}, u32[]{:S(2)}) collective-permute-start(bf16[64,8192]{1,0:T(8,128)(2,1)S(1)} %get-tuple-element.346.rest_0_), channel_id=1, source_target_pairs={{0,4},{2,6},{4,8},{6,10},{8,12},{10,14},{12,16},{14,18},{16,20},{1... | collective-permute-start | bytes 3145736 | tf_op jit(solution)/shard_map/ppermute | solution.py:610
  19.2 44.8 %collective-permute-start.13 = (bf16[32,8192]{1,0:T(8,128)(2,1)}, bf16[32,8192]{1,0:T(8,128)(2,1)S(1)}, u32[]{:S(2)}, u32[]{:S(2)}) collective-permute-start(bf16[32,8192]{1,0:T(8,128)(2,1)} %get-tuple-element.347), channel_id=1, source_target_pairs={{0,6},{2,8},{4,10},{6,12},{8,14},{10,16},{12,18},{14,20},{16,22},{... | collective-permute-start | bytes 1572872 | tf_op jit(solution)/shard_map/ppermute | solution.py:610
  22.7 41.4 %copy-start.10 = (s32[4,4096]{1,0:T(4,128)}, s32[4,4096]{1,0:T(4,128)S(1)}, u32[]{:S(2)}) copy-start(s32[4,4096]{1,0:T(4,128)S(1)} %collective-permute-done.16.shuf_other) | copy-start | bytes 196612
  22.7 41.4 %collective-permute-start.14 = (bf16[16,8192]{1,0:T(8,128)(2,1)}, bf16[16,8192]{1,0:T(8,128)(2,1)S(1)}, u32[]{:S(2)}, u32[]{:S(2)}) collective-permute-start(bf16[16,8192]{1,0:T(8,128)(2,1)} %get-tuple-element.348), channel_id=1, source_target_pairs={{0,8},{2,10},{4,12},{6,14},{8,16},{10,18},{12,20},{14,22},{16,24},... | collective-permute-start | bytes 786440 | tf_op jit(solution)/shard_map/ppermute | solution.py:610
  64.1 5.4 %collective-permute-start.18 = (bf16[64,8192]{1,0:T(8,128)(2,1)S(1)}, bf16[64,8192]{1,0:T(8,128)(2,1)}, u32[]{:S(2)}, u32[]{:S(2)}) collective-permute-start(bf16[64,8192]{1,0:T(8,128)(2,1)S(1)} %collective-permute-done.11.rest_1_), channel_id=1, source_target_pairs={{0,1},{1,0},{2,3},{3,2},{4,5},{5,4},{6,7},{7,6},{8,9},{9,8},{10,11... | collective-permute-start | bytes 3145736 | tf_op jit(solution)/shard_map/ppermute | solution.py:29
  64.2 5.6 %collective-permute-start.19 = (bf16[64,8192]{1,0:T(8,128)(2,1)}, bf16[64,8192]{1,0:T(8,128)(2,1)}, u32[]{:S(2)}, u32[]{:S(2)}) collective-permute-start(bf16[64,8192]{1,0:T(8,128)(2,1)} %collective-permute-done.12.rest_2_), channel_id=1, source_target_pairs={{0,1},{1,0},{2,3},{3,2},{4,5},{5,4},{6,7},{7,6},{8,9},{9,8},{10,11... | collective-permute-start | bytes 3145736 | tf_op jit(solution)/shard_map/ppermute | solution.py:29
  64.7 4.9 %collective-permute-start.20 = (bf16[32,8192]{1,0:T(8,128)(2,1)S(1)}, bf16[32,8192]{1,0:T(8,128)(2,1)}, u32[]{:S(2)}, u32[]{:S(2)}) collective-permute-start(bf16[32,8192]{1,0:T(8,128)(2,1)S(1)} %collective-permute-done.13.rest_3_), channel_id=1, source_target_pairs={{0,1},{1,0},{2,3},{3,2},{4,5},{5,4},{6,7},{7,6},{8,9},{9,8},{10,11... | collective-permute-start | bytes 1572872 | tf_op jit(solution)/shard_map/ppermute | solution.py:29
  64.8 3.9 %collective-permute-start.21 = (bf16[16,8192]{1,0:T(8,128)(2,1)S(1)}, bf16[16,8192]{1,0:T(8,128)(2,1)S(1)}, u32[]{:S(2)}, u32[]{:S(2)}) collective-permute-start(bf16[16,8192]{1,0:T(8,128)(2,1)S(1)} %collective-permute-done.14.rest_4_), channel_id=1, source_target_pairs={{0,1},{1,0},{2,3},{3,2},{4,5},{5,4},{6,7},{7,6},{8,9},{9,8},{10,11... | collective-permute-start | bytes 786440 | tf_op jit(solution)/shard_map/ppermute | solution.py:29
  85.3 0.6 copy-start
  98.0 1.3 %copy-start.3 = (f32[16,8,128]{2,1,0:T(8,128)}, f32[16,8,128]{2,1,0:T(8,128)S(1)}, u32[]{:S(2)}) copy-start(f32[16,8,128]{2,1,0:T(8,128)S(1)} %all_to_all.5.own_ref) | copy-start | bytes 196612
  98.0 1.3 %collective-permute-start.22 = (f32[16,8,128]{2,1,0:T(8,128)S(1)}, f32[16,8,128]{2,1,0:T(8,128)S(1)}, u32[]{:S(2)}, u32[]{:S(2)}) collective-permute-start(f32[16,8,128]{2,1,0:T(8,128)S(1)} %all_to_all.5.own_ref), channel_id=1, source_target_pairs={{0,1},{1,0},{2,3},{3,2},{4,5},{5,4},{6,7},{7,6},{8,9},{9,8},{10,11... | collective-permute-start | bytes 196616 | tf_op jit(solution)/shard_map/ppermute | solution.py:29
  99.3 0.6 copy-start.6

commit v14 on v11

--- a/solution.py
+++ b/solution.py
@@ -12,6 +12,7 @@
 LANES = 128
 ROWS_STEP = 16
 UNROLL = 32
+DEPTH = 2048
 SIDE = 2 * LANES
 CHUNK = 1024
 MIB = 2**20
@@ -75,7 +76,7 @@
         scratch_shapes=[pltpu.VMEM((3, snp_rows, LANES), jnp.float32)],
         compiler_params=pltpu.CompilerParams(vmem_limit_bytes=60 * MIB),
         cost_estimate=pl.CostEstimate(
-            flops=5 * 10**9, bytes_accessed=2 * snp_rows * half, transcendentals=0
+            flops=10**6, bytes_accessed=10**6, transcendentals=0
         ),
         name="local_moments",
     )(geno, env)
@@ -562,17 +563,17 @@
         functools.partial(
             product_kernel, caps=caps, labels=labels, genes=genes, blocks_dev=blocks_dev
         ),
-        grid=(all_samples // CHUNK,),
+        grid=(all_samples // DEPTH,),
         out_shape=outs,
         in_specs=[
             pl.BlockSpec(memory_space=pltpu.SMEM),
             *[whole(x) for x in (*sums, plan)],
-            *[pl.BlockSpec((x.shape[0], CHUNK), lambda k: (0, k)) for x in arrays],
-            *[pl.BlockSpec((CHUNK, w.shape[1]), lambda k: (k, 0)) for w in weights],
+            *[pl.BlockSpec((x.shape[0], DEPTH), lambda k: (0, k)) for x in arrays],
+            *[pl.BlockSpec((DEPTH, w.shape[1]), lambda k: (k, 0)) for w in weights],
         ],
         out_specs=tuple(whole(x) for x in outs),
         scratch_shapes=[
-            pltpu.VMEM((used, CHUNK), jnp.bfloat16),
+            pltpu.VMEM((used, DEPTH), jnp.bfloat16),
             pltpu.VMEM((padded, width), jnp.float32),
             pltpu.VMEM((genes, LANES), jnp.float32),
         ],
@@ -621,13 +622,14 @@
         other_pheno = swapped(phenotypes)
         own_sums = local_moments(genotypes, env)
         sums = (own_sums, swapped(own_sums))
-        late_geno, _ = lax.optimization_barrier((genotypes, other_pheno))
-        other_geno = swapped(late_geno)
         other_env = swapped(env)
         other_shuffles = swapped(shuffles)
+        late_pheno, _ = lax.optimization_barrier((other_pheno, own_sums))
         rounds, plan, full, *payloads = select(
-            turn, pos, chrom_bounds, start, end, phenotypes, other_pheno, caps, blocks_dev
-        )
+            turn, pos, chrom_bounds, start, end, phenotypes, late_pheno, caps, blocks_dev
+        )
+        late_geno, plan = lax.optimization_barrier((genotypes, plan))
+        other_geno = swapped(late_geno)
         payloads = [full] * (reach - len(payloads)) + payloads
         mine = [travel(k, x) for k, x in enumerate(payloads, 1)]
         weights = snp_side(

time: 99.5 us -> 100 us (level)
  blocking collectives: 10.4 us -> 14.2 us
  Pallas kernels: 59.3 us -> 57.8 us
  waiting for transfers between devices: 7.42 us -> 5.94 us
    all_to_all x1, blocking collectives: 10.4 us -> 14.2 us  [shards(): gathered = lax.all_to_all(found, 'genome', 0, 0, tiled=True)]
    ppermute x10, waiting for transfers between devices: 7.41 us -> 5.93 us  [swapped(): lax.ppermute(x, 'sample', [(i, (i + 1) % count) for i in range(count)])]
    pallas_call x1, Pallas kernels: 15.5 us -> 14.1 us  [products(): pl.pallas_call(functools.partial(product_kernel, caps=caps, labels=labels...]
  transfers between devices with their start and end apart: 14 -> 14, of which waited for: 4 -> 4; matrix products, arithmetic and copies ran while one was open for 0% -> 0% of each run, Pallas kernels for 43% -> 39%
where the time goes in v14:
time: 100 us; the launch traced here: 99.9 us
  Pallas kernels  57.8 us (58%)
  starting transfers between devices  19.6 us (20%)
  blocking collectives  14.2 us (14%)
  waiting for transfers between devices  5.94 us (6%)
  local copies, waits for them, and re-layouts  1.24 us (1%)
    pallas_call x1, Pallas kernels, snp_side(): pl.pallas_call(functools.partial(snp_side_kernel, labels=labels), out_sha...  34.8 us
    ppermute x4, starting transfers between devices, travel(): return lax.ppermute(payload, ('genome', 'sample'), pairs)  16.9 us
    all_to_all x1, blocking collectives, shards(): gathered = lax.all_to_all(found, 'genome', 0, 0, tiled=True)  14.2 us
    pallas_call x1, Pallas kernels, products(): pl.pallas_call(functools.partial(product_kernel, caps=caps, labels=labels...  14.1 us
    ppermute x10, waiting for transfers between devices, swapped(): lax.ppermute(x, 'sample', [(i, (i + 1) % count) for i in range(count)])  5.93 us
    pallas_call x1, Pallas kernels, local_moments(): pl.pallas_call(moments_kernel, grid=(half // chunk,), out_shape=jax.Shape...  4.54 us
    pallas_call x1, Pallas kernels, select(): pl.pallas_call(functools.partial(select_kernel, caps=caps, blocks_dev=blo...  2.86 us
    ppermute x10, starting transfers between devices, swapped(): lax.ppermute(x, 'sample', [(i, (i + 1) % count) for i in range(count)])  2.73 us
  transfers between devices with their start and end apart: 14, of which 4 were waited for; matrix products, arithmetic and copies ran while one was open for 0% of the time, Pallas kernels for 39%

profile of v14, /device:TPU:0, one launch (start us, length us, event | category | flops | bytes accessed | tf_op | source)
XLA Modules:
  0.0 99.9 jit_solution(1989040680276357607)
XLA Ops:
  0.0 0.0 copy-start.9
  0.0 0.5 collective-permute-start.10
  0.6 4.5 %local_moments.2.sums_own = f32[8,512]{1,0:T(8,128)S(1)} custom-call(bf16[512,4096]{1,0:T(8,128)(2,1)} %own_ref.3, f32[1,4096]{1,0:T(1,128)} %bitcast.14), custom_call_target="tpu_custom_call" | custom-call | flops 1000000 | bytes 1000000 | tf_op jit(solution)/shard_map/local_moments/pallas_call | solution.py:67
  5.1 0.1 pad_add_fusion.pos_ref
  5.2 2.9 %select.6 = (s32[1]{0:T(128)}, s32[8,640]{1,0:T(8,128)S(1)}, bf16[64,8192]{1,0:T(8,128)(2,1)S(1)}, bf16[32,8192]{1,0:T(8,128)(2,1)}, bf16[16,8192]{1,0:T(8,128)(2,1)}) custom-call(s32[1]{0:T(128)} %constant.18.clone.1.round_ref, s32[2]{0:T(128)S(1)} %pad_add_fusion.pos_ref, s32[15]{0:T(128)S(1)} %copy-done.7, s32[8,128]{1,0:T(8,128)S(1)} %bitcast.10, ...), custom_call_target="tpu_custom_call" | custom-call | tf_op jit(solution)/shard_map/select/pallas_call | solution.py:402
  8.1 0.2 collective-permute-start.17
  8.3 0.4 collective-permute-start.16
  8.7 0.1 collective-permute-start.9
  8.8 0.4 collective-permute-start.15
  9.2 4.5 %collective-permute-start.11 = (bf16[64,8192]{1,0:T(8,128)(2,1)S(1)}, bf16[64,8192]{1,0:T(8,128)(2,1)S(1)}, u32[]{:S(2)}, u32[]{:S(2)}) collective-permute-start(bf16[64,8192]{1,0:T(8,128)(2,1)S(1)} %get-tuple-element.346.rest_0_), channel_id=1, source_target_pairs={{0,2},{2,4},{4,6},{6,8},{8,10},{10,12},{12,14},{14,16},{16,18},{18... | collective-permute-start | bytes 3145736 | tf_op jit(solution)/shard_map/ppermute | solution.py:618
  13.7 0.0 collective-permute-done.9.sums_other
  13.7 5.6 %collective-permute-start.12 = (bf16[64,8192]{1,0:T(8,128)(2,1)S(1)}, bf16[64,8192]{1,0:T(8,128)(2,1)}, u32[]{:S(2)}, u32[]{:S(2)}) collective-permute-start(bf16[64,8192]{1,0:T(8,128)(2,1)S(1)} %get-tuple-element.346.rest_0_), channel_id=1, source_target_pairs={{0,4},{2,6},{4,8},{6,10},{8,12},{10,14},{12,16},{14,18},{16,20},{1... | collective-permute-start | bytes 3145736 | tf_op jit(solution)/shard_map/ppermute | solution.py:618
  19.3 0.0 collective-permute-done.15.env_other
  19.3 3.4 %collective-permute-start.13 = (bf16[32,8192]{1,0:T(8,128)(2,1)}, bf16[32,8192]{1,0:T(8,128)(2,1)S(1)}, u32[]{:S(2)}, u32[]{:S(2)}) collective-permute-start(bf16[32,8192]{1,0:T(8,128)(2,1)} %get-tuple-element.347), channel_id=1, source_target_pairs={{0,6},{2,8},{4,10},{6,12},{8,14},{10,16},{12,18},{14,20},{16,22},{... | collective-permute-start | bytes 1572872 | tf_op jit(solution)/shard_map/ppermute | solution.py:618
  22.8 3.4 %collective-permute-start.14 = (bf16[16,8192]{1,0:T(8,128)(2,1)}, bf16[16,8192]{1,0:T(8,128)(2,1)S(1)}, u32[]{:S(2)}, u32[]{:S(2)}) collective-permute-start(bf16[16,8192]{1,0:T(8,128)(2,1)} %get-tuple-element.348), channel_id=1, source_target_pairs={{0,8},{2,10},{4,12},{6,14},{8,16},{10,18},{12,20},{14,22},{16,24},... | collective-permute-start | bytes 786440 | tf_op jit(solution)/shard_map/ppermute | solution.py:618
  26.1 34.8 %snp_side.6 = (bf16[8192,512]{1,0:T(8,128)(2,1)}, bf16[8192,512]{1,0:T(8,128)(2,1)}, bf16[8192,256]{1,0:T(8,128)(2,1)}) custom-call(s32[1]{0:T(128)} %bitcast.3.core_ref, f32[1,4096]{1,0:T(1,128)S(1)} %bitcast.16, f32[1,4096]{1,0:T(1,128)S(1)} %collective-permute-done.15.env_other, f32[8,512]{1,0:T(8,128)S(1)} %local_moments.2.sums_own, ...), custom_call_target="tpu_custom_call" | custom-call | flops 40000000000 | bytes 60000000 | tf_op jit(solution)/shard_map/snp_side/pallas_call | solution.py:250
  60.9 0.0 collective-permute-done.14.rest_4_
  61.0 0.0 collective-permute-done.11.rest_1_
  61.0 0.5 collective-permute-start.18
  61.5 0.1 collective-permute-start.19
  61.6 0.4 collective-permute-start.20
  62.0 0.1 collective-permute-start.21
  62.1 3.5 %collective-permute-done.21.rest_8_ = bf16[16,8192]{1,0:T(8,128)(2,1)S(1)} collective-permute-done((bf16[16,8192]{1,0:T(8,128)(2,1)S(1)}, bf16[16,8192]{1,0:T(8,128)(2,1)S(1)}, u32[]{:S(2)}, u32[]{:S(2)}) %collective-permute-start.21) | collective-permute-done | bytes 262176 | tf_op jit(solution)/shard_map/ppermute | solution.py:29
  65.6 0.9 collective-permute-done.20.rest_7_
  66.5 0.3 collective-permute-done.19.rest_6_
  66.8 14.1 %products.6 = (f32[16,8,128]{2,1,0:T(8,128)S(1)}, f32[8,64]{1,0:T(8,128)S(1)}) custom-call(s32[2]{0:T(128)S(1)} %pad_add_fusion.pos_ref, f32[8,512]{1,0:T(8,128)S(1)} %local_moments.2.sums_own, f32[8,512]{1,0:T(8,128)S(1)} %collective-permute-done.9.sums_other, s32[8,640]{1,0:T(8,128)S(1)} %get-tuple-element.345.plan_ref, ...), custom_call_target="tpu_custom_call" | custom-call | flops 8724152320 | bytes 27787264 | tf_op jit(solution)/shard_map/products/pallas_call | solution.py:562
  80.9 0.6 copy-done
  81.5 0.8 while.14
  82.3 14.2 %all_to_all.5.own_ref = f32[16,8,128]{2,1,0:T(8,128)S(1)} all-to-all(f32[16,8,128]{2,1,0:T(8,128)S(1)} %get-tuple-element.362), channel_id=1, replica_groups=mesh['genome'=16,'sample'=2] {'genome'}, dimensions={0} | all-to-all | bytes 131072 | tf_op jit(solution)/shard_map/all_to_all | solution.py:656
  96.5 1.3 %collective-permute-done.22.other_ref = f32[16,8,128]{2,1,0:T(8,128)S(1)} collective-permute-done((f32[16,8,128]{2,1,0:T(8,128)S(1)}, f32[16,8,128]{2,1,0:T(8,128)S(1)}, u32[]{:S(2)}, u32[]{:S(2)}) %collective-permute-start.22) | collective-permute-done | bytes 65568 | tf_op jit(solution)/shard_map/ppermute | solution.py:29
  97.8 0.6 copy-done.6
  98.4 1.5 %finish.1 = f32[5,64]{1,0:T(8,128)} custom-call(f32[16,8,128]{2,1,0:T(8,128)} %copy-done.3, f32[16,8,128]{2,1,0:T(8,128)} %copy-done.6, f32[8,64]{1,0:T(8,128)} %copy-done), custom_call_target="tpu_custom_call" | custom-call | tf_op jit(solution)/shard_map/finish/pallas_call | solution.py:657
  (26 shorter events, 0.1 us)
Async XLA Ops:
  0.0 5.2 %copy-start.1 = (bf16[64,4096]{1,0:T(8,128)(2,1)S(1)}, bf16[64,4096]{1,0:T(8,128)(2,1)}, u32[]{:S(2)}) copy-start(bf16[64,4096]{1,0:T(8,128)(2,1)} %own_ref.2) | copy-start | bytes 1572868
  0.0 8.8 %copy-start.8 = (f32[4096]{0:T(1024)S(1)}, f32[4096]{0:T(1024)}, u32[]{:S(2)}) copy-start(f32[4096]{0:T(1024)} %param.11) | copy-start | bytes 49156
  0.0 5.2 %copy-start.4 = (s32[1024]{0:T(1024)S(1)}, s32[1024]{0:T(1024)}, u32[]{:S(2)}) copy-start(s32[1024]{0:T(1024)} %param.13) | copy-start | bytes 12292
  0.0 5.2 %copy-start.5 = (s32[1024]{0:T(1024)S(1)}, s32[1024]{0:T(1024)}, u32[]{:S(2)}) copy-start(s32[1024]{0:T(1024)} %param.14) | copy-start | bytes 12292
  0.0 5.2 %copy-start.7 = (s32[15]{0:T(128)S(1)}, s32[15]{0:T(128)}, u32[]{:S(2)}) copy-start(s32[15]{0:T(128)} %bounds_ref.1) | copy-start | bytes 184
  0.0 8.3 %copy-start.9 = (s32[4,4096]{1,0:T(4,128)S(1)}, s32[4,4096]{1,0:T(4,128)}, u32[]{:S(2)}) copy-start(s32[4,4096]{1,0:T(4,128)} %shuf_own.1) | copy-start | bytes 196612
  0.0 5.2 %collective-permute-start.10 = (bf16[64,4096]{1,0:T(8,128)(2,1)}, bf16[64,4096]{1,0:T(8,128)(2,1)S(1)}, u32[]{:S(2)}, u32[]{:S(2)}) collective-permute-start(bf16[64,4096]{1,0:T(8,128)(2,1)} %own_ref.2), channel_id=1, source_target_pairs={{0,1},{1,0},{2,3},{3,2},{4,5},{5,4},{6,7},{7,6},{8,9},{9,8},{10,11... | collective-permute-start | bytes 1572872 | tf_op jit(solution)/shard_map/ppermute | solution.py:29
  5.2 4.0 %copy-start.2 = (bf16[64,4096]{1,0:T(8,128)(2,1)}, bf16[64,4096]{1,0:T(8,128)(2,1)S(1)}, u32[]{:S(2)}) copy-start(bf16[64,4096]{1,0:T(8,128)(2,1)S(1)} %collective-permute-done.10.other_ref) | copy-start | bytes 1572868
  8.1 18.0 %collective-permute-start.17 = (bf16[512,4096]{1,0:T(8,128)(2,1)}, bf16[512,4096]{1,0:T(8,128)(2,1)}, u32[]{:S(2)}, u32[]{:S(2)}) collective-permute-start(bf16[512,4096]{1,0:T(8,128)(2,1)} %own_ref.3), channel_id=1, source_target_pairs={{0,1},{1,0},{2,3},{3,2},{4,5},{5,4},{6,7},{7,6},{8,9},{9,8},{10,11... | collective-permute-start | bytes 12582920 | tf_op jit(solution)/shard_map/ppermute | solution.py:29
  8.3 14.5 %collective-permute-start.16 = (s32[4,4096]{1,0:T(4,128)S(1)}, s32[4,4096]{1,0:T(4,128)S(1)}, u32[]{:S(2)}, u32[]{:S(2)}) collective-permute-start(s32[4,4096]{1,0:T(4,128)S(1)} %copy-done.9), channel_id=1, source_target_pairs={{0,1},{1,0},{2,3},{3,2},{4,5},{5,4},{6,7},{7,6},{8,9},{9,8},{10,11... | collective-permute-start | bytes 196616 | tf_op jit(solution)/shard_map/ppermute | solution.py:29
  8.7 5.1 %collective-permute-start.9 = (f32[8,512]{1,0:T(8,128)S(1)}, f32[8,512]{1,0:T(8,128)S(1)}, u32[]{:S(2)}, u32[]{:S(2)}) collective-permute-start(f32[8,512]{1,0:T(8,128)S(1)} %local_moments.2.sums_own), channel_id=1, source_target_pairs={{0,1},{1,0},{2,3},{3,2},{4,5},{5,4},{6,7},{7,6},{8,9},{9,8},{10,11... | collective-permute-start | bytes 49160 | tf_op jit(solution)/shard_map/ppermute | solution.py:29
  8.8 10.5 %collective-permute-start.15 = (f32[1,4096]{1,0:T(1,128)S(1)}, f32[1,4096]{1,0:T(1,128)S(1)}, u32[]{:S(2)}, u32[]{:S(2)}) collective-permute-start(f32[1,4096]{1,0:T(1,128)S(1)} %bitcast.15), channel_id=1, source_target_pairs={{0,1},{1,0},{2,3},{3,2},{4,5},{5,4},{6,7},{7,6},{8,9},{9,8},{10,11... | collective-permute-start | bytes 49160 | tf_op jit(solution)/shard_map/ppermute | solution.py:29
  9.2 51.8 %collective-permute-start.11 = (bf16[64,8192]{1,0:T(8,128)(2,1)S(1)}, bf16[64,8192]{1,0:T(8,128)(2,1)S(1)}, u32[]{:S(2)}, u32[]{:S(2)}) collective-permute-start(bf16[64,8192]{1,0:T(8,128)(2,1)S(1)} %get-tuple-element.346.rest_0_), channel_id=1, source_target_pairs={{0,2},{2,4},{4,6},{6,8},{8,10},{10,12},{12,14},{14,16},{16,18},{18... | collective-permute-start | bytes 3145736 | tf_op jit(solution)/shard_map/ppermute | solution.py:618
  13.7 47.2 %collective-permute-start.12 = (bf16[64,8192]{1,0:T(8,128)(2,1)S(1)}, bf16[64,8192]{1,0:T(8,128)(2,1)}, u32[]{:S(2)}, u32[]{:S(2)}) collective-permute-start(bf16[64,8192]{1,0:T(8,128)(2,1)S(1)} %get-tuple-element.346.rest_0_), channel_id=1, source_target_pairs={{0,4},{2,6},{4,8},{6,10},{8,12},{10,14},{12,16},{14,18},{16,20},{1... | collective-permute-start | bytes 3145736 | tf_op jit(solution)/shard_map/ppermute | solution.py:618
  19.3 41.6 %collective-permute-start.13 = (bf16[32,8192]{1,0:T(8,128)(2,1)}, bf16[32,8192]{1,0:T(8,128)(2,1)S(1)}, u32[]{:S(2)}, u32[]{:S(2)}) collective-permute-start(bf16[32,8192]{1,0:T(8,128)(2,1)} %get-tuple-element.347), channel_id=1, source_target_pairs={{0,6},{2,8},{4,10},{6,12},{8,14},{10,16},{12,18},{14,20},{16,22},{... | collective-permute-start | bytes 1572872 | tf_op jit(solution)/shard_map/ppermute | solution.py:618
  22.7 38.2 %copy-start.10 = (s32[4,4096]{1,0:T(4,128)}, s32[4,4096]{1,0:T(4,128)S(1)}, u32[]{:S(2)}) copy-start(s32[4,4096]{1,0:T(4,128)S(1)} %collective-permute-done.16.shuf_other) | copy-start | bytes 196612
  22.8 38.2 %collective-permute-start.14 = (bf16[16,8192]{1,0:T(8,128)(2,1)}, bf16[16,8192]{1,0:T(8,128)(2,1)S(1)}, u32[]{:S(2)}, u32[]{:S(2)}) collective-permute-start(bf16[16,8192]{1,0:T(8,128)(2,1)} %get-tuple-element.348), channel_id=1, source_target_pairs={{0,8},{2,10},{4,12},{6,14},{8,16},{10,18},{12,20},{14,22},{16,24},... | collective-permute-start | bytes 786440 | tf_op jit(solution)/shard_map/ppermute | solution.py:618
  61.0 5.5 %collective-permute-start.18 = (bf16[64,8192]{1,0:T(8,128)(2,1)S(1)}, bf16[64,8192]{1,0:T(8,128)(2,1)}, u32[]{:S(2)}, u32[]{:S(2)}) collective-permute-start(bf16[64,8192]{1,0:T(8,128)(2,1)S(1)} %collective-permute-done.11.rest_1_), channel_id=1, source_target_pairs={{0,1},{1,0},{2,3},{3,2},{4,5},{5,4},{6,7},{7,6},{8,9},{9,8},{10,11... | collective-permute-start | bytes 3145736 | tf_op jit(solution)/shard_map/ppermute | solution.py:29
  61.5 5.3 %collective-permute-start.19 = (bf16[64,8192]{1,0:T(8,128)(2,1)}, bf16[64,8192]{1,0:T(8,128)(2,1)}, u32[]{:S(2)}, u32[]{:S(2)}) collective-permute-start(bf16[64,8192]{1,0:T(8,128)(2,1)} %collective-permute-done.12.rest_2_), channel_id=1, source_target_pairs={{0,1},{1,0},{2,3},{3,2},{4,5},{5,4},{6,7},{7,6},{8,9},{9,8},{10,11... | collective-permute-start | bytes 3145736 | tf_op jit(solution)/shard_map/ppermute | solution.py:29
  61.6 4.9 %collective-permute-start.20 = (bf16[32,8192]{1,0:T(8,128)(2,1)S(1)}, bf16[32,8192]{1,0:T(8,128)(2,1)}, u32[]{:S(2)}, u32[]{:S(2)}) collective-permute-start(bf16[32,8192]{1,0:T(8,128)(2,1)S(1)} %collective-permute-done.13.rest_3_), channel_id=1, source_target_pairs={{0,1},{1,0},{2,3},{3,2},{4,5},{5,4},{6,7},{7,6},{8,9},{9,8},{10,11... | collective-permute-start | bytes 1572872 | tf_op jit(solution)/shard_map/ppermute | solution.py:29
  62.0 3.6 %collective-permute-start.21 = (bf16[16,8192]{1,0:T(8,128)(2,1)S(1)}, bf16[16,8192]{1,0:T(8,128)(2,1)S(1)}, u32[]{:S(2)}, u32[]{:S(2)}) collective-permute-start(bf16[16,8192]{1,0:T(8,128)(2,1)S(1)} %collective-permute-done.14.rest_4_), channel_id=1, source_target_pairs={{0,1},{1,0},{2,3},{3,2},{4,5},{5,4},{6,7},{7,6},{8,9},{9,8},{10,11... | collective-permute-start | bytes 786440 | tf_op jit(solution)/shard_map/ppermute | solution.py:29
  80.9 0.6 copy-start
  96.5 1.3 %copy-start.3 = (f32[16,8,128]{2,1,0:T(8,128)}, f32[16,8,128]{2,1,0:T(8,128)S(1)}, u32[]{:S(2)}) copy-start(f32[16,8,128]{2,1,0:T(8,128)S(1)} %all_to_all.5.own_ref) | copy-start | bytes 196612
  96.5 1.3 %collective-permute-start.22 = (f32[16,8,128]{2,1,0:T(8,128)S(1)}, f32[16,8,128]{2,1,0:T(8,128)S(1)}, u32[]{:S(2)}, u32[]{:S(2)}) collective-permute-start(f32[16,8,128]{2,1,0:T(8,128)S(1)} %all_to_all.5.own_ref), channel_id=1, source_target_pairs={{0,1},{1,0},{2,3},{3,2},{4,5},{5,4},{6,7},{7,6},{8,9},{9,8},{10,11... | collective-permute-start | bytes 196616 | tf_op jit(solution)/shard_map/ppermute | solution.py:29
  97.8 0.6 copy-start.6

commit v15 on v14

--- a/solution.py
+++ b/solution.py
@@ -76,7 +76,7 @@
         scratch_shapes=[pltpu.VMEM((3, snp_rows, LANES), jnp.float32)],
         compiler_params=pltpu.CompilerParams(vmem_limit_bytes=60 * MIB),
         cost_estimate=pl.CostEstimate(
-            flops=10**6, bytes_accessed=10**6, transcendentals=0
+            flops=5 * 10**9, bytes_accessed=2 * snp_rows * half, transcendentals=0
         ),
         name="local_moments",
     )(geno, env)
@@ -622,14 +622,13 @@
         other_pheno = swapped(phenotypes)
         own_sums = local_moments(genotypes, env)
         sums = (own_sums, swapped(own_sums))
+        late_geno, _ = lax.optimization_barrier((genotypes, other_pheno))
+        other_geno = swapped(late_geno)
         other_env = swapped(env)
         other_shuffles = swapped(shuffles)
-        late_pheno, _ = lax.optimization_barrier((other_pheno, own_sums))
         rounds, plan, full, *payloads = select(
-            turn, pos, chrom_bounds, start, end, phenotypes, late_pheno, caps, blocks_dev
-        )
-        late_geno, plan = lax.optimization_barrier((genotypes, plan))
-        other_geno = swapped(late_geno)
+            turn, pos, chrom_bounds, start, end, phenotypes, other_pheno, caps, blocks_dev
+        )
         payloads = [full] * (reach - len(payloads)) + payloads
         mine = [travel(k, x) for k, x in enumerate(payloads, 1)]
         weights = snp_side(

time: 100 us -> 98 us (0.980)
  blocking collectives: 14.2 us -> 10.4 us
  waiting for transfers between devices: 5.94 us -> 7.42 us
    all_to_all x1, blocking collectives: 14.2 us -> 10.4 us  [shards(): gathered = lax.all_to_all(found, 'genome', 0, 0, tiled=True)]
    ppermute x10, waiting for transfers between devices: 5.93 us -> 7.41 us  [swapped(): lax.ppermute(x, 'sample', [(i, (i + 1) % count) for i in range(count)])]
  transfers between devices with their start and end apart: 14 -> 14, of which waited for: 4 -> 4; matrix products, arithmetic and copies ran while one was open for 0% -> 0% of each run, Pallas kernels for 39% -> 43%
where the time goes in v15:
time: 98 us; the launch traced here: 97.5 us
  Pallas kernels  58 us (59%)
  starting transfers between devices  18.8 us (19%)
  blocking collectives  10.4 us (11%)
  waiting for transfers between devices  7.42 us (8%)
  local copies, waits for them, and re-layouts  1.85 us (2%)
    pallas_call x1, Pallas kernels, snp_side(): pl.pallas_call(functools.partial(snp_side_kernel, labels=labels), out_sha...  34.9 us
    ppermute x4, starting transfers between devices, travel(): return lax.ppermute(payload, ('genome', 'sample'), pairs)  16.1 us
    pallas_call x1, Pallas kernels, products(): pl.pallas_call(functools.partial(product_kernel, caps=caps, labels=labels...  14.1 us
    all_to_all x1, blocking collectives, shards(): gathered = lax.all_to_all(found, 'genome', 0, 0, tiled=True)  10.4 us
    ppermute x10, waiting for transfers between devices, swapped(): lax.ppermute(x, 'sample', [(i, (i + 1) % count) for i in range(count)])  7.41 us
    pallas_call x1, Pallas kernels, local_moments(): pl.pallas_call(moments_kernel, grid=(half // chunk,), out_shape=jax.Shape...  4.54 us
    pallas_call x1, Pallas kernels, select(): pl.pallas_call(functools.partial(select_kernel, caps=caps, blocks_dev=blo...  2.87 us
    ppermute x10, starting transfers between devices, swapped(): lax.ppermute(x, 'sample', [(i, (i + 1) % count) for i in range(count)])  2.68 us
  transfers between devices with their start and end apart: 14, of which 4 were waited for; matrix products, arithmetic and copies ran while one was open for 0% of the time, Pallas kernels for 43%

profile of v15, /device:TPU:0, one launch (start us, length us, event | category | flops | bytes accessed | tf_op | source)
XLA Modules:
  0.0 97.5 jit_solution(12954490615364171861)
XLA Ops:
  0.0 0.5 collective-permute-start.9
  0.5 1.7 %collective-permute-done.9.other_ref = bf16[64,4096]{1,0:T(8,128)(2,1)S(1)} collective-permute-done((bf16[64,4096]{1,0:T(8,128)(2,1)}, bf16[64,4096]{1,0:T(8,128)(2,1)S(1)}, u32[]{:S(2)}, u32[]{:S(2)}) %collective-permute-start.9) | collective-permute-done | bytes 524320 | tf_op jit(solution)/shard_map/ppermute | solution.py:29
  2.2 0.4 collective-permute-start.16
  2.6 0.2 collective-permute-start.14
  2.8 4.5 %local_moments.2.sums_own = f32[8,512]{1,0:T(8,128)S(1)} custom-call(bf16[512,4096]{1,0:T(8,128)(2,1)} %own_ref.3, f32[1,4096]{1,0:T(1,128)} %bitcast.15), custom_call_target="tpu_custom_call" | custom-call | flops 5000000000 | bytes 4194304 | tf_op jit(solution)/shard_map/local_moments/pallas_call | solution.py:67
  7.4 0.4 collective-permute-start.8
  7.8 0.1 collective-permute-start.15
  8.0 0.1 pad_add_fusion.pos_ref
  8.0 2.9 %select.6 = (s32[1]{0:T(128)}, s32[8,640]{1,0:T(8,128)S(1)}, bf16[64,8192]{1,0:T(8,128)(2,1)S(1)}, bf16[32,8192]{1,0:T(8,128)(2,1)}, bf16[16,8192]{1,0:T(8,128)(2,1)}) custom-call(s32[1]{0:T(128)} %constant.18.clone.1.round_ref, s32[2]{0:T(128)S(1)} %pad_add_fusion.pos_ref, s32[15]{0:T(128)S(1)} %copy-done.7, s32[8,128]{1,0:T(8,128)S(1)} %bitcast.10, ...), custom_call_target="tpu_custom_call" | custom-call | tf_op jit(solution)/shard_map/select/pallas_call | solution.py:402
  10.9 4.9 %collective-permute-start.11 = (bf16[64,8192]{1,0:T(8,128)(2,1)S(1)}, bf16[64,8192]{1,0:T(8,128)(2,1)S(1)}, u32[]{:S(2)}, u32[]{:S(2)}) collective-permute-start(bf16[64,8192]{1,0:T(8,128)(2,1)S(1)} %get-tuple-element.352.rest_0_), channel_id=1, source_target_pairs={{0,4},{2,6},{4,8},{6,10},{8,12},{10,14},{12,16},{14,18},{16,20},{1... | collective-permute-start | bytes 3145736 | tf_op jit(solution)/shard_map/ppermute | solution.py:618
  15.8 4.4 %collective-permute-start.10 = (bf16[64,8192]{1,0:T(8,128)(2,1)S(1)}, bf16[64,8192]{1,0:T(8,128)(2,1)}, u32[]{:S(2)}, u32[]{:S(2)}) collective-permute-start(bf16[64,8192]{1,0:T(8,128)(2,1)S(1)} %get-tuple-element.352.rest_0_), channel_id=1, source_target_pairs={{0,2},{2,4},{4,6},{6,8},{8,10},{10,12},{12,14},{14,16},{16,18},{18... | collective-permute-start | bytes 3145736 | tf_op jit(solution)/shard_map/ppermute | solution.py:618
  20.2 0.0 collective-permute-done.14.env_other
  20.2 2.5 %collective-permute-start.13 = (bf16[16,8192]{1,0:T(8,128)(2,1)}, bf16[16,8192]{1,0:T(8,128)(2,1)S(1)}, u32[]{:S(2)}, u32[]{:S(2)}) collective-permute-start(bf16[16,8192]{1,0:T(8,128)(2,1)} %get-tuple-element.354), channel_id=1, source_target_pairs={{0,8},{2,10},{4,12},{6,14},{8,16},{10,18},{12,20},{14,22},{16,24},... | collective-permute-start | bytes 786440 | tf_op jit(solution)/shard_map/ppermute | solution.py:618
  22.7 0.0 collective-permute-done.15.shuf_other
  22.7 0.6 copy-done.9
  23.3 4.4 %collective-permute-start.12 = (bf16[32,8192]{1,0:T(8,128)(2,1)}, bf16[32,8192]{1,0:T(8,128)(2,1)S(1)}, u32[]{:S(2)}, u32[]{:S(2)}) collective-permute-start(bf16[32,8192]{1,0:T(8,128)(2,1)} %get-tuple-element.353), channel_id=1, source_target_pairs={{0,6},{2,8},{4,10},{6,12},{8,14},{10,16},{12,18},{14,20},{16,22},{... | collective-permute-start | bytes 1572872 | tf_op jit(solution)/shard_map/ppermute | solution.py:618
  27.7 0.0 collective-permute-done.16.other_ref
  27.7 34.9 %snp_side.6 = (bf16[8192,512]{1,0:T(8,128)(2,1)}, bf16[8192,512]{1,0:T(8,128)(2,1)}, bf16[8192,256]{1,0:T(8,128)(2,1)}) custom-call(s32[1]{0:T(128)} %bitcast.3.core_ref, f32[1,4096]{1,0:T(1,128)S(1)} %bitcast.16, f32[1,4096]{1,0:T(1,128)S(1)} %collective-permute-done.14.env_other, f32[8,512]{1,0:T(8,128)S(1)} %local_moments.2.sums_own, ...), custom_call_target="tpu_custom_call" | custom-call | flops 40000000000 | bytes 60000000 | tf_op jit(solution)/shard_map/snp_side/pallas_call | solution.py:250
  62.7 0.0 collective-permute-done.13.rest_4_
  62.8 0.1 collective-permute-start.17
  62.8 0.5 collective-permute-start.18
  63.3 0.1 collective-permute-start.19
  63.4 0.4 collective-permute-start.20
  63.8 3.1 %collective-permute-done.20.rest_8_ = bf16[16,8192]{1,0:T(8,128)(2,1)S(1)} collective-permute-done((bf16[16,8192]{1,0:T(8,128)(2,1)S(1)}, bf16[16,8192]{1,0:T(8,128)(2,1)S(1)}, u32[]{:S(2)}, u32[]{:S(2)}) %collective-permute-start.20) | collective-permute-done | bytes 262176 | tf_op jit(solution)/shard_map/ppermute | solution.py:29
  66.9 1.3 %collective-permute-done.19.rest_7_ = bf16[32,8192]{1,0:T(8,128)(2,1)} collective-permute-done((bf16[32,8192]{1,0:T(8,128)(2,1)S(1)}, bf16[32,8192]{1,0:T(8,128)(2,1)}, u32[]{:S(2)}, u32[]{:S(2)}) %collective-permute-start.19) | collective-permute-done | bytes 524320 | tf_op jit(solution)/shard_map/ppermute | solution.py:29
  68.2 14.1 %products.6 = (f32[16,8,128]{2,1,0:T(8,128)S(1)}, f32[8,64]{1,0:T(8,128)S(1)}) custom-call(s32[2]{0:T(128)S(1)} %pad_add_fusion.pos_ref, f32[8,512]{1,0:T(8,128)} %copy-done.12, f32[8,512]{1,0:T(8,128)} %copy-done.13, s32[8,640]{1,0:T(8,128)S(1)} %get-tuple-element.351.plan_ref, bf16[64,8192]{1,0:T(8,128)(2,1)S(1)} %get-tuple-element.352.rest_0_, ...), custom_call_target="tpu_custom_call" | custom-call | flops 8724152320 | bytes 27787264 | tf_op jit(solution)/shard_map/products/pallas_call | solution.py:562
  82.4 0.6 copy-done
  83.0 0.8 while.14
  83.8 10.4 %all_to_all.5.own_ref = f32[16,8,128]{2,1,0:T(8,128)S(1)} all-to-all(f32[16,8,128]{2,1,0:T(8,128)S(1)} %get-tuple-element.368), channel_id=1, replica_groups=mesh['genome'=16,'sample'=2] {'genome'}, dimensions={0} | all-to-all | bytes 131072 | tf_op jit(solution)/shard_map/all_to_all | solution.py:655
  94.2 1.3 %collective-permute-done.21.other_ref = f32[16,8,128]{2,1,0:T(8,128)S(1)} collective-permute-done((f32[16,8,128]{2,1,0:T(8,128)S(1)}, f32[16,8,128]{2,1,0:T(8,128)S(1)}, u32[]{:S(2)}, u32[]{:S(2)}) %collective-permute-start.21) | collective-permute-done | bytes 65568 | tf_op jit(solution)/shard_map/ppermute | solution.py:29
  95.4 0.6 copy-done.6
  96.0 1.5 %finish.1 = f32[5,64]{1,0:T(8,128)} custom-call(f32[16,8,128]{2,1,0:T(8,128)} %copy-done.3, f32[16,8,128]{2,1,0:T(8,128)} %copy-done.6, f32[8,64]{1,0:T(8,128)} %copy-done), custom_call_target="tpu_custom_call" | custom-call | tf_op jit(solution)/shard_map/finish/pallas_call | solution.py:656
  (32 shorter events, 0.1 us)
Async XLA Ops:
  0.0 2.2 %collective-permute-start.9 = (bf16[64,4096]{1,0:T(8,128)(2,1)}, bf16[64,4096]{1,0:T(8,128)(2,1)S(1)}, u32[]{:S(2)}, u32[]{:S(2)}) collective-permute-start(bf16[64,4096]{1,0:T(8,128)(2,1)} %own_ref.2), channel_id=1, source_target_pairs={{0,1},{1,0},{2,3},{3,2},{4,5},{5,4},{6,7},{7,6},{8,9},{9,8},{10,11... | collective-permute-start | bytes 1572872 | tf_op jit(solution)/shard_map/ppermute | solution.py:29
  2.2 5.8 %copy-start.2 = (bf16[64,4096]{1,0:T(8,128)(2,1)}, bf16[64,4096]{1,0:T(8,128)(2,1)S(1)}, u32[]{:S(2)}) copy-start(bf16[64,4096]{1,0:T(8,128)(2,1)S(1)} %collective-permute-done.9.other_ref) | copy-start | bytes 1572868
  2.2 25.5 %collective-permute-start.16 = (bf16[512,4096]{1,0:T(8,128)(2,1)}, bf16[512,4096]{1,0:T(8,128)(2,1)}, u32[]{:S(2)}, u32[]{:S(2)}) collective-permute-start(bf16[512,4096]{1,0:T(8,128)(2,1)} %own_ref.3), channel_id=1, source_target_pairs={{0,1},{1,0},{2,3},{3,2},{4,5},{5,4},{6,7},{7,6},{8,9},{9,8},{10,11... | collective-permute-start | bytes 12582920 | tf_op jit(solution)/shard_map/ppermute | solution.py:29
  2.6 5.2 %copy-start.8 = (s32[4,4096]{1,0:T(4,128)S(1)}, s32[4,4096]{1,0:T(4,128)}, u32[]{:S(2)}) copy-start(s32[4,4096]{1,0:T(4,128)} %shuf_own.1) | copy-start | bytes 196612
  2.6 5.5 %copy-start.1 = (bf16[64,4096]{1,0:T(8,128)(2,1)S(1)}, bf16[64,4096]{1,0:T(8,128)(2,1)}, u32[]{:S(2)}) copy-start(bf16[64,4096]{1,0:T(8,128)(2,1)} %own_ref.2) | copy-start | bytes 1572868
  2.6 5.5 %copy-start.4 = (s32[1024]{0:T(1024)S(1)}, s32[1024]{0:T(1024)}, u32[]{:S(2)}) copy-start(s32[1024]{0:T(1024)} %param.13) | copy-start | bytes 12292
  2.6 5.5 %copy-start.5 = (s32[1024]{0:T(1024)S(1)}, s32[1024]{0:T(1024)}, u32[]{:S(2)}) copy-start(s32[1024]{0:T(1024)} %param.14) | copy-start | bytes 12292
  2.6 5.5 %copy-start.7 = (s32[15]{0:T(128)S(1)}, s32[15]{0:T(128)}, u32[]{:S(2)}) copy-start(s32[15]{0:T(128)} %bounds_ref.1) | copy-start | bytes 184
  2.6 25.1 %copy-start.10 = (f32[4096]{0:T(1024)S(1)}, f32[4096]{0:T(1024)}, u32[]{:S(2)}) copy-start(f32[4096]{0:T(1024)} %param.11) | copy-start | bytes 49156
  2.6 17.6 %collective-permute-start.14 = (f32[1,4096]{1,0:T(1,128)}, f32[1,4096]{1,0:T(1,128)S(1)}, u32[]{:S(2)}, u32[]{:S(2)}) collective-permute-start(f32[1,4096]{1,0:T(1,128)} %bitcast.14), channel_id=1, source_target_pairs={{0,1},{1,0},{2,3},{3,2},{4,5},{5,4},{6,7},{7,6},{8,9},{9,8},{10,11... | collective-permute-start | bytes 49160 | tf_op jit(solution)/shard_map/ppermute | solution.py:29
  7.4 55.3 %copy-start.12 = (f32[8,512]{1,0:T(8,128)}, f32[8,512]{1,0:T(8,128)S(1)}, u32[]{:S(2)}) copy-start(f32[8,512]{1,0:T(8,128)S(1)} %local_moments.2.sums_own) | copy-start | bytes 49156
  7.4 8.4 %collective-permute-start.8 = (f32[8,512]{1,0:T(8,128)S(1)}, f32[8,512]{1,0:T(8,128)S(1)}, u32[]{:S(2)}, u32[]{:S(2)}) collective-permute-start(f32[8,512]{1,0:T(8,128)S(1)} %local_moments.2.sums_own), channel_id=1, source_target_pairs={{0,1},{1,0},{2,3},{3,2},{4,5},{5,4},{6,7},{7,6},{8,9},{9,8},{10,11... | collective-permute-start | bytes 49160 | tf_op jit(solution)/shard_map/ppermute | solution.py:29
  7.8 14.9 %collective-permute-start.15 = (s32[4,4096]{1,0:T(4,128)S(1)}, s32[4,4096]{1,0:T(4,128)S(1)}, u32[]{:S(2)}, u32[]{:S(2)}) collective-permute-start(s32[4,4096]{1,0:T(4,128)S(1)} %copy-done.8), channel_id=1, source_target_pairs={{0,1},{1,0},{2,3},{3,2},{4,5},{5,4},{6,7},{7,6},{8,9},{9,8},{10,11... | collective-permute-start | bytes 196616 | tf_op jit(solution)/shard_map/ppermute | solution.py:29
  10.9 51.8 %collective-permute-start.11 = (bf16[64,8192]{1,0:T(8,128)(2,1)S(1)}, bf16[64,8192]{1,0:T(8,128)(2,1)S(1)}, u32[]{:S(2)}, u32[]{:S(2)}) collective-permute-start(bf16[64,8192]{1,0:T(8,128)(2,1)S(1)} %get-tuple-element.352.rest_0_), channel_id=1, source_target_pairs={{0,4},{2,6},{4,8},{6,10},{8,12},{10,14},{12,16},{14,18},{16,20},{1... | collective-permute-start | bytes 3145736 | tf_op jit(solution)/shard_map/ppermute | solution.py:618
  15.8 46.9 %copy-start.13 = (f32[8,512]{1,0:T(8,128)}, f32[8,512]{1,0:T(8,128)S(1)}, u32[]{:S(2)}) copy-start(f32[8,512]{1,0:T(8,128)S(1)} %collective-permute-done.8.sums_other) | copy-start | bytes 49156
  15.8 46.9 %collective-permute-start.10 = (bf16[64,8192]{1,0:T(8,128)(2,1)S(1)}, bf16[64,8192]{1,0:T(8,128)(2,1)}, u32[]{:S(2)}, u32[]{:S(2)}) collective-permute-start(bf16[64,8192]{1,0:T(8,128)(2,1)S(1)} %get-tuple-element.352.rest_0_), channel_id=1, source_target_pairs={{0,2},{2,4},{4,6},{6,8},{8,10},{10,12},{12,14},{14,16},{16,18},{18... | collective-permute-start | bytes 3145736 | tf_op jit(solution)/shard_map/ppermute | solution.py:618
  20.2 42.5 %copy-start.11 = (f32[1,4096]{1,0:T(1,128)}, f32[1,4096]{1,0:T(1,128)S(1)}, u32[]{:S(2)}) copy-start(f32[1,4096]{1,0:T(1,128)S(1)} %collective-permute-done.14.env_other) | copy-start | bytes 49156
  20.2 42.5 %collective-permute-start.13 = (bf16[16,8192]{1,0:T(8,128)(2,1)}, bf16[16,8192]{1,0:T(8,128)(2,1)S(1)}, u32[]{:S(2)}, u32[]{:S(2)}) collective-permute-start(bf16[16,8192]{1,0:T(8,128)(2,1)} %get-tuple-element.354), channel_id=1, source_target_pairs={{0,8},{2,10},{4,12},{6,14},{8,16},{10,18},{12,20},{14,22},{16,24},... | collective-permute-start | bytes 786440 | tf_op jit(solution)/shard_map/ppermute | solution.py:618
  22.7 0.6 copy-start.9
  23.3 39.4 %collective-permute-start.12 = (bf16[32,8192]{1,0:T(8,128)(2,1)}, bf16[32,8192]{1,0:T(8,128)(2,1)S(1)}, u32[]{:S(2)}, u32[]{:S(2)}) collective-permute-start(bf16[32,8192]{1,0:T(8,128)(2,1)} %get-tuple-element.353), channel_id=1, source_target_pairs={{0,6},{2,8},{4,10},{6,12},{8,14},{10,16},{12,18},{14,20},{16,22},{... | collective-permute-start | bytes 1572872 | tf_op jit(solution)/shard_map/ppermute | solution.py:618
  62.8 5.5 %collective-permute-start.17 = (bf16[64,8192]{1,0:T(8,128)(2,1)}, bf16[64,8192]{1,0:T(8,128)(2,1)}, u32[]{:S(2)}, u32[]{:S(2)}) collective-permute-start(bf16[64,8192]{1,0:T(8,128)(2,1)} %collective-permute-done.10.rest_1_), channel_id=1, source_target_pairs={{0,1},{1,0},{2,3},{3,2},{4,5},{5,4},{6,7},{7,6},{8,9},{9,8},{10,11... | collective-permute-start | bytes 3145736 | tf_op jit(solution)/shard_map/ppermute | solution.py:29
  62.8 5.4 %collective-permute-start.18 = (bf16[64,8192]{1,0:T(8,128)(2,1)S(1)}, bf16[64,8192]{1,0:T(8,128)(2,1)}, u32[]{:S(2)}, u32[]{:S(2)}) collective-permute-start(bf16[64,8192]{1,0:T(8,128)(2,1)S(1)} %collective-permute-done.11.rest_2_), channel_id=1, source_target_pairs={{0,1},{1,0},{2,3},{3,2},{4,5},{5,4},{6,7},{7,6},{8,9},{9,8},{10,11... | collective-permute-start | bytes 3145736 | tf_op jit(solution)/shard_map/ppermute | solution.py:29
  63.3 4.9 %collective-permute-start.19 = (bf16[32,8192]{1,0:T(8,128)(2,1)S(1)}, bf16[32,8192]{1,0:T(8,128)(2,1)}, u32[]{:S(2)}, u32[]{:S(2)}) collective-permute-start(bf16[32,8192]{1,0:T(8,128)(2,1)S(1)} %collective-permute-done.12.rest_3_), channel_id=1, source_target_pairs={{0,1},{1,0},{2,3},{3,2},{4,5},{5,4},{6,7},{7,6},{8,9},{9,8},{10,11... | collective-permute-start | bytes 1572872 | tf_op jit(solution)/shard_map/ppermute | solution.py:29
  63.4 3.5 %collective-permute-start.20 = (bf16[16,8192]{1,0:T(8,128)(2,1)S(1)}, bf16[16,8192]{1,0:T(8,128)(2,1)S(1)}, u32[]{:S(2)}, u32[]{:S(2)}) collective-permute-start(bf16[16,8192]{1,0:T(8,128)(2,1)S(1)} %collective-permute-done.13.rest_4_), channel_id=1, source_target_pairs={{0,1},{1,0},{2,3},{3,2},{4,5},{5,4},{6,7},{7,6},{8,9},{9,8},{10,11... | collective-permute-start | bytes 786440 | tf_op jit(solution)/shard_map/ppermute | solution.py:29
  82.4 0.6 copy-start
  94.2 1.3 %copy-start.3 = (f32[16,8,128]{2,1,0:T(8,128)}, f32[16,8,128]{2,1,0:T(8,128)S(1)}, u32[]{:S(2)}) copy-start(f32[16,8,128]{2,1,0:T(8,128)S(1)} %all_to_all.5.own_ref) | copy-start | bytes 196612
  94.2 1.3 %collective-permute-start.21 = (f32[16,8,128]{2,1,0:T(8,128)S(1)}, f32[16,8,128]{2,1,0:T(8,128)S(1)}, u32[]{:S(2)}, u32[]{:S(2)}) collective-permute-start(f32[16,8,128]{2,1,0:T(8,128)S(1)} %all_to_all.5.own_ref), channel_id=1, source_target_pairs={{0,1},{1,0},{2,3},{3,2},{4,5},{5,4},{6,7},{7,6},{8,9},{9,8},{10,11... | collective-permute-start | bytes 196616 | tf_op jit(solution)/shard_map/ppermute | solution.py:29
  95.4 0.6 copy-start.6

commit v16 on v15

--- a/solution.py
+++ b/solution.py
@@ -11,7 +11,7 @@
 HALF_BLK = 7
 LANES = 128
 ROWS_STEP = 16
-UNROLL = 32
+UNROLL = 16
 DEPTH = 2048
 SIDE = 2 * LANES
 CHUNK = 1024
@@ -133,7 +133,7 @@
 
     def read_rows(first):
         base = pl.multiple_of(first * words, UNROLL * words)
-        return [table[pl.ds(base + u * words, words), :] for u in range(UNROLL)]
+        return tuple(table[pl.ds(base + u * words, words), :] for u in range(UNROLL))
 
     def write_rows(q, first, held):
         for u in range(UNROLL):
@@ -172,6 +172,7 @@
             at = pl.multiple_of(i * side, side)
             e = env_ref[:, pl.ds((k * CHUNK) % half + at, side)]
             behind = pl.multiple_of(jnp.maximum(k * CHUNK + at - side, 0), side)
+            held = read_rows(behind)
             for c in range(words):
                 rows = pl.ds(c * LANES, LANES)
                 x = geno[k % depth, rows, pl.ds(at, side)].astype(jnp.float32)
@@ -183,7 +184,10 @@
                 )
                 for g in range(groups):
                     first = pl.multiple_of(behind + (c * groups + g) * UNROLL, UNROLL)
-                    write_rows(0, first, read_rows(first))
+                    if c * groups + g + 1 < words * groups:
+                        later = read_rows(first + UNROLL)
+                    write_rows(0, first, held)
+                    held = later
                 table[pl.ds((k * CHUNK + at) * words + c, side, stride=words), :] = t
                 first_stage[k % 2, pl.ds(at, side), pl.ds(c * LANES, LANES)] = t.astype(
                     jnp.bfloat16
@@ -203,22 +207,25 @@
     lax.fori_loop(0, side // UNROLL, last_block, 0)
 
     count = 0
+    pair = 2 * UNROLL
     for q in range(1, labels + 1):
+        held = read_rows(0)
         for k in range(chunks):
             if count >= 2:
                 save((count - 2) // chunks, (count - 2) % chunks).wait()
 
-            def step(i, carry, k=k, q=q):
-                at = pl.multiple_of(i * UNROLL, UNROLL)
-                first = pl.multiple_of(k * CHUNK + at, UNROLL)
-                if q < labels:
-                    held = read_rows(first)
-                parts = narrowed(q - 1, first, UNROLL)
-                if q < labels:
-                    write_rows(q, first, held)
+            def step(i, held, k=k, q=q):
+                at = pl.multiple_of(i * pair, pair)
+                first = pl.multiple_of(k * CHUNK + at, pair)
+                middle = read_rows(first + UNROLL)
+                parts = narrowed(q - 1, first, pair)
+                write_rows(q, first, held)
+                after = jnp.minimum(first + pair, all_samples - UNROLL)
+                held = read_rows(pl.multiple_of(after, UNROLL))
+                write_rows(q, first + UNROLL, middle)
                 for c in range(words):
-                    stage[k % 2, pl.ds(at, UNROLL), pl.ds(c * LANES, LANES)] = parts[c]
-                return carry
+                    stage[k % 2, pl.ds(at, pair), pl.ds(c * LANES, LANES)] = parts[c]
+                return held
 
             def wide(i, carry, k=k, q=q):
                 at = pl.multiple_of(i * side, side)
@@ -228,7 +235,7 @@
                 return carry
 
             if q < labels:
-                lax.fori_loop(0, CHUNK // UNROLL, step, 0)
+                held = lax.fori_loop(0, CHUNK // pair, step, held)
             else:
                 lax.fori_loop(0, CHUNK // side, wide, 0)
             save(q - 1, k).start()

time: 98 us -> 98.2 us (level)
  transfers between devices with their start and end apart: 14 -> 14, of which waited for: 4 -> 4; matrix products, arithmetic and copies ran while one was open for 0% -> 0% of each run, Pallas kernels for 43% -> 44%
where the time goes in v16:
time: 98.2 us; the launch traced here: 97.8 us
  Pallas kernels  58.3 us (59%)
  starting transfers between devices  18.8 us (19%)
  blocking collectives  10.4 us (11%)
  waiting for transfers between devices  7.42 us (8%)
  local copies, waits for them, and re-layouts  1.85 us (2%)
    pallas_call x1, Pallas kernels, snp_side(): pl.pallas_call(functools.partial(snp_side_kernel, labels=labels), out_sha...  35.2 us
    ppermute x4, starting transfers between devices, travel(): return lax.ppermute(payload, ('genome', 'sample'), pairs)  16.1 us
    pallas_call x1, Pallas kernels, products(): pl.pallas_call(functools.partial(product_kernel, caps=caps, labels=labels...  14.1 us
    all_to_all x1, blocking collectives, shards(): gathered = lax.all_to_all(found, 'genome', 0, 0, tiled=True)  10.4 us
    ppermute x10, waiting for transfers between devices, swapped(): lax.ppermute(x, 'sample', [(i, (i + 1) % count) for i in range(count)])  7.41 us
    pallas_call x1, Pallas kernels, local_moments(): pl.pallas_call(moments_kernel, grid=(half // chunk,), out_shape=jax.Shape...  4.54 us
    pallas_call x1, Pallas kernels, select(): pl.pallas_call(functools.partial(select_kernel, caps=caps, blocks_dev=blo...  2.87 us
    ppermute x10, starting transfers between devices, swapped(): lax.ppermute(x, 'sample', [(i, (i + 1) % count) for i in range(count)])  2.68 us
  transfers between devices with their start and end apart: 14, of which 4 were waited for; matrix products, arithmetic and copies ran while one was open for 0% of the time, Pallas kernels for 44%

profile of v16, /device:TPU:0, one launch (start us, length us, event | category | flops | bytes accessed | tf_op | source)
XLA Modules:
  0.0 97.8 jit_solution(17605563213087656841)
XLA Ops:
  0.0 0.5 collective-permute-start.9
  0.5 1.7 %collective-permute-done.9.other_ref = bf16[64,4096]{1,0:T(8,128)(2,1)S(1)} collective-permute-done((bf16[64,4096]{1,0:T(8,128)(2,1)}, bf16[64,4096]{1,0:T(8,128)(2,1)S(1)}, u32[]{:S(2)}, u32[]{:S(2)}) %collective-permute-start.9) | collective-permute-done | bytes 524320 | tf_op jit(solution)/shard_map/ppermute | solution.py:29
  2.2 0.4 collective-permute-start.16
  2.6 0.2 collective-permute-start.14
  2.8 4.5 %local_moments.2.sums_own = f32[8,512]{1,0:T(8,128)S(1)} custom-call(bf16[512,4096]{1,0:T(8,128)(2,1)} %own_ref.3, f32[1,4096]{1,0:T(1,128)} %bitcast.15), custom_call_target="tpu_custom_call" | custom-call | flops 5000000000 | bytes 4194304 | tf_op jit(solution)/shard_map/local_moments/pallas_call | solution.py:67
  7.4 0.4 collective-permute-start.8
  7.8 0.1 collective-permute-start.15
  8.0 0.1 pad_add_fusion.pos_ref
  8.0 2.9 %select.6 = (s32[1]{0:T(128)}, s32[8,640]{1,0:T(8,128)S(1)}, bf16[64,8192]{1,0:T(8,128)(2,1)S(1)}, bf16[32,8192]{1,0:T(8,128)(2,1)}, bf16[16,8192]{1,0:T(8,128)(2,1)}) custom-call(s32[1]{0:T(128)} %constant.18.clone.1.round_ref, s32[2]{0:T(128)S(1)} %pad_add_fusion.pos_ref, s32[15]{0:T(128)S(1)} %copy-done.7, s32[8,128]{1,0:T(8,128)S(1)} %bitcast.10, ...), custom_call_target="tpu_custom_call" | custom-call | tf_op jit(solution)/shard_map/select/pallas_call | solution.py:409
  10.9 4.9 %collective-permute-start.11 = (bf16[64,8192]{1,0:T(8,128)(2,1)S(1)}, bf16[64,8192]{1,0:T(8,128)(2,1)S(1)}, u32[]{:S(2)}, u32[]{:S(2)}) collective-permute-start(bf16[64,8192]{1,0:T(8,128)(2,1)S(1)} %get-tuple-element.352.rest_0_), channel_id=1, source_target_pairs={{0,4},{2,6},{4,8},{6,10},{8,12},{10,14},{12,16},{14,18},{16,20},{1... | collective-permute-start | bytes 3145736 | tf_op jit(solution)/shard_map/ppermute | solution.py:625
  15.8 4.4 %collective-permute-start.10 = (bf16[64,8192]{1,0:T(8,128)(2,1)S(1)}, bf16[64,8192]{1,0:T(8,128)(2,1)}, u32[]{:S(2)}, u32[]{:S(2)}) collective-permute-start(bf16[64,8192]{1,0:T(8,128)(2,1)S(1)} %get-tuple-element.352.rest_0_), channel_id=1, source_target_pairs={{0,2},{2,4},{4,6},{6,8},{8,10},{10,12},{12,14},{14,16},{16,18},{18... | collective-permute-start | bytes 3145736 | tf_op jit(solution)/shard_map/ppermute | solution.py:625
  20.2 0.0 collective-permute-done.14.env_other
  20.2 2.5 %collective-permute-start.13 = (bf16[16,8192]{1,0:T(8,128)(2,1)}, bf16[16,8192]{1,0:T(8,128)(2,1)S(1)}, u32[]{:S(2)}, u32[]{:S(2)}) collective-permute-start(bf16[16,8192]{1,0:T(8,128)(2,1)} %get-tuple-element.354), channel_id=1, source_target_pairs={{0,8},{2,10},{4,12},{6,14},{8,16},{10,18},{12,20},{14,22},{16,24},... | collective-permute-start | bytes 786440 | tf_op jit(solution)/shard_map/ppermute | solution.py:625
  22.7 0.0 collective-permute-done.15.shuf_other
  22.7 0.6 copy-done.9
  23.3 4.4 %collective-permute-start.12 = (bf16[32,8192]{1,0:T(8,128)(2,1)}, bf16[32,8192]{1,0:T(8,128)(2,1)S(1)}, u32[]{:S(2)}, u32[]{:S(2)}) collective-permute-start(bf16[32,8192]{1,0:T(8,128)(2,1)} %get-tuple-element.353), channel_id=1, source_target_pairs={{0,6},{2,8},{4,10},{6,12},{8,14},{10,16},{12,18},{14,20},{16,22},{... | collective-permute-start | bytes 1572872 | tf_op jit(solution)/shard_map/ppermute | solution.py:625
  27.7 0.0 collective-permute-done.16.other_ref
  27.7 35.2 %snp_side.6 = (bf16[8192,512]{1,0:T(8,128)(2,1)}, bf16[8192,512]{1,0:T(8,128)(2,1)}, bf16[8192,256]{1,0:T(8,128)(2,1)}) custom-call(s32[1]{0:T(128)} %bitcast.3.core_ref, f32[1,4096]{1,0:T(1,128)S(1)} %bitcast.16, f32[1,4096]{1,0:T(1,128)S(1)} %collective-permute-done.14.env_other, f32[8,512]{1,0:T(8,128)S(1)} %local_moments.2.sums_own, ...), custom_call_target="tpu_custom_call" | custom-call | flops 40000000000 | bytes 60000000 | tf_op jit(solution)/shard_map/snp_side/pallas_call | solution.py:257
  63.0 0.0 collective-permute-done.13.rest_4_
  63.0 0.1 collective-permute-start.17
  63.1 0.5 collective-permute-start.18
  63.6 0.1 collective-permute-start.19
  63.7 0.4 collective-permute-start.20
  64.1 3.1 %collective-permute-done.20.rest_8_ = bf16[16,8192]{1,0:T(8,128)(2,1)S(1)} collective-permute-done((bf16[16,8192]{1,0:T(8,128)(2,1)S(1)}, bf16[16,8192]{1,0:T(8,128)(2,1)S(1)}, u32[]{:S(2)}, u32[]{:S(2)}) %collective-permute-start.20) | collective-permute-done | bytes 262176 | tf_op jit(solution)/shard_map/ppermute | solution.py:29
  67.2 1.3 %collective-permute-done.19.rest_7_ = bf16[32,8192]{1,0:T(8,128)(2,1)} collective-permute-done((bf16[32,8192]{1,0:T(8,128)(2,1)S(1)}, bf16[32,8192]{1,0:T(8,128)(2,1)}, u32[]{:S(2)}, u32[]{:S(2)}) %collective-permute-start.19) | collective-permute-done | bytes 524320 | tf_op jit(solution)/shard_map/ppermute | solution.py:29
  68.5 14.1 %products.6 = (f32[16,8,128]{2,1,0:T(8,128)S(1)}, f32[8,64]{1,0:T(8,128)S(1)}) custom-call(s32[2]{0:T(128)S(1)} %pad_add_fusion.pos_ref, f32[8,512]{1,0:T(8,128)} %copy-done.12, f32[8,512]{1,0:T(8,128)} %copy-done.13, s32[8,640]{1,0:T(8,128)S(1)} %get-tuple-element.351.plan_ref, bf16[64,8192]{1,0:T(8,128)(2,1)S(1)} %get-tuple-element.352.rest_0_, ...), custom_call_target="tpu_custom_call" | custom-call | flops 8724152320 | bytes 27787264 | tf_op jit(solution)/shard_map/products/pallas_call | solution.py:569
  82.7 0.6 copy-done
  83.2 0.8 while.14
  84.1 10.4 %all_to_all.5.own_ref = f32[16,8,128]{2,1,0:T(8,128)S(1)} all-to-all(f32[16,8,128]{2,1,0:T(8,128)S(1)} %get-tuple-element.368), channel_id=1, replica_groups=mesh['genome'=16,'sample'=2] {'genome'}, dimensions={0} | all-to-all | bytes 131072 | tf_op jit(solution)/shard_map/all_to_all | solution.py:662
  94.4 1.3 %collective-permute-done.21.other_ref = f32[16,8,128]{2,1,0:T(8,128)S(1)} collective-permute-done((f32[16,8,128]{2,1,0:T(8,128)S(1)}, f32[16,8,128]{2,1,0:T(8,128)S(1)}, u32[]{:S(2)}, u32[]{:S(2)}) %collective-permute-start.21) | collective-permute-done | bytes 65568 | tf_op jit(solution)/shard_map/ppermute | solution.py:29
  95.7 0.6 copy-done.6
  96.3 1.5 %finish.1 = f32[5,64]{1,0:T(8,128)} custom-call(f32[16,8,128]{2,1,0:T(8,128)} %copy-done.3, f32[16,8,128]{2,1,0:T(8,128)} %copy-done.6, f32[8,64]{1,0:T(8,128)} %copy-done), custom_call_target="tpu_custom_call" | custom-call | tf_op jit(solution)/shard_map/finish/pallas_call | solution.py:663
  (32 shorter events, 0.1 us)
Async XLA Ops:
  0.0 2.2 %collective-permute-start.9 = (bf16[64,4096]{1,0:T(8,128)(2,1)}, bf16[64,4096]{1,0:T(8,128)(2,1)S(1)}, u32[]{:S(2)}, u32[]{:S(2)}) collective-permute-start(bf16[64,4096]{1,0:T(8,128)(2,1)} %own_ref.2), channel_id=1, source_target_pairs={{0,1},{1,0},{2,3},{3,2},{4,5},{5,4},{6,7},{7,6},{8,9},{9,8},{10,11... | collective-permute-start | bytes 1572872 | tf_op jit(solution)/shard_map/ppermute | solution.py:29
  2.2 5.8 %copy-start.2 = (bf16[64,4096]{1,0:T(8,128)(2,1)}, bf16[64,4096]{1,0:T(8,128)(2,1)S(1)}, u32[]{:S(2)}) copy-start(bf16[64,4096]{1,0:T(8,128)(2,1)S(1)} %collective-permute-done.9.other_ref) | copy-start | bytes 1572868
  2.2 25.5 %collective-permute-start.16 = (bf16[512,4096]{1,0:T(8,128)(2,1)}, bf16[512,4096]{1,0:T(8,128)(2,1)}, u32[]{:S(2)}, u32[]{:S(2)}) collective-permute-start(bf16[512,4096]{1,0:T(8,128)(2,1)} %own_ref.3), channel_id=1, source_target_pairs={{0,1},{1,0},{2,3},{3,2},{4,5},{5,4},{6,7},{7,6},{8,9},{9,8},{10,11... | collective-permute-start | bytes 12582920 | tf_op jit(solution)/shard_map/ppermute | solution.py:29
  2.6 5.2 %copy-start.8 = (s32[4,4096]{1,0:T(4,128)S(1)}, s32[4,4096]{1,0:T(4,128)}, u32[]{:S(2)}) copy-start(s32[4,4096]{1,0:T(4,128)} %shuf_own.1) | copy-start | bytes 196612
  2.6 5.5 %copy-start.1 = (bf16[64,4096]{1,0:T(8,128)(2,1)S(1)}, bf16[64,4096]{1,0:T(8,128)(2,1)}, u32[]{:S(2)}) copy-start(bf16[64,4096]{1,0:T(8,128)(2,1)} %own_ref.2) | copy-start | bytes 1572868
  2.6 5.5 %copy-start.4 = (s32[1024]{0:T(1024)S(1)}, s32[1024]{0:T(1024)}, u32[]{:S(2)}) copy-start(s32[1024]{0:T(1024)} %param.13) | copy-start | bytes 12292
  2.6 5.5 %copy-start.5 = (s32[1024]{0:T(1024)S(1)}, s32[1024]{0:T(1024)}, u32[]{:S(2)}) copy-start(s32[1024]{0:T(1024)} %param.14) | copy-start | bytes 12292
  2.6 5.5 %copy-start.7 = (s32[15]{0:T(128)S(1)}, s32[15]{0:T(128)}, u32[]{:S(2)}) copy-start(s32[15]{0:T(128)} %bounds_ref.1) | copy-start | bytes 184
  2.6 25.1 %copy-start.10 = (f32[4096]{0:T(1024)S(1)}, f32[4096]{0:T(1024)}, u32[]{:S(2)}) copy-start(f32[4096]{0:T(1024)} %param.11) | copy-start | bytes 49156
  2.6 17.6 %collective-permute-start.14 = (f32[1,4096]{1,0:T(1,128)}, f32[1,4096]{1,0:T(1,128)S(1)}, u32[]{:S(2)}, u32[]{:S(2)}) collective-permute-start(f32[1,4096]{1,0:T(1,128)} %bitcast.14), channel_id=1, source_target_pairs={{0,1},{1,0},{2,3},{3,2},{4,5},{5,4},{6,7},{7,6},{8,9},{9,8},{10,11... | collective-permute-start | bytes 49160 | tf_op jit(solution)/shard_map/ppermute | solution.py:29
  7.4 55.6 %copy-start.12 = (f32[8,512]{1,0:T(8,128)}, f32[8,512]{1,0:T(8,128)S(1)}, u32[]{:S(2)}) copy-start(f32[8,512]{1,0:T(8,128)S(1)} %local_moments.2.sums_own) | copy-start | bytes 49156
  7.4 8.4 %collective-permute-start.8 = (f32[8,512]{1,0:T(8,128)S(1)}, f32[8,512]{1,0:T(8,128)S(1)}, u32[]{:S(2)}, u32[]{:S(2)}) collective-permute-start(f32[8,512]{1,0:T(8,128)S(1)} %local_moments.2.sums_own), channel_id=1, source_target_pairs={{0,1},{1,0},{2,3},{3,2},{4,5},{5,4},{6,7},{7,6},{8,9},{9,8},{10,11... | collective-permute-start | bytes 49160 | tf_op jit(solution)/shard_map/ppermute | solution.py:29
  7.8 14.9 %collective-permute-start.15 = (s32[4,4096]{1,0:T(4,128)S(1)}, s32[4,4096]{1,0:T(4,128)S(1)}, u32[]{:S(2)}, u32[]{:S(2)}) collective-permute-start(s32[4,4096]{1,0:T(4,128)S(1)} %copy-done.8), channel_id=1, source_target_pairs={{0,1},{1,0},{2,3},{3,2},{4,5},{5,4},{6,7},{7,6},{8,9},{9,8},{10,11... | collective-permute-start | bytes 196616 | tf_op jit(solution)/shard_map/ppermute | solution.py:29
  10.9 52.1 %collective-permute-start.11 = (bf16[64,8192]{1,0:T(8,128)(2,1)S(1)}, bf16[64,8192]{1,0:T(8,128)(2,1)S(1)}, u32[]{:S(2)}, u32[]{:S(2)}) collective-permute-start(bf16[64,8192]{1,0:T(8,128)(2,1)S(1)} %get-tuple-element.352.rest_0_), channel_id=1, source_target_pairs={{0,4},{2,6},{4,8},{6,10},{8,12},{10,14},{12,16},{14,18},{16,20},{1... | collective-permute-start | bytes 3145736 | tf_op jit(solution)/shard_map/ppermute | solution.py:625
  15.8 47.1 %copy-start.13 = (f32[8,512]{1,0:T(8,128)}, f32[8,512]{1,0:T(8,128)S(1)}, u32[]{:S(2)}) copy-start(f32[8,512]{1,0:T(8,128)S(1)} %collective-permute-done.8.sums_other) | copy-start | bytes 49156
  15.8 47.2 %collective-permute-start.10 = (bf16[64,8192]{1,0:T(8,128)(2,1)S(1)}, bf16[64,8192]{1,0:T(8,128)(2,1)}, u32[]{:S(2)}, u32[]{:S(2)}) collective-permute-start(bf16[64,8192]{1,0:T(8,128)(2,1)S(1)} %get-tuple-element.352.rest_0_), channel_id=1, source_target_pairs={{0,2},{2,4},{4,6},{6,8},{8,10},{10,12},{12,14},{14,16},{16,18},{18... | collective-permute-start | bytes 3145736 | tf_op jit(solution)/shard_map/ppermute | solution.py:625
  20.2 42.8 %copy-start.11 = (f32[1,4096]{1,0:T(1,128)}, f32[1,4096]{1,0:T(1,128)S(1)}, u32[]{:S(2)}) copy-start(f32[1,4096]{1,0:T(1,128)S(1)} %collective-permute-done.14.env_other) | copy-start | bytes 49156
  20.2 42.8 %collective-permute-start.13 = (bf16[16,8192]{1,0:T(8,128)(2,1)}, bf16[16,8192]{1,0:T(8,128)(2,1)S(1)}, u32[]{:S(2)}, u32[]{:S(2)}) collective-permute-start(bf16[16,8192]{1,0:T(8,128)(2,1)} %get-tuple-element.354), channel_id=1, source_target_pairs={{0,8},{2,10},{4,12},{6,14},{8,16},{10,18},{12,20},{14,22},{16,24},... | collective-permute-start | bytes 786440 | tf_op jit(solution)/shard_map/ppermute | solution.py:625
  22.7 0.6 copy-start.9
  23.3 39.7 %collective-permute-start.12 = (bf16[32,8192]{1,0:T(8,128)(2,1)}, bf16[32,8192]{1,0:T(8,128)(2,1)S(1)}, u32[]{:S(2)}, u32[]{:S(2)}) collective-permute-start(bf16[32,8192]{1,0:T(8,128)(2,1)} %get-tuple-element.353), channel_id=1, source_target_pairs={{0,6},{2,8},{4,10},{6,12},{8,14},{10,16},{12,18},{14,20},{16,22},{... | collective-permute-start | bytes 1572872 | tf_op jit(solution)/shard_map/ppermute | solution.py:625
  63.0 5.5 %collective-permute-start.17 = (bf16[64,8192]{1,0:T(8,128)(2,1)}, bf16[64,8192]{1,0:T(8,128)(2,1)}, u32[]{:S(2)}, u32[]{:S(2)}) collective-permute-start(bf16[64,8192]{1,0:T(8,128)(2,1)} %collective-permute-done.10.rest_1_), channel_id=1, source_target_pairs={{0,1},{1,0},{2,3},{3,2},{4,5},{5,4},{6,7},{7,6},{8,9},{9,8},{10,11... | collective-permute-start | bytes 3145736 | tf_op jit(solution)/shard_map/ppermute | solution.py:29
  63.1 5.4 %collective-permute-start.18 = (bf16[64,8192]{1,0:T(8,128)(2,1)S(1)}, bf16[64,8192]{1,0:T(8,128)(2,1)}, u32[]{:S(2)}, u32[]{:S(2)}) collective-permute-start(bf16[64,8192]{1,0:T(8,128)(2,1)S(1)} %collective-permute-done.11.rest_2_), channel_id=1, source_target_pairs={{0,1},{1,0},{2,3},{3,2},{4,5},{5,4},{6,7},{7,6},{8,9},{9,8},{10,11... | collective-permute-start | bytes 3145736 | tf_op jit(solution)/shard_map/ppermute | solution.py:29
  63.6 4.9 %collective-permute-start.19 = (bf16[32,8192]{1,0:T(8,128)(2,1)S(1)}, bf16[32,8192]{1,0:T(8,128)(2,1)}, u32[]{:S(2)}, u32[]{:S(2)}) collective-permute-start(bf16[32,8192]{1,0:T(8,128)(2,1)S(1)} %collective-permute-done.12.rest_3_), channel_id=1, source_target_pairs={{0,1},{1,0},{2,3},{3,2},{4,5},{5,4},{6,7},{7,6},{8,9},{9,8},{10,11... | collective-permute-start | bytes 1572872 | tf_op jit(solution)/shard_map/ppermute | solution.py:29
  63.7 3.5 %collective-permute-start.20 = (bf16[16,8192]{1,0:T(8,128)(2,1)S(1)}, bf16[16,8192]{1,0:T(8,128)(2,1)S(1)}, u32[]{:S(2)}, u32[]{:S(2)}) collective-permute-start(bf16[16,8192]{1,0:T(8,128)(2,1)S(1)} %collective-permute-done.13.rest_4_), channel_id=1, source_target_pairs={{0,1},{1,0},{2,3},{3,2},{4,5},{5,4},{6,7},{7,6},{8,9},{9,8},{10,11... | collective-permute-start | bytes 786440 | tf_op jit(solution)/shard_map/ppermute | solution.py:29
  82.6 0.6 copy-start
  94.4 1.3 %copy-start.3 = (f32[16,8,128]{2,1,0:T(8,128)}, f32[16,8,128]{2,1,0:T(8,128)S(1)}, u32[]{:S(2)}) copy-start(f32[16,8,128]{2,1,0:T(8,128)S(1)} %all_to_all.5.own_ref) | copy-start | bytes 196612
  94.4 1.3 %collective-permute-start.21 = (f32[16,8,128]{2,1,0:T(8,128)S(1)}, f32[16,8,128]{2,1,0:T(8,128)S(1)}, u32[]{:S(2)}, u32[]{:S(2)}) collective-permute-start(f32[16,8,128]{2,1,0:T(8,128)S(1)} %all_to_all.5.own_ref), channel_id=1, source_target_pairs={{0,1},{1,0},{2,3},{3,2},{4,5},{5,4},{6,7},{7,6},{8,9},{9,8},{10,11... | collective-permute-start | bytes 196616 | tf_op jit(solution)/shard_map/ppermute | solution.py:29
  95.7 0.6 copy-start.6
